TPU v7x, 32 devices: a whole 2x2x4 slice. The times are simulated.
32 devices in a mesh: narrow: 2 (over x), wide: 16 (over z, y, core).
Axes of the slice: x: 2, y: 2, z: 4, core: 2. Of those that a mesh axis runs over, the one named last changes fastest.
Arguments:
- features: float32 [512, 49, 512], P(('narrow', 'wide')), may hold values from -6 to 6
- cotangent: bfloat16 [512, 49, 512], P(('narrow', 'wide')), may hold values from -6 to 6
- counts: int32 [32], P(('narrow', 'wide')), may hold values from 1 to 16, as said below
- hidden_weight: float32 [512, 2048], P(None, 'wide'), may hold values from -0.25 to 0.25
- hidden_bias: float32 [2048], replicated, may hold values from -3 to 3
- output_weight: float32 [2048, 512], P('wide'), may hold values from -0.125 to 0.125
- vectors: float32 [7, 512], replicated
- hidden_moment: float32 [512, 2048], P(None, 'wide'), may hold values from -32 to 32
- hidden_square: float32 [512, 2048], P(None, 'wide'), may hold values from 2.25792 to 9.03168
- bias_moment: float32 [2048], replicated, may hold values from -32 to 32
- bias_square: float32 [2048], replicated, may hold values from 2.25792 to 9.03168
- output_moment: float32 [2048, 512], P('wide'), may hold values from -56 to 56
- output_square: float32 [2048, 512], P('wide'), may hold values from 6.272 to 25.088
- vector_moment: float32 [7, 512], replicated, may hold values from -80 to 80
- vector_square: float32 [7, 512], replicated, may hold values from 16.05632 to 65.2288
Outputs:
- block_out: float32 [512, 49, 512], P(('narrow', 'wide'))
- input_grad: float32 [512, 49, 512], P(('narrow', 'wide'))
- hidden_weight_new: float32 [512, 2048], P(None, 'wide')
- hidden_moment_new: float32 [512, 2048], P(None, 'wide')
- hidden_square_new: float32 [512, 2048], P(None, 'wide')
- hidden_bias_new: float32 [2048], replicated
- bias_moment_new: float32 [2048], replicated
- bias_square_new: float32 [2048], replicated
- output_weight_new: float32 [2048, 512], P('wide')
- output_moment_new: float32 [2048, 512], P('wide')
- output_square_new: float32 [2048, 512], P('wide')
- vectors_new: float32 [7, 512], replicated
- vector_moment_new: float32 [7, 512], replicated
- vector_square_new: float32 [7, 512], replicated
Inputs may be any that keep to these rules, and one draw needn't show every extreme that they name: Device i holds counts[i] valid images, in its first slots; the remaining slots of its 16 are padding; the last device's slots are all valid.
All inputs are finite; a program needn't handle non-finite values.
Results may differ from a plain program's by a relative error of at most 0.0062.
Values may be sent and summed in bfloat16 or wider, within the bound.
No kernel may reach another device: no remote copies, remote signals or barrier semaphores. Data moves between devices by JAX's collectives and lax.ppermute only.
A program may use at most 320 MiB of HBM per device.

v0:
```python
import math

import jax
import jax.numpy as jnp
from jax import lax
from jax.sharding import PartitionSpec as P

SIDE = 7
STEP = 5


norm_epsilon = 1e-05
first_decay = 0.9
second_decay = 0.999
adam_epsilon = 1e-08
weight_shrink = 0.05


def pool_matrix(side):
    places = jnp.arange(side * side, dtype=jnp.int32)
    place_row = places // side
    place_col = places % side
    nearby = (jnp.abs(place_row[:, None] - place_row[None, :]) <= 1) & (
        jnp.abs(place_col[:, None] - place_col[None, :]) <= 1
    )
    nearby = nearby.astype(jnp.float32)
    return nearby / jnp.sum(nearby, axis=1, keepdims=True)


def norm_parts(values, gain, shift):
    centre = jnp.mean(values, axis=(1, 2), keepdims=True)
    spread = jnp.mean((values - centre) ** 2, axis=(1, 2), keepdims=True)
    inverse = lax.rsqrt(spread + norm_epsilon)
    scaled = (values - centre) * inverse
    return (scaled * gain + shift, scaled, inverse)


def norm_back(upstream, scaled, inverse):
    first_mean = jnp.mean(upstream, axis=(1, 2), keepdims=True)
    second_mean = jnp.mean(upstream * scaled, axis=(1, 2), keepdims=True)
    return inverse * (upstream - first_mean - scaled * second_mean)


def gelu_slope(values):
    return 0.5 * (1.0 + lax.erf(values / math.sqrt(2.0))) + values * jnp.exp(
        -0.5 * values * values
    ) / math.sqrt(2.0 * math.pi)


def contract_rows(left, right):
    return lax.dot_general(
        left, right, (((0,), (0,)), ((), ())), preferred_element_type=jnp.float32
    )


def contract_cols(left, right):
    return lax.dot_general(
        left, right, (((1,), (1,)), ((), ())), preferred_element_type=jnp.float32
    )


def adamw_update(param, grad, moment, square, rate, shrink):
    moment_new = first_decay * moment + (1.0 - first_decay) * grad
    square_new = second_decay * square + (1.0 - second_decay) * grad * grad
    moment_hat = moment_new / (1.0 - first_decay**STEP)
    square_hat = square_new / (1.0 - second_decay**STEP)
    param_new = param - rate * (moment_hat / (jnp.sqrt(square_hat) + adam_epsilon) + shrink * param)
    return (param_new, moment_new, square_new)


def local(
    features,
    cotangent,
    counts,
    hidden_weight,
    hidden_bias,
    output_weight,
    vectors,
    hidden_moment,
    hidden_square,
    bias_moment,
    bias_square,
    output_moment,
    output_square,
    vector_moment,
    vector_square,
):
    images, pixels, width = features.shape
    rows = images * pixels
    units = hidden_weight.shape[1]
    pool = pool_matrix(SIDE)
    valid = (jnp.arange(images, dtype=jnp.int32) < counts[0]).astype(jnp.float32)
    weighted = cotangent.astype(jnp.float32) * valid[:, None, None]
    normed, first_scaled, first_inverse = norm_parts(features, vectors[0], vectors[1])
    mixed = jnp.einsum("pq,iqc->ipc", pool, normed, precision=lax.Precision.HIGHEST) - normed
    middle = features + vectors[2] * mixed
    second, second_scaled, second_inverse = norm_parts(middle, vectors[3], vectors[4])
    second_low = second.reshape(rows, width).astype(jnp.bfloat16)
    hidden_low = hidden_weight.astype(jnp.bfloat16)
    output_low = output_weight.astype(jnp.bfloat16)
    branch_grad = (weighted * vectors[5]).reshape(rows, width)
    branch_low = branch_grad.astype(jnp.bfloat16)
    offset = lax.axis_index("wide") * units
    local_bias = lax.dynamic_slice_in_dim(hidden_bias, offset, units)
    hidden_all = (
        jnp.dot(
            lax.all_gather(second_low, "wide", axis=0, tiled=True),
            hidden_low,
            preferred_element_type=jnp.float32,
        )
        + local_bias
    )
    active_all = jax.nn.gelu(hidden_all, approximate=False).astype(jnp.bfloat16)
    slope_all = gelu_slope(hidden_all)
    block = active_all
    branch = lax.psum_scatter(
        jnp.dot(block, output_low, preferred_element_type=jnp.float32),
        "wide",
        scatter_dimension=0,
        tiled=True,
    )
    piece = lax.all_gather(branch_low, "wide", axis=0, tiled=True)
    block = active_all
    output_total = contract_rows(block, piece)
    active_grad = contract_cols(piece, output_low)
    hidden_grad = (active_grad * slope_all).astype(jnp.bfloat16)
    local_bias_grad = jnp.sum(hidden_grad.astype(jnp.float32), axis=0)
    bias_part = lax.dynamic_update_slice_in_dim(
        jnp.zeros(hidden_bias.shape, jnp.float32), local_bias_grad, offset, 0
    )
    block = hidden_grad
    second_grad = lax.psum_scatter(
        contract_cols(block, hidden_low), "wide", scatter_dimension=0, tiled=True
    )
    block = hidden_grad
    hidden_part = contract_rows(lax.all_gather(second_low, "wide", axis=0, tiled=True), block)
    branch_full = (branch + vectors[6]).reshape(images, pixels, width)
    block_out = middle + vectors[5] * branch_full
    grad_scale_two = jnp.sum(weighted * branch_full, axis=(0, 1))
    grad_shift_out = jnp.sum(branch_grad, axis=0)
    second_grad = second_grad.reshape(images, pixels, width)
    grad_gain_two = jnp.sum(second_grad * second_scaled, axis=(0, 1))
    grad_shift_two = jnp.sum(second_grad, axis=(0, 1))
    middle_grad = weighted + norm_back(second_grad * vectors[3], second_scaled, second_inverse)
    grad_scale_one = jnp.sum(middle_grad * mixed, axis=(0, 1))
    mixed_grad = middle_grad * vectors[2]
    normed_grad = (
        jnp.einsum("qp,iqc->ipc", pool, mixed_grad, precision=lax.Precision.HIGHEST) - mixed_grad
    )
    grad_gain_one = jnp.sum(normed_grad * first_scaled, axis=(0, 1))
    grad_shift_one = jnp.sum(normed_grad, axis=(0, 1))
    input_grad = middle_grad + norm_back(normed_grad * vectors[0], first_scaled, first_inverse)
    vector_part = jnp.stack(
        [
            grad_gain_one,
            grad_shift_one,
            grad_scale_one,
            grad_gain_two,
            grad_shift_two,
            grad_scale_two,
            grad_shift_out,
        ]
    )
    vector_grad, bias_grad = lax.psum((vector_part, bias_part), ("narrow", "wide"))
    hidden_grad_sum, output_grad_sum = lax.psum((hidden_part, output_total), "narrow")
    hidden_new = adamw_update(
        hidden_weight, hidden_grad_sum, hidden_moment, hidden_square, 0.04, weight_shrink
    )
    bias_new = adamw_update(hidden_bias, bias_grad, bias_moment, bias_square, 0.2, 0.0)
    output_new = adamw_update(
        output_weight, output_grad_sum, output_moment, output_square, 0.02, weight_shrink
    )
    vector_new = adamw_update(vectors, vector_grad, vector_moment, vector_square, 0.3, 0.0)
    return (
        block_out,
        input_grad,
        hidden_new[0],
        hidden_new[1],
        hidden_new[2],
        bias_new[0],
        bias_new[1],
        bias_new[2],
        output_new[0],
        output_new[1],
        output_new[2],
        vector_new[0],
        vector_new[1],
        vector_new[2],
    )


def solution(mesh):
    in_specs = (
        P(("narrow", "wide"), None, None),
        P(("narrow", "wide"), None, None),
        P(("narrow", "wide")),
        P(None, "wide"),
        P(),
        P("wide", None),
        P(),
        P(None, "wide"),
        P(None, "wide"),
        P(),
        P(),
        P("wide", None),
        P("wide", None),
        P(),
        P(),
    )
    out_specs = (
        P(("narrow", "wide"), None, None),
        P(("narrow", "wide"), None, None),
        P(None, "wide"),
        P(None, "wide"),
        P(None, "wide"),
        P(),
        P(),
        P(),
        P("wide", None),
        P("wide", None),
        P("wide", None),
        P(),
        P(),
        P(),
    )
    return jax.shard_map(local, mesh=mesh, in_specs=in_specs, out_specs=out_specs, check_vma=False)
```

profile of v0, /device:TPU:0, one launch (start us, length us, event | category | flops | bytes accessed | tf_op | source)
XLA Modules:
  0.0 851.8 jit_solution(7420678193047710889)
XLA Ops:
  7.2 0.0 copy-start.1
  7.2 0.0 copy-start.4
  7.2 0.0 all-gather.3.cloned.1.call-start
  7.3 1.9 reduce_sum.160
  9.1 2.4 multiply_reduce_fusion.7
  11.6 0.0 copy-done.4
  11.6 0.1 convert_reduce_fusion.1
  11.7 0.0 copy-done.1
  11.7 5.0 fusion.55
  16.7 0.4 multiply_reduce_fusion.6
  17.1 1.3 add_convert_fusion
  18.4 2.3 convert_element_type.44
  20.8 0.0 all-gather.3.cloned.1.call-update
  20.8 0.0 all-gather.5.cloned.1.call-start
  21.5 2.6 fusion.17
  24.1 2.4 convert_element_type.51
  26.4 0.0 all-gather.5.cloned.1.call-update
  26.5 0.2 all-reduce.4.cloned.1.call-start
  26.7 0.0 copy-done.7
  26.7 0.1 dynamic_slice.3
  26.8 99.2 %all-gather.3.cloned.1.call-done = bf16[12544,512]{1,0:T(8,128)(2,1)} async-done(((bf16[784,512]{1,0:T(8,128)(2,1)}), bf16[12544,512]{1,0:T(8,128)(2,1)}) %all-gather.3.cloned.1.call-update) | async-done | bytes 12845072 | tf_op jit(solution)/shard_map/all_gather | solution.py:107
  126.0 18.2 %fusion.3 = (bf16[12544,128]{1,0:T(8,128)(2,1)}, f32[12544,128]{1,0:T(8,128)}) fusion(f32[128]{0:T(128)S(1)} %dynamic_slice.3, bf16[12544,512]{1,0:T(8,128)(2,1)} %all-gather.3.cloned.1.call-done, f32[512,128]{1,0:T(8,128)} %param.18), kind=kOutput, calls=%fused_computation.7 | convolution fusion | flops 1750204416 | bytes 22741504 | tf_op jit(solution)/shard_map/dot_general | solution.py:106
  144.2 84.7 %all-gather.5.cloned.1.call-done = bf16[12544,512]{1,0:T(8,128)(2,1)} async-done(((bf16[784,512]{1,0:T(8,128)(2,1)}), bf16[12544,512]{1,0:T(8,128)(2,1)}) %all-gather.5.cloned.1.call-update) | async-done | bytes 12845072 | tf_op jit(solution)/shard_map/all_gather | solution.py:122
  228.9 8.3 fusion.58
  237.2 1.0 copy-done
  238.3 0.0 copy-done.3
  238.3 1.9 copy-done.10
  240.2 4.2 convert_reduce_fusion
  244.4 0.0 copy-start.2
  244.4 1.7 copy-done.2
  246.1 7.3 fusion.57
  253.4 0.0 all-reduce.4.cloned.1.call-update
  253.4 0.0 reduce-scatter.5.cloned.1.call-start
  253.4 14.0 %fusion.35 = f32[12544,512]{1,0:T(8,128)} fusion(bf16[12544,128]{1,0:T(8,128)(2,1)} %copy-done.2, f32[512,128]{1,0:T(8,128)} %param.18), kind=kOutput, calls=%fused_computation.73 | convolution fusion | flops 1644232704 | bytes 29163520 | tf_op jit(solution)/shard_map/dot_general | solution.py:57
  267.5 0.0 reduce-scatter.5.cloned.1.call-update
  267.5 0.0 reduce-scatter.3.cloned.1.call-start
  267.5 14.0 %fusion.33 = f32[12544,512]{1,0:T(8,128)} fusion(bf16[12544,128]{1,0:T(8,128)(2,1)} %get-tuple-element.97, f32[128,512]{1,0:T(8,128)} %param.20), kind=kOutput, calls=%fused_computation.71 | convolution fusion | flops 1644232704 | bytes 29163520 | tf_op jit(solution)/shard_map/dot_general | solution.py:117
  281.5 0.0 reduce-scatter.3.cloned.1.call-update
  281.6 0.5 dynamic_update_slice.3
  282.1 2.2 multiply_subtract_fusion.1
  284.2 2.2 multiply_subtract_fusion
  286.4 246.8 %reduce-scatter.5.cloned.1.call-done = f32[784,512]{1,0:T(8,128)} async-done(((f32[12544,512]{1,0:T(8,128)}), f32[784,512]{1,0:T(8,128)}) %reduce-scatter.5.cloned.1.call-update) | async-done | bytes 1605648 | tf_op jit(solution)/shard_map/reduce_scatter | solution.py:132
  533.3 1.7 fusion.50
  534.9 0.1 reduce_sum.166
  535.0 0.1 reduce_sum.167
  535.1 2.9 reshape.131
  538.0 2.2 multiply_reduce_fusion.1
  540.2 244.9 %reduce-scatter.3.cloned.1.call-done = f32[784,512]{1,0:T(8,128)} async-done(((f32[12544,512]{1,0:T(8,128)}), f32[784,512]{1,0:T(8,128)}) %reduce-scatter.3.cloned.1.call-update) | async-done | bytes 1605648 | tf_op jit(solution)/shard_map/reduce_scatter | solution.py:116
  785.1 2.8 broadcast_add_fusion
  787.9 2.9 reshape.130
  790.8 4.4 fusion.16
  795.1 2.1 copy.45
  797.2 3.6 multiply_reduce_fusion.3
  800.8 1.5 multiply_add_fusion
  802.3 0.0 copy-start.8
  802.3 0.0 copy-start.9
  802.3 0.0 copy-start.5
  802.3 0.0 copy-start.6
  802.3 2.1 copy.46
  804.5 39.6 %all-reduce = (f32[2048]{0:T(1024)S(1)}, f32[7,512]{1,0:T(8,128)S(1)}) all-reduce(f32[2048]{0:T(1024)S(1)} %dynamic_update_slice.3, f32[7,512]{1,0:T(8,128)S(1)} %stack.31), channel_id=1, replica_groups=mesh['narrow'=2,'wide'=16] {'narrow','wide'}, use_global_device_ids=true, to_apply=%region_14.15 | all-reduce | flops 5632 | bytes 45056 | tf_op jit(solution)/shard_map/psum | solution.py:164
  844.0 0.0 copy-done.8
  844.0 0.0 copy-done.9
  844.0 0.6 multiply_subtract_fusion.3
  844.7 0.6 multiply_subtract_fusion.2
  (20 shorter events, 0.1 us)
Async XLA Ops:
  7.2 4.5 copy-start.1
  7.2 4.4 copy-start.4
  7.2 118.8 %all-gather.3.cloned.1.call-start = ((), (), s32[]{:S(2)}) async-start(), calls=%async_computation.2 | async-start | bytes 13647872 | tf_op jit(solution)/shard_map/all_gather | solution.py:107
  18.4 8.3 copy-start.7
  20.8 208.1 %all-gather.5.cloned.1.call-start = ((), (), s32[]{:S(2)}) async-start(), calls=%async_computation.4 | async-start | bytes 13647872 | tf_op jit(solution)/shard_map/all_gather | solution.py:122
  26.5 255.6 %all-reduce.4.cloned.1.call-start = ((), (), s32[]{:S(2)}) async-start(), calls=%async_computation.6 | async-start | bytes 1048576 | tf_op jit(solution)/shard_map/psum | solution.py:165
  228.9 9.4 %copy-start = (bf16[12544,512]{1,0:T(8,128)(2,1)S(1)}, bf16[12544,512]{1,0:T(8,128)(2,1)}, u32[]{:S(2)}) copy-start(bf16[12544,512]{1,0:T(8,128)(2,1)} %all-gather.5.cloned.1.call-done) | copy-start | bytes 38535172
  228.9 9.4 %copy-start.3 = (f32[128,512]{1,0:T(8,128)S(1)}, f32[128,512]{1,0:T(8,128)}, u32[]{:S(2)}) copy-start(f32[128,512]{1,0:T(8,128)} %param.20) | copy-start | bytes 786436
  228.9 11.3 %copy-start.10 = (f32[12544,128]{1,0:T(8,128)S(1)}, f32[12544,128]{1,0:T(8,128)}, u32[]{:S(2)}) copy-start(f32[12544,128]{1,0:T(8,128)} %get-tuple-element.98) | copy-start | bytes 19267588
  244.4 1.7 copy-start.2
  253.4 279.9 %reduce-scatter.5.cloned.1.call-start = ((), (), s32[]{:S(2)}) async-start(), calls=%async_computation.5 | async-start | bytes 27295744 | tf_op jit(solution)/shard_map/reduce_scatter | solution.py:132
  267.5 517.6 %reduce-scatter.3.cloned.1.call-start = ((), (), s32[]{:S(2)}) async-start(), calls=%async_computation.3 | async-start | bytes 27295744 | tf_op jit(solution)/shard_map/reduce_scatter | solution.py:116
  802.3 41.7 %copy-start.8 = (f32[2048]{0:T(1024)S(1)}, f32[2048]{0:T(1024)}, u32[]{:S(2)}) copy-start(f32[2048]{0:T(1024)} %param.24) | copy-start | bytes 24580
  802.3 41.7 %copy-start.9 = (f32[2048]{0:T(1024)S(1)}, f32[2048]{0:T(1024)}, u32[]{:S(2)}) copy-start(f32[2048]{0:T(1024)} %param.25) | copy-start | bytes 24580
  802.3 42.3 %copy-start.5 = (f32[7,512]{1,0:T(8,128)S(1)}, f32[7,512]{1,0:T(8,128)}, u32[]{:S(2)}) copy-start(f32[7,512]{1,0:T(8,128)} %param.28) | copy-start | bytes 43012
  802.3 42.3 %copy-start.6 = (f32[7,512]{1,0:T(8,128)S(1)}, f32[7,512]{1,0:T(8,128)}, u32[]{:S(2)}) copy-start(f32[7,512]{1,0:T(8,128)} %param.29) | copy-start | bytes 43012
Sparse Core Ops, SparseCore 0:
  20.9 105.0 all-gather.2
  128.3 100.5 all-gather.4
  253.5 26.9 all-reduce.3
  285.0 248.1 reduce-scatter.4
  537.8 247.2 reduce-scatter.2
where the time goes:
time: 852 us
  waiting for transfers between devices  676 us (79%)
  matrix products  74.7 us (9%)
  blocking collectives  39.6 us (5%)
  other arithmetic  26.9 us (3%)
  local copies, waits for them, and re-layouts  20 us (2%)
  between operations  14.6 us (2%)
    reduce_scatter x1, waiting for transfers between devices, local(): lax.psum_scatter(contract_cols(block, hidden_low), 'wide', scatter_dimens...  247 us
    reduce_scatter x1, waiting for transfers between devices, local(): lax.psum_scatter(jnp.dot(block, output_low, preferred_element_type=jnp.fl...  245 us
    all_gather x1, waiting for transfers between devices, local(): lax.all_gather(second_low, 'wide', axis=0, tiled=True)  99.2 us
    all_gather x1, waiting for transfers between devices, local(): piece = lax.all_gather(branch_low, 'wide', axis=0, tiled=True)  84.7 us
    psum x1, blocking collectives, local(): lax.psum((vector_part, bias_part), ('narrow', 'wide'))  39.6 us
    dot_general x2, matrix products, contract_cols(): lax.dot_general(left, right, (((1,), (1,)), ((), ())), preferred_element_...  18.3 us
    dot_general x1, matrix products, local(): jnp.dot(lax.all_gather(second_low, 'wide', axis=0, tiled=True), hidden_lo...  18.2 us
  transfers between devices with their start and end apart: 5, of which 4 were waited for; matrix products, arithmetic and copies ran while one was open for 7% of the time, Pallas kernels for 0%

commit v1 on v0

--- a/solution.py
+++ b/solution.py
@@ -1,8 +1,11 @@
+import functools
 import math
 
 import jax
 import jax.numpy as jnp
 from jax import lax
+from jax.experimental import pallas as pl
+from jax.experimental.pallas import tpu as pltpu
 from jax.sharding import PartitionSpec as P
 
 SIDE = 7
@@ -189,6 +192,420 @@
     )
 
 
+BLOCKS = 8
+PAIRS = BLOCKS // 2
+f32 = jnp.float32
+bf16 = jnp.bfloat16
+VMEM = pl.BlockSpec(memory_space=pltpu.VMEM)
+SMEM = pl.BlockSpec(memory_space=pltpu.SMEM)
+
+
+def row_total(values):
+    return jnp.sum(values, axis=1, keepdims=True)
+
+
+def span(i):
+    return min(i + 1, SIDE - 1) - max(i - 1, 0) + 1
+
+
+def near_share(p):
+    return 1.0 / (span(p // SIDE) * span(p % SIDE))
+
+
+def along_row(load, p):
+    c = p % SIDE
+    total = load(p)
+    if c > 0:
+        total = total + load(p - 1)
+    if c < SIDE - 1:
+        total = total + load(p + 1)
+    return total
+
+
+def along_col(load, p):
+    r = p // SIDE
+    total = load(p)
+    if r > 0:
+        total = total + load(p - SIDE)
+    if r < SIDE - 1:
+        total = total + load(p + SIDE)
+    return total
+
+
+def valid_gate(counts_ref, shape):
+    slots = lax.broadcasted_iota(jnp.int32, shape, 0)
+    return jnp.where(slots < counts_ref[0], 1.0, 0.0)
+
+
+def pre_kernel(counts_ref, x_ref, cot_ref, vec_ref, sb_ref, q_ref, stat_ref, d_ref, h_ref):
+    pixels, images, width = x_ref.shape
+    size = pixels * width
+    zero = jnp.zeros((images, width), f32)
+
+    def loop(body, init):
+        return lax.fori_loop(0, pixels, body, init, unroll=7)
+
+    mu1 = row_total(loop(lambda p, s: s + x_ref[p], zero)) / size
+
+    def centre(p, s):
+        d = x_ref[p] - mu1
+        d_ref[p] = d
+        return s + d * d
+
+    r1 = lax.rsqrt(row_total(loop(centre, zero)) / size + norm_epsilon)
+    for p in range(pixels):
+        h_ref[p] = along_row(lambda i: d_ref[i], p)
+    lift = vec_ref[2:3, :] * (r1 * vec_ref[0:1, :])
+    total = zero
+    for p in range(pixels):
+        q = along_col(lambda i: h_ref[i], p) * near_share(p) - d_ref[p]
+        q_ref[p] = q
+        total = total + (x_ref[p] + lift * q)
+    mu2 = row_total(total) / size
+
+    def spread(p, s):
+        d = x_ref[p] + lift * q_ref[p] - mu2
+        d_ref[p] = d
+        return s + d * d
+
+    r2 = lax.rsqrt(row_total(loop(spread, zero)) / size + norm_epsilon)
+    scale = r2 * vec_ref[3:4, :]
+    shift = jnp.broadcast_to(vec_ref[4:5, :], (images, width))
+    gate = valid_gate(counts_ref, (images, width)) * vec_ref[5:6, :]
+
+    def finish(p, carry):
+        sb_ref[0, p] = (d_ref[p] * scale + shift).astype(bf16)
+        sb_ref[1, p] = (cot_ref[p].astype(f32) * gate).astype(bf16)
+        return carry
+
+    loop(finish, 0)
+    for i, stat in enumerate((mu1, r1, mu2, r2)):
+        stat_ref[i] = jnp.broadcast_to(stat, (images, 128))
+
+
+def normal_parts(h):
+    a = jnp.abs(h)
+    t = 1.0 / (1.0 + (0.3275911 / math.sqrt(2.0)) * a)
+    series = 0.5 * 1.061405429
+    for c in (-1.453152027, 1.421413741, -0.284496736, 0.254829592):
+        series = series * t + 0.5 * c
+    e = jnp.exp(-0.5 * h * h)
+    tail = series * t * e
+    phi = jnp.where(h < 0.0, tail, 1.0 - tail)
+    return phi, phi + h * (e * (1.0 / math.sqrt(2.0 * math.pi)))
+
+
+def dot(left, right, dims):
+    return lax.dot_general(left, right, (dims, ((), ())), preferred_element_type=f32)
+
+
+def hidden_kernel(place_ref, own_ref, oth_ref, bias_ref, *refs):
+    w_refs, (act_ref, slope_ref, grad_ref, w_ref, h_ref) = refs[:BLOCKS], refs[BLOCKS:]
+    j = pl.program_id(0)
+
+    @pl.when(j == 0)
+    def _():
+        for k in range(BLOCKS):
+            w_ref[k // 2, :, (k % 2) * 128 : (k % 2 + 1) * 128] = w_refs[k][...]
+
+    bias = jnp.concatenate(
+        [bias_ref[pl.ds(place_ref[2 * j], 1), :], bias_ref[pl.ds(place_ref[2 * j + 1], 1), :]], axis=1
+    )
+    weight = w_ref[j]
+    grad = None
+    for r, sb_ref in enumerate((own_ref, oth_ref)):
+        h_ref[...] = dot(sb_ref[0], weight, ((1,), (0,))) + bias
+
+        def tile(i, carry):
+            rows = pl.ds(pl.multiple_of(i * 112, 16), 112)
+            h = h_ref[rows, :]
+            phi, slope = normal_parts(h)
+            act_ref[r, rows, :] = (h * phi).astype(bf16)
+            slope_ref[r, rows, :] = slope.astype(bf16)
+            return carry
+
+        lax.fori_loop(0, h_ref.shape[0] // 112, tile, 0)
+        part = dot(sb_ref[1], act_ref[r], ((0,), (0,)))
+        grad = part if grad is None else grad + part
+    for k in range(2):
+        grad_ref[k] = grad[:, k * 128 : (k + 1) * 128].astype(bf16)
+
+
+def slope_kernel(place_ref, own_ref, oth_ref, slope_ref, *refs):
+    w_refs, (hg_ref, grad_ref, sums_ref, w_ref) = refs[:BLOCKS], refs[BLOCKS:]
+    j = pl.program_id(0)
+
+    @pl.when(j == 0)
+    def _():
+        sums_ref[...] = jnp.zeros_like(sums_ref)
+        for k in range(BLOCKS):
+            w_ref[k // 2, :, (k % 2) * 128 : (k % 2 + 1) * 128] = w_refs[k][...]
+
+    weight = w_ref[j]
+    grad = sums = None
+    for r, sb_ref in enumerate((own_ref, oth_ref)):
+        back = dot(sb_ref[1], weight, ((1,), (0,)))
+        low = (back * slope_ref[r].astype(f32)).astype(bf16)
+        hg_ref[r] = low
+        column = jnp.sum(low.astype(f32), axis=0, keepdims=True)
+        part = dot(sb_ref[0], low, ((0,), (0,)))
+        grad = part if grad is None else grad + part
+        sums = column if sums is None else sums + column
+    for k in range(2):
+        grad_ref[k] = grad[:, k * 128 : (k + 1) * 128].astype(bf16)
+        sums_ref[pl.ds(place_ref[2 * j + k], 1), :] = sums[:, k * 128 : (k + 1) * 128]
+
+
+def back_kernel(act_ref, hg_ref, *refs):
+    a_refs, b_refs, (out_ref,) = refs[:BLOCKS], refs[BLOCKS : 2 * BLOCKS], refs[2 * BLOCKS :]
+    for i, (left_ref, w_refs) in enumerate(((act_ref, b_refs), (hg_ref, a_refs))):
+        total = None
+        for j in range(PAIRS):
+            weight = jnp.concatenate([w_refs[2 * j][...], w_refs[2 * j + 1][...]], axis=1)
+            part = dot(left_ref[0, :, j * 256 : (j + 1) * 256], weight, ((1,), (1,)))
+            total = part if total is None else total + part
+        out_ref[i] = total.astype(out_ref.dtype)
+
+
+def post_kernel(
+    counts_ref, x_ref, cot_ref, vec_ref, q_ref, stat_ref, own_ref, got_ref,
+    out_ref, grad_ref, sums_ref, t_ref, h_ref,
+):
+    pixels, images, width = x_ref.shape
+    size = pixels * width
+    zero = jnp.zeros((images, width), f32)
+    gate = valid_gate(counts_ref, (images, width))
+    mu1, r1, mu2, r2 = (stat_ref[i][:, 0:1] for i in range(4))
+    gain1, mix, gain2, scale, lower = (vec_ref[i : i + 1, :] for i in (0, 2, 3, 5, 6))
+    lift = mix * (r1 * gain1)
+
+    def loop(body, init):
+        return lax.fori_loop(0, pixels, body, init, unroll=7)
+
+    def column(values):
+        return jnp.sum(values, axis=0, keepdims=True)
+
+    def first(p, carry):
+        g_scale, g_lower, g_gain2, g_shift2 = carry
+        middle = x_ref[p] + lift * q_ref[p]
+        branch = own_ref[0, p] + got_ref[0, p].astype(f32) + lower
+        out_ref[p] = middle + scale * branch
+        weighted = cot_ref[p].astype(f32) * gate
+        back = own_ref[1, p] + got_ref[1, p].astype(f32)
+        h2 = (middle - mu2) * r2
+        return (g_scale + weighted * branch, g_lower + weighted, g_gain2 + back * h2, g_shift2 + back)
+
+    g_scale, g_lower, g_gain2, g_shift2 = loop(first, (zero,) * 4)
+    mean2 = row_total(g_shift2 * gain2) / size
+    mean2h = row_total(g_gain2 * gain2) / size
+
+    def second(p, g_mix):
+        middle = x_ref[p] + lift * q_ref[p]
+        back = own_ref[1, p] + got_ref[1, p].astype(f32)
+        h2 = (middle - mu2) * r2
+        grad = cot_ref[p].astype(f32) * gate + r2 * (back * gain2 - mean2 - h2 * mean2h)
+        grad_ref[p] = grad
+        t_ref[p] = grad * mix
+        return g_mix + grad * q_ref[p]
+
+    g_mix = loop(second, zero) * (r1 * gain1)
+    for p in range(pixels):
+        h_ref[p] = along_row(lambda i: t_ref[i] * near_share(i), p)
+    g_gain1 = g_shift1 = zero
+    for p in range(pixels):
+        ng = along_col(lambda i: h_ref[i], p) - t_ref[p]
+        t_ref[p] = ng
+        g_gain1 = g_gain1 + ng * ((x_ref[p] - mu1) * r1)
+        g_shift1 = g_shift1 + ng
+    mean1 = row_total(g_shift1 * gain1) / size
+    mean1h = row_total(g_gain1 * gain1) / size
+
+    def third(p, carry):
+        h1 = (x_ref[p] - mu1) * r1
+        grad_ref[p] = grad_ref[p] + r1 * (t_ref[p] * gain1 - mean1 - h1 * mean1h)
+        return carry
+
+    loop(third, 0)
+    for i, total in enumerate((g_gain1, g_shift1, g_mix, g_gain2, g_shift2, g_scale, g_lower * scale)):
+        sums_ref[i : i + 1, :] = column(total)
+
+
+def call(kernel, outs, ins, scratch=(), vmem=48, **kw):
+    return pl.pallas_call(
+        kernel,
+        out_shape=outs,
+        scratch_shapes=list(scratch),
+        compiler_params=pltpu.CompilerParams(vmem_limit_bytes=vmem * 2**20),
+        **kw,
+    )(*ins)
+
+
+def struct(shape, dtype=f32):
+    return jax.ShapeDtypeStruct(shape, dtype)
+
+
+def joint(change):
+    return [(n * 16 + w, n * 16 + change(n, w)) for n in range(2) for w in range(16)]
+
+
+BOTH = ("narrow", "wide")
+
+
+def flip(values, bit):
+    return lax.ppermute(values, "wide", [(w, w ^ bit) for w in range(16)])
+
+
+def far(values):
+    return lax.ppermute(values, BOTH, joint(lambda n, w: w ^ (12 if n else 8)))
+
+
+def across(values):
+    return lax.ppermute(values, "narrow", [(0, 1), (1, 0)])
+
+
+def gather_blocks(own):
+    z1 = flip(own, 4)
+    zf = far(own)
+    y0 = flip(own, 2)
+    y1 = flip(z1, 2)
+    yf = flip(zf, 2)
+    zo = across(zf)
+    yo = across(yf)
+    return [own, z1, zf, zo, y0, y1, yf, yo]
+
+
+def reduce_blocks(g):
+    x = across(jnp.stack([g[3], g[7]]))
+    y = flip(g[4:6], 2)
+    wide = lambda v: v.astype(f32)
+    yf = flip((wide(g[6]) + wide(x[1])).astype(bf16), 2)
+    z1 = flip((wide(g[1]) + wide(y[1])).astype(bf16), 4)
+    zf = far((wide(g[2]) + wide(x[0]) + wide(yf)).astype(bf16))
+    own = (wide(g[0]) + wide(y[0]) + wide(z1) + wide(zf)).astype(bf16)
+    return wide(own) + wide(across(own))
+
+
+def sum_all(values):
+    for bit in (1, 2):
+        values = values + flip(values, bit)
+    values = values + across(values)
+    for bit in (4, 8):
+        values = values + flip(values, bit)
+    return values
+
+
+def local_tree(
+    features,
+    cotangent,
+    counts,
+    hidden_weight,
+    hidden_bias,
+    output_weight,
+    vectors,
+    hidden_moment,
+    hidden_square,
+    bias_moment,
+    bias_square,
+    output_moment,
+    output_square,
+    vector_moment,
+    vector_square,
+):
+    images, pixels, width = features.shape
+    rows = images * pixels
+    units = hidden_weight.shape[1]
+    near, wide = lax.axis_index("narrow"), lax.axis_index("wide")
+    first_far = jnp.where(near == 0, 8, 12)
+    marks = jnp.stack([0 * first_far, 0 * first_far + 4, first_far, 20 - first_far])
+    place = wide ^ jnp.concatenate([marks, marks ^ 2])
+    place = place.astype(jnp.int32)
+
+    x = features.transpose(1, 0, 2)
+    cot = cotangent.transpose(1, 0, 2)
+    a_blocks = gather_blocks(hidden_weight.astype(bf16))
+    b_blocks = gather_blocks(output_weight.T.astype(bf16))
+    big = struct((pixels, images, width))
+    keep = pltpu.VMEM((pixels, images, width), f32)
+    sb, q, stat = call(
+        pre_kernel,
+        [struct((2, pixels, images, width), bf16), big, struct((4, images, 128))],
+        (counts, x, cot, vectors),
+        [keep, keep],
+        in_specs=[SMEM, VMEM, VMEM, VMEM],
+        out_specs=[VMEM] * 3,
+    )
+    sb = sb.reshape(2, rows, width)
+    other = flip(sb, 1)
+    bias = hidden_bias.reshape(-1, 128)
+    tall = pl.BlockSpec((2, rows, 256), lambda j: (0, 0, j))
+    pair = pl.BlockSpec((2, width, 128), lambda j: (j, 0, 0))
+    hidden = struct((2, rows, BLOCKS * 128), bf16)
+    grads = struct((BLOCKS, width, 128), bf16)
+    w_keep = pltpu.VMEM((PAIRS, width, 256), bf16)
+    active, slope, out_part = call(
+        hidden_kernel,
+        [hidden, hidden, grads],
+        (place, sb, other, bias, *a_blocks),
+        [w_keep, pltpu.VMEM((rows, 256), f32)],
+        grid=(PAIRS,),
+        in_specs=[SMEM] + [VMEM] * (3 + BLOCKS),
+        out_specs=[tall, tall, pair],
+    )
+    hidden_grad, hidden_part, bias_part = call(
+        slope_kernel,
+        [hidden, grads, struct(bias.shape)],
+        (place, sb, other, slope, *b_blocks),
+        [w_keep],
+        grid=(PAIRS,),
+        in_specs=[SMEM, VMEM, VMEM, tall] + [VMEM] * BLOCKS,
+        out_specs=[tall, pair, pl.BlockSpec(bias.shape, lambda j: (0, 0))],
+    )
+
+    def back(r, dtype):
+        half = pl.BlockSpec((1, rows, BLOCKS * 128), lambda j: (r, 0, 0))
+        return call(
+            back_kernel,
+            struct((2, rows, width), dtype),
+            (active, hidden_grad, *a_blocks, *b_blocks),
+            grid=(1,),
+            in_specs=[half, half] + [VMEM] * (2 * BLOCKS),
+            out_specs=VMEM,
+        )
+
+    got = flip(back(1, bf16), 1).reshape(2, pixels, images, width)
+    mine = back(0, f32).reshape(2, pixels, images, width)
+    block_out, input_grad, vector_part = call(
+        post_kernel,
+        [big, big, struct((7, width))],
+        (counts, x, cot, vectors, q, stat, mine, got),
+        [keep, keep],
+        in_specs=[SMEM] + [VMEM] * 7,
+        out_specs=[VMEM] * 3,
+    )
+    output_grad = reduce_blocks(out_part).T
+    weight_grad = reduce_blocks(hidden_part)
+    sums = sum_all(jnp.concatenate([bias_part, vector_part.reshape(-1, 128)]))
+    split = bias.shape[0]
+    bias_grad = sums[:split].reshape(hidden_bias.shape)
+    vector_grad = sums[split:].reshape(vectors.shape)
+    hidden_new = adamw_update(
+        hidden_weight, weight_grad, hidden_moment, hidden_square, 0.04, weight_shrink
+    )
+    bias_new = adamw_update(hidden_bias, bias_grad, bias_moment, bias_square, 0.2, 0.0)
+    output_new = adamw_update(
+        output_weight, output_grad, output_moment, output_square, 0.02, weight_shrink
+    )
+    vector_new = adamw_update(vectors, vector_grad, vector_moment, vector_square, 0.3, 0.0)
+    return (
+        block_out.transpose(1, 0, 2),
+        input_grad.transpose(1, 0, 2),
+        *hidden_new,
+        *bias_new,
+        *output_new,
+        *vector_new,
+    )
+
+
 def solution(mesh):
     in_specs = (
         P(("narrow", "wide"), None, None),
@@ -223,4 +640,5 @@
         P(),
         P(),
     )
-    return jax.shard_map(local, mesh=mesh, in_specs=in_specs, out_specs=out_specs, check_vma=False)
+    body = local_tree if dict(mesh.shape) == {"narrow": 2, "wide": 16} else local
+    return jax.shard_map(body, mesh=mesh, in_specs=in_specs, out_specs=out_specs, check_vma=False)

time: 852 us -> 159 us (0.19)
  waiting for transfers between devices: 676 us -> 54.1 us
  matrix products: 74.7 us -> 0 us
  Pallas kernels: 0 us -> 43.3 us
  blocking collectives: 39.6 us -> 0 us
  starting transfers between devices: 0.39 us -> 38.4 us
  other arithmetic: 26.9 us -> 6.72 us
  between operations: 14.6 us -> 1.69 us
    reduce_scatter x2 -> x0, waiting for transfers between devices: 492 us -> none  [the longest x1 247 us: local(): lax.psum_scatter(contract_cols(block, hidden_low), 'wide', scatter_dimens...]
    all_gather x2 -> x0, waiting for transfers between devices: 184 us -> none  [the longest x1 99.2 us: local(): lax.all_gather(second_low, 'wide', axis=0, tiled=True)]
    dot_general x8 -> x0, matrix products: 74.7 us -> none  [the longest x2 18.3 us: contract_cols(): lax.dot_general(left, right, (((1,), (1,)), ((), ())), preferred_element_...]
    ppermute x0 -> x33, waiting for transfers between devices: none -> 54.1 us  [the longest x20 23.5 us: flip(): return lax.ppermute(values, 'wide', [(w, w ^ bit) for w in range(16)])]
    pallas_call x0 -> x6, Pallas kernels: none -> 43.3 us  [call(): pl.pallas_call(kernel, out_shape=outs, scratch_shapes=list(scratch), comp...]
    psum x1 -> x0, blocking collectives: 39.6 us -> none  [local(): lax.psum((vector_part, bias_part), ('narrow', 'wide'))]
    ppermute x0 -> x33, starting transfers between devices: none -> 38.4 us  [the longest x20 24 us: flip(): return lax.ppermute(values, 'wide', [(w, w ^ bit) for w in range(16)])]
    reduce_sum x8 -> x0, other arithmetic: 13.1 us -> none  [the longest x1 4.35 us: local(): grad_shift_out = jnp.sum(branch_grad, axis=0)]
  transfers between devices with their start and end apart: 5 -> 33, of which waited for: 4 -> 23; matrix products, arithmetic and copies ran while one was open for 7% -> 7% of each run, Pallas kernels for 0% -> 7%
where the time goes in v1:
time: 159 us; the launch traced here: 158 us
  waiting for transfers between devices  54.1 us (34%)
  Pallas kernels  43.3 us (27%)
  starting transfers between devices  38.4 us (24%)
  local copies, waits for them, and re-layouts  14.2 us (9%)
  other arithmetic  6.72 us (4%)
  between operations  1.69 us (1%)
    pallas_call x6, Pallas kernels, call(): pl.pallas_call(kernel, out_shape=outs, scratch_shapes=list(scratch), comp...  43.3 us
    ppermute x20, starting transfers between devices, flip(): return lax.ppermute(values, 'wide', [(w, w ^ bit) for w in range(16)])  24 us
    ppermute x20, waiting for transfers between devices, flip(): return lax.ppermute(values, 'wide', [(w, w ^ bit) for w in range(16)])  23.5 us
    ppermute x9, waiting for transfers between devices, across(): return lax.ppermute(values, 'narrow', [(0, 1), (1, 0)])  17.3 us
    unnamed x63, local copies, waits for them, and re-layouts  14 us
    ppermute x4, waiting for transfers between devices, far(): return lax.ppermute(values, BOTH, joint(lambda n, w: w ^ (12 if n else 8)))  13.3 us
    ppermute x4, starting transfers between devices, far(): return lax.ppermute(values, BOTH, joint(lambda n, w: w ^ (12 if n else 8)))  7.23 us
    ppermute x9, starting transfers between devices, across(): return lax.ppermute(values, 'narrow', [(0, 1), (1, 0)])  7.17 us
  transfers between devices with their start and end apart: 33, of which 23 were waited for; matrix products, arithmetic and copies ran while one was open for 7% of the time, Pallas kernels for 7%

profile of v1, /device:TPU:0, one launch (start us, length us, event | category | flops | bytes accessed | tf_op | source)
XLA Modules:
  0.0 158.4 jit_solution(15211442608146740432)
XLA Ops:
  1.3 1.4 copy-done.1
  2.7 1.1 copy-done.3
  3.9 0.7 copy-done.14
  4.6 1.6 %shard_map.254 = (bf16[2,49,16,512]{3,2,1,0:T(8,128)(2,1)S(1)}, f32[49,16,512]{2,1,0:T(8,128)S(1)}, f32[4,16,128]{2,1,0:T(8,128)S(1)}) custom-call(s32[1]{0:T(128)S(6)} %copy.38.counts_ref, f32[49,16,512]{2,1,0:T(8,128)S(1)} %bitcast.56, bf16[49,16,512]{2,1,0:T(8,128)(2,1)S(1)} %bitcast.61, f32[7,512]{1,0:T(8,128)S(1)} %copy-done.14), custom_call_target="tpu_custom_call" | custom-call | tf_op jit(solution)/shard_map/pallas_call | solution.py:434
  6.2 1.1 copy-done.5
  7.9 3.7 %collective-permute-start.2 = (bf16[512,128]{1,0:T(8,128)(2,1)S(1)}, bf16[512,128]{1,0:T(8,128)(2,1)S(1)}, u32[]{:S(2)}, u32[]{:S(2)}) collective-permute-start(bf16[512,128]{1,0:T(8,128)(2,1)S(1)} %convert_element_type.138.refs_0_), channel_id=1, source_target_pairs={{0,8},{1,9},{2,10},{3,11},{4,12},{5,13},{6,14},{7,15},{8,0},{9,1},... | collective-permute-start | bytes 393224 | tf_op jit(solution)/shard_map/ppermute | solution.py:459
  11.5 1.6 collective-permute-start.1
  13.1 5.5 %collective-permute-done.2.refs_2_ = bf16[512,128]{1,0:T(8,128)(2,1)S(1)} collective-permute-done((bf16[512,128]{1,0:T(8,128)(2,1)S(1)}, bf16[512,128]{1,0:T(8,128)(2,1)S(1)}, u32[]{:S(2)}, u32[]{:S(2)}) %collective-permute-start.2) | collective-permute-done | bytes 131104 | tf_op jit(solution)/shard_map/ppermute | solution.py:459
  18.6 1.6 collective-permute-start.6
  20.8 1.6 %collective-permute-start.5 = (bf16[512,128]{1,0:T(8,128)(2,1)}, bf16[512,128]{1,0:T(8,128)(2,1)S(1)}, u32[]{:S(2)}, u32[]{:S(2)}) collective-permute-start(bf16[512,128]{1,0:T(8,128)(2,1)} %collective-permute-done.1.refs_1_), channel_id=1, source_target_pairs={{0,2},{1,3},{2,0},{3,1},{4,6},{5,7},{6,4},{7,5},{8,10},{9,11},{10,... | collective-permute-start | bytes 393224 | tf_op jit(solution)/shard_map/ppermute | solution.py:455
  22.4 2.6 %collective-permute-done.6.refs_6_ = bf16[512,128]{1,0:T(8,128)(2,1)} collective-permute-done((bf16[512,128]{1,0:T(8,128)(2,1)S(1)}, bf16[512,128]{1,0:T(8,128)(2,1)}, u32[]{:S(2)}, u32[]{:S(2)}) %collective-permute-start.6) | collective-permute-done | bytes 131104 | tf_op jit(solution)/shard_map/ppermute | solution.py:455
  25.1 2.8 %collective-permute-done.4.refs_4_ = bf16[512,128]{1,0:T(8,128)(2,1)} collective-permute-done((bf16[512,128]{1,0:T(8,128)(2,1)S(1)}, bf16[512,128]{1,0:T(8,128)(2,1)}, u32[]{:S(2)}, u32[]{:S(2)}) %collective-permute-start.4) | collective-permute-done | bytes 131104 | tf_op jit(solution)/shard_map/ppermute | solution.py:455
  27.9 1.6 %collective-permute-done.5.refs_5_ = bf16[512,128]{1,0:T(8,128)(2,1)S(1)} collective-permute-done((bf16[512,128]{1,0:T(8,128)(2,1)}, bf16[512,128]{1,0:T(8,128)(2,1)S(1)}, u32[]{:S(2)}, u32[]{:S(2)}) %collective-permute-start.5) | collective-permute-done | bytes 131104 | tf_op jit(solution)/shard_map/ppermute | solution.py:455
  29.5 0.8 collective-permute-done.7.refs_7_
  30.3 16.9 %shard_map.255 = (bf16[2,784,1024]{2,1,0:T(8,128)(2,1)}, bf16[2,784,1024]{2,1,0:T(8,128)(2,1)}, bf16[8,512,128]{2,1,0:T(8,128)(2,1)S(1)}) custom-call(s32[8]{0:T(128)S(1)} %broadcast_xor_fusion.place_ref, bf16[2,784,512]{2,1,0:T(8,128)(2,1)S(1)} %bitcast.59, bf16[2,784,512]{2,1,0:T(8,128)(2,1)S(1)} %collective-permute-done.oth_ref, f32[16,128]{1,0:T(8,128)S(1)} %bitcast.64, ...), custom_call_target="tpu_custom_call" | custom-call | tf_op jit(solution)/shard_map/pallas_call | solution.py:434
  47.4 1.7 %collective-permute-start.27 = (bf16[2,512,128]{2,1,0:T(8,128)(2,1)S(1)}, bf16[2,512,128]{2,1,0:T(8,128)(2,1)S(1)}, u32[]{:S(2)}, u32[]{:S(2)}) collective-permute-start(bf16[2,512,128]{2,1,0:T(8,128)(2,1)S(1)} %slice.85), channel_id=1, source_target_pairs={{0,2},{1,3},{2,0},{3,1},{4,6},{5,7},{6,4},{7,5},{8,10},{9,11},{10,... | collective-permute-start | bytes 786440 | tf_op jit(solution)/shard_map/ppermute | solution.py:455
  49.0 4.8 %collective-permute-done.29 = bf16[2,512,128]{2,1,0:T(8,128)(2,1)S(1)} collective-permute-done((bf16[2,512,128]{2,1,0:T(8,128)(2,1)S(1)}, bf16[2,512,128]{2,1,0:T(8,128)(2,1)S(1)}, u32[]{:S(2)}, u32[]{:S(2)}) %collective-permute-start.29) | collective-permute-done | bytes 262176 | tf_op jit(solution)/shard_map/ppermute | solution.py:463
  54.0 2.1 %collective-permute-start.30 = (bf16[512,128]{1,0:T(8,128)(2,1)S(1)}, bf16[512,128]{1,0:T(8,128)(2,1)S(1)}, u32[]{:S(2)}, u32[]{:S(2)}) collective-permute-start(bf16[512,128]{1,0:T(8,128)(2,1)S(1)} %get-tuple-element.65), channel_id=1, source_target_pairs={{0,2},{1,3},{2,0},{3,1},{4,6},{5,7},{6,4},{7,5},{8,10},{9,11},{10,... | collective-permute-start | bytes 393224 | tf_op jit(solution)/shard_map/ppermute | solution.py:455
  56.1 1.8 %collective-permute-start.28 = (bf16[512,128]{1,0:T(8,128)(2,1)S(1)}, bf16[512,128]{1,0:T(8,128)(2,1)S(1)}, u32[]{:S(2)}, u32[]{:S(2)}) collective-permute-start(bf16[512,128]{1,0:T(8,128)(2,1)S(1)} %get-tuple-element.64), channel_id=1, source_target_pairs={{0,4},{1,5},{2,6},{3,7},{4,0},{5,1},{6,2},{7,3},{8,12},{9,13},{10,... | collective-permute-start | bytes 393224 | tf_op jit(solution)/shard_map/ppermute | solution.py:455
  57.9 1.1 collective-permute-done.30
  59.1 3.2 %collective-permute-start.31 = (bf16[512,128]{1,0:T(8,128)(2,1)S(1)}, bf16[512,128]{1,0:T(8,128)(2,1)S(1)}, u32[]{:S(2)}, u32[]{:S(2)}) collective-permute-start(bf16[512,128]{1,0:T(8,128)(2,1)S(1)} %fusion.3), channel_id=1, source_target_pairs={{0,8},{1,9},{2,10},{3,11},{4,12},{5,13},{6,14},{7,15},{8,0},{9,1},... | collective-permute-start | bytes 393224 | tf_op jit(solution)/shard_map/ppermute | solution.py:459
  62.2 2.9 %collective-permute-done.31 = bf16[512,128]{1,0:T(8,128)(2,1)S(1)} collective-permute-done((bf16[512,128]{1,0:T(8,128)(2,1)S(1)}, bf16[512,128]{1,0:T(8,128)(2,1)S(1)}, u32[]{:S(2)}, u32[]{:S(2)}) %collective-permute-start.31) | collective-permute-done | bytes 131104 | tf_op jit(solution)/shard_map/ppermute | solution.py:459
  65.2 0.7 fusion.5
  65.9 2.7 %collective-permute-start.32 = (bf16[512,128]{1,0:T(8,128)(2,1)}, bf16[512,128]{1,0:T(8,128)(2,1)}, u32[]{:S(2)}, u32[]{:S(2)}) collective-permute-start(bf16[512,128]{1,0:T(8,128)(2,1)} %fusion.5), channel_id=1, source_target_pairs={{0,16},{16,0},{1,17},{17,1},{2,18},{18,2},{3,19},{19,3},{4,20},{20... | collective-permute-start | bytes 393224 | tf_op jit(solution)/shard_map/ppermute | solution.py:463
  68.6 1.8 %copy.29 = f32[128,512]{0,1:T(8,128)} copy(f32[128,512]{1,0:T(8,128)} %param.20) | data formatting | bytes 524288 | tf_op args[5]
  70.4 1.8 %copy.30 = f32[128,512]{0,1:T(8,128)} copy(f32[128,512]{1,0:T(8,128)} %param.26) | data formatting | bytes 524288 | tf_op args[11]
  72.2 1.8 %copy.31 = f32[128,512]{0,1:T(8,128)} copy(f32[128,512]{1,0:T(8,128)} %param.27) | data formatting | bytes 524288 | tf_op args[12]
  73.9 2.3 %multiply_subtract_fusion = (f32[128,512]{0,1:T(8,128)}, f32[128,512]{0,1:T(8,128)}, f32[128,512]{0,1:T(8,128)}, bf16[512,128]{1,0:T(8,128)(2,1)S(1)}) fusion(f32[128,512]{0,1:T(8,128)} %copy.29, bf16[512,128]{1,0:T(8,128)(2,1)} %collective-permute-done.32, bf16[512,128]{1,0:T(8,128)(2,1)} %fusion.5, f32[128,512]{0,1:T(8,128)} %copy.30, f32[128,512]{0,1:T(8,128)} %copy.31), kind=kLoop, calls=%fused_computation.18 | loop fusion | flops 1245184 | bytes 1966080 | tf_op jit(solution)/shard_map/sub | solution.py:70
  76.6 3.8 %collective-permute-start.8 = (bf16[512,128]{1,0:T(8,128)(2,1)S(1)}, bf16[512,128]{1,0:T(8,128)(2,1)S(1)}, u32[]{:S(2)}, u32[]{:S(2)}) collective-permute-start(bf16[512,128]{1,0:T(8,128)(2,1)S(1)} %get-tuple-element.72.refs_0_.refs_8_), channel_id=1, source_target_pairs={{0,4},{1,5},{2,6},{3,7},{4,0},{5,1},{6,2},{7,3},{8,12},{9,13},{10,... | collective-permute-start | bytes 393224 | tf_op jit(solution)/shard_map/ppermute | solution.py:455
  80.4 3.2 %collective-permute-done.9.refs_2_.refs_10_ = bf16[512,128]{1,0:T(8,128)(2,1)S(1)} collective-permute-done((bf16[512,128]{1,0:T(8,128)(2,1)S(1)}, bf16[512,128]{1,0:T(8,128)(2,1)S(1)}, u32[]{:S(2)}, u32[]{:S(2)}) %collective-permute-start.9) | collective-permute-done | bytes 131104 | tf_op jit(solution)/shard_map/ppermute | solution.py:459
  83.6 2.0 %collective-permute-start.13 = (bf16[512,128]{1,0:T(8,128)(2,1)S(1)}, bf16[512,128]{1,0:T(8,128)(2,1)S(1)}, u32[]{:S(2)}, u32[]{:S(2)}) collective-permute-start(bf16[512,128]{1,0:T(8,128)(2,1)S(1)} %collective-permute-done.9.refs_2_.refs_10_), channel_id=1, source_target_pairs={{0,2},{1,3},{2,0},{3,1},{4,6},{5,7},{6,4},{7,5},{8,10},{9,11},{10,... | collective-permute-start | bytes 393224 | tf_op jit(solution)/shard_map/ppermute | solution.py:455
  85.7 2.0 %collective-permute-start.12 = (bf16[512,128]{1,0:T(8,128)(2,1)S(1)}, bf16[512,128]{1,0:T(8,128)(2,1)S(1)}, u32[]{:S(2)}, u32[]{:S(2)}) collective-permute-start(bf16[512,128]{1,0:T(8,128)(2,1)S(1)} %collective-permute-done.8.refs_1_.refs_9_), channel_id=1, source_target_pairs={{0,2},{1,3},{2,0},{3,1},{4,6},{5,7},{6,4},{7,5},{8,10},{9,11},{10,... | collective-permute-start | bytes 393224 | tf_op jit(solution)/shard_map/ppermute | solution.py:455
  87.7 0.9 collective-permute-done.13.refs_6_.refs_14_
  88.6 1.1 collective-permute-start.14
  89.7 0.9 collective-permute-done.11.refs_4_.refs_12_
  90.7 1.4 collective-permute-done.12.refs_5_.refs_13_
  92.0 1.5 collective-permute-done.14.refs_7_.refs_15_
  93.6 9.3 %shard_map.256 = (bf16[2,784,1024]{2,1,0:T(8,128)(2,1)}, bf16[8,512,128]{2,1,0:T(8,128)(2,1)S(1)}, f32[16,128]{1,0:T(8,128)S(1)}) custom-call(s32[8]{0:T(128)S(1)} %broadcast_xor_fusion.place_ref, bf16[2,784,512]{2,1,0:T(8,128)(2,1)S(1)} %bitcast.60, bf16[2,784,512]{2,1,0:T(8,128)(2,1)S(1)} %collective-permute-done.oth_ref, ...), custom_call_target="tpu_custom_call" | custom-call | tf_op jit(solution)/shard_map/pallas_call | solution.py:434
  102.9 4.2 %shard_map.258 = bf16[2,784,512]{2,1,0:T(8,128)(2,1)S(1)} custom-call(bf16[2,784,1024]{2,1,0:T(8,128)(2,1)} %get-tuple-element.29.act_ref, bf16[2,784,1024]{2,1,0:T(8,128)(2,1)} %get-tuple-element.31.hg_ref, bf16[512,128]{1,0:T(8,128)(2,1)S(1)} %convert_element_type.138.refs_0_, bf16[512,128]{1,0:T(8,128)(2,1)} %collective-permute-done.1.refs_1_, ...), custom_call_target="tpu_custom_call" | custom-call | tf_op jit(solution)/shard_map/pallas_call | solution.py:434
  107.2 1.2 collective-permute-start.18
  108.4 1.0 collective-permute-start.16
  109.4 6.6 %collective-permute-done.18 = bf16[2,512,128]{2,1,0:T(8,128)(2,1)S(1)} collective-permute-done((bf16[2,512,128]{2,1,0:T(8,128)(2,1)S(1)}, bf16[2,512,128]{2,1,0:T(8,128)(2,1)S(1)}, u32[]{:S(2)}, u32[]{:S(2)}) %collective-permute-start.18) | collective-permute-done | bytes 262176 | tf_op jit(solution)/shard_map/ppermute | solution.py:463
  116.0 0.8 collective-permute-done.16
  116.9 1.3 collective-permute-start.19
  118.2 3.7 %collective-permute-done.19 = bf16[512,128]{1,0:T(8,128)(2,1)S(1)} collective-permute-done((bf16[512,128]{1,0:T(8,128)(2,1)S(1)}, bf16[512,128]{1,0:T(8,128)(2,1)S(1)}, u32[]{:S(2)}, u32[]{:S(2)}) %collective-permute-start.19) | collective-permute-done | bytes 131104 | tf_op jit(solution)/shard_map/ppermute | solution.py:455
  122.1 4.0 %shard_map.257 = f32[2,784,512]{2,1,0:T(8,128)S(1)} custom-call(bf16[2,784,1024]{2,1,0:T(8,128)(2,1)} %get-tuple-element.29.act_ref, bf16[2,784,1024]{2,1,0:T(8,128)(2,1)} %get-tuple-element.31.hg_ref, bf16[512,128]{1,0:T(8,128)(2,1)S(1)} %convert_element_type.138.refs_0_, bf16[512,128]{1,0:T(8,128)(2,1)} %collective-permute-done.1.refs_1_, ...), custom_call_target="tpu_custom_call" | custom-call | tf_op jit(solution)/shard_map/pallas_call | solution.py:434
  126.1 1.6 %copy-done = f32[2,784,512]{2,1,0:T(8,128)} copy-done((f32[2,784,512]{2,1,0:T(8,128)}, f32[2,784,512]{2,1,0:T(8,128)S(1)}, u32[]{:S(2)}) %copy-start) | copy-done | bytes 3211288
  127.8 1.7 %collective-permute-done.20 = bf16[512,128]{1,0:T(8,128)(2,1)S(1)} collective-permute-done((bf16[512,128]{1,0:T(8,128)(2,1)S(1)}, bf16[512,128]{1,0:T(8,128)(2,1)S(1)}, u32[]{:S(2)}, u32[]{:S(2)}) %collective-permute-start.20) | collective-permute-done | bytes 131104 | tf_op jit(solution)/shard_map/ppermute | solution.py:459
  129.4 1.0 fusion.8
  130.4 1.8 %collective-permute-start.21 = (bf16[512,128]{1,0:T(8,128)(2,1)S(1)}, bf16[512,128]{1,0:T(8,128)(2,1)S(1)}, u32[]{:S(2)}, u32[]{:S(2)}) collective-permute-start(bf16[512,128]{1,0:T(8,128)(2,1)S(1)} %fusion.8), channel_id=1, source_target_pairs={{0,16},{16,0},{1,17},{17,1},{2,18},{18,2},{3,19},{19,3},{4,20},{20... | collective-permute-start | bytes 393224 | tf_op jit(solution)/shard_map/ppermute | solution.py:463
  132.3 7.3 %shard_map.259 = (f32[49,16,512]{2,1,0:T(8,128)}, f32[49,16,512]{2,1,0:T(8,128)}, f32[7,512]{1,0:T(8,128)S(1)}) custom-call(s32[1]{0:T(128)S(6)} %copy.38.counts_ref, f32[49,16,512]{2,1,0:T(8,128)S(1)} %bitcast.57, bf16[49,16,512]{2,1,0:T(8,128)(2,1)S(1)} %bitcast.62, f32[7,512]{1,0:T(8,128)S(1)} %copy-done.15, f32[49,16,512]{2,1,0:T(8,128)S(1)} %copy-done.6, ...), custom_call_target="tpu_custom_call" | custom-call | tf_op jit(solution)/shard_map/pallas_call | solution.py:434
  139.7 1.2 collective-permute-done.22
  140.9 1.3 collective-permute-start.23
  142.2 2.5 %collective-permute-done.23 = f32[44,128]{1,0:T(8,128)S(1)} collective-permute-done((f32[44,128]{1,0:T(8,128)S(1)}, f32[44,128]{1,0:T(8,128)S(1)}, u32[]{:S(2)}, u32[]{:S(2)}) %collective-permute-start.23) | collective-permute-done | bytes 22560 | tf_op jit(solution)/shard_map/ppermute | solution.py:455
  145.0 3.5 %collective-permute-done.24 = f32[44,128]{1,0:T(8,128)S(1)} collective-permute-done((f32[44,128]{1,0:T(8,128)S(1)}, f32[44,128]{1,0:T(8,128)S(1)}, u32[]{:S(2)}, u32[]{:S(2)}) %collective-permute-start.24) | collective-permute-done | bytes 22560 | tf_op jit(solution)/shard_map/ppermute | solution.py:463
  148.5 0.8 copy.34
  149.4 0.8 copy.35
  150.2 0.8 copy.36
  151.1 1.3 collective-permute-done.25
  152.4 1.1 collective-permute-start.26
  153.5 1.0 multiply_subtract_fusion.1
  154.5 2.6 %collective-permute-done.26 = f32[44,128]{1,0:T(8,128)S(1)} collective-permute-done((f32[44,128]{1,0:T(8,128)S(1)}, f32[44,128]{1,0:T(8,128)S(1)}, u32[]{:S(2)}, u32[]{:S(2)}) %collective-permute-start.26) | collective-permute-done | bytes 22560 | tf_op jit(solution)/shard_map/ppermute | solution.py:455
  157.1 0.6 multiply_subtract_fusion.3
  157.8 0.6 multiply_subtract_fusion.2
  (100 shorter events, 2.8 us)
Async XLA Ops:
  1.3 1.4 copy-start.1
  2.7 1.1 copy-start.3
  3.9 0.7 copy-start.14
  4.6 3.3 %copy-start.17 = (f32[512,128]{1,0:T(8,128)S(1)}, f32[512,128]{1,0:T(8,128)}, u32[]{:S(2)}) copy-start(f32[512,128]{1,0:T(8,128)} %param.18) | copy-start | bytes 786436
  4.6 25.7 %copy-start.16 = (f32[2048]{0:T(1024)S(1)}, f32[2048]{0:T(1024)}, u32[]{:S(2)}) copy-start(f32[2048]{0:T(1024)} %param.19) | copy-start | bytes 24580
  6.2 1.2 copy-start.5
  7.4 22.9 %collective-permute-start = (bf16[2,784,512]{2,1,0:T(8,128)(2,1)S(1)}, bf16[2,784,512]{2,1,0:T(8,128)(2,1)S(1)}, u32[]{:S(2)}, u32[]{:S(2)}) collective-permute-start(bf16[2,784,512]{2,1,0:T(8,128)(2,1)S(1)} %bitcast.58), channel_id=1, source_target_pairs={{0,1},{1,0},{2,3},{3,2},{4,5},{5,4},{6,7},{7,6},{8,9},{9,8},{10,11... | collective-permute-start | bytes 4816904 | tf_op jit(solution)/shard_map/ppermute | solution.py:455
  7.9 10.7 %collective-permute-start.2 = (bf16[512,128]{1,0:T(8,128)(2,1)S(1)}, bf16[512,128]{1,0:T(8,128)(2,1)S(1)}, u32[]{:S(2)}, u32[]{:S(2)}) collective-permute-start(bf16[512,128]{1,0:T(8,128)(2,1)S(1)} %convert_element_type.138.refs_0_), channel_id=1, source_target_pairs={{0,8},{1,9},{2,10},{3,11},{4,12},{5,13},{6,14},{7,15},{8,0},{9,1},... | collective-permute-start | bytes 393224 | tf_op jit(solution)/shard_map/ppermute | solution.py:459
  11.5 9.3 %collective-permute-start.1 = (bf16[512,128]{1,0:T(8,128)(2,1)S(1)}, bf16[512,128]{1,0:T(8,128)(2,1)}, u32[]{:S(2)}, u32[]{:S(2)}) collective-permute-start(bf16[512,128]{1,0:T(8,128)(2,1)S(1)} %convert_element_type.138.refs_0_), channel_id=1, source_target_pairs={{0,4},{1,5},{2,6},{3,7},{4,0},{5,1},{6,2},{7,3},{8,12},{9,13},{10,... | collective-permute-start | bytes 393224 | tf_op jit(solution)/shard_map/ppermute | solution.py:455
  18.6 6.5 %collective-permute-start.6 = (bf16[512,128]{1,0:T(8,128)(2,1)S(1)}, bf16[512,128]{1,0:T(8,128)(2,1)}, u32[]{:S(2)}, u32[]{:S(2)}) collective-permute-start(bf16[512,128]{1,0:T(8,128)(2,1)S(1)} %collective-permute-done.2.refs_2_), channel_id=1, source_target_pairs={{0,2},{1,3},{2,0},{3,1},{4,6},{5,7},{6,4},{7,5},{8,10},{9,11},{10,... | collective-permute-start | bytes 393224 | tf_op jit(solution)/shard_map/ppermute | solution.py:455
  20.2 7.7 %collective-permute-start.4 = (bf16[512,128]{1,0:T(8,128)(2,1)S(1)}, bf16[512,128]{1,0:T(8,128)(2,1)}, u32[]{:S(2)}, u32[]{:S(2)}) collective-permute-start(bf16[512,128]{1,0:T(8,128)(2,1)S(1)} %convert_element_type.138.refs_0_), channel_id=1, source_target_pairs={{0,2},{1,3},{2,0},{3,1},{4,6},{5,7},{6,4},{7,5},{8,10},{9,11},{10,... | collective-permute-start | bytes 393224 | tf_op jit(solution)/shard_map/ppermute | solution.py:455
  20.8 7.1 %collective-permute-start.3 = (bf16[512,128]{1,0:T(8,128)(2,1)S(1)}, bf16[512,128]{1,0:T(8,128)(2,1)S(1)}, u32[]{:S(2)}, u32[]{:S(2)}) collective-permute-start(bf16[512,128]{1,0:T(8,128)(2,1)S(1)} %collective-permute-done.2.refs_2_), channel_id=1, source_target_pairs={{0,16},{16,0},{1,17},{17,1},{2,18},{18,2},{3,19},{19,3},{4,20},{20... | collective-permute-start | bytes 393224 | tf_op jit(solution)/shard_map/ppermute | solution.py:463
  20.8 8.7 %collective-permute-start.5 = (bf16[512,128]{1,0:T(8,128)(2,1)}, bf16[512,128]{1,0:T(8,128)(2,1)S(1)}, u32[]{:S(2)}, u32[]{:S(2)}) collective-permute-start(bf16[512,128]{1,0:T(8,128)(2,1)} %collective-permute-done.1.refs_1_), channel_id=1, source_target_pairs={{0,2},{1,3},{2,0},{3,1},{4,6},{5,7},{6,4},{7,5},{8,10},{9,11},{10,... | collective-permute-start | bytes 393224 | tf_op jit(solution)/shard_map/ppermute | solution.py:455
  25.1 5.2 %collective-permute-start.7 = (bf16[512,128]{1,0:T(8,128)(2,1)}, bf16[512,128]{1,0:T(8,128)(2,1)S(1)}, u32[]{:S(2)}, u32[]{:S(2)}) collective-permute-start(bf16[512,128]{1,0:T(8,128)(2,1)} %collective-permute-done.6.refs_6_), channel_id=1, source_target_pairs={{0,16},{16,0},{1,17},{17,1},{2,18},{18,2},{3,19},{19,3},{4,20},{20... | collective-permute-start | bytes 393224 | tf_op jit(solution)/shard_map/ppermute | solution.py:463
  27.9 19.3 %copy-start.7 = (bf16[512,128]{1,0:T(8,128)(2,1)}, bf16[512,128]{1,0:T(8,128)(2,1)S(1)}, u32[]{:S(2)}) copy-start(bf16[512,128]{1,0:T(8,128)(2,1)S(1)} %collective-permute-done.3.refs_3_) | copy-start | bytes 393220
  29.5 17.7 %copy-start.9 = (bf16[512,128]{1,0:T(8,128)(2,1)}, bf16[512,128]{1,0:T(8,128)(2,1)S(1)}, u32[]{:S(2)}) copy-start(bf16[512,128]{1,0:T(8,128)(2,1)S(1)} %collective-permute-done.5.refs_5_) | copy-start | bytes 393220
  30.3 16.9 %copy-start.11 = (bf16[512,128]{1,0:T(8,128)(2,1)}, bf16[512,128]{1,0:T(8,128)(2,1)S(1)}, u32[]{:S(2)}) copy-start(bf16[512,128]{1,0:T(8,128)(2,1)S(1)} %collective-permute-done.7.refs_7_) | copy-start | bytes 393220
  47.3 6.5 %collective-permute-start.29 = (bf16[2,512,128]{2,1,0:T(8,128)(2,1)S(1)}, bf16[2,512,128]{2,1,0:T(8,128)(2,1)S(1)}, u32[]{:S(2)}, u32[]{:S(2)}) collective-permute-start(bf16[2,512,128]{2,1,0:T(8,128)(2,1)S(1)} %pad_maximum_fusion.1), channel_id=1, source_target_pairs={{0,16},{16,0},{1,17},{17,1},{2,18},{18,2},{3,19},{19,3},{4,20},{20... | collective-permute-start | bytes 786440 | tf_op jit(solution)/shard_map/ppermute | solution.py:463
  47.4 6.5 %collective-permute-start.27 = (bf16[2,512,128]{2,1,0:T(8,128)(2,1)S(1)}, bf16[2,512,128]{2,1,0:T(8,128)(2,1)S(1)}, u32[]{:S(2)}, u32[]{:S(2)}) collective-permute-start(bf16[2,512,128]{2,1,0:T(8,128)(2,1)S(1)} %slice.85), channel_id=1, source_target_pairs={{0,2},{1,3},{2,0},{3,1},{4,6},{5,7},{6,4},{7,5},{8,10},{9,11},{10,... | collective-permute-start | bytes 786440 | tf_op jit(solution)/shard_map/ppermute | solution.py:455
  54.0 5.0 %collective-permute-start.30 = (bf16[512,128]{1,0:T(8,128)(2,1)S(1)}, bf16[512,128]{1,0:T(8,128)(2,1)S(1)}, u32[]{:S(2)}, u32[]{:S(2)}) collective-permute-start(bf16[512,128]{1,0:T(8,128)(2,1)S(1)} %get-tuple-element.65), channel_id=1, source_target_pairs={{0,2},{1,3},{2,0},{3,1},{4,6},{5,7},{6,4},{7,5},{8,10},{9,11},{10,... | collective-permute-start | bytes 393224 | tf_op jit(solution)/shard_map/ppermute | solution.py:455
  56.1 6.2 %collective-permute-start.28 = (bf16[512,128]{1,0:T(8,128)(2,1)S(1)}, bf16[512,128]{1,0:T(8,128)(2,1)S(1)}, u32[]{:S(2)}, u32[]{:S(2)}) collective-permute-start(bf16[512,128]{1,0:T(8,128)(2,1)S(1)} %get-tuple-element.64), channel_id=1, source_target_pairs={{0,4},{1,5},{2,6},{3,7},{4,0},{5,1},{6,2},{7,3},{8,12},{9,13},{10,... | collective-permute-start | bytes 393224 | tf_op jit(solution)/shard_map/ppermute | solution.py:455
  59.1 6.1 %collective-permute-start.31 = (bf16[512,128]{1,0:T(8,128)(2,1)S(1)}, bf16[512,128]{1,0:T(8,128)(2,1)S(1)}, u32[]{:S(2)}, u32[]{:S(2)}) collective-permute-start(bf16[512,128]{1,0:T(8,128)(2,1)S(1)} %fusion.3), channel_id=1, source_target_pairs={{0,8},{1,9},{2,10},{3,11},{4,12},{5,13},{6,14},{7,15},{8,0},{9,1},... | collective-permute-start | bytes 393224 | tf_op jit(solution)/shard_map/ppermute | solution.py:459
  65.9 8.0 %collective-permute-start.32 = (bf16[512,128]{1,0:T(8,128)(2,1)}, bf16[512,128]{1,0:T(8,128)(2,1)}, u32[]{:S(2)}, u32[]{:S(2)}) collective-permute-start(bf16[512,128]{1,0:T(8,128)(2,1)} %fusion.5), channel_id=1, source_target_pairs={{0,16},{16,0},{1,17},{17,1},{2,18},{18,2},{3,19},{19,3},{4,20},{20... | collective-permute-start | bytes 393224 | tf_op jit(solution)/shard_map/ppermute | solution.py:463
  76.3 7.4 %collective-permute-start.9 = (bf16[512,128]{1,0:T(8,128)(2,1)S(1)}, bf16[512,128]{1,0:T(8,128)(2,1)S(1)}, u32[]{:S(2)}, u32[]{:S(2)}) collective-permute-start(bf16[512,128]{1,0:T(8,128)(2,1)S(1)} %get-tuple-element.72.refs_0_.refs_8_), channel_id=1, source_target_pairs={{0,8},{1,9},{2,10},{3,11},{4,12},{5,13},{6,14},{7,15},{8,0},{9,1},... | collective-permute-start | bytes 393224 | tf_op jit(solution)/shard_map/ppermute | solution.py:459
  76.6 9.1 %collective-permute-start.8 = (bf16[512,128]{1,0:T(8,128)(2,1)S(1)}, bf16[512,128]{1,0:T(8,128)(2,1)S(1)}, u32[]{:S(2)}, u32[]{:S(2)}) collective-permute-start(bf16[512,128]{1,0:T(8,128)(2,1)S(1)} %get-tuple-element.72.refs_0_.refs_8_), channel_id=1, source_target_pairs={{0,4},{1,5},{2,6},{3,7},{4,0},{5,1},{6,2},{7,3},{8,12},{9,13},{10,... | collective-permute-start | bytes 393224 | tf_op jit(solution)/shard_map/ppermute | solution.py:455
  83.6 5.0 %collective-permute-start.13 = (bf16[512,128]{1,0:T(8,128)(2,1)S(1)}, bf16[512,128]{1,0:T(8,128)(2,1)S(1)}, u32[]{:S(2)}, u32[]{:S(2)}) collective-permute-start(bf16[512,128]{1,0:T(8,128)(2,1)S(1)} %collective-permute-done.9.refs_2_.refs_10_), channel_id=1, source_target_pairs={{0,2},{1,3},{2,0},{3,1},{4,6},{5,7},{6,4},{7,5},{8,10},{9,11},{10,... | collective-permute-start | bytes 393224 | tf_op jit(solution)/shard_map/ppermute | solution.py:455
  85.7 5.0 %collective-permute-start.11 = (bf16[512,128]{1,0:T(8,128)(2,1)S(1)}, bf16[512,128]{1,0:T(8,128)(2,1)S(1)}, u32[]{:S(2)}, u32[]{:S(2)}) collective-permute-start(bf16[512,128]{1,0:T(8,128)(2,1)S(1)} %get-tuple-element.72.refs_0_.refs_8_), channel_id=1, source_target_pairs={{0,2},{1,3},{2,0},{3,1},{4,6},{5,7},{6,4},{7,5},{8,10},{9,11},{10,... | collective-permute-start | bytes 393224 | tf_op jit(solution)/shard_map/ppermute | solution.py:455
  85.7 5.0 %collective-permute-start.10 = (bf16[512,128]{1,0:T(8,128)(2,1)S(1)}, bf16[512,128]{1,0:T(8,128)(2,1)S(1)}, u32[]{:S(2)}, u32[]{:S(2)}) collective-permute-start(bf16[512,128]{1,0:T(8,128)(2,1)S(1)} %collective-permute-done.9.refs_2_.refs_10_), channel_id=1, source_target_pairs={{0,16},{16,0},{1,17},{17,1},{2,18},{18,2},{3,19},{19,3},{4,20},{20... | collective-permute-start | bytes 393224 | tf_op jit(solution)/shard_map/ppermute | solution.py:463
  85.7 6.3 %collective-permute-start.12 = (bf16[512,128]{1,0:T(8,128)(2,1)S(1)}, bf16[512,128]{1,0:T(8,128)(2,1)S(1)}, u32[]{:S(2)}, u32[]{:S(2)}) collective-permute-start(bf16[512,128]{1,0:T(8,128)(2,1)S(1)} %collective-permute-done.8.refs_1_.refs_9_), channel_id=1, source_target_pairs={{0,2},{1,3},{2,0},{3,1},{4,6},{5,7},{6,4},{7,5},{8,10},{9,11},{10,... | collective-permute-start | bytes 393224 | tf_op jit(solution)/shard_map/ppermute | solution.py:455
  88.6 5.0 %collective-permute-start.14 = (bf16[512,128]{1,0:T(8,128)(2,1)S(1)}, bf16[512,128]{1,0:T(8,128)(2,1)S(1)}, u32[]{:S(2)}, u32[]{:S(2)}) collective-permute-start(bf16[512,128]{1,0:T(8,128)(2,1)S(1)} %collective-permute-done.13.refs_6_.refs_14_), channel_id=1, source_target_pairs={{0,16},{16,0},{1,17},{17,1},{2,18},{18,2},{3,19},{19,3},{4,20},{20... | collective-permute-start | bytes 393224 | tf_op jit(solution)/shard_map/ppermute | solution.py:463
  93.6 9.3 %copy-start.8 = (bf16[512,128]{1,0:T(8,128)(2,1)S(1)}, bf16[512,128]{1,0:T(8,128)(2,1)}, u32[]{:S(2)}) copy-start(bf16[512,128]{1,0:T(8,128)(2,1)} %copy-done.7) | copy-start | bytes 393220
  93.6 9.3 %copy-start.10 = (bf16[512,128]{1,0:T(8,128)(2,1)S(1)}, bf16[512,128]{1,0:T(8,128)(2,1)}, u32[]{:S(2)}) copy-start(bf16[512,128]{1,0:T(8,128)(2,1)} %copy-done.9) | copy-start | bytes 393220
  93.6 9.3 %copy-start.12 = (bf16[512,128]{1,0:T(8,128)(2,1)S(1)}, bf16[512,128]{1,0:T(8,128)(2,1)}, u32[]{:S(2)}) copy-start(bf16[512,128]{1,0:T(8,128)(2,1)} %copy-done.11) | copy-start | bytes 393220
  102.8 19.1 %copy-start.13 = (bf16[8,512,128]{2,1,0:T(8,128)(2,1)}, bf16[8,512,128]{2,1,0:T(8,128)(2,1)S(1)}, u32[]{:S(2)}) copy-start(bf16[8,512,128]{2,1,0:T(8,128)(2,1)S(1)} %get-tuple-element.34) | copy-start | bytes 3145732
  107.1 25.2 %collective-permute-start.15 = (bf16[2,784,512]{2,1,0:T(8,128)(2,1)S(1)}, bf16[2,784,512]{2,1,0:T(8,128)(2,1)S(1)}, u32[]{:S(2)}, u32[]{:S(2)}) collective-permute-start(bf16[2,784,512]{2,1,0:T(8,128)(2,1)S(1)} %shard_map.258), channel_id=1, source_target_pairs={{0,1},{1,0},{2,3},{3,2},{4,5},{5,4},{6,7},{7,6},{8,9},{9,8},{10,11... | collective-permute-start | bytes 4816904 | tf_op jit(solution)/shard_map/ppermute | solution.py:455
  107.2 8.8 %collective-permute-start.18 = (bf16[2,512,128]{2,1,0:T(8,128)(2,1)S(1)}, bf16[2,512,128]{2,1,0:T(8,128)(2,1)S(1)}, u32[]{:S(2)}, u32[]{:S(2)}) collective-permute-start(bf16[2,512,128]{2,1,0:T(8,128)(2,1)S(1)} %pad_maximum_fusion), channel_id=1, source_target_pairs={{0,16},{16,0},{1,17},{17,1},{2,18},{18,2},{3,19},{19,3},{4,20},{20... | collective-permute-start | bytes 786440 | tf_op jit(solution)/shard_map/ppermute | solution.py:463
  108.4 8.4 %collective-permute-start.16 = (bf16[2,512,128]{2,1,0:T(8,128)(2,1)S(1)}, bf16[2,512,128]{2,1,0:T(8,128)(2,1)S(1)}, u32[]{:S(2)}, u32[]{:S(2)}) collective-permute-start(bf16[2,512,128]{2,1,0:T(8,128)(2,1)S(1)} %slice.73), channel_id=1, source_target_pairs={{0,2},{1,3},{2,0},{3,1},{4,6},{5,7},{6,4},{7,5},{8,10},{9,11},{10,... | collective-permute-start | bytes 786440 | tf_op jit(solution)/shard_map/ppermute | solution.py:455
  116.9 5.0 %collective-permute-start.19 = (bf16[512,128]{1,0:T(8,128)(2,1)S(1)}, bf16[512,128]{1,0:T(8,128)(2,1)S(1)}, u32[]{:S(2)}, u32[]{:S(2)}) collective-permute-start(bf16[512,128]{1,0:T(8,128)(2,1)S(1)} %get-tuple-element.69), channel_id=1, source_target_pairs={{0,2},{1,3},{2,0},{3,1},{4,6},{5,7},{6,4},{7,5},{8,10},{9,11},{10,... | collective-permute-start | bytes 393224 | tf_op jit(solution)/shard_map/ppermute | solution.py:455
  118.2 9.6 %collective-permute-start.17 = (bf16[512,128]{1,0:T(8,128)(2,1)S(1)}, bf16[512,128]{1,0:T(8,128)(2,1)S(1)}, u32[]{:S(2)}, u32[]{:S(2)}) collective-permute-start(bf16[512,128]{1,0:T(8,128)(2,1)S(1)} %get-tuple-element.68), channel_id=1, source_target_pairs={{0,4},{1,5},{2,6},{3,7},{4,0},{5,1},{6,2},{7,3},{8,12},{9,13},{10,... | collective-permute-start | bytes 393224 | tf_op jit(solution)/shard_map/ppermute | solution.py:455
  122.0 10.2 %copy-start.4 = (bf16[16,49,512]{2,0,1:T(8,128)(2,1)S(1)}, bf16[16,49,512]{2,0,1:T(8,128)(2,1)}, u32[]{:S(2)}) copy-start(bf16[16,49,512]{2,0,1:T(8,128)(2,1)} %param.16) | copy-start | bytes 2408452
  122.0 10.2 %copy-start.15 = (f32[7,512]{1,0:T(8,128)S(1)}, f32[7,512]{1,0:T(8,128)}, u32[]{:S(2)}) copy-start(f32[7,512]{1,0:T(8,128)} %vec_ref.3) | copy-start | bytes 43012
  122.0 7.4 %collective-permute-start.20 = (bf16[512,128]{1,0:T(8,128)(2,1)S(1)}, bf16[512,128]{1,0:T(8,128)(2,1)S(1)}, u32[]{:S(2)}, u32[]{:S(2)}) collective-permute-start(bf16[512,128]{1,0:T(8,128)(2,1)S(1)} %fusion.6), channel_id=1, source_target_pairs={{0,8},{1,9},{2,10},{3,11},{4,12},{5,13},{6,14},{7,15},{8,0},{9,1},... | collective-permute-start | bytes 393224 | tf_op jit(solution)/shard_map/ppermute | solution.py:459
  122.1 10.1 %copy-start.2 = (f32[16,49,512]{2,0,1:T(8,128)S(1)}, f32[16,49,512]{2,0,1:T(8,128)}, u32[]{:S(2)}) copy-start(f32[16,49,512]{2,0,1:T(8,128)} %param.15) | copy-start | bytes 4816900
  122.1 10.1 %copy-start.6 = (f32[49,16,512]{2,1,0:T(8,128)S(1)}, f32[49,16,512]{2,1,0:T(8,128)}, u32[]{:S(2)}) copy-start(f32[49,16,512]{2,1,0:T(8,128)} %copy-done.5) | copy-start | bytes 4816900
  126.1 1.7 %copy-start = (f32[2,784,512]{2,1,0:T(8,128)}, f32[2,784,512]{2,1,0:T(8,128)S(1)}, u32[]{:S(2)}) copy-start(f32[2,784,512]{2,1,0:T(8,128)S(1)} %shard_map.257) | copy-start | bytes 9633796
  130.4 23.0 %collective-permute-start.21 = (bf16[512,128]{1,0:T(8,128)(2,1)S(1)}, bf16[512,128]{1,0:T(8,128)(2,1)S(1)}, u32[]{:S(2)}, u32[]{:S(2)}) collective-permute-start(bf16[512,128]{1,0:T(8,128)(2,1)S(1)} %fusion.8), channel_id=1, source_target_pairs={{0,16},{16,0},{1,17},{17,1},{2,18},{18,2},{3,19},{19,3},{4,20},{20... | collective-permute-start | bytes 393224 | tf_op jit(solution)/shard_map/ppermute | solution.py:463
  132.2 16.3 %copy-start.21 = (f32[128,512]{0,1:T(8,128)S(1)}, f32[128,512]{0,1:T(8,128)}, u32[]{:S(2)}) copy-start(f32[128,512]{0,1:T(8,128)} %get-tuple-element.55) | copy-start | bytes 786436
  132.2 17.1 %copy-start.20 = (f32[128,512]{0,1:T(8,128)S(1)}, f32[128,512]{0,1:T(8,128)}, u32[]{:S(2)}) copy-start(f32[128,512]{0,1:T(8,128)} %get-tuple-element.56) | copy-start | bytes 786436
  132.3 18.0 %copy-start.19 = (f32[128,512]{0,1:T(8,128)S(1)}, f32[128,512]{0,1:T(8,128)}, u32[]{:S(2)}) copy-start(f32[128,512]{0,1:T(8,128)} %get-tuple-element.57) | copy-start | bytes 786436
  139.6 13.9 %copy-start.18 = (f32[512,128]{1,0:T(8,128)S(1)}, f32[512,128]{1,0:T(8,128)}, u32[]{:S(2)}) copy-start(f32[512,128]{1,0:T(8,128)} %param.18) | copy-start | bytes 786436
  139.6 13.9 %copy-start.22 = (f32[512,128]{1,0:T(8,128)S(1)}, f32[512,128]{1,0:T(8,128)}, u32[]{:S(2)}) copy-start(f32[512,128]{1,0:T(8,128)} %param.22) | copy-start | bytes 786436
  139.6 13.9 %copy-start.23 = (f32[512,128]{1,0:T(8,128)S(1)}, f32[512,128]{1,0:T(8,128)}, u32[]{:S(2)}) copy-start(f32[512,128]{1,0:T(8,128)} %param.23) | copy-start | bytes 786436
  139.6 1.3 collective-permute-start.22
  140.9 3.8 %collective-permute-start.23 = (f32[44,128]{1,0:T(8,128)S(1)}, f32[44,128]{1,0:T(8,128)S(1)}, u32[]{:S(2)}, u32[]{:S(2)}) collective-permute-start(f32[44,128]{1,0:T(8,128)S(1)} %add.154), channel_id=1, source_target_pairs={{0,2},{1,3},{2,0},{3,1},{4,6},{5,7},{6,4},{7,5},{8,10},{9,11},{10,... | collective-permute-start | bytes 67592 | tf_op jit(solution)/shard_map/ppermute | solution.py:455
  144.7 3.8 %collective-permute-start.24 = (f32[44,128]{1,0:T(8,128)S(1)}, f32[44,128]{1,0:T(8,128)S(1)}, u32[]{:S(2)}, u32[]{:S(2)}) collective-permute-start(f32[44,128]{1,0:T(8,128)S(1)} %add.155), channel_id=1, source_target_pairs={{0,16},{16,0},{1,17},{17,1},{2,18},{18,2},{3,19},{19,3},{4,20},{20... | collective-permute-start | bytes 67592 | tf_op jit(solution)/shard_map/ppermute | solution.py:463
  148.5 3.8 %collective-permute-start.25 = (f32[44,128]{1,0:T(8,128)S(1)}, f32[44,128]{1,0:T(8,128)S(1)}, u32[]{:S(2)}, u32[]{:S(2)}) collective-permute-start(f32[44,128]{1,0:T(8,128)S(1)} %add.156), channel_id=1, source_target_pairs={{0,4},{1,5},{2,6},{3,7},{4,0},{5,1},{6,2},{7,3},{8,12},{9,13},{10,... | collective-permute-start | bytes 67592 | tf_op jit(solution)/shard_map/ppermute | solution.py:455
  149.4 7.7 %copy-start.26 = (f32[2048]{0:T(1024)S(1)}, f32[2048]{0:T(1024)}, u32[]{:S(2)}) copy-start(f32[2048]{0:T(1024)} %param.24) | copy-start | bytes 24580
  149.4 7.7 %copy-start.27 = (f32[2048]{0:T(1024)S(1)}, f32[2048]{0:T(1024)}, u32[]{:S(2)}) copy-start(f32[2048]{0:T(1024)} %param.25) | copy-start | bytes 24580
  149.4 8.4 %copy-start.24 = (f32[7,512]{1,0:T(8,128)S(1)}, f32[7,512]{1,0:T(8,128)}, u32[]{:S(2)}) copy-start(f32[7,512]{1,0:T(8,128)} %param.28) | copy-start | bytes 43012
  149.4 8.4 %copy-start.25 = (f32[7,512]{1,0:T(8,128)S(1)}, f32[7,512]{1,0:T(8,128)}, u32[]{:S(2)}) copy-start(f32[7,512]{1,0:T(8,128)} %param.29) | copy-start | bytes 43012
  152.4 4.7 %collective-permute-start.26 = (f32[44,128]{1,0:T(8,128)S(1)}, f32[44,128]{1,0:T(8,128)S(1)}, u32[]{:S(2)}, u32[]{:S(2)}) collective-permute-start(f32[44,128]{1,0:T(8,128)S(1)} %add.157), channel_id=1, source_target_pairs={{0,8},{1,9},{2,10},{3,11},{4,12},{5,13},{6,14},{7,15},{8,0},{9,1},... | collective-permute-start | bytes 67592 | tf_op jit(solution)/shard_map/ppermute | solution.py:455

commit v2 on v1

--- a/solution.py
+++ b/solution.py
@@ -192,8 +192,6 @@
     )
 
 
-BLOCKS = 8
-PAIRS = BLOCKS // 2
 f32 = jnp.float32
 bf16 = jnp.bfloat16
 VMEM = pl.BlockSpec(memory_space=pltpu.VMEM)
@@ -284,12 +282,13 @@
 
 
 def normal_parts(h):
-    a = jnp.abs(h)
-    t = 1.0 / (1.0 + (0.3275911 / math.sqrt(2.0)) * a)
+    d = 1.0 + (0.3275911 / math.sqrt(2.0)) * jnp.abs(h)
+    t = pl.reciprocal(d, approx=True)
+    t = t * (2.0 - d * t)
     series = 0.5 * 1.061405429
     for c in (-1.453152027, 1.421413741, -0.284496736, 0.254829592):
         series = series * t + 0.5 * c
-    e = jnp.exp(-0.5 * h * h)
+    e = jnp.exp2((-0.5 * math.log2(math.e)) * (h * h))
     tail = series * t * e
     phi = jnp.where(h < 0.0, tail, 1.0 - tail)
     return phi, phi + h * (e * (1.0 / math.sqrt(2.0 * math.pi)))
@@ -299,78 +298,79 @@
     return lax.dot_general(left, right, (dims, ((), ())), preferred_element_type=f32)
 
 
-def hidden_kernel(place_ref, own_ref, oth_ref, bias_ref, *refs):
-    w_refs, (act_ref, slope_ref, grad_ref, w_ref, h_ref) = refs[:BLOCKS], refs[BLOCKS:]
-    j = pl.program_id(0)
-
-    @pl.when(j == 0)
-    def _():
-        for k in range(BLOCKS):
-            w_ref[k // 2, :, (k % 2) * 128 : (k % 2 + 1) * 128] = w_refs[k][...]
-
-    bias = jnp.concatenate(
-        [bias_ref[pl.ds(place_ref[2 * j], 1), :], bias_ref[pl.ds(place_ref[2 * j + 1], 1), :]], axis=1
-    )
-    weight = w_ref[j]
-    grad = None
-    for r, sb_ref in enumerate((own_ref, oth_ref)):
-        h_ref[...] = dot(sb_ref[0], weight, ((1,), (0,))) + bias
-
-        def tile(i, carry):
-            rows = pl.ds(pl.multiple_of(i * 112, 16), 112)
-            h = h_ref[rows, :]
+def side_by_side(refs, j):
+    left, right = refs[2 * j], refs[2 * j + 1]
+    return jnp.concatenate([left[...], right[...]], axis=1)
+
+
+def cast_kernel(a_ref, b_ref, out_ref):
+    out_ref[0] = a_ref[...].astype(bf16)
+    out_ref[1] = b_ref[...].T.astype(bf16)
+
+
+def block_kernel(first, count, started, place_ref, own_ref, oth_ref, bias_ref, *refs):
+    w_refs, refs = refs[:count], refs[count:]
+    old, refs = (refs[:2], refs[2:]) if started else (None, refs)
+    totals, sums_ref, outs = refs[:2], refs[2], refs[3:]
+    sums_ref[...] = jnp.zeros_like(sums_ref)
+    sides = (own_ref, oth_ref)
+    runs = [[None, None], [None, None]]
+    for j in range(count // 2):
+        lines = [pl.ds(place_ref[first + 2 * j + k], 1) for k in range(2)]
+        bias = jnp.concatenate([bias_ref[line, :] for line in lines], axis=1)
+        a, b = (jnp.concatenate([w_refs[2 * j + k][i] for k in range(2)], axis=1) for i in range(2))
+        grads = [None, None]
+        sums = None
+        for r, sb_ref in enumerate(sides):
+            h = dot(sb_ref[0], a, ((1,), (0,))) + bias
+            back = dot(sb_ref[1], b, ((1,), (0,)))
             phi, slope = normal_parts(h)
-            act_ref[r, rows, :] = (h * phi).astype(bf16)
-            slope_ref[r, rows, :] = slope.astype(bf16)
-            return carry
-
-        lax.fori_loop(0, h_ref.shape[0] // 112, tile, 0)
-        part = dot(sb_ref[1], act_ref[r], ((0,), (0,)))
-        grad = part if grad is None else grad + part
-    for k in range(2):
-        grad_ref[k] = grad[:, k * 128 : (k + 1) * 128].astype(bf16)
-
-
-def slope_kernel(place_ref, own_ref, oth_ref, slope_ref, *refs):
-    w_refs, (hg_ref, grad_ref, sums_ref, w_ref) = refs[:BLOCKS], refs[BLOCKS:]
-    j = pl.program_id(0)
-
-    @pl.when(j == 0)
-    def _():
-        sums_ref[...] = jnp.zeros_like(sums_ref)
-        for k in range(BLOCKS):
-            w_ref[k // 2, :, (k % 2) * 128 : (k % 2 + 1) * 128] = w_refs[k][...]
-
-    weight = w_ref[j]
-    grad = sums = None
-    for r, sb_ref in enumerate((own_ref, oth_ref)):
-        back = dot(sb_ref[1], weight, ((1,), (0,)))
-        low = (back * slope_ref[r].astype(f32)).astype(bf16)
-        hg_ref[r] = low
-        column = jnp.sum(low.astype(f32), axis=0, keepdims=True)
-        part = dot(sb_ref[0], low, ((0,), (0,)))
-        grad = part if grad is None else grad + part
-        sums = column if sums is None else sums + column
-    for k in range(2):
-        grad_ref[k] = grad[:, k * 128 : (k + 1) * 128].astype(bf16)
-        sums_ref[pl.ds(place_ref[2 * j + k], 1), :] = sums[:, k * 128 : (k + 1) * 128]
-
-
-def back_kernel(act_ref, hg_ref, *refs):
-    a_refs, b_refs, (out_ref,) = refs[:BLOCKS], refs[BLOCKS : 2 * BLOCKS], refs[2 * BLOCKS :]
-    for i, (left_ref, w_refs) in enumerate(((act_ref, b_refs), (hg_ref, a_refs))):
-        total = None
-        for j in range(PAIRS):
-            weight = jnp.concatenate([w_refs[2 * j][...], w_refs[2 * j + 1][...]], axis=1)
-            part = dot(left_ref[0, :, j * 256 : (j + 1) * 256], weight, ((1,), (1,)))
-            total = part if total is None else total + part
-        out_ref[i] = total.astype(out_ref.dtype)
+            active = (h * phi).astype(bf16)
+            low = (back * slope).astype(bf16)
+            column = jnp.sum(low.astype(f32), axis=0, keepdims=True)
+            sums = column if r == 0 else sums + column
+            for i, (left, right) in enumerate(((sb_ref[0], low), (sb_ref[1], active))):
+                part = dot(left, right, ((0,), (0,)))
+                grads[i] = part if r == 0 else grads[i] + part
+            for i, (left, right) in enumerate(((active, b), (low, a))):
+                part = dot(left, right, ((1,), (1,)))
+                runs[r][i] = part if j == 0 else runs[r][i] + part
+        for k in range(2):
+            half = slice(k * 128, (k + 1) * 128)
+            sums_ref[lines[k], :] = sums[:, half]
+            for i, grad in enumerate(grads):
+                outs[2 * j + k][i] = grad[:, half].astype(outs[2 * j + k].dtype)
+    for r, total_ref in enumerate(totals):
+        for i in range(2):
+            total = runs[r][i] if old is None else old[r][i] + runs[r][i]
+            total_ref[i] = total.astype(total_ref.dtype)
+
+
+def update_kernel(own_ref, got_ref, sums_ref, *refs):
+    state, outs = [refs[i : i + 3] for i in range(0, 12, 3)], refs[12:]
+    grads = own_ref[...].astype(f32) + got_ref[...].astype(f32)
+    lines = state[1][0].shape[0]
+    wide = [
+        jnp.concatenate([sums_ref[lines + 4 * i + k : lines + 4 * i + k + 1, :] for k in range(4)], axis=1)
+        for i in range(state[3][0].shape[0])
+    ]
+    settings = (
+        (grads[0], 0.04, weight_shrink),
+        (sums_ref[:lines, :], 0.2, 0.0),
+        (grads[1].T, 0.02, weight_shrink),
+        (jnp.concatenate(wide, axis=0), 0.3, 0.0),
+    )
+    for n, (grad, rate, shrink) in enumerate(settings):
+        param, moment, square = (ref[...] for ref in state[n])
+        new = adamw_update(param, grad, moment, square, rate, shrink)
+        for ref, values in zip(outs[3 * n : 3 * n + 3], new):
+            ref[...] = values
 
 
 def post_kernel(
-    counts_ref, x_ref, cot_ref, vec_ref, q_ref, stat_ref, own_ref, got_ref,
-    out_ref, grad_ref, sums_ref, t_ref, h_ref,
+    counts_ref, x_ref, cot_ref, vec_ref, q_ref, stat_ref, own_ref, got_ref, *refs
 ):
+    bias_refs, (out_ref, grad_ref, sums_ref, t_ref, h_ref) = refs[:-5], refs[-5:]
     pixels, images, width = x_ref.shape
     size = pixels * width
     zero = jnp.zeros((images, width), f32)
@@ -426,17 +426,31 @@
         return carry
 
     loop(third, 0)
+    lines = bias_refs[0].shape[0]
+    sums_ref[:lines, :] = bias_refs[0][...] + bias_refs[1][...] + bias_refs[2][...]
     for i, total in enumerate((g_gain1, g_shift1, g_mix, g_gain2, g_shift2, g_scale, g_lower * scale)):
-        sums_ref[i : i + 1, :] = column(total)
-
-
-def call(kernel, outs, ins, scratch=(), vmem=48, **kw):
+        total = column(total)
+        for k in range(width // 128):
+            row = lines + (width // 128) * i + k
+            sums_ref[row : row + 1, :] = total[:, k * 128 : (k + 1) * 128]
+
+
+def call(kernel, outs, ins, scratch=(), vmem=12, flops=0, smem=0, hold=True):
+    many = isinstance(outs, (list, tuple))
+    arrays = (*ins, *(outs if many else [outs]))
+    moved = sum(math.prod(v.shape) * v.dtype.itemsize for v in arrays)
+    if hold:
+        outs = [pltpu.VMEM(v.shape, v.dtype) for v in outs] if many else pltpu.VMEM(outs.shape, outs.dtype)
+        ins = [v if i < smem else pltpu.with_memory_space_constraint(v, pltpu.VMEM) for i, v in enumerate(ins)]
     return pl.pallas_call(
         kernel,
         out_shape=outs,
+        in_specs=[SMEM] * smem + [VMEM] * (len(ins) - smem),
+        out_specs=[VMEM] * len(outs) if many else VMEM,
         scratch_shapes=list(scratch),
+        name=getattr(kernel, "func", kernel).__name__,
         compiler_params=pltpu.CompilerParams(vmem_limit_bytes=vmem * 2**20),
-        **kw,
+        cost_estimate=pl.CostEstimate(flops=flops, bytes_accessed=moved, transcendentals=0),
     )(*ins)
 
 
@@ -444,11 +458,12 @@
     return jax.ShapeDtypeStruct(shape, dtype)
 
 
-def joint(change):
-    return [(n * 16 + w, n * 16 + change(n, w)) for n in range(2) for w in range(16)]
-
-
 BOTH = ("narrow", "wide")
+
+
+def joint(values, change):
+    pairs = [(n * 16 + w, change(n, w)) for n in range(2) for w in range(16)]
+    return lax.ppermute(values, BOTH, [(s, n * 16 + w) for s, (n, w) in pairs])
 
 
 def flip(values, bit):
@@ -456,42 +471,26 @@
 
 
 def far(values):
-    return lax.ppermute(values, BOTH, joint(lambda n, w: w ^ (12 if n else 8)))
+    return joint(values, lambda n, w: (n, w ^ (12 if n else 8)))
 
 
 def across(values):
     return lax.ppermute(values, "narrow", [(0, 1), (1, 0)])
 
 
-def gather_blocks(own):
-    z1 = flip(own, 4)
-    zf = far(own)
-    y0 = flip(own, 2)
-    y1 = flip(z1, 2)
-    yf = flip(zf, 2)
-    zo = across(zf)
-    yo = across(yf)
-    return [own, z1, zf, zo, y0, y1, yf, yo]
-
-
-def reduce_blocks(g):
-    x = across(jnp.stack([g[3], g[7]]))
-    y = flip(g[4:6], 2)
-    wide = lambda v: v.astype(f32)
-    yf = flip((wide(g[6]) + wide(x[1])).astype(bf16), 2)
-    z1 = flip((wide(g[1]) + wide(y[1])).astype(bf16), 4)
-    zf = far((wide(g[2]) + wide(x[0]) + wide(yf)).astype(bf16))
-    own = (wide(g[0]) + wide(y[0]) + wide(z1) + wide(zf)).astype(bf16)
-    return wide(own) + wide(across(own))
-
-
-def sum_all(values):
-    for bit in (1, 2):
-        values = values + flip(values, bit)
-    values = values + across(values)
-    for bit in (4, 8):
-        values = values + flip(values, bit)
-    return values
+def diagonal(values):
+    return joint(values, lambda n, w: (1 - n, w ^ 2))
+
+
+def after(values, *others):
+    return lax.optimization_barrier((values, *others))[0]
+
+
+def wide_sum(*parts):
+    total = parts[0].astype(f32)
+    for part in parts[1:]:
+        total = total + part.astype(f32)
+    return total
 
 
 def local_tree(
@@ -516,14 +515,18 @@
     units = hidden_weight.shape[1]
     near, wide = lax.axis_index("narrow"), lax.axis_index("wide")
     first_far = jnp.where(near == 0, 8, 12)
-    marks = jnp.stack([0 * first_far, 0 * first_far + 4, first_far, 20 - first_far])
-    place = wide ^ jnp.concatenate([marks, marks ^ 2])
-    place = place.astype(jnp.int32)
-
+    last_far = 20 - first_far
+    zero = 0 * first_far
+    place = [zero, zero + 4, first_far, zero + 2, zero + 6, first_far ^ 2, last_far, last_far ^ 2]
+    place = (wide ^ jnp.stack(place)).astype(jnp.int32)
+
+    pair, pair_f = struct((2, width, units), bf16), struct((2, width, units))
+    w0 = call(cast_kernel, pair, (hidden_weight, output_weight))
+    wz1, wzf, wy0 = flip(w0, 4), far(w0), flip(w0, 2)
+    features, cotangent, wz1, wy0 = lax.optimization_barrier((features, cotangent, wz1, wy0))
+    wy1 = flip(wz1, 2)
     x = features.transpose(1, 0, 2)
     cot = cotangent.transpose(1, 0, 2)
-    a_blocks = gather_blocks(hidden_weight.astype(bf16))
-    b_blocks = gather_blocks(output_weight.T.astype(bf16))
     big = struct((pixels, images, width))
     keep = pltpu.VMEM((pixels, images, width), f32)
     sb, q, stat = call(
@@ -531,71 +534,68 @@
         [struct((2, pixels, images, width), bf16), big, struct((4, images, 128))],
         (counts, x, cot, vectors),
         [keep, keep],
-        in_specs=[SMEM, VMEM, VMEM, VMEM],
-        out_specs=[VMEM] * 3,
-    )
-    sb = sb.reshape(2, rows, width)
+        smem=1,
+    )
+    sb = after(sb.reshape(2, rows, width), wzf, wy1)
     other = flip(sb, 1)
+    wyf, wzo, wyo = flip(wzf, 2), across(wzf), diagonal(wzf)
     bias = hidden_bias.reshape(-1, 128)
-    tall = pl.BlockSpec((2, rows, 256), lambda j: (0, 0, j))
-    pair = pl.BlockSpec((2, width, 128), lambda j: (j, 0, 0))
-    hidden = struct((2, rows, BLOCKS * 128), bf16)
-    grads = struct((BLOCKS, width, 128), bf16)
-    w_keep = pltpu.VMEM((PAIRS, width, 256), bf16)
-    active, slope, out_part = call(
-        hidden_kernel,
-        [hidden, hidden, grads],
-        (place, sb, other, bias, *a_blocks),
-        [w_keep, pltpu.VMEM((rows, 256), f32)],
-        grid=(PAIRS,),
-        in_specs=[SMEM] + [VMEM] * (3 + BLOCKS),
-        out_specs=[tall, tall, pair],
-    )
-    hidden_grad, hidden_part, bias_part = call(
-        slope_kernel,
-        [hidden, grads, struct(bias.shape)],
-        (place, sb, other, slope, *b_blocks),
-        [w_keep],
-        grid=(PAIRS,),
-        in_specs=[SMEM, VMEM, VMEM, tall] + [VMEM] * BLOCKS,
-        out_specs=[tall, pair, pl.BlockSpec(bias.shape, lambda j: (0, 0))],
-    )
-
-    def back(r, dtype):
-        half = pl.BlockSpec((1, rows, BLOCKS * 128), lambda j: (r, 0, 0))
+    total, total_low = struct((2, rows, width)), struct((2, rows, width), bf16)
+
+    def blocks(first, weights, grads, old=(), last=False):
         return call(
-            back_kernel,
-            struct((2, rows, width), dtype),
-            (active, hidden_grad, *a_blocks, *b_blocks),
-            grid=(1,),
-            in_specs=[half, half] + [VMEM] * (2 * BLOCKS),
-            out_specs=VMEM,
+            functools.partial(block_kernel, first, len(weights), bool(old)),
+            [total, total_low if last else total, struct(bias.shape), *grads],
+            (place, sb, other, bias, *weights, *old),
+            smem=1,
+            vmem=20,
         )
 
-    got = flip(back(1, bf16), 1).reshape(2, pixels, images, width)
-    mine = back(0, f32).reshape(2, pixels, images, width)
-    block_out, input_grad, vector_part = call(
+    *old, sums1, g0, gz1, gzf, gy0 = blocks(0, [w0, wz1, wzf, wy0], [pair_f] * 3 + [pair])
+    wy1, wyf, _ = lax.optimization_barrier((wy1, wyf, old[0]))
+    *old, sums2, gy1, gyf = blocks(4, [wy1, wyf], [pair, pair], old)
+    yf = flip(gyf, 2)
+    wzo, wyo, _ = lax.optimization_barrier((wzo, wyo, old[0]))
+    mine, theirs, sums3, gzo, gyo = blocks(6, [wzo, wyo], [pair, pair], old, True)
+    xs, ds, got = across(gzo), diagonal(gyo), flip(theirs, 1)
+    y1, y0 = flip(after(gy1, got), 2), flip(after(gy0, got), 2)
+
+    shape = (2, pixels, images, width)
+    payload = struct((bias.shape[0] + vectors.size // 128, 128))
+    block_out, input_grad, sums = call(
         post_kernel,
-        [big, big, struct((7, width))],
-        (counts, x, cot, vectors, q, stat, mine, got),
+        [big, big, payload],
+        (counts, x, cot, vectors, q, stat, mine.reshape(shape), got.reshape(shape), sums1, sums2, sums3),
         [keep, keep],
-        in_specs=[SMEM] + [VMEM] * 7,
-        out_specs=[VMEM] * 3,
-    )
-    output_grad = reduce_blocks(out_part).T
-    weight_grad = reduce_blocks(hidden_part)
-    sums = sum_all(jnp.concatenate([bias_part, vector_part.reshape(-1, 128)]))
-    split = bias.shape[0]
-    bias_grad = sums[:split].reshape(hidden_bias.shape)
-    vector_grad = sums[split:].reshape(vectors.shape)
-    hidden_new = adamw_update(
-        hidden_weight, weight_grad, hidden_moment, hidden_square, 0.04, weight_shrink
-    )
-    bias_new = adamw_update(hidden_bias, bias_grad, bias_moment, bias_square, 0.2, 0.0)
-    output_new = adamw_update(
-        output_weight, output_grad, output_moment, output_square, 0.02, weight_shrink
-    )
-    vector_new = adamw_update(vectors, vector_grad, vector_moment, vector_square, 0.3, 0.0)
+        smem=1,
+        hold=False,
+    )
+    xs, yf, ds, _ = lax.optimization_barrier((xs, yf, ds, sums))
+    sum_f = wide_sum(gzf, xs, yf, ds).astype(bf16)
+    zf = far(sum_f)
+    y1, y0, _ = lax.optimization_barrier((y1, y0, sum_f))
+    z1 = flip(wide_sum(gz1, y1).astype(bf16), 4)
+    for bit in (1, 4, 8):
+        sums = sums + flip(sums, bit)
+    own = wide_sum(g0, y0, z1, zf).astype(bf16)
+    own, sums = lax.optimization_barrier((own, sums))
+    got = across(own)
+    sums = sums + across(sums)
+    sums = sums + flip(sums, 2)
+    state = (
+        (hidden_weight, hidden_moment, hidden_square),
+        tuple(v.reshape(bias.shape) for v in (hidden_bias, bias_moment, bias_square)),
+        (output_weight, output_moment, output_square),
+        (vectors, vector_moment, vector_square),
+    )
+    new = call(
+        update_kernel,
+        [struct(v.shape) for group in state for v in group],
+        (own, got, sums, *(v for group in state for v in group)),
+        hold=False,
+    )
+    hidden_new, output_new, vector_new = new[:3], new[6:9], new[9:]
+    bias_new = [v.reshape(hidden_bias.shape) for v in new[3:6]]
     return (
         block_out.transpose(1, 0, 2),
         input_grad.transpose(1, 0, 2),

time: 159 us -> 107 us (0.67)
  waiting for transfers between devices: 54.1 us -> 38.8 us
  Pallas kernels: 43.3 us -> 28.5 us
  starting transfers between devices: 38.4 us -> 26.8 us
  other arithmetic: 6.72 us -> 0.35 us
  local copies, waits for them, and re-layouts: 14.2 us -> 9.82 us
    pallas_call x6 -> x7, Pallas kernels: 43.3 us -> 28.5 us  [call(): pl.pallas_call(kernel, out_shape=outs, in_specs=[SMEM] * smem + [VMEM] *...]
    ppermute x9 -> x4, waiting for transfers between devices: 17.3 us -> 4.62 us  [across(): return lax.ppermute(values, 'narrow', [(0, 1), (1, 0)])]
    ppermute x4, waiting for transfers between devices: 13.3 us -> 3.4 us  [joint(): return lax.ppermute(values, BOTH, [(s, n * 16 + w) for s, (n, w) in pairs])]
    ppermute x20 -> x14, starting transfers between devices: 24 us -> 16.6 us  [flip(): return lax.ppermute(values, 'wide', [(w, w ^ bit) for w in range(16)])]
    ppermute x20 -> x14, waiting for transfers between devices: 23.5 us -> 30.8 us  [flip(): return lax.ppermute(values, 'wide', [(w, w ^ bit) for w in range(16)])]
    ppermute x9 -> x4, starting transfers between devices: 7.17 us -> 2.16 us  [across(): return lax.ppermute(values, 'narrow', [(0, 1), (1, 0)])]
    sub x4 -> x0, other arithmetic: 4.58 us -> none  [adamw_update(): param - rate * (moment_hat / (jnp.sqrt(square_hat) + adam_epsilon) + shri...]
    unnamed x63 -> x54, local copies, waits for them, and re-layouts: 14 us -> 9.74 us
  transfers between devices with their start and end apart: 33 -> 22, of which waited for: 23 -> 10; matrix products, arithmetic and copies ran while one was open for 7% -> 0% of each run, Pallas kernels for 7% -> 20%
where the time goes in v2:
time: 107 us; the launch traced here: 106 us
  waiting for transfers between devices  38.8 us (36%)
  Pallas kernels  28.5 us (27%)
  starting transfers between devices  26.8 us (25%)
  local copies, waits for them, and re-layouts  9.82 us (9%)
  between operations  1.84 us (2%)
    ppermute x14, waiting for transfers between devices, flip(): return lax.ppermute(values, 'wide', [(w, w ^ bit) for w in range(16)])  30.8 us
    pallas_call x7, Pallas kernels, call(): pl.pallas_call(kernel, out_shape=outs, in_specs=[SMEM] * smem + [VMEM] *...  28.5 us
    ppermute x14, starting transfers between devices, flip(): return lax.ppermute(values, 'wide', [(w, w ^ bit) for w in range(16)])  16.6 us
    unnamed x54, local copies, waits for them, and re-layouts  9.74 us
    ppermute x4, starting transfers between devices, joint(): return lax.ppermute(values, BOTH, [(s, n * 16 + w) for s, (n, w) in pairs])  8.04 us
    ppermute x4, waiting for transfers between devices, across(): return lax.ppermute(values, 'narrow', [(0, 1), (1, 0)])  4.62 us
    ppermute x4, waiting for transfers between devices, joint(): return lax.ppermute(values, BOTH, [(s, n * 16 + w) for s, (n, w) in pairs])  3.4 us
    ppermute x4, starting transfers between devices, across(): return lax.ppermute(values, 'narrow', [(0, 1), (1, 0)])  2.16 us
  transfers between devices with their start and end apart: 22, of which 10 were waited for; matrix products, arithmetic and copies ran while one was open for 0% of the time, Pallas kernels for 20%

profile of v2, /device:TPU:0, one launch (start us, length us, event | category | flops | bytes accessed | tf_op | source)
XLA Modules:
  0.0 106.1 jit_solution(8278318707482331850)
XLA Ops:
  0.6 0.0 copy-start.6
  0.7 0.9 copy-done.6
  1.6 0.9 copy-done.8
  2.5 0.1 cast_kernel.1.refs_0_
  2.7 3.1 %collective-permute-start = (bf16[2,512,128]{2,1,0:T(8,128)(2,1)S(1)}, bf16[2,512,128]{2,1,0:T(8,128)(2,1)S(1)}, u32[]{:S(2)}, u32[]{:S(2)}) collective-permute-start(bf16[2,512,128]{2,1,0:T(8,128)(2,1)S(1)} %cast_kernel.1.refs_0_), channel_id=1, source_target_pairs={{0,4},{1,5},{2,6},{3,7},{4,0},{5,1},{6,2},{7,3},{8,12},{9,13},{10,... | collective-permute-start | bytes 786440 | tf_op jit(solution)/shard_map/ppermute | solution.py:470
  5.7 1.5 %collective-permute-start.1 = (bf16[2,512,128]{2,1,0:T(8,128)(2,1)S(1)}, bf16[2,512,128]{2,1,0:T(8,128)(2,1)S(1)}, u32[]{:S(2)}, u32[]{:S(2)}) collective-permute-start(bf16[2,512,128]{2,1,0:T(8,128)(2,1)S(1)} %cast_kernel.1.refs_0_), channel_id=1, source_target_pairs={{0,2},{1,3},{2,0},{3,1},{4,6},{5,7},{6,4},{7,5},{8,10},{9,11},{10,... | collective-permute-start | bytes 786440 | tf_op jit(solution)/shard_map/ppermute | solution.py:470
  7.3 2.6 %collective-permute-start.2 = (bf16[2,512,128]{2,1,0:T(8,128)(2,1)S(1)}, bf16[2,512,128]{2,1,0:T(8,128)(2,1)}, u32[]{:S(2)}, u32[]{:S(2)}) collective-permute-start(bf16[2,512,128]{2,1,0:T(8,128)(2,1)S(1)} %cast_kernel.1.refs_0_), channel_id=1, source_target_pairs={{0,8},{1,9},{2,10},{3,11},{4,12},{5,13},{6,14},{7,15},{8,0},{9,1},... | collective-permute-start | bytes 786440 | tf_op jit(solution)/shard_map/ppermute | solution.py:466
  9.9 6.5 %collective-permute-done.refs_1_ = bf16[2,512,128]{2,1,0:T(8,128)(2,1)S(1)} collective-permute-done((bf16[2,512,128]{2,1,0:T(8,128)(2,1)S(1)}, bf16[2,512,128]{2,1,0:T(8,128)(2,1)S(1)}, u32[]{:S(2)}, u32[]{:S(2)}) %collective-permute-start) | collective-permute-done | bytes 262176 | tf_op jit(solution)/shard_map/ppermute | solution.py:470
  16.3 0.7 copy-done.16
  17.1 2.7 %collective-permute-start.3 = (bf16[2,512,128]{2,1,0:T(8,128)(2,1)S(1)}, bf16[2,512,128]{2,1,0:T(8,128)(2,1)S(1)}, u32[]{:S(2)}, u32[]{:S(2)}) collective-permute-start(bf16[2,512,128]{2,1,0:T(8,128)(2,1)S(1)} %collective-permute-done.refs_1_), channel_id=1, source_target_pairs={{0,2},{1,3},{2,0},{3,1},{4,6},{5,7},{6,4},{7,5},{8,10},{9,11},{10,... | collective-permute-start | bytes 786440 | tf_op jit(solution)/shard_map/ppermute | solution.py:470
  20.4 0.0 copy-start
  20.4 1.4 %copy-done = f32[16,49,512]{2,0,1:T(8,128)S(1)} copy-done((f32[16,49,512]{2,0,1:T(8,128)S(1)}, f32[16,49,512]{2,0,1:T(8,128)}, u32[]{:S(2)}) %copy-start) | copy-done | bytes 1605656
  21.8 1.1 %copy-done.2 = bf16[16,49,512]{2,0,1:T(8,128)(2,1)S(1)} copy-done((bf16[16,49,512]{2,0,1:T(8,128)(2,1)S(1)}, bf16[16,49,512]{2,0,1:T(8,128)(2,1)}, u32[]{:S(2)}) %copy-start.2) | copy-done | bytes 802840
  23.0 0.7 copy-done.20
  23.7 1.6 %pre_kernel.1 = (bf16[2,49,16,512]{3,2,1,0:T(8,128)(2,1)S(1)}, f32[49,16,512]{2,1,0:T(8,128)S(1)}, f32[4,16,128]{2,1,0:T(8,128)S(1)}) custom-call(s32[1]{0:T(128)S(6)} %copy.29.counts_ref, f32[49,16,512]{2,1,0:T(8,128)S(1)} %bitcast.21, bf16[49,16,512]{2,1,0:T(8,128)(2,1)S(1)} %bitcast.24, f32[7,512]{1,0:T(8,128)S(1)} %copy-done.20), custom_call_target="tpu_custom_call" | custom-call | bytes 5666820 | tf_op jit(solution)/shard_map/pre_kernel/pallas_call | solution.py:445
  25.3 0.0 copy-start.4
  25.3 1.1 %copy-done.4 = f32[49,16,512]{2,1,0:T(8,128)} copy-done((f32[49,16,512]{2,1,0:T(8,128)}, f32[49,16,512]{2,1,0:T(8,128)S(1)}, u32[]{:S(2)}) %copy-start.4) | copy-done | bytes 1605656
  26.4 0.7 copy-done.18
  27.1 0.6 collective-permute-start.7
  27.7 2.9 %collective-permute-start.6 = (bf16[2,512,128]{2,1,0:T(8,128)(2,1)}, bf16[2,512,128]{2,1,0:T(8,128)(2,1)}, u32[]{:S(2)}, u32[]{:S(2)}) collective-permute-start(bf16[2,512,128]{2,1,0:T(8,128)(2,1)} %collective-permute-done.2.refs_2_), channel_id=1, source_target_pairs={{0,18},{1,19},{2,16},{3,17},{4,22},{5,23},{6,20},{7,21},{8,26},{9,... | collective-permute-start | bytes 786440 | tf_op jit(solution)/shard_map/ppermute | solution.py:466
  30.6 0.1 stack.19
  30.7 0.0 copy-start.15
  30.8 0.9 copy-done.15
  31.7 0.9 copy-done.17
  32.6 8.7 %block_kernel.3 = (f32[2,784,512]{2,1,0:T(8,128)S(1)}, f32[2,784,512]{2,1,0:T(8,128)S(1)}, f32[16,128]{1,0:T(8,128)S(1)}, f32[2,512,128]{2,1,0:T(8,128)S(1)}, f3...) custom-call(s32[8]{0:T(128)S(1)} %broadcast_xor_fusion.place_ref, ...), custom_call_target="tpu_custom_call" | custom-call | bytes 12533792 | tf_op jit(solution)/shard_map/block_kernel/pallas_call | solution.py:445
  41.4 5.3 %block_kernel.4 = (f32[2,784,512]{2,1,0:T(8,128)S(1)}, f32[2,784,512]{2,1,0:T(8,128)S(1)}, f32[16,128]{1,0:T(8,128)S(1)}, bf16[2,512,128]{2,1,0:T(8,128)(2,1)S(1)}, bf16[2,512,128]{2,1,0:T(8,128)(2,1)S(1)}) custom-call(s32[8]{0:T(128)S(1)} %broadcast_xor_fusion.place_ref, bf16[2,784,512]{2,1,0:T(8,128)(2,1)S(1)} %bitcast.19, ...), custom_call_target="tpu_custom_call" | custom-call | bytes 17121312 | tf_op jit(solution)/shard_map/block_kernel/pallas_call | solution.py:445
  46.8 0.0 copy-start.1
  46.8 0.0 copy-start.3
  46.8 0.0 copy-start.5
  46.8 0.0 copy-start.21
  46.8 5.7 %block_kernel.5 = (f32[2,784,512]{2,1,0:T(8,128)S(1)}, bf16[2,784,512]{2,1,0:T(8,128)(2,1)S(1)}, f32[16,128]{1,0:T(8,128)S(1)}, bf16[2,512,128]{2,1,0:T(8,128)(2,1)S(1)}, bf16[2,512,128]{2,1,0:T(8,128)(2,1)S(1)}) custom-call(s32[8]{0:T(128)S(1)} %broadcast_xor_fusion.place_ref, bf16[2,784,512]{2,1,0:T(8,128)(2,1)S(1)} %bitcast.20, ...), custom_call_target="tpu_custom_call" | custom-call | bytes 15515680 | tf_op jit(solution)/shard_map/block_kernel/pallas_call | solution.py:445
  52.5 0.1 collective-permute-start.8
  52.6 0.1 collective-permute-start.11
  52.6 2.0 %collective-permute-start.13 = (bf16[2,512,128]{2,1,0:T(8,128)(2,1)S(1)}, bf16[2,512,128]{2,1,0:T(8,128)(2,1)S(1)}, u32[]{:S(2)}, u32[]{:S(2)}) collective-permute-start(bf16[2,512,128]{2,1,0:T(8,128)(2,1)S(1)} %get-tuple-element.98), channel_id=1, source_target_pairs={{0,18},{1,19},{2,16},{3,17},{4,22},{5,23},{6,20},{7,21},{8,26},{9,... | collective-permute-start | bytes 786440 | tf_op jit(solution)/shard_map/ppermute | solution.py:466
  54.7 1.4 %collective-permute-start.12 = (bf16[2,512,128]{2,1,0:T(8,128)(2,1)S(1)}, bf16[2,512,128]{2,1,0:T(8,128)(2,1)S(1)}, u32[]{:S(2)}, u32[]{:S(2)}) collective-permute-start(bf16[2,512,128]{2,1,0:T(8,128)(2,1)S(1)} %get-tuple-element.97), channel_id=1, source_target_pairs={{0,2},{1,3},{2,0},{3,1},{4,6},{5,7},{6,4},{7,5},{8,10},{9,11},{10,... | collective-permute-start | bytes 786440 | tf_op jit(solution)/shard_map/ppermute | solution.py:470
  56.1 0.6 collective-permute-start.10
  56.7 1.4 %collective-permute-start.9 = (bf16[2,512,128]{2,1,0:T(8,128)(2,1)S(1)}, bf16[2,512,128]{2,1,0:T(8,128)(2,1)S(1)}, u32[]{:S(2)}, u32[]{:S(2)}) collective-permute-start(bf16[2,512,128]{2,1,0:T(8,128)(2,1)S(1)} %get-tuple-element.92), channel_id=1, source_target_pairs={{0,2},{1,3},{2,0},{3,1},{4,6},{5,7},{6,4},{7,5},{8,10},{9,11},{10,... | collective-permute-start | bytes 786440 | tf_op jit(solution)/shard_map/ppermute | solution.py:470
  58.2 5.5 %post_kernel.1 = (f32[49,16,512]{2,1,0:T(8,128)}, f32[49,16,512]{2,1,0:T(8,128)}, f32[44,128]{1,0:T(8,128)S(1)}) custom-call(s32[1]{0:T(128)S(6)} %copy.29.counts_ref, f32[49,16,512]{2,1,0:T(8,128)S(1)} %bitcast.22, bf16[49,16,512]{2,1,0:T(8,128)(2,1)S(1)} %bitcast.25, f32[7,512]{1,0:T(8,128)S(1)} %copy-done.21, f32[49,16,512]{2,1,0:T(8,128)S(1)} %copy-done.5, ...), custom_call_target="tpu_custom_call" | custom-call | bytes 12136452 | tf_op jit(solution)/shard_map/post_kernel/pallas_call | solution.py:445
  63.6 3.4 %collective-permute-done.13 = bf16[2,512,128]{2,1,0:T(8,128)(2,1)S(1)} collective-permute-done((bf16[2,512,128]{2,1,0:T(8,128)(2,1)S(1)}, bf16[2,512,128]{2,1,0:T(8,128)(2,1)S(1)}, u32[]{:S(2)}, u32[]{:S(2)}) %collective-permute-start.13) | collective-permute-done | bytes 262176 | tf_op jit(solution)/shard_map/ppermute | solution.py:466
  67.0 2.5 %collective-permute-done.12 = bf16[2,512,128]{2,1,0:T(8,128)(2,1)S(1)} collective-permute-done((bf16[2,512,128]{2,1,0:T(8,128)(2,1)S(1)}, bf16[2,512,128]{2,1,0:T(8,128)(2,1)S(1)}, u32[]{:S(2)}, u32[]{:S(2)}) %collective-permute-start.12) | collective-permute-done | bytes 262176 | tf_op jit(solution)/shard_map/ppermute | solution.py:470
  69.5 0.1 add_convert_fusion.2
  69.6 0.0 copy-start.7
  69.6 0.0 copy-start.10
  69.7 0.0 copy-start.11
  69.7 0.0 copy-start.23
  69.7 0.0 copy-start.24
  69.7 0.5 collective-permute-start.15
  70.3 4.8 %collective-permute-done.10 = bf16[2,512,128]{2,1,0:T(8,128)(2,1)S(1)} collective-permute-done((bf16[2,512,128]{2,1,0:T(8,128)(2,1)S(1)}, bf16[2,512,128]{2,1,0:T(8,128)(2,1)S(1)}, u32[]{:S(2)}, u32[]{:S(2)}) %collective-permute-start.10) | collective-permute-done | bytes 262176 | tf_op jit(solution)/shard_map/ppermute | solution.py:470
  75.1 4.5 %collective-permute-done.9 = bf16[2,512,128]{2,1,0:T(8,128)(2,1)S(1)} collective-permute-done((bf16[2,512,128]{2,1,0:T(8,128)(2,1)S(1)}, bf16[2,512,128]{2,1,0:T(8,128)(2,1)S(1)}, u32[]{:S(2)}, u32[]{:S(2)}) %collective-permute-start.9) | collective-permute-done | bytes 262176 | tf_op jit(solution)/shard_map/ppermute | solution.py:470
  79.6 0.1 add_convert_fusion.1
  79.7 0.1 collective-permute-start.14
  79.8 0.1 collective-permute-start.16
  79.8 1.2 %collective-permute-done.16 = f32[44,128]{1,0:T(8,128)S(1)} collective-permute-done((f32[44,128]{1,0:T(8,128)S(1)}, f32[44,128]{1,0:T(8,128)S(1)}, u32[]{:S(2)}, u32[]{:S(2)}) %collective-permute-start.16) | collective-permute-done | bytes 22560 | tf_op jit(solution)/shard_map/ppermute | solution.py:470
  81.0 1.9 %collective-permute-start.17 = (f32[44,128]{1,0:T(8,128)S(1)}, f32[44,128]{1,0:T(8,128)S(1)}, u32[]{:S(2)}, u32[]{:S(2)}) collective-permute-start(f32[44,128]{1,0:T(8,128)S(1)} %add.43), channel_id=1, source_target_pairs={{0,4},{1,5},{2,6},{3,7},{4,0},{5,1},{6,2},{7,3},{8,12},{9,13},{10,... | collective-permute-start | bytes 67592 | tf_op jit(solution)/shard_map/ppermute | solution.py:470
  83.0 5.6 %collective-permute-done.17 = f32[44,128]{1,0:T(8,128)S(1)} collective-permute-done((f32[44,128]{1,0:T(8,128)S(1)}, f32[44,128]{1,0:T(8,128)S(1)}, u32[]{:S(2)}, u32[]{:S(2)}) %collective-permute-start.17) | collective-permute-done | bytes 22560 | tf_op jit(solution)/shard_map/ppermute | solution.py:470
  88.6 1.7 %collective-permute-start.18 = (f32[44,128]{1,0:T(8,128)S(1)}, f32[44,128]{1,0:T(8,128)S(1)}, u32[]{:S(2)}, u32[]{:S(2)}) collective-permute-start(f32[44,128]{1,0:T(8,128)S(1)} %add.44), channel_id=1, source_target_pairs={{0,8},{1,9},{2,10},{3,11},{4,12},{5,13},{6,14},{7,15},{8,0},{9,1},... | collective-permute-start | bytes 67592 | tf_op jit(solution)/shard_map/ppermute | solution.py:470
  90.3 3.2 %collective-permute-done.18 = f32[44,128]{1,0:T(8,128)S(1)} collective-permute-done((f32[44,128]{1,0:T(8,128)S(1)}, f32[44,128]{1,0:T(8,128)S(1)}, u32[]{:S(2)}, u32[]{:S(2)}) %collective-permute-start.18) | collective-permute-done | bytes 22560 | tf_op jit(solution)/shard_map/ppermute | solution.py:470
  93.6 0.1 add_convert_fusion.own_ref
  93.7 0.1 collective-permute-start.19
  93.8 2.0 %collective-permute-start.20 = (f32[44,128]{1,0:T(8,128)S(1)}, f32[44,128]{1,0:T(8,128)S(1)}, u32[]{:S(2)}, u32[]{:S(2)}) collective-permute-start(f32[44,128]{1,0:T(8,128)S(1)} %add.45), channel_id=1, source_target_pairs={{0,16},{16,0},{1,17},{17,1},{2,18},{18,2},{3,19},{19,3},{4,20},{20... | collective-permute-start | bytes 67592 | tf_op jit(solution)/shard_map/ppermute | solution.py:478
  95.8 4.6 %collective-permute-done.20 = f32[44,128]{1,0:T(8,128)S(1)} collective-permute-done((f32[44,128]{1,0:T(8,128)S(1)}, f32[44,128]{1,0:T(8,128)S(1)}, u32[]{:S(2)}, u32[]{:S(2)}) %collective-permute-start.20) | collective-permute-done | bytes 22560 | tf_op jit(solution)/shard_map/ppermute | solution.py:478
  100.4 1.4 %collective-permute-start.21 = (f32[44,128]{1,0:T(8,128)S(1)}, f32[44,128]{1,0:T(8,128)S(1)}, u32[]{:S(2)}, u32[]{:S(2)}) collective-permute-start(f32[44,128]{1,0:T(8,128)S(1)} %add.46), channel_id=1, source_target_pairs={{0,2},{1,3},{2,0},{3,1},{4,6},{5,7},{6,4},{7,5},{8,10},{9,11},{10,... | collective-permute-start | bytes 67592 | tf_op jit(solution)/shard_map/ppermute | solution.py:470
  101.8 2.5 %collective-permute-done.21 = f32[44,128]{1,0:T(8,128)S(1)} collective-permute-done((f32[44,128]{1,0:T(8,128)S(1)}, f32[44,128]{1,0:T(8,128)S(1)}, u32[]{:S(2)}, u32[]{:S(2)}) %collective-permute-start.21) | collective-permute-done | bytes 22560 | tf_op jit(solution)/shard_map/ppermute | solution.py:470
  104.4 1.6 %update_kernel.1 = (f32[512,128]{1,0:T(8,128)}, f32[512,128]{1,0:T(8,128)}, f32[512,128]{1,0:T(8,128)}, f32[16,128]{1,0:T(8,128)}, f32[16,128]{1,0:T(8,128)}, /*...) custom-call(bf16[2,512,128]{2,1,0:T(8,128)(2,1)S(1)} %add_convert_fu, ...), custom_call_target="tpu_custom_call" | custom-call | bytes 3827712 | tf_op jit(solution)/shard_map/update_kernel/pallas_call | solution.py:445
  (51 shorter events, 0.1 us)
Async XLA Ops:
  0.6 1.0 copy-start.6
  1.6 0.9 copy-start.8
  2.5 28.2 %copy-start.22 = (f32[2048]{0:T(1024)S(1)}, f32[2048]{0:T(1024)}, u32[]{:S(2)}) copy-start(f32[2048]{0:T(1024)} %param.19) | copy-start | bytes 24580
  2.7 13.7 %collective-permute-start = (bf16[2,512,128]{2,1,0:T(8,128)(2,1)S(1)}, bf16[2,512,128]{2,1,0:T(8,128)(2,1)S(1)}, u32[]{:S(2)}, u32[]{:S(2)}) collective-permute-start(bf16[2,512,128]{2,1,0:T(8,128)(2,1)S(1)} %cast_kernel.1.refs_0_), channel_id=1, source_target_pairs={{0,4},{1,5},{2,6},{3,7},{4,0},{5,1},{6,2},{7,3},{8,12},{9,13},{10,... | collective-permute-start | bytes 786440 | tf_op jit(solution)/shard_map/ppermute | solution.py:470
  5.7 10.6 %collective-permute-start.1 = (bf16[2,512,128]{2,1,0:T(8,128)(2,1)S(1)}, bf16[2,512,128]{2,1,0:T(8,128)(2,1)S(1)}, u32[]{:S(2)}, u32[]{:S(2)}) collective-permute-start(bf16[2,512,128]{2,1,0:T(8,128)(2,1)S(1)} %cast_kernel.1.refs_0_), channel_id=1, source_target_pairs={{0,2},{1,3},{2,0},{3,1},{4,6},{5,7},{6,4},{7,5},{8,10},{9,11},{10,... | collective-permute-start | bytes 786440 | tf_op jit(solution)/shard_map/ppermute | solution.py:470
  7.3 19.2 %collective-permute-start.2 = (bf16[2,512,128]{2,1,0:T(8,128)(2,1)S(1)}, bf16[2,512,128]{2,1,0:T(8,128)(2,1)}, u32[]{:S(2)}, u32[]{:S(2)}) collective-permute-start(bf16[2,512,128]{2,1,0:T(8,128)(2,1)S(1)} %cast_kernel.1.refs_0_), channel_id=1, source_target_pairs={{0,8},{1,9},{2,10},{3,11},{4,12},{5,13},{6,14},{7,15},{8,0},{9,1},... | collective-permute-start | bytes 786440 | tf_op jit(solution)/shard_map/ppermute | solution.py:466
  16.3 10.8 %copy-start.14 = (bf16[2,512,128]{2,1,0:T(8,128)(2,1)}, bf16[2,512,128]{2,1,0:T(8,128)(2,1)S(1)}, u32[]{:S(2)}) copy-start(bf16[2,512,128]{2,1,0:T(8,128)(2,1)S(1)} %collective-permute-done.refs_1_) | copy-start | bytes 786436
  16.3 0.7 copy-start.16
  17.1 9.4 %collective-permute-start.3 = (bf16[2,512,128]{2,1,0:T(8,128)(2,1)S(1)}, bf16[2,512,128]{2,1,0:T(8,128)(2,1)S(1)}, u32[]{:S(2)}, u32[]{:S(2)}) collective-permute-start(bf16[2,512,128]{2,1,0:T(8,128)(2,1)S(1)} %collective-permute-done.refs_1_), channel_id=1, source_target_pairs={{0,2},{1,3},{2,0},{3,1},{4,6},{5,7},{6,4},{7,5},{8,10},{9,11},{10,... | collective-permute-start | bytes 786440 | tf_op jit(solution)/shard_map/ppermute | solution.py:470
  20.4 1.4 %copy-start = (f32[16,49,512]{2,0,1:T(8,128)S(1)}, f32[16,49,512]{2,0,1:T(8,128)}, u32[]{:S(2)}) copy-start(f32[16,49,512]{2,0,1:T(8,128)} %param.15) | copy-start | bytes 4816900
  21.8 1.1 %copy-start.2 = (bf16[16,49,512]{2,0,1:T(8,128)(2,1)S(1)}, bf16[16,49,512]{2,0,1:T(8,128)(2,1)}, u32[]{:S(2)}) copy-start(bf16[16,49,512]{2,0,1:T(8,128)(2,1)} %param.16) | copy-start | bytes 2408452
  23.0 0.7 copy-start.20
  25.3 1.2 %copy-start.4 = (f32[49,16,512]{2,1,0:T(8,128)}, f32[49,16,512]{2,1,0:T(8,128)S(1)}, u32[]{:S(2)}) copy-start(f32[49,16,512]{2,1,0:T(8,128)S(1)} %get-tuple-element.69.q_ref) | copy-start | bytes 4816900
  26.4 0.7 copy-start.18
  27.1 3.6 %collective-permute-start.4 = (bf16[2,784,512]{2,1,0:T(8,128)(2,1)S(1)}, bf16[2,784,512]{2,1,0:T(8,128)(2,1)S(1)}, u32[]{:S(2)}, u32[]{:S(2)}) collective-permute-start(bf16[2,784,512]{2,1,0:T(8,128)(2,1)S(1)} %bitcast.17), channel_id=1, source_target_pairs={{0,1},{1,0},{2,3},{3,2},{4,5},{5,4},{6,7},{7,6},{8,9},{9,8},{10,11... | collective-permute-start | bytes 4816904 | tf_op jit(solution)/shard_map/ppermute | solution.py:470
  27.1 14.3 %collective-permute-start.7 = (bf16[2,512,128]{2,1,0:T(8,128)(2,1)}, bf16[2,512,128]{2,1,0:T(8,128)(2,1)}, u32[]{:S(2)}, u32[]{:S(2)}) collective-permute-start(bf16[2,512,128]{2,1,0:T(8,128)(2,1)} %collective-permute-done.2.refs_2_), channel_id=1, source_target_pairs={{0,2},{1,3},{2,0},{3,1},{4,6},{5,7},{6,4},{7,5},{8,10},{9,11},{10,... | collective-permute-start | bytes 786440 | tf_op jit(solution)/shard_map/ppermute | solution.py:470
  27.7 19.0 %collective-permute-start.5 = (bf16[2,512,128]{2,1,0:T(8,128)(2,1)}, bf16[2,512,128]{2,1,0:T(8,128)(2,1)}, u32[]{:S(2)}, u32[]{:S(2)}) collective-permute-start(bf16[2,512,128]{2,1,0:T(8,128)(2,1)} %collective-permute-done.2.refs_2_), channel_id=1, source_target_pairs={{0,16},{16,0},{1,17},{17,1},{2,18},{18,2},{3,19},{19,3},{4,20},{20... | collective-permute-start | bytes 786440 | tf_op jit(solution)/shard_map/ppermute | solution.py:478
  27.7 19.0 %collective-permute-start.6 = (bf16[2,512,128]{2,1,0:T(8,128)(2,1)}, bf16[2,512,128]{2,1,0:T(8,128)(2,1)}, u32[]{:S(2)}, u32[]{:S(2)}) collective-permute-start(bf16[2,512,128]{2,1,0:T(8,128)(2,1)} %collective-permute-done.2.refs_2_), channel_id=1, source_target_pairs={{0,18},{1,19},{2,16},{3,17},{4,22},{5,23},{6,20},{7,21},{8,26},{9,... | collective-permute-start | bytes 786440 | tf_op jit(solution)/shard_map/ppermute | solution.py:466
  30.7 1.0 copy-start.15
  31.7 0.9 copy-start.17
  32.6 8.8 %copy-start.19 = (bf16[2,512,128]{2,1,0:T(8,128)(2,1)S(1)}, bf16[2,512,128]{2,1,0:T(8,128)(2,1)}, u32[]{:S(2)}) copy-start(bf16[2,512,128]{2,1,0:T(8,128)(2,1)} %copy-done.18) | copy-start | bytes 786436
  46.8 11.4 %copy-start.1 = (f32[16,49,512]{2,0,1:T(8,128)S(1)}, f32[16,49,512]{2,0,1:T(8,128)}, u32[]{:S(2)}) copy-start(f32[16,49,512]{2,0,1:T(8,128)} %param.15) | copy-start | bytes 4816900
  46.8 11.4 %copy-start.3 = (bf16[16,49,512]{2,0,1:T(8,128)(2,1)S(1)}, bf16[16,49,512]{2,0,1:T(8,128)(2,1)}, u32[]{:S(2)}) copy-start(bf16[16,49,512]{2,0,1:T(8,128)(2,1)} %param.16) | copy-start | bytes 2408452
  46.8 11.4 %copy-start.5 = (f32[49,16,512]{2,1,0:T(8,128)S(1)}, f32[49,16,512]{2,1,0:T(8,128)}, u32[]{:S(2)}) copy-start(f32[49,16,512]{2,1,0:T(8,128)} %copy-done.4) | copy-start | bytes 4816900
  46.8 11.4 %copy-start.21 = (f32[7,512]{1,0:T(8,128)S(1)}, f32[7,512]{1,0:T(8,128)}, u32[]{:S(2)}) copy-start(f32[7,512]{1,0:T(8,128)} %refs_9_.1) | copy-start | bytes 43012
  52.5 3.6 %collective-permute-start.8 = (bf16[2,784,512]{2,1,0:T(8,128)(2,1)S(1)}, bf16[2,784,512]{2,1,0:T(8,128)(2,1)S(1)}, u32[]{:S(2)}, u32[]{:S(2)}) collective-permute-start(bf16[2,784,512]{2,1,0:T(8,128)(2,1)S(1)} %get-tuple-element.84), channel_id=1, source_target_pairs={{0,1},{1,0},{2,3},{3,2},{4,5},{5,4},{6,7},{7,6},{8,9},{9,8},{10,11... | collective-permute-start | bytes 4816904 | tf_op jit(solution)/shard_map/ppermute | solution.py:470
  52.6 11.1 %collective-permute-start.11 = (bf16[2,512,128]{2,1,0:T(8,128)(2,1)S(1)}, bf16[2,512,128]{2,1,0:T(8,128)(2,1)S(1)}, u32[]{:S(2)}, u32[]{:S(2)}) collective-permute-start(bf16[2,512,128]{2,1,0:T(8,128)(2,1)S(1)} %get-tuple-element.96), channel_id=1, source_target_pairs={{0,16},{16,0},{1,17},{17,1},{2,18},{18,2},{3,19},{19,3},{4,20},{20... | collective-permute-start | bytes 786440 | tf_op jit(solution)/shard_map/ppermute | solution.py:478
  52.6 14.4 %collective-permute-start.13 = (bf16[2,512,128]{2,1,0:T(8,128)(2,1)S(1)}, bf16[2,512,128]{2,1,0:T(8,128)(2,1)S(1)}, u32[]{:S(2)}, u32[]{:S(2)}) collective-permute-start(bf16[2,512,128]{2,1,0:T(8,128)(2,1)S(1)} %get-tuple-element.98), channel_id=1, source_target_pairs={{0,18},{1,19},{2,16},{3,17},{4,22},{5,23},{6,20},{7,21},{8,26},{9,... | collective-permute-start | bytes 786440 | tf_op jit(solution)/shard_map/ppermute | solution.py:466
  54.7 14.8 %collective-permute-start.12 = (bf16[2,512,128]{2,1,0:T(8,128)(2,1)S(1)}, bf16[2,512,128]{2,1,0:T(8,128)(2,1)S(1)}, u32[]{:S(2)}, u32[]{:S(2)}) collective-permute-start(bf16[2,512,128]{2,1,0:T(8,128)(2,1)S(1)} %get-tuple-element.97), channel_id=1, source_target_pairs={{0,2},{1,3},{2,0},{3,1},{4,6},{5,7},{6,4},{7,5},{8,10},{9,11},{10,... | collective-permute-start | bytes 786440 | tf_op jit(solution)/shard_map/ppermute | solution.py:470
  56.1 19.0 %collective-permute-start.10 = (bf16[2,512,128]{2,1,0:T(8,128)(2,1)S(1)}, bf16[2,512,128]{2,1,0:T(8,128)(2,1)S(1)}, u32[]{:S(2)}, u32[]{:S(2)}) collective-permute-start(bf16[2,512,128]{2,1,0:T(8,128)(2,1)S(1)} %get-tuple-element.94), channel_id=1, source_target_pairs={{0,2},{1,3},{2,0},{3,1},{4,6},{5,7},{6,4},{7,5},{8,10},{9,11},{10,... | collective-permute-start | bytes 786440 | tf_op jit(solution)/shard_map/ppermute | solution.py:470
  56.7 22.9 %collective-permute-start.9 = (bf16[2,512,128]{2,1,0:T(8,128)(2,1)S(1)}, bf16[2,512,128]{2,1,0:T(8,128)(2,1)S(1)}, u32[]{:S(2)}, u32[]{:S(2)}) collective-permute-start(bf16[2,512,128]{2,1,0:T(8,128)(2,1)S(1)} %get-tuple-element.92), channel_id=1, source_target_pairs={{0,2},{1,3},{2,0},{3,1},{4,6},{5,7},{6,4},{7,5},{8,10},{9,11},{10,... | collective-permute-start | bytes 786440 | tf_op jit(solution)/shard_map/ppermute | solution.py:470
  69.6 34.6 %copy-start.7 = (f32[512,128]{1,0:T(8,128)S(1)}, f32[512,128]{1,0:T(8,128)}, u32[]{:S(2)}) copy-start(f32[512,128]{1,0:T(8,128)} %refs_0_.1) | copy-start | bytes 786436
  69.6 34.6 %copy-start.9 = (f32[128,512]{1,0:T(8,128)S(1)}, f32[128,512]{1,0:T(8,128)}, u32[]{:S(2)}) copy-start(f32[128,512]{1,0:T(8,128)} %refs_6_.1) | copy-start | bytes 786436
  69.6 34.6 %copy-start.10 = (f32[512,128]{1,0:T(8,128)S(1)}, f32[512,128]{1,0:T(8,128)}, u32[]{:S(2)}) copy-start(f32[512,128]{1,0:T(8,128)} %refs_1_.1) | copy-start | bytes 786436
  69.7 34.6 %copy-start.11 = (f32[512,128]{1,0:T(8,128)S(1)}, f32[512,128]{1,0:T(8,128)}, u32[]{:S(2)}) copy-start(f32[512,128]{1,0:T(8,128)} %refs_2_.1) | copy-start | bytes 786436
  69.7 34.6 %copy-start.12 = (f32[128,512]{1,0:T(8,128)S(1)}, f32[128,512]{1,0:T(8,128)}, u32[]{:S(2)}) copy-start(f32[128,512]{1,0:T(8,128)} %refs_7_.1) | copy-start | bytes 786436
  69.7 34.6 %copy-start.13 = (f32[128,512]{1,0:T(8,128)S(1)}, f32[128,512]{1,0:T(8,128)}, u32[]{:S(2)}) copy-start(f32[128,512]{1,0:T(8,128)} %refs_8_.1) | copy-start | bytes 786436
  69.7 34.6 %copy-start.23 = (f32[7,512]{1,0:T(8,128)S(1)}, f32[7,512]{1,0:T(8,128)}, u32[]{:S(2)}) copy-start(f32[7,512]{1,0:T(8,128)} %refs_10_.1) | copy-start | bytes 43012
  69.7 34.6 %copy-start.24 = (f32[7,512]{1,0:T(8,128)S(1)}, f32[7,512]{1,0:T(8,128)}, u32[]{:S(2)}) copy-start(f32[7,512]{1,0:T(8,128)} %refs_11_.1) | copy-start | bytes 43012
  69.7 34.6 %copy-start.25 = (f32[2048]{0:T(1024)S(1)}, f32[2048]{0:T(1024)}, u32[]{:S(2)}) copy-start(f32[2048]{0:T(1024)} %param.24) | copy-start | bytes 24580
  69.7 34.6 %copy-start.26 = (f32[2048]{0:T(1024)S(1)}, f32[2048]{0:T(1024)}, u32[]{:S(2)}) copy-start(f32[2048]{0:T(1024)} %param.25) | copy-start | bytes 24580
  69.7 23.8 %collective-permute-start.15 = (bf16[2,512,128]{2,1,0:T(8,128)(2,1)S(1)}, bf16[2,512,128]{2,1,0:T(8,128)(2,1)S(1)}, u32[]{:S(2)}, u32[]{:S(2)}) collective-permute-start(bf16[2,512,128]{2,1,0:T(8,128)(2,1)S(1)} %add_convert_fusion.2), channel_id=1, source_target_pairs={{0,8},{1,9},{2,10},{3,11},{4,12},{5,13},{6,14},{7,15},{8,0},{9,1},... | collective-permute-start | bytes 786440 | tf_op jit(solution)/shard_map/ppermute | solution.py:466
  79.7 13.9 %collective-permute-start.14 = (bf16[2,512,128]{2,1,0:T(8,128)(2,1)S(1)}, bf16[2,512,128]{2,1,0:T(8,128)(2,1)S(1)}, u32[]{:S(2)}, u32[]{:S(2)}) collective-permute-start(bf16[2,512,128]{2,1,0:T(8,128)(2,1)S(1)} %add_convert_fusion.1), channel_id=1, source_target_pairs={{0,4},{1,5},{2,6},{3,7},{4,0},{5,1},{6,2},{7,3},{8,12},{9,13},{10,... | collective-permute-start | bytes 786440 | tf_op jit(solution)/shard_map/ppermute | solution.py:470
  79.8 1.3 %collective-permute-start.16 = (f32[44,128]{1,0:T(8,128)S(1)}, f32[44,128]{1,0:T(8,128)S(1)}, u32[]{:S(2)}, u32[]{:S(2)}) collective-permute-start(f32[44,128]{1,0:T(8,128)S(1)} %get-tuple-element.99), channel_id=1, source_target_pairs={{0,1},{1,0},{2,3},{3,2},{4,5},{5,4},{6,7},{7,6},{8,9},{9,8},{10,11... | collective-permute-start | bytes 67592 | tf_op jit(solution)/shard_map/ppermute | solution.py:470
  81.0 7.6 %collective-permute-start.17 = (f32[44,128]{1,0:T(8,128)S(1)}, f32[44,128]{1,0:T(8,128)S(1)}, u32[]{:S(2)}, u32[]{:S(2)}) collective-permute-start(f32[44,128]{1,0:T(8,128)S(1)} %add.43), channel_id=1, source_target_pairs={{0,4},{1,5},{2,6},{3,7},{4,0},{5,1},{6,2},{7,3},{8,12},{9,13},{10,... | collective-permute-start | bytes 67592 | tf_op jit(solution)/shard_map/ppermute | solution.py:470
  88.6 4.9 %collective-permute-start.18 = (f32[44,128]{1,0:T(8,128)S(1)}, f32[44,128]{1,0:T(8,128)S(1)}, u32[]{:S(2)}, u32[]{:S(2)}) collective-permute-start(f32[44,128]{1,0:T(8,128)S(1)} %add.44), channel_id=1, source_target_pairs={{0,8},{1,9},{2,10},{3,11},{4,12},{5,13},{6,14},{7,15},{8,0},{9,1},... | collective-permute-start | bytes 67592 | tf_op jit(solution)/shard_map/ppermute | solution.py:470
  93.7 10.5 %collective-permute-start.19 = (bf16[2,512,128]{2,1,0:T(8,128)(2,1)S(1)}, bf16[2,512,128]{2,1,0:T(8,128)(2,1)S(1)}, u32[]{:S(2)}, u32[]{:S(2)}) collective-permute-start(bf16[2,512,128]{2,1,0:T(8,128)(2,1)S(1)} %add_convert_fusion.own_ref), channel_id=1, source_target_pairs={{0,16},{16,0},{1,17},{17,1},{2,18},{18,2},{3,19},{19,3},{4,20},{20... | collective-permute-start | bytes 786440 | tf_op jit(solution)/shard_map/ppermute | solution.py:478
  93.8 6.6 %collective-permute-start.20 = (f32[44,128]{1,0:T(8,128)S(1)}, f32[44,128]{1,0:T(8,128)S(1)}, u32[]{:S(2)}, u32[]{:S(2)}) collective-permute-start(f32[44,128]{1,0:T(8,128)S(1)} %add.45), channel_id=1, source_target_pairs={{0,16},{16,0},{1,17},{17,1},{2,18},{18,2},{3,19},{19,3},{4,20},{20... | collective-permute-start | bytes 67592 | tf_op jit(solution)/shard_map/ppermute | solution.py:478
  100.4 3.8 %collective-permute-start.21 = (f32[44,128]{1,0:T(8,128)S(1)}, f32[44,128]{1,0:T(8,128)S(1)}, u32[]{:S(2)}, u32[]{:S(2)}) collective-permute-start(f32[44,128]{1,0:T(8,128)S(1)} %add.46), channel_id=1, source_target_pairs={{0,2},{1,3},{2,0},{3,1},{4,6},{5,7},{6,4},{7,5},{8,10},{9,11},{10,... | collective-permute-start | bytes 67592 | tf_op jit(solution)/shard_map/ppermute | solution.py:470

commit v3 on v2

--- a/solution.py
+++ b/solution.py
@@ -235,7 +235,15 @@
     return jnp.where(slots < counts_ref[0], 1.0, 0.0)
 
 
-def pre_kernel(counts_ref, x_ref, cot_ref, vec_ref, sb_ref, q_ref, stat_ref, d_ref, h_ref):
+def mixed_parts(x_ref, mu1, r1, vec_ref, h_ref, q_ref):
+    for p in range(x_ref.shape[0]):
+        h_ref[p] = along_row(lambda i: x_ref[i] - mu1, p)
+    for p in range(x_ref.shape[0]):
+        q_ref[p] = along_col(lambda i: h_ref[i], p) * near_share(p) - (x_ref[p] - mu1)
+    return vec_ref[2:3, :] * (r1 * vec_ref[0:1, :])
+
+
+def pre_kernel(counts_ref, x_ref, cot_ref, vec_ref, sb_ref, stat_ref, d_ref, h_ref):
     pixels, images, width = x_ref.shape
     size = pixels * width
     zero = jnp.zeros((images, width), f32)
@@ -247,22 +255,21 @@
 
     def centre(p, s):
         d = x_ref[p] - mu1
-        d_ref[p] = d
         return s + d * d
 
     r1 = lax.rsqrt(row_total(loop(centre, zero)) / size + norm_epsilon)
-    for p in range(pixels):
-        h_ref[p] = along_row(lambda i: d_ref[i], p)
-    lift = vec_ref[2:3, :] * (r1 * vec_ref[0:1, :])
-    total = zero
-    for p in range(pixels):
-        q = along_col(lambda i: h_ref[i], p) * near_share(p) - d_ref[p]
-        q_ref[p] = q
-        total = total + (x_ref[p] + lift * q)
+    lift = mixed_parts(x_ref, mu1, r1, vec_ref, h_ref, d_ref)
+
+    def middle(p, s):
+        m = x_ref[p] + lift * d_ref[p]
+        h_ref[p] = m
+        return s + m
+
+    total = loop(middle, zero)
     mu2 = row_total(total) / size
 
     def spread(p, s):
-        d = x_ref[p] + lift * q_ref[p] - mu2
+        d = h_ref[p] - mu2
         d_ref[p] = d
         return s + d * d
 
@@ -308,20 +315,23 @@
     out_ref[1] = b_ref[...].T.astype(bf16)
 
 
+def joined(refs, i):
+    return jnp.concatenate([refs[0][i], refs[1][i]], axis=1)
+
+
 def block_kernel(first, count, started, place_ref, own_ref, oth_ref, bias_ref, *refs):
     w_refs, refs = refs[:count], refs[count:]
     old, refs = (refs[:2], refs[2:]) if started else (None, refs)
     totals, sums_ref, outs = refs[:2], refs[2], refs[3:]
     sums_ref[...] = jnp.zeros_like(sums_ref)
-    sides = (own_ref, oth_ref)
     runs = [[None, None], [None, None]]
     for j in range(count // 2):
         lines = [pl.ds(place_ref[first + 2 * j + k], 1) for k in range(2)]
         bias = jnp.concatenate([bias_ref[line, :] for line in lines], axis=1)
-        a, b = (jnp.concatenate([w_refs[2 * j + k][i] for k in range(2)], axis=1) for i in range(2))
+        a, b = (joined(w_refs[2 * j : 2 * j + 2], i) for i in range(2))
         grads = [None, None]
         sums = None
-        for r, sb_ref in enumerate(sides):
+        for r, sb_ref in enumerate((own_ref, oth_ref)):
             h = dot(sb_ref[0], a, ((1,), (0,))) + bias
             back = dot(sb_ref[1], b, ((1,), (0,)))
             phi, slope = normal_parts(h)
@@ -339,7 +349,10 @@
             half = slice(k * 128, (k + 1) * 128)
             sums_ref[lines[k], :] = sums[:, half]
             for i, grad in enumerate(grads):
-                outs[2 * j + k][i] = grad[:, half].astype(outs[2 * j + k].dtype)
+                if len(outs) == 2 * count:
+                    outs[2 * k + i][...] = grad[:, half].astype(bf16)
+                else:
+                    outs[2 * j + k][i] = grad[:, half].astype(outs[2 * j + k].dtype)
     for r, total_ref in enumerate(totals):
         for i in range(2):
             total = runs[r][i] if old is None else old[r][i] + runs[r][i]
@@ -348,7 +361,7 @@
 
 def update_kernel(own_ref, got_ref, sums_ref, *refs):
     state, outs = [refs[i : i + 3] for i in range(0, 12, 3)], refs[12:]
-    grads = own_ref[...].astype(f32) + got_ref[...].astype(f32)
+    grads = wide_sum(own_ref[...], got_ref[...])
     lines = state[1][0].shape[0]
     wide = [
         jnp.concatenate([sums_ref[lines + 4 * i + k : lines + 4 * i + k + 1, :] for k in range(4)], axis=1)
@@ -368,16 +381,16 @@
 
 
 def post_kernel(
-    counts_ref, x_ref, cot_ref, vec_ref, q_ref, stat_ref, own_ref, got_ref, *refs
+    counts_ref, x_ref, cot_ref, vec_ref, stat_ref, own_ref, got_ref, *refs
 ):
-    bias_refs, (out_ref, grad_ref, sums_ref, t_ref, h_ref) = refs[:-5], refs[-5:]
+    bias_refs, (out_ref, grad_ref, sums_ref, t_ref, h_ref, q_ref) = refs[:-6], refs[-6:]
     pixels, images, width = x_ref.shape
     size = pixels * width
     zero = jnp.zeros((images, width), f32)
     gate = valid_gate(counts_ref, (images, width))
     mu1, r1, mu2, r2 = (stat_ref[i][:, 0:1] for i in range(4))
     gain1, mix, gain2, scale, lower = (vec_ref[i : i + 1, :] for i in (0, 2, 3, 5, 6))
-    lift = mix * (r1 * gain1)
+    lift = mixed_parts(x_ref, mu1, r1, vec_ref, h_ref, q_ref)
 
     def loop(body, init):
         return lax.fori_loop(0, pixels, body, init, unroll=7)
@@ -435,13 +448,18 @@
             sums_ref[row : row + 1, :] = total[:, k * 128 : (k + 1) * 128]
 
 
-def call(kernel, outs, ins, scratch=(), vmem=12, flops=0, smem=0, hold=True):
+def call(kernel, outs, ins, scratch=(), vmem=12, smem=0, hold=True, loose=()):
     many = isinstance(outs, (list, tuple))
     arrays = (*ins, *(outs if many else [outs]))
     moved = sum(math.prod(v.shape) * v.dtype.itemsize for v in arrays)
     if hold:
         outs = [pltpu.VMEM(v.shape, v.dtype) for v in outs] if many else pltpu.VMEM(outs.shape, outs.dtype)
-        ins = [v if i < smem else pltpu.with_memory_space_constraint(v, pltpu.VMEM) for i, v in enumerate(ins)]
+    ins = [
+        v
+        if i < smem or not (hold or i in loose)
+        else pltpu.with_memory_space_constraint(v, pltpu.HBM if i in loose else pltpu.VMEM)
+        for i, v in enumerate(ins)
+    ]
     return pl.pallas_call(
         kernel,
         out_shape=outs,
@@ -450,7 +468,7 @@
         scratch_shapes=list(scratch),
         name=getattr(kernel, "func", kernel).__name__,
         compiler_params=pltpu.CompilerParams(vmem_limit_bytes=vmem * 2**20),
-        cost_estimate=pl.CostEstimate(flops=flops, bytes_accessed=moved, transcendentals=0),
+        cost_estimate=pl.CostEstimate(flops=0, bytes_accessed=moved, transcendentals=0),
     )(*ins)
 
 
@@ -517,71 +535,81 @@
     first_far = jnp.where(near == 0, 8, 12)
     last_far = 20 - first_far
     zero = 0 * first_far
-    place = [zero, zero + 4, first_far, zero + 2, zero + 6, first_far ^ 2, last_far, last_far ^ 2]
+    place = [zero, zero + 4, zero + 2, zero + 6, first_far, last_far, first_far ^ 2, last_far ^ 2]
     place = (wide ^ jnp.stack(place)).astype(jnp.int32)
 
     pair, pair_f = struct((2, width, units), bf16), struct((2, width, units))
-    w0 = call(cast_kernel, pair, (hidden_weight, output_weight))
+    w0 = call(cast_kernel, pair, (hidden_weight, output_weight), loose=(0, 1))
     wz1, wzf, wy0 = flip(w0, 4), far(w0), flip(w0, 2)
-    features, cotangent, wz1, wy0 = lax.optimization_barrier((features, cotangent, wz1, wy0))
     wy1 = flip(wz1, 2)
+    vectors_late = after(vectors, wz1)
     x = features.transpose(1, 0, 2)
     cot = cotangent.transpose(1, 0, 2)
     big = struct((pixels, images, width))
     keep = pltpu.VMEM((pixels, images, width), f32)
-    sb, q, stat = call(
+    sb, stat = call(
         pre_kernel,
-        [struct((2, pixels, images, width), bf16), big, struct((4, images, 128))],
-        (counts, x, cot, vectors),
+        [struct((2, pixels, images, width), bf16), struct((4, images, 128))],
+        (counts, x, cot, vectors_late),
         [keep, keep],
         smem=1,
-    )
-    sb = after(sb.reshape(2, rows, width), wzf, wy1)
+        loose=(1, 2, 3),
+    )
+    sb = after(sb.reshape(2, rows, width), wzf, wy1, wy0)
     other = flip(sb, 1)
-    wyf, wzo, wyo = flip(wzf, 2), across(wzf), diagonal(wzf)
+    wyo, wyf, wzo = diagonal(wzf), flip(wzf, 2), across(wzf)
     bias = hidden_bias.reshape(-1, 128)
     total, total_low = struct((2, rows, width)), struct((2, rows, width), bf16)
 
-    def blocks(first, weights, grads, old=(), last=False):
+    def blocks(first, weights, results, started, old=(), loose=()):
         return call(
-            functools.partial(block_kernel, first, len(weights), bool(old)),
-            [total, total_low if last else total, struct(bias.shape), *grads],
+            functools.partial(block_kernel, first, len(weights), started),
+            results,
             (place, sb, other, bias, *weights, *old),
             smem=1,
             vmem=20,
+            loose=loose,
         )
 
-    *old, sums1, g0, gz1, gzf, gy0 = blocks(0, [w0, wz1, wzf, wy0], [pair_f] * 3 + [pair])
-    wy1, wyf, _ = lax.optimization_barrier((wy1, wyf, old[0]))
-    *old, sums2, gy1, gyf = blocks(4, [wy1, wyf], [pair, pair], old)
-    yf = flip(gyf, 2)
-    wzo, wyo, _ = lax.optimization_barrier((wzo, wyo, old[0]))
-    mine, theirs, sums3, gzo, gyo = blocks(6, [wzo, wyo], [pair, pair], old, True)
-    xs, ds, got = across(gzo), diagonal(gyo), flip(theirs, 1)
-    y1, y0 = flip(after(gy1, got), 2), flip(after(gy0, got), 2)
+    lines = struct(bias.shape)
+    *old, sums1, g0, gz1, gy0, gy1 = blocks(
+        0, [w0, wz1, wy0, wy1], [total, total, lines, pair_f, pair_f, pair, pair], False, loose=(5, 6, 7)
+    )
+    y1 = flip(gy1, 2)
+    wzf, wzo, _ = lax.optimization_barrier((wzf, wzo, old[0]))
+    *old, sums2, gzf, gzo = blocks(4, [wzf, wzo], [total, total, lines, pair_f, pair], True, old, loose=(4,))
+    wyf, wyo, _ = lax.optimization_barrier((wyf, wyo, old[0]))
+    block = struct((width, units), bf16)
+    mine, theirs, sums3, *gy = blocks(6, [wyf, wyo], [total, total_low, lines] + [block] * 4, True, old)
+    xs = across(gzo)
+    ds, yf = [diagonal(gy[2]), diagonal(gy[3])], [flip(gy[0], 2), flip(gy[1], 2)]
+    theirs, y1, xs = lax.optimization_barrier((theirs, y1, xs))
+    got = flip(theirs, 1)
+    z1 = flip(wide_sum(gz1, y1).astype(bf16), 4)
 
     shape = (2, pixels, images, width)
     payload = struct((bias.shape[0] + vectors.size // 128, 128))
     block_out, input_grad, sums = call(
         post_kernel,
         [big, big, payload],
-        (counts, x, cot, vectors, q, stat, mine.reshape(shape), got.reshape(shape), sums1, sums2, sums3),
-        [keep, keep],
+        (counts, x, cot, vectors, stat, mine.reshape(shape), got.reshape(shape), sums1, sums2, sums3),
+        [keep, keep, keep],
         smem=1,
         hold=False,
     )
-    xs, yf, ds, _ = lax.optimization_barrier((xs, yf, ds, sums))
-    sum_f = wide_sum(gzf, xs, yf, ds).astype(bf16)
+    y0 = flip(after(gy0, sums), 2)
+    xs, ya, da, yb, db, z1, _ = lax.optimization_barrier((xs, yf[0], ds[0], yf[1], ds[1], z1, sums))
+    sum_f = jnp.stack([wide_sum(gzf[0], xs[0], ya, da), wide_sum(gzf[1], xs[1], yb, db)]).astype(bf16)
     zf = far(sum_f)
-    y1, y0, _ = lax.optimization_barrier((y1, y0, sum_f))
-    z1 = flip(wide_sum(gz1, y1).astype(bf16), 4)
-    for bit in (1, 4, 8):
-        sums = sums + flip(sums, bit)
+    sums = sums + flip(sums, 1)
+    sums = after(sums, sum_f)
+    sums = sums + across(sums)
+    sums = sums + flip(sums, 2)
     own = wide_sum(g0, y0, z1, zf).astype(bf16)
     own, sums = lax.optimization_barrier((own, sums))
     got = across(own)
-    sums = sums + across(sums)
-    sums = sums + flip(sums, 2)
+    for bit in (4, 8):
+        sums = sums + flip(sums, bit)
     state = (
         (hidden_weight, hidden_moment, hidden_square),
         tuple(v.reshape(bias.shape) for v in (hidden_bias, bias_moment, bias_square)),

time: 107 us -> 93.7 us (0.88)
  local copies, waits for them, and re-layouts: 9.82 us -> 0.87 us
  waiting for transfers between devices: 38.8 us -> 30.3 us
  Pallas kernels: 28.5 us -> 31.2 us
  starting transfers between devices: 26.8 us -> 29.1 us
    unnamed x54 -> x34, local copies, waits for them, and re-layouts: 9.74 us -> 0.79 us
    ppermute x14 -> x15, waiting for transfers between devices: 30.8 us -> 22.6 us  [flip(): return lax.ppermute(values, 'wide', [(w, w ^ bit) for w in range(16)])]
    ppermute x4 -> x5, starting transfers between devices: 8.04 us -> 11.9 us  [joint(): return lax.ppermute(values, BOTH, [(s, n * 16 + w) for s, (n, w) in pairs])]
    pallas_call x7, Pallas kernels: 28.5 us -> 31.2 us  [call(): pl.pallas_call(kernel, out_shape=outs, in_specs=[SMEM] * smem + [VMEM] *...]
    ppermute x4, starting transfers between devices: 2.16 us -> 0.31 us  [across(): return lax.ppermute(values, 'narrow', [(0, 1), (1, 0)])]
    ppermute x4 -> x5, waiting for transfers between devices: 3.4 us -> 2.35 us  [joint(): return lax.ppermute(values, BOTH, [(s, n * 16 + w) for s, (n, w) in pairs])]
    ppermute x14 -> x15, starting transfers between devices: 16.6 us -> 16.8 us  [flip(): return lax.ppermute(values, 'wide', [(w, w ^ bit) for w in range(16)])]
  transfers between devices with their start and end apart: 22 -> 24, of which waited for: 10 -> 12; matrix products, arithmetic and copies ran while one was open for 0% -> 0% of each run, Pallas kernels for 20% -> 30%
where the time goes in v3:
time: 93.7 us; the launch traced here: 93.5 us
  Pallas kernels  31.2 us (33%)
  waiting for transfers between devices  30.3 us (32%)
  starting transfers between devices  29.1 us (31%)
  between operations  1.78 us (2%)
    pallas_call x7, Pallas kernels, call(): pl.pallas_call(kernel, out_shape=outs, in_specs=[SMEM] * smem + [VMEM] *...  31.2 us
    ppermute x15, waiting for transfers between devices, flip(): return lax.ppermute(values, 'wide', [(w, w ^ bit) for w in range(16)])  22.6 us
    ppermute x15, starting transfers between devices, flip(): return lax.ppermute(values, 'wide', [(w, w ^ bit) for w in range(16)])  16.8 us
    ppermute x5, starting transfers between devices, joint(): return lax.ppermute(values, BOTH, [(s, n * 16 + w) for s, (n, w) in pairs])  11.9 us
    ppermute x4, waiting for transfers between devices, across(): return lax.ppermute(values, 'narrow', [(0, 1), (1, 0)])  5.31 us
    ppermute x5, waiting for transfers between devices, joint(): return lax.ppermute(values, BOTH, [(s, n * 16 + w) for s, (n, w) in pairs])  2.35 us
  transfers between devices with their start and end apart: 24, of which 12 were waited for; matrix products, arithmetic and copies ran while one was open for 0% of the time, Pallas kernels for 30%

profile of v3, /device:TPU:0, one launch (start us, length us, event | category | flops | bytes accessed | tf_op | source)
XLA Modules:
  0.0 93.5 jit_solution(16562092843459392346)
XLA Ops:
  0.7 1.1 %cast_kernel.1.refs_0_ = bf16[2,512,128]{2,1,0:T(8,128)(2,1)S(1)} custom-call(f32[512,128]{1,0:T(8,128)} %refs_0_.1, f32[128,512]{1,0:T(8,128)} %refs_6_.1), custom_call_target="tpu_custom_call" | custom-call | bytes 786432 | tf_op jit(solution)/shard_map/cast_kernel/pallas_call | solution.py:463
  1.8 3.1 %collective-permute-start = (bf16[2,512,128]{2,1,0:T(8,128)(2,1)S(1)}, bf16[2,512,128]{2,1,0:T(8,128)(2,1)S(1)}, u32[]{:S(2)}, u32[]{:S(2)}) collective-permute-start(bf16[2,512,128]{2,1,0:T(8,128)(2,1)S(1)} %cast_kernel.1.refs_0_), channel_id=1, source_target_pairs={{0,4},{1,5},{2,6},{3,7},{4,0},{5,1},{6,2},{7,3},{8,12},{9,13},{10,... | collective-permute-start | bytes 786440 | tf_op jit(solution)/shard_map/ppermute | solution.py:488
  4.9 2.6 %collective-permute-start.1 = (bf16[2,512,128]{2,1,0:T(8,128)(2,1)S(1)}, bf16[2,512,128]{2,1,0:T(8,128)(2,1)}, u32[]{:S(2)}, u32[]{:S(2)}) collective-permute-start(bf16[2,512,128]{2,1,0:T(8,128)(2,1)S(1)} %cast_kernel.1.refs_0_), channel_id=1, source_target_pairs={{0,8},{1,9},{2,10},{3,11},{4,12},{5,13},{6,14},{7,15},{8,0},{9,1},... | collective-permute-start | bytes 786440 | tf_op jit(solution)/shard_map/ppermute | solution.py:484
  7.5 1.5 %collective-permute-start.3 = (bf16[2,512,128]{2,1,0:T(8,128)(2,1)S(1)}, bf16[2,512,128]{2,1,0:T(8,128)(2,1)S(1)}, u32[]{:S(2)}, u32[]{:S(2)}) collective-permute-start(bf16[2,512,128]{2,1,0:T(8,128)(2,1)S(1)} %cast_kernel.1.refs_0_), channel_id=1, source_target_pairs={{0,2},{1,3},{2,0},{3,1},{4,6},{5,7},{6,4},{7,5},{8,10},{9,11},{10,... | collective-permute-start | bytes 786440 | tf_op jit(solution)/shard_map/ppermute | solution.py:488
  9.0 7.7 %collective-permute-done.refs_1_ = bf16[2,512,128]{2,1,0:T(8,128)(2,1)S(1)} collective-permute-done((bf16[2,512,128]{2,1,0:T(8,128)(2,1)S(1)}, bf16[2,512,128]{2,1,0:T(8,128)(2,1)S(1)}, u32[]{:S(2)}, u32[]{:S(2)}) %collective-permute-start) | collective-permute-done | bytes 262176 | tf_op jit(solution)/shard_map/ppermute | solution.py:488
  16.7 1.7 %collective-permute-start.2 = (bf16[2,512,128]{2,1,0:T(8,128)(2,1)S(1)}, bf16[2,512,128]{2,1,0:T(8,128)(2,1)S(1)}, u32[]{:S(2)}, u32[]{:S(2)}) collective-permute-start(bf16[2,512,128]{2,1,0:T(8,128)(2,1)S(1)} %collective-permute-done.refs_1_), channel_id=1, source_target_pairs={{0,2},{1,3},{2,0},{3,1},{4,6},{5,7},{6,4},{7,5},{8,10},{9,11},{10,... | collective-permute-start | bytes 786440 | tf_op jit(solution)/shard_map/ppermute | solution.py:488
  19.0 3.3 %pre_kernel.1 = (bf16[2,49,16,512]{3,2,1,0:T(8,128)(2,1)S(1)}, f32[4,16,128]{2,1,0:T(8,128)S(1)}) custom-call(s32[1]{0:T(128)S(6)} %copy.29.counts_ref, f32[49,16,512]{2,1,0:T(8,128)} %bitcast.41, bf16[49,16,512]{2,1,0:T(8,128)(2,1)} %bitcast.44, f32[7,512]{1,0:T(8,128)} %refs_9_.1), custom_call_target="tpu_custom_call" | custom-call | bytes 4061188 | tf_op jit(solution)/shard_map/pre_kernel/pallas_call | solution.py:463
  22.4 0.0 collective-permute-done.1.refs_0_
  22.4 0.0 copy-start.15
  22.4 1.9 %collective-permute-done.2.refs_3_ = bf16[2,512,128]{2,1,0:T(8,128)(2,1)S(1)} collective-permute-done((bf16[2,512,128]{2,1,0:T(8,128)(2,1)S(1)}, bf16[2,512,128]{2,1,0:T(8,128)(2,1)S(1)}, u32[]{:S(2)}, u32[]{:S(2)}) %collective-permute-start.2) | collective-permute-done | bytes 262176 | tf_op jit(solution)/shard_map/ppermute | solution.py:488
  24.3 0.7 copy-done.16
  25.0 0.0 collective-permute-start.4
  25.0 0.0 collective-permute-start.7
  25.0 0.1 stack.31
  25.1 1.4 %collective-permute-start.5 = (bf16[2,512,128]{2,1,0:T(8,128)(2,1)}, bf16[2,512,128]{2,1,0:T(8,128)(2,1)S(1)}, u32[]{:S(2)}, u32[]{:S(2)}) collective-permute-start(bf16[2,512,128]{2,1,0:T(8,128)(2,1)} %collective-permute-done.1.refs_0_), channel_id=1, source_target_pairs={{0,2},{1,3},{2,0},{3,1},{4,6},{5,7},{6,4},{7,5},{8,10},{9,11},{10,... | collective-permute-start | bytes 786440 | tf_op jit(solution)/shard_map/ppermute | solution.py:488
  26.5 2.1 %collective-permute-start.6 = (bf16[2,512,128]{2,1,0:T(8,128)(2,1)}, bf16[2,512,128]{2,1,0:T(8,128)(2,1)S(1)}, u32[]{:S(2)}, u32[]{:S(2)}) collective-permute-start(bf16[2,512,128]{2,1,0:T(8,128)(2,1)} %collective-permute-done.1.refs_0_), channel_id=1, source_target_pairs={{0,18},{1,19},{2,16},{3,17},{4,22},{5,23},{6,20},{7,21},{8,26},{9,... | collective-permute-start | bytes 786440 | tf_op jit(solution)/shard_map/ppermute | solution.py:484
  28.7 8.8 %block_kernel.3 = (f32[2,784,512]{2,1,0:T(8,128)S(1)}, f32[2,784,512]{2,1,0:T(8,128)S(1)}, f32[16,128]{1,0:T(8,128)S(1)}, f32[2,512,128]{2,1,0:T(8,128)S(1)}, f3...) custom-call(s32[8]{0:T(128)S(1)} %broadcast_xor_fusion.place_ref, ...), custom_call_target="tpu_custom_call" | custom-call | bytes 12271648 | tf_op jit(solution)/shard_map/block_kernel/pallas_call | solution.py:463
  37.5 0.0 collective-permute-done.7.refs_1_
  37.5 5.4 %block_kernel.4 = (f32[2,784,512]{2,1,0:T(8,128)S(1)}, f32[2,784,512]{2,1,0:T(8,128)S(1)}, f32[16,128]{1,0:T(8,128)S(1)}, f32[2,512,128]{2,1,0:T(8,128)S(1)}, bf16[2,512,128]{2,1,0:T(8,128)(2,1)S(1)}) custom-call(s32[8]{0:T(128)S(1)} %broadcast_xor_fusion.place_ref, bf16[2,784,512]{2,1,0:T(8,128)(2,1)S(1)} %bitcast.39, ...), custom_call_target="tpu_custom_call" | custom-call | bytes 17383456 | tf_op jit(solution)/shard_map/block_kernel/pallas_call | solution.py:463
  42.9 0.1 collective-permute-start.9
  42.9 1.4 %collective-permute-start.8 = (bf16[2,512,128]{2,1,0:T(8,128)(2,1)S(1)}, bf16[2,512,128]{2,1,0:T(8,128)(2,1)S(1)}, u32[]{:S(2)}, u32[]{:S(2)}) collective-permute-start(bf16[2,512,128]{2,1,0:T(8,128)(2,1)S(1)} %get-tuple-element.83), channel_id=1, source_target_pairs={{0,2},{1,3},{2,0},{3,1},{4,6},{5,7},{6,4},{7,5},{8,10},{9,11},{10,... | collective-permute-start | bytes 786440 | tf_op jit(solution)/shard_map/ppermute | solution.py:488
  44.4 0.0 copy-start.8
  44.4 5.0 %block_kernel.5 = (f32[2,784,512]{2,1,0:T(8,128)S(1)}, bf16[2,784,512]{2,1,0:T(8,128)(2,1)S(1)}, f32[16,128]{1,0:T(8,128)S(1)}, bf16[512,128]{1,0:T(8,128)(2,1)S...) custom-call(s32[8]{0:T(128)S(1)} %broadcast_xor_fusion.place_ref, ...), custom_call_target="tpu_custom_call" | custom-call | bytes 15515680 | tf_op jit(solution)/shard_map/block_kernel/pallas_call | solution.py:463
  49.5 0.0 copy-start.1
  49.5 1.6 %collective-permute-done.9 = bf16[2,512,128]{2,1,0:T(8,128)(2,1)S(1)} collective-permute-done((bf16[2,512,128]{2,1,0:T(8,128)(2,1)S(1)}, bf16[2,512,128]{2,1,0:T(8,128)(2,1)S(1)}, u32[]{:S(2)}, u32[]{:S(2)}) %collective-permute-start.9) | collective-permute-done | bytes 262176 | tf_op jit(solution)/shard_map/ppermute | solution.py:496
  51.1 0.1 collective-permute-done.8
  51.2 0.1 add_convert_fusion.1
  51.2 0.1 collective-permute-start.16
  51.3 1.4 %collective-permute-start.12 = (bf16[512,128]{1,0:T(8,128)(2,1)S(1)}, bf16[512,128]{1,0:T(8,128)(2,1)S(1)}, u32[]{:S(2)}, u32[]{:S(2)}) collective-permute-start(bf16[512,128]{1,0:T(8,128)(2,1)S(1)} %get-tuple-element.96), channel_id=1, source_target_pairs={{0,2},{1,3},{2,0},{3,1},{4,6},{5,7},{6,4},{7,5},{8,10},{9,11},{10,... | collective-permute-start | bytes 393224 | tf_op jit(solution)/shard_map/ppermute | solution.py:488
  52.8 1.8 %collective-permute-start.13 = (bf16[512,128]{1,0:T(8,128)(2,1)S(1)}, bf16[512,128]{1,0:T(8,128)(2,1)S(1)}, u32[]{:S(2)}, u32[]{:S(2)}) collective-permute-start(bf16[512,128]{1,0:T(8,128)(2,1)S(1)} %get-tuple-element.97), channel_id=1, source_target_pairs={{0,18},{1,19},{2,16},{3,17},{4,22},{5,23},{6,20},{7,21},{8,26},{9,... | collective-permute-start | bytes 393224 | tf_op jit(solution)/shard_map/ppermute | solution.py:484
  54.5 1.4 %collective-permute-start.14 = (bf16[512,128]{1,0:T(8,128)(2,1)S(1)}, bf16[512,128]{1,0:T(8,128)(2,1)S(1)}, u32[]{:S(2)}, u32[]{:S(2)}) collective-permute-start(bf16[512,128]{1,0:T(8,128)(2,1)S(1)} %get-tuple-element.98), channel_id=1, source_target_pairs={{0,2},{1,3},{2,0},{3,1},{4,6},{5,7},{6,4},{7,5},{8,10},{9,11},{10,... | collective-permute-start | bytes 393224 | tf_op jit(solution)/shard_map/ppermute | solution.py:488
  55.9 0.0 collective-permute-done.10
  55.9 1.2 %collective-permute-start.15 = (bf16[512,128]{1,0:T(8,128)(2,1)S(1)}, bf16[512,128]{1,0:T(8,128)(2,1)S(1)}, u32[]{:S(2)}, u32[]{:S(2)}) collective-permute-start(bf16[512,128]{1,0:T(8,128)(2,1)S(1)} %get-tuple-element.99), channel_id=1, source_target_pairs={{0,18},{1,19},{2,16},{3,17},{4,22},{5,23},{6,20},{7,21},{8,26},{9,... | collective-permute-start | bytes 393224 | tf_op jit(solution)/shard_map/ppermute | solution.py:484
  57.1 5.9 %post_kernel.1 = (f32[49,16,512]{2,1,0:T(8,128)}, f32[49,16,512]{2,1,0:T(8,128)}, f32[44,128]{1,0:T(8,128)S(1)}) custom-call(s32[1]{0:T(128)S(6)} %copy.29.counts_ref, f32[49,16,512]{2,1,0:T(8,128)S(1)} %bitcast.42, bf16[49,16,512]{2,1,0:T(8,128)(2,1)S(1)} %bitcast.45, f32[7,512]{1,0:T(8,128)S(1)} %copy-done.8, ...), custom_call_target="tpu_custom_call" | custom-call | bytes 10530820 | tf_op jit(solution)/shard_map/post_kernel/pallas_call | solution.py:463
  63.0 0.3 collective-permute-done.12
  63.3 0.0 collective-permute-done.13
  63.3 2.4 %collective-permute-done.14 = bf16[512,128]{1,0:T(8,128)(2,1)S(1)} collective-permute-done((bf16[512,128]{1,0:T(8,128)(2,1)S(1)}, bf16[512,128]{1,0:T(8,128)(2,1)S(1)}, u32[]{:S(2)}, u32[]{:S(2)}) %collective-permute-start.14) | collective-permute-done | bytes 131104 | tf_op jit(solution)/shard_map/ppermute | solution.py:488
  65.7 0.0 collective-permute-done.15
  65.7 1.4 %collective-permute-start.11 = (bf16[2,512,128]{2,1,0:T(8,128)(2,1)S(1)}, bf16[2,512,128]{2,1,0:T(8,128)(2,1)S(1)}, u32[]{:S(2)}, u32[]{:S(2)}) collective-permute-start(bf16[2,512,128]{2,1,0:T(8,128)(2,1)S(1)} %get-tuple-element.94), channel_id=1, source_target_pairs={{0,2},{1,3},{2,0},{3,1},{4,6},{5,7},{6,4},{7,5},{8,10},{9,11},{10,... | collective-permute-start | bytes 786440 | tf_op jit(solution)/shard_map/ppermute | solution.py:488
  67.1 0.1 fusion.4
  67.2 0.0 copy-start.2
  67.3 0.0 copy-start.3
  67.3 0.0 copy-start.4
  67.3 0.0 copy-start.5
  67.3 0.0 copy-start.6
  67.3 0.0 copy-start.7
  67.3 0.0 copy-start.10
  67.3 0.0 copy-start.11
  67.3 0.0 copy-start.12
  67.4 0.0 copy-start.13
  67.4 4.2 %collective-permute-start.17 = (bf16[2,512,128]{2,1,0:T(8,128)(2,1)S(1)}, bf16[2,512,128]{2,1,0:T(8,128)(2,1)S(1)}, u32[]{:S(2)}, u32[]{:S(2)}) collective-permute-start(bf16[2,512,128]{2,1,0:T(8,128)(2,1)S(1)} %pad_maximum_fusion), channel_id=1, source_target_pairs={{0,8},{1,9},{2,10},{3,11},{4,12},{5,13},{6,14},{7,15},{8,0},{9,1},... | collective-permute-start | bytes 786440 | tf_op jit(solution)/shard_map/ppermute | solution.py:484
  71.6 1.2 %collective-permute-done.18 = f32[44,128]{1,0:T(8,128)S(1)} collective-permute-done((f32[44,128]{1,0:T(8,128)S(1)}, f32[44,128]{1,0:T(8,128)S(1)}, u32[]{:S(2)}, u32[]{:S(2)}) %collective-permute-start.18) | collective-permute-done | bytes 22560 | tf_op jit(solution)/shard_map/ppermute | solution.py:488
  72.8 0.2 collective-permute-start.19
  73.0 3.7 %collective-permute-done.19 = f32[44,128]{1,0:T(8,128)S(1)} collective-permute-done((f32[44,128]{1,0:T(8,128)S(1)}, f32[44,128]{1,0:T(8,128)S(1)}, u32[]{:S(2)}, u32[]{:S(2)}) %collective-permute-start.19) | collective-permute-done | bytes 22560 | tf_op jit(solution)/shard_map/ppermute | solution.py:496
  76.6 0.5 collective-permute-start.20
  77.2 3.3 %collective-permute-done.20 = f32[44,128]{1,0:T(8,128)S(1)} collective-permute-done((f32[44,128]{1,0:T(8,128)S(1)}, f32[44,128]{1,0:T(8,128)S(1)}, u32[]{:S(2)}, u32[]{:S(2)}) %collective-permute-start.20) | collective-permute-done | bytes 22560 | tf_op jit(solution)/shard_map/ppermute | solution.py:488
  80.5 2.3 %collective-permute-done.17 = bf16[2,512,128]{2,1,0:T(8,128)(2,1)S(1)} collective-permute-done((bf16[2,512,128]{2,1,0:T(8,128)(2,1)S(1)}, bf16[2,512,128]{2,1,0:T(8,128)(2,1)S(1)}, u32[]{:S(2)}, u32[]{:S(2)}) %collective-permute-start.17) | collective-permute-done | bytes 262176 | tf_op jit(solution)/shard_map/ppermute | solution.py:484
  82.8 0.1 add_convert_fusion.own_ref
  83.0 0.1 collective-permute-start.21
  83.1 0.9 collective-permute-start.22
  84.0 3.0 %collective-permute-done.22 = f32[44,128]{1,0:T(8,128)S(1)} collective-permute-done((f32[44,128]{1,0:T(8,128)S(1)}, f32[44,128]{1,0:T(8,128)S(1)}, u32[]{:S(2)}, u32[]{:S(2)}) %collective-permute-start.22) | collective-permute-done | bytes 22560 | tf_op jit(solution)/shard_map/ppermute | solution.py:488
  87.0 2.0 %collective-permute-start.23 = (f32[44,128]{1,0:T(8,128)S(1)}, f32[44,128]{1,0:T(8,128)S(1)}, u32[]{:S(2)}, u32[]{:S(2)}) collective-permute-start(f32[44,128]{1,0:T(8,128)S(1)} %add.66), channel_id=1, source_target_pairs={{0,8},{1,9},{2,10},{3,11},{4,12},{5,13},{6,14},{7,15},{8,0},{9,1},... | collective-permute-start | bytes 67592 | tf_op jit(solution)/shard_map/ppermute | solution.py:488
  89.0 2.7 %collective-permute-done.23 = f32[44,128]{1,0:T(8,128)S(1)} collective-permute-done((f32[44,128]{1,0:T(8,128)S(1)}, f32[44,128]{1,0:T(8,128)S(1)}, u32[]{:S(2)}, u32[]{:S(2)}) %collective-permute-start.23) | collective-permute-done | bytes 22560 | tf_op jit(solution)/shard_map/ppermute | solution.py:488
  91.8 1.6 %update_kernel.1 = (f32[512,128]{1,0:T(8,128)}, f32[512,128]{1,0:T(8,128)}, f32[512,128]{1,0:T(8,128)}, f32[16,128]{1,0:T(8,128)}, f32[16,128]{1,0:T(8,128)}, /*...) custom-call(bf16[2,512,128]{2,1,0:T(8,128)(2,1)S(1)} %add_convert_fu, ...), custom_call_target="tpu_custom_call" | custom-call | bytes 3827712 | tf_op jit(solution)/shard_map/update_kernel/pallas_call | solution.py:463
  (36 shorter events, 0.1 us)
Async XLA Ops:
  0.6 28.0 %copy-start.9 = (f32[2048]{0:T(1024)S(1)}, f32[2048]{0:T(1024)}, u32[]{:S(2)}) copy-start(f32[2048]{0:T(1024)} %param.19) | copy-start | bytes 24580
  1.8 14.9 %collective-permute-start = (bf16[2,512,128]{2,1,0:T(8,128)(2,1)S(1)}, bf16[2,512,128]{2,1,0:T(8,128)(2,1)S(1)}, u32[]{:S(2)}, u32[]{:S(2)}) collective-permute-start(bf16[2,512,128]{2,1,0:T(8,128)(2,1)S(1)} %cast_kernel.1.refs_0_), channel_id=1, source_target_pairs={{0,4},{1,5},{2,6},{3,7},{4,0},{5,1},{6,2},{7,3},{8,12},{9,13},{10,... | collective-permute-start | bytes 786440 | tf_op jit(solution)/shard_map/ppermute | solution.py:488
  4.9 17.5 %collective-permute-start.1 = (bf16[2,512,128]{2,1,0:T(8,128)(2,1)S(1)}, bf16[2,512,128]{2,1,0:T(8,128)(2,1)}, u32[]{:S(2)}, u32[]{:S(2)}) collective-permute-start(bf16[2,512,128]{2,1,0:T(8,128)(2,1)S(1)} %cast_kernel.1.refs_0_), channel_id=1, source_target_pairs={{0,8},{1,9},{2,10},{3,11},{4,12},{5,13},{6,14},{7,15},{8,0},{9,1},... | collective-permute-start | bytes 786440 | tf_op jit(solution)/shard_map/ppermute | solution.py:484
  7.5 14.9 %collective-permute-start.3 = (bf16[2,512,128]{2,1,0:T(8,128)(2,1)S(1)}, bf16[2,512,128]{2,1,0:T(8,128)(2,1)S(1)}, u32[]{:S(2)}, u32[]{:S(2)}) collective-permute-start(bf16[2,512,128]{2,1,0:T(8,128)(2,1)S(1)} %cast_kernel.1.refs_0_), channel_id=1, source_target_pairs={{0,2},{1,3},{2,0},{3,1},{4,6},{5,7},{6,4},{7,5},{8,10},{9,11},{10,... | collective-permute-start | bytes 786440 | tf_op jit(solution)/shard_map/ppermute | solution.py:488
  16.7 7.6 %copy-start.14 = (bf16[2,512,128]{2,1,0:T(8,128)(2,1)}, bf16[2,512,128]{2,1,0:T(8,128)(2,1)S(1)}, u32[]{:S(2)}) copy-start(bf16[2,512,128]{2,1,0:T(8,128)(2,1)S(1)} %collective-permute-done.refs_1_) | copy-start | bytes 786436
  16.7 7.6 %collective-permute-start.2 = (bf16[2,512,128]{2,1,0:T(8,128)(2,1)S(1)}, bf16[2,512,128]{2,1,0:T(8,128)(2,1)S(1)}, u32[]{:S(2)}, u32[]{:S(2)}) collective-permute-start(bf16[2,512,128]{2,1,0:T(8,128)(2,1)S(1)} %collective-permute-done.refs_1_), channel_id=1, source_target_pairs={{0,2},{1,3},{2,0},{3,1},{4,6},{5,7},{6,4},{7,5},{8,10},{9,11},{10,... | collective-permute-start | bytes 786440 | tf_op jit(solution)/shard_map/ppermute | solution.py:488
  22.4 1.9 %copy-start.15 = (bf16[2,512,128]{2,1,0:T(8,128)(2,1)}, bf16[2,512,128]{2,1,0:T(8,128)(2,1)S(1)}, u32[]{:S(2)}) copy-start(bf16[2,512,128]{2,1,0:T(8,128)(2,1)S(1)} %collective-permute-done.3.refs_2_) | copy-start | bytes 786436
  24.3 0.7 copy-start.16
  25.0 3.6 %collective-permute-start.4 = (bf16[2,784,512]{2,1,0:T(8,128)(2,1)S(1)}, bf16[2,784,512]{2,1,0:T(8,128)(2,1)S(1)}, u32[]{:S(2)}, u32[]{:S(2)}) collective-permute-start(bf16[2,784,512]{2,1,0:T(8,128)(2,1)S(1)} %bitcast.37), channel_id=1, source_target_pairs={{0,1},{1,0},{2,3},{3,2},{4,5},{5,4},{6,7},{7,6},{8,9},{9,8},{10,11... | collective-permute-start | bytes 4816904 | tf_op jit(solution)/shard_map/ppermute | solution.py:488
  25.0 12.5 %collective-permute-start.7 = (bf16[2,512,128]{2,1,0:T(8,128)(2,1)}, bf16[2,512,128]{2,1,0:T(8,128)(2,1)}, u32[]{:S(2)}, u32[]{:S(2)}) collective-permute-start(bf16[2,512,128]{2,1,0:T(8,128)(2,1)} %collective-permute-done.1.refs_0_), channel_id=1, source_target_pairs={{0,16},{16,0},{1,17},{17,1},{2,18},{18,2},{3,19},{19,3},{4,20},{20... | collective-permute-start | bytes 786440 | tf_op jit(solution)/shard_map/ppermute | solution.py:496
  25.1 19.3 %collective-permute-start.5 = (bf16[2,512,128]{2,1,0:T(8,128)(2,1)}, bf16[2,512,128]{2,1,0:T(8,128)(2,1)S(1)}, u32[]{:S(2)}, u32[]{:S(2)}) collective-permute-start(bf16[2,512,128]{2,1,0:T(8,128)(2,1)} %collective-permute-done.1.refs_0_), channel_id=1, source_target_pairs={{0,2},{1,3},{2,0},{3,1},{4,6},{5,7},{6,4},{7,5},{8,10},{9,11},{10,... | collective-permute-start | bytes 786440 | tf_op jit(solution)/shard_map/ppermute | solution.py:488
  26.5 17.9 %collective-permute-start.6 = (bf16[2,512,128]{2,1,0:T(8,128)(2,1)}, bf16[2,512,128]{2,1,0:T(8,128)(2,1)S(1)}, u32[]{:S(2)}, u32[]{:S(2)}) collective-permute-start(bf16[2,512,128]{2,1,0:T(8,128)(2,1)} %collective-permute-done.1.refs_0_), channel_id=1, source_target_pairs={{0,18},{1,19},{2,16},{3,17},{4,22},{5,23},{6,20},{7,21},{8,26},{9,... | collective-permute-start | bytes 786440 | tf_op jit(solution)/shard_map/ppermute | solution.py:484
  42.9 8.2 %collective-permute-start.9 = (bf16[2,512,128]{2,1,0:T(8,128)(2,1)S(1)}, bf16[2,512,128]{2,1,0:T(8,128)(2,1)S(1)}, u32[]{:S(2)}, u32[]{:S(2)}) collective-permute-start(bf16[2,512,128]{2,1,0:T(8,128)(2,1)S(1)} %get-tuple-element.84), channel_id=1, source_target_pairs={{0,16},{16,0},{1,17},{17,1},{2,18},{18,2},{3,19},{19,3},{4,20},{20... | collective-permute-start | bytes 786440 | tf_op jit(solution)/shard_map/ppermute | solution.py:496
  42.9 8.2 %collective-permute-start.8 = (bf16[2,512,128]{2,1,0:T(8,128)(2,1)S(1)}, bf16[2,512,128]{2,1,0:T(8,128)(2,1)S(1)}, u32[]{:S(2)}, u32[]{:S(2)}) collective-permute-start(bf16[2,512,128]{2,1,0:T(8,128)(2,1)S(1)} %get-tuple-element.83), channel_id=1, source_target_pairs={{0,2},{1,3},{2,0},{3,1},{4,6},{5,7},{6,4},{7,5},{8,10},{9,11},{10,... | collective-permute-start | bytes 786440 | tf_op jit(solution)/shard_map/ppermute | solution.py:488
  44.4 12.7 %copy-start = (f32[16,49,512]{2,0,1:T(8,128)S(1)}, f32[16,49,512]{2,0,1:T(8,128)}, u32[]{:S(2)}) copy-start(f32[16,49,512]{2,0,1:T(8,128)} %param.15) | copy-start | bytes 4816900
  44.4 12.7 %copy-start.8 = (f32[7,512]{1,0:T(8,128)S(1)}, f32[7,512]{1,0:T(8,128)}, u32[]{:S(2)}) copy-start(f32[7,512]{1,0:T(8,128)} %refs_9_.1) | copy-start | bytes 43012
  49.5 7.7 %copy-start.1 = (bf16[16,49,512]{2,0,1:T(8,128)(2,1)S(1)}, bf16[16,49,512]{2,0,1:T(8,128)(2,1)}, u32[]{:S(2)}) copy-start(bf16[16,49,512]{2,0,1:T(8,128)(2,1)} %param.16) | copy-start | bytes 2408452
  51.2 4.7 %collective-permute-start.10 = (bf16[2,784,512]{2,1,0:T(8,128)(2,1)S(1)}, bf16[2,784,512]{2,1,0:T(8,128)(2,1)S(1)}, u32[]{:S(2)}, u32[]{:S(2)}) collective-permute-start(bf16[2,784,512]{2,1,0:T(8,128)(2,1)S(1)} %get-tuple-element.85), channel_id=1, source_target_pairs={{0,1},{1,0},{2,3},{3,2},{4,5},{5,4},{6,7},{7,6},{8,9},{9,8},{10,11... | collective-permute-start | bytes 4816904 | tf_op jit(solution)/shard_map/ppermute | solution.py:488
  51.2 14.5 %collective-permute-start.16 = (bf16[2,512,128]{2,1,0:T(8,128)(2,1)S(1)}, bf16[2,512,128]{2,1,0:T(8,128)(2,1)S(1)}, u32[]{:S(2)}, u32[]{:S(2)}) collective-permute-start(bf16[2,512,128]{2,1,0:T(8,128)(2,1)S(1)} %add_convert_fusion.1), channel_id=1, source_target_pairs={{0,4},{1,5},{2,6},{3,7},{4,0},{5,1},{6,2},{7,3},{8,12},{9,13},{10,... | collective-permute-start | bytes 786440 | tf_op jit(solution)/shard_map/ppermute | solution.py:488
  51.3 12.0 %collective-permute-start.12 = (bf16[512,128]{1,0:T(8,128)(2,1)S(1)}, bf16[512,128]{1,0:T(8,128)(2,1)S(1)}, u32[]{:S(2)}, u32[]{:S(2)}) collective-permute-start(bf16[512,128]{1,0:T(8,128)(2,1)S(1)} %get-tuple-element.96), channel_id=1, source_target_pairs={{0,2},{1,3},{2,0},{3,1},{4,6},{5,7},{6,4},{7,5},{8,10},{9,11},{10,... | collective-permute-start | bytes 393224 | tf_op jit(solution)/shard_map/ppermute | solution.py:488
  52.8 10.6 %collective-permute-start.13 = (bf16[512,128]{1,0:T(8,128)(2,1)S(1)}, bf16[512,128]{1,0:T(8,128)(2,1)S(1)}, u32[]{:S(2)}, u32[]{:S(2)}) collective-permute-start(bf16[512,128]{1,0:T(8,128)(2,1)S(1)} %get-tuple-element.97), channel_id=1, source_target_pairs={{0,18},{1,19},{2,16},{3,17},{4,22},{5,23},{6,20},{7,21},{8,26},{9,... | collective-permute-start | bytes 393224 | tf_op jit(solution)/shard_map/ppermute | solution.py:484
  54.5 11.2 %collective-permute-start.14 = (bf16[512,128]{1,0:T(8,128)(2,1)S(1)}, bf16[512,128]{1,0:T(8,128)(2,1)S(1)}, u32[]{:S(2)}, u32[]{:S(2)}) collective-permute-start(bf16[512,128]{1,0:T(8,128)(2,1)S(1)} %get-tuple-element.98), channel_id=1, source_target_pairs={{0,2},{1,3},{2,0},{3,1},{4,6},{5,7},{6,4},{7,5},{8,10},{9,11},{10,... | collective-permute-start | bytes 393224 | tf_op jit(solution)/shard_map/ppermute | solution.py:488
  55.9 9.8 %collective-permute-start.15 = (bf16[512,128]{1,0:T(8,128)(2,1)S(1)}, bf16[512,128]{1,0:T(8,128)(2,1)S(1)}, u32[]{:S(2)}, u32[]{:S(2)}) collective-permute-start(bf16[512,128]{1,0:T(8,128)(2,1)S(1)} %get-tuple-element.99), channel_id=1, source_target_pairs={{0,18},{1,19},{2,16},{3,17},{4,22},{5,23},{6,20},{7,21},{8,26},{9,... | collective-permute-start | bytes 393224 | tf_op jit(solution)/shard_map/ppermute | solution.py:484
  65.7 14.7 %collective-permute-start.11 = (bf16[2,512,128]{2,1,0:T(8,128)(2,1)S(1)}, bf16[2,512,128]{2,1,0:T(8,128)(2,1)S(1)}, u32[]{:S(2)}, u32[]{:S(2)}) collective-permute-start(bf16[2,512,128]{2,1,0:T(8,128)(2,1)S(1)} %get-tuple-element.94), channel_id=1, source_target_pairs={{0,2},{1,3},{2,0},{3,1},{4,6},{5,7},{6,4},{7,5},{8,10},{9,11},{10,... | collective-permute-start | bytes 786440 | tf_op jit(solution)/shard_map/ppermute | solution.py:488
  67.2 24.5 %copy-start.2 = (f32[512,128]{1,0:T(8,128)S(1)}, f32[512,128]{1,0:T(8,128)}, u32[]{:S(2)}) copy-start(f32[512,128]{1,0:T(8,128)} %refs_0_.1) | copy-start | bytes 786436
  67.3 24.4 %copy-start.3 = (f32[128,512]{1,0:T(8,128)S(1)}, f32[128,512]{1,0:T(8,128)}, u32[]{:S(2)}) copy-start(f32[128,512]{1,0:T(8,128)} %refs_6_.1) | copy-start | bytes 786436
  67.3 24.4 %copy-start.4 = (f32[512,128]{1,0:T(8,128)S(1)}, f32[512,128]{1,0:T(8,128)}, u32[]{:S(2)}) copy-start(f32[512,128]{1,0:T(8,128)} %refs_1_.1) | copy-start | bytes 786436
  67.3 24.4 %copy-start.5 = (f32[512,128]{1,0:T(8,128)S(1)}, f32[512,128]{1,0:T(8,128)}, u32[]{:S(2)}) copy-start(f32[512,128]{1,0:T(8,128)} %refs_2_.1) | copy-start | bytes 786436
  67.3 24.4 %copy-start.6 = (f32[128,512]{1,0:T(8,128)S(1)}, f32[128,512]{1,0:T(8,128)}, u32[]{:S(2)}) copy-start(f32[128,512]{1,0:T(8,128)} %refs_7_.1) | copy-start | bytes 786436
  67.3 24.4 %copy-start.7 = (f32[128,512]{1,0:T(8,128)S(1)}, f32[128,512]{1,0:T(8,128)}, u32[]{:S(2)}) copy-start(f32[128,512]{1,0:T(8,128)} %refs_8_.1) | copy-start | bytes 786436
  67.3 24.4 %copy-start.10 = (f32[7,512]{1,0:T(8,128)S(1)}, f32[7,512]{1,0:T(8,128)}, u32[]{:S(2)}) copy-start(f32[7,512]{1,0:T(8,128)} %refs_10_.1) | copy-start | bytes 43012
  67.3 24.4 %copy-start.11 = (f32[7,512]{1,0:T(8,128)S(1)}, f32[7,512]{1,0:T(8,128)}, u32[]{:S(2)}) copy-start(f32[7,512]{1,0:T(8,128)} %refs_11_.1) | copy-start | bytes 43012
  67.3 24.4 %copy-start.12 = (f32[2048]{0:T(1024)S(1)}, f32[2048]{0:T(1024)}, u32[]{:S(2)}) copy-start(f32[2048]{0:T(1024)} %param.24) | copy-start | bytes 24580
  67.4 24.4 %copy-start.13 = (f32[2048]{0:T(1024)S(1)}, f32[2048]{0:T(1024)}, u32[]{:S(2)}) copy-start(f32[2048]{0:T(1024)} %param.25) | copy-start | bytes 24580
  67.4 15.4 %collective-permute-start.17 = (bf16[2,512,128]{2,1,0:T(8,128)(2,1)S(1)}, bf16[2,512,128]{2,1,0:T(8,128)(2,1)S(1)}, u32[]{:S(2)}, u32[]{:S(2)}) collective-permute-start(bf16[2,512,128]{2,1,0:T(8,128)(2,1)S(1)} %pad_maximum_fusion), channel_id=1, source_target_pairs={{0,8},{1,9},{2,10},{3,11},{4,12},{5,13},{6,14},{7,15},{8,0},{9,1},... | collective-permute-start | bytes 786440 | tf_op jit(solution)/shard_map/ppermute | solution.py:484
  71.6 1.2 %collective-permute-start.18 = (f32[44,128]{1,0:T(8,128)S(1)}, f32[44,128]{1,0:T(8,128)S(1)}, u32[]{:S(2)}, u32[]{:S(2)}) collective-permute-start(f32[44,128]{1,0:T(8,128)S(1)} %get-tuple-element.93), channel_id=1, source_target_pairs={{0,1},{1,0},{2,3},{3,2},{4,5},{5,4},{6,7},{7,6},{8,9},{9,8},{10,11... | collective-permute-start | bytes 67592 | tf_op jit(solution)/shard_map/ppermute | solution.py:488
  72.8 3.8 %collective-permute-start.19 = (f32[44,128]{1,0:T(8,128)S(1)}, f32[44,128]{1,0:T(8,128)S(1)}, u32[]{:S(2)}, u32[]{:S(2)}) collective-permute-start(f32[44,128]{1,0:T(8,128)S(1)} %add.63), channel_id=1, source_target_pairs={{0,16},{16,0},{1,17},{17,1},{2,18},{18,2},{3,19},{19,3},{4,20},{20... | collective-permute-start | bytes 67592 | tf_op jit(solution)/shard_map/ppermute | solution.py:496
  76.6 3.8 %collective-permute-start.20 = (f32[44,128]{1,0:T(8,128)S(1)}, f32[44,128]{1,0:T(8,128)S(1)}, u32[]{:S(2)}, u32[]{:S(2)}) collective-permute-start(f32[44,128]{1,0:T(8,128)S(1)} %add.64), channel_id=1, source_target_pairs={{0,2},{1,3},{2,0},{3,1},{4,6},{5,7},{6,4},{7,5},{8,10},{9,11},{10,... | collective-permute-start | bytes 67592 | tf_op jit(solution)/shard_map/ppermute | solution.py:488
  83.0 8.7 %collective-permute-start.21 = (bf16[2,512,128]{2,1,0:T(8,128)(2,1)S(1)}, bf16[2,512,128]{2,1,0:T(8,128)(2,1)S(1)}, u32[]{:S(2)}, u32[]{:S(2)}) collective-permute-start(bf16[2,512,128]{2,1,0:T(8,128)(2,1)S(1)} %add_convert_fusion.own_ref), channel_id=1, source_target_pairs={{0,16},{16,0},{1,17},{17,1},{2,18},{18,2},{3,19},{19,3},{4,20},{20... | collective-permute-start | bytes 786440 | tf_op jit(solution)/shard_map/ppermute | solution.py:496
  83.1 3.9 %collective-permute-start.22 = (f32[44,128]{1,0:T(8,128)S(1)}, f32[44,128]{1,0:T(8,128)S(1)}, u32[]{:S(2)}, u32[]{:S(2)}) collective-permute-start(f32[44,128]{1,0:T(8,128)S(1)} %add.65), channel_id=1, source_target_pairs={{0,4},{1,5},{2,6},{3,7},{4,0},{5,1},{6,2},{7,3},{8,12},{9,13},{10,... | collective-permute-start | bytes 67592 | tf_op jit(solution)/shard_map/ppermute | solution.py:488
  87.0 4.7 %collective-permute-start.23 = (f32[44,128]{1,0:T(8,128)S(1)}, f32[44,128]{1,0:T(8,128)S(1)}, u32[]{:S(2)}, u32[]{:S(2)}) collective-permute-start(f32[44,128]{1,0:T(8,128)S(1)} %add.66), channel_id=1, source_target_pairs={{0,8},{1,9},{2,10},{3,11},{4,12},{5,13},{6,14},{7,15},{8,0},{9,1},... | collective-permute-start | bytes 67592 | tf_op jit(solution)/shard_map/ppermute | solution.py:488

commit v4 on v3

--- a/solution.py
+++ b/solution.py
@@ -319,16 +319,14 @@
     return jnp.concatenate([refs[0][i], refs[1][i]], axis=1)
 
 
-def block_kernel(first, count, started, place_ref, own_ref, oth_ref, bias_ref, *refs):
-    w_refs, refs = refs[:count], refs[count:]
-    old, refs = (refs[:2], refs[2:]) if started else (None, refs)
-    totals, sums_ref, outs = refs[:2], refs[2], refs[3:]
+def block_kernel(first, count, place_ref, own_ref, oth_ref, bias_ref, *refs):
+    w_refs, (act_ref, low_ref, sums_ref), outs = refs[:count], refs[count : count + 3], refs[count + 3 :]
     sums_ref[...] = jnp.zeros_like(sums_ref)
-    runs = [[None, None], [None, None]]
     for j in range(count // 2):
         lines = [pl.ds(place_ref[first + 2 * j + k], 1) for k in range(2)]
         bias = jnp.concatenate([bias_ref[line, :] for line in lines], axis=1)
         a, b = (joined(w_refs[2 * j : 2 * j + 2], i) for i in range(2))
+        columns = slice(j * 256, (j + 1) * 256)
         grads = [None, None]
         sums = None
         for r, sb_ref in enumerate((own_ref, oth_ref)):
@@ -337,26 +335,36 @@
             phi, slope = normal_parts(h)
             active = (h * phi).astype(bf16)
             low = (back * slope).astype(bf16)
+            act_ref[r, :, columns] = active
+            low_ref[r, :, columns] = low
             column = jnp.sum(low.astype(f32), axis=0, keepdims=True)
             sums = column if r == 0 else sums + column
             for i, (left, right) in enumerate(((sb_ref[0], low), (sb_ref[1], active))):
                 part = dot(left, right, ((0,), (0,)))
                 grads[i] = part if r == 0 else grads[i] + part
-            for i, (left, right) in enumerate(((active, b), (low, a))):
-                part = dot(left, right, ((1,), (1,)))
-                runs[r][i] = part if j == 0 else runs[r][i] + part
         for k in range(2):
             half = slice(k * 128, (k + 1) * 128)
             sums_ref[lines[k], :] = sums[:, half]
             for i, grad in enumerate(grads):
-                if len(outs) == 2 * count:
-                    outs[2 * k + i][...] = grad[:, half].astype(bf16)
-                else:
-                    outs[2 * j + k][i] = grad[:, half].astype(outs[2 * j + k].dtype)
-    for r, total_ref in enumerate(totals):
-        for i in range(2):
-            total = runs[r][i] if old is None else old[r][i] + runs[r][i]
-            total_ref[i] = total.astype(total_ref.dtype)
+                outs[2 * j + k][i] = grad[:, half].astype(outs[2 * j + k].dtype)
+
+
+def back_kernel(sides, counts, started, *refs):
+    n = len(counts)
+    acts, lows, refs = refs[:n], refs[n : 2 * n], refs[2 * n :]
+    w_refs, refs = refs[: sum(counts)], refs[sum(counts) :]
+    old, totals = (refs[: len(sides)], refs[len(sides) :]) if started else (None, refs)
+    for at, r in enumerate(sides):
+        for i, lefts in enumerate((acts, lows)):
+            total = None if old is None else old[at][i]
+            w = 0
+            for left_ref in lefts:
+                for j in range(left_ref.shape[2] // 256):
+                    left = left_ref[r, :, j * 256 : (j + 1) * 256]
+                    part = dot(left, joined(w_refs[w : w + 2], 1 - i), ((1,), (1,)))
+                    total = part if total is None else total + part
+                    w += 2
+            totals[at][i] = total.astype(totals[at].dtype)
 
 
 def update_kernel(own_ref, got_ref, sums_ref, *refs):
@@ -535,13 +543,12 @@
     first_far = jnp.where(near == 0, 8, 12)
     last_far = 20 - first_far
     zero = 0 * first_far
-    place = [zero, zero + 4, zero + 2, zero + 6, first_far, last_far, first_far ^ 2, last_far ^ 2]
+    place = [zero, zero + 4, first_far, zero + 2, first_far ^ 2, last_far, last_far ^ 2, zero + 6]
     place = (wide ^ jnp.stack(place)).astype(jnp.int32)
 
     pair, pair_f = struct((2, width, units), bf16), struct((2, width, units))
     w0 = call(cast_kernel, pair, (hidden_weight, output_weight), loose=(0, 1))
     wz1, wzf, wy0 = flip(w0, 4), far(w0), flip(w0, 2)
-    wy1 = flip(wz1, 2)
     vectors_late = after(vectors, wz1)
     x = features.transpose(1, 0, 2)
     cot = cotangent.transpose(1, 0, 2)
@@ -555,37 +562,46 @@
         smem=1,
         loose=(1, 2, 3),
     )
-    sb = after(sb.reshape(2, rows, width), wzf, wy1, wy0)
+    sb = after(sb.reshape(2, rows, width), wzf, wy0)
     other = flip(sb, 1)
     wyo, wyf, wzo = diagonal(wzf), flip(wzf, 2), across(wzf)
     bias = hidden_bias.reshape(-1, 128)
     total, total_low = struct((2, rows, width)), struct((2, rows, width), bf16)
 
-    def blocks(first, weights, results, started, old=(), loose=()):
+    lines = struct(bias.shape)
+
+    def blocks(first, weights, results, **kw):
+        tall = struct((2, rows, 128 * len(weights)), bf16)
         return call(
-            functools.partial(block_kernel, first, len(weights), started),
-            results,
-            (place, sb, other, bias, *weights, *old),
+            functools.partial(block_kernel, first, len(weights)),
+            [tall, tall, lines, *results],
+            (place, sb, other, bias, *weights),
             smem=1,
             vmem=20,
-            loose=loose,
+            **kw,
         )
 
-    lines = struct(bias.shape)
-    *old, sums1, g0, gz1, gy0, gy1 = blocks(
-        0, [w0, wz1, wy0, wy1], [total, total, lines, pair_f, pair_f, pair, pair], False, loose=(5, 6, 7)
-    )
-    y1 = flip(gy1, 2)
-    wzf, wzo, _ = lax.optimization_barrier((wzf, wzo, old[0]))
-    *old, sums2, gzf, gzo = blocks(4, [wzf, wzo], [total, total, lines, pair_f, pair], True, old, loose=(4,))
-    wyf, wyo, _ = lax.optimization_barrier((wyf, wyo, old[0]))
-    block = struct((width, units), bf16)
-    mine, theirs, sums3, *gy = blocks(6, [wyf, wyo], [total, total_low, lines] + [block] * 4, True, old)
-    xs = across(gzo)
-    ds, yf = [diagonal(gy[2]), diagonal(gy[3])], [flip(gy[0], 2), flip(gy[1], 2)]
-    theirs, y1, xs = lax.optimization_barrier((theirs, y1, xs))
+    def back(sides, results, hidden, weights, old=(), loose=()):
+        acts, lows = zip(*hidden)
+        counts = [act.shape[2] // 128 for act in acts]
+        kernel = functools.partial(back_kernel, sides, counts, bool(old))
+        return call(kernel, results, (*acts, *lows, *weights, *old), loose=loose)
+
+    w_near = [w0, wz1, wzf, wy0]
+    *near_hidden, sums1, g0, gz1, gzf, gy0 = blocks(0, w_near, [pair_f, pair, pair_f, pair], loose=(5, 6, 7))
+    z1 = flip(gz1, 4)
+    wy1 = flip(after(wz1, sums1), 2)
+    wyf, wzo, _ = lax.optimization_barrier((wyf, wzo, sums1))
+    *far_hidden, sums2, gyf, gzo = blocks(4, [wyf, wzo], [pair, pair])
+    yf, xs = flip(gyf, 2), across(gzo)
+    old = back((0, 1), [total, total], (near_hidden, far_hidden), [*w_near, wyf, wzo], loose=(5, 6, 7))
+    wyo, wy1, _ = lax.optimization_barrier((wyo, wy1, old[0]))
+    *last_hidden, sums3, gyo, gy1 = blocks(6, [wyo, wy1], [pair, pair])
+    ds, zy = diagonal(gyo), flip(gy1, 4)
+    theirs = back((1,), [total_low], (last_hidden,), [wyo, wy1], old[1:])[0]
+    theirs, yf, xs, z1 = lax.optimization_barrier((theirs, yf, xs, z1))
     got = flip(theirs, 1)
-    z1 = flip(wide_sum(gz1, y1).astype(bf16), 4)
+    mine = back((0,), [total], (last_hidden,), [wyo, wy1], old[:1])[0]
 
     shape = (2, pixels, images, width)
     payload = struct((bias.shape[0] + vectors.size // 128, 128))
@@ -597,9 +613,9 @@
         smem=1,
         hold=False,
     )
-    y0 = flip(after(gy0, sums), 2)
-    xs, ya, da, yb, db, z1, _ = lax.optimization_barrier((xs, yf[0], ds[0], yf[1], ds[1], z1, sums))
-    sum_f = jnp.stack([wide_sum(gzf[0], xs[0], ya, da), wide_sum(gzf[1], xs[1], yb, db)]).astype(bf16)
+    ds, zy, _ = lax.optimization_barrier((ds, zy, sums))
+    sum_f = wide_sum(gzf, xs, yf, ds).astype(bf16)
+    y0 = flip(after(wide_sum(gy0, zy).astype(bf16), sum_f), 2)
     zf = far(sum_f)
     sums = sums + flip(sums, 1)
     sums = after(sums, sum_f)

time: 93.7 us -> 86.6 us (0.924)
  waiting for transfers between devices: 30.3 us -> 22.5 us
  starting transfers between devices: 29.1 us -> 28 us
  Pallas kernels: 31.2 us -> 32.2 us
    ppermute x15 -> x14, waiting for transfers between devices: 22.6 us -> 17.1 us  [flip(): return lax.ppermute(values, 'wide', [(w, w ^ bit) for w in range(16)])]
    ppermute x4, waiting for transfers between devices: 5.31 us -> 3.18 us  [across(): return lax.ppermute(values, 'narrow', [(0, 1), (1, 0)])]
    pallas_call x7 -> x10, Pallas kernels: 31.2 us -> 32.2 us  [call(): pl.pallas_call(kernel, out_shape=outs, in_specs=[SMEM] * smem + [VMEM] *...]
    ppermute x5 -> x4, starting transfers between devices: 11.9 us -> 11 us  [joint(): return lax.ppermute(values, BOTH, [(s, n * 16 + w) for s, (n, w) in pairs])]
    ppermute x15 -> x14, starting transfers between devices: 16.8 us -> 16 us  [flip(): return lax.ppermute(values, 'wide', [(w, w ^ bit) for w in range(16)])]
    ppermute x5 -> x4, waiting for transfers between devices: 2.35 us -> 2.14 us  [joint(): return lax.ppermute(values, BOTH, [(s, n * 16 + w) for s, (n, w) in pairs])]
  transfers between devices with their start and end apart: 24 -> 22, of which waited for: 12 -> 9; matrix products, arithmetic and copies ran while one was open for 0% -> 0% of each run, Pallas kernels for 30% -> 34%
where the time goes in v4:
time: 86.6 us; the launch traced here: 86.4 us
  Pallas kernels  32.2 us (37%)
  starting transfers between devices  28 us (32%)
  waiting for transfers between devices  22.5 us (26%)
  between operations  1.81 us (2%)
  local copies, waits for them, and re-layouts  1.57 us (2%)
    pallas_call x10, Pallas kernels, call(): pl.pallas_call(kernel, out_shape=outs, in_specs=[SMEM] * smem + [VMEM] *...  32.2 us
    ppermute x14, waiting for transfers between devices, flip(): return lax.ppermute(values, 'wide', [(w, w ^ bit) for w in range(16)])  17.1 us
    ppermute x14, starting transfers between devices, flip(): return lax.ppermute(values, 'wide', [(w, w ^ bit) for w in range(16)])  16 us
    ppermute x4, starting transfers between devices, joint(): return lax.ppermute(values, BOTH, [(s, n * 16 + w) for s, (n, w) in pairs])  11 us
    ppermute x4, waiting for transfers between devices, across(): return lax.ppermute(values, 'narrow', [(0, 1), (1, 0)])  3.18 us
    ppermute x4, waiting for transfers between devices, joint(): return lax.ppermute(values, BOTH, [(s, n * 16 + w) for s, (n, w) in pairs])  2.14 us
  transfers between devices with their start and end apart: 22, of which 9 were waited for; matrix products, arithmetic and copies ran while one was open for 0% of the time, Pallas kernels for 34%

profile of v4, /device:TPU:0, one launch (start us, length us, event | category | flops | bytes accessed | tf_op | source)
XLA Modules:
  0.0 86.4 jit_solution(13837539197129099274)
XLA Ops:
  0.7 1.1 %cast_kernel.1.refs_0_.refs_4_ = bf16[2,512,128]{2,1,0:T(8,128)(2,1)S(1)} custom-call(f32[512,128]{1,0:T(8,128)} %refs_0_.1, f32[128,512]{1,0:T(8,128)} %refs_6_.1), custom_call_target="tpu_custom_call" | custom-call | bytes 786432 | tf_op jit(solution)/shard_map/cast_kernel/pallas_call | solution.py:471
  1.8 3.1 %collective-permute-start = (bf16[2,512,128]{2,1,0:T(8,128)(2,1)S(1)}, bf16[2,512,128]{2,1,0:T(8,128)(2,1)S(1)}, u32[]{:S(2)}, u32[]{:S(2)}) collective-permute-start(bf16[2,512,128]{2,1,0:T(8,128)(2,1)S(1)} %cast_kernel.1.refs_0_.refs_4_), channel_id=1, source_target_pairs={{0,4},{1,5},{2,6},{3,7},{4,0},{5,1},{6,2},{7,3},{8,12},{9,13},{10,... | collective-permute-start | bytes 786440 | tf_op jit(solution)/shard_map/ppermute | solution.py:496
  4.9 2.6 %collective-permute-start.1 = (bf16[2,512,128]{2,1,0:T(8,128)(2,1)S(1)}, bf16[2,512,128]{2,1,0:T(8,128)(2,1)}, u32[]{:S(2)}, u32[]{:S(2)}) collective-permute-start(bf16[2,512,128]{2,1,0:T(8,128)(2,1)S(1)} %cast_kernel.1.refs_0_.refs_4_), channel_id=1, source_target_pairs={{0,8},{1,9},{2,10},{3,11},{4,12},{5,13},{6,14},{7,15},{8,0},{9,1},... | collective-permute-start | bytes 786440 | tf_op jit(solution)/shard_map/ppermute | solution.py:492
  7.5 1.5 %collective-permute-start.2 = (bf16[2,512,128]{2,1,0:T(8,128)(2,1)S(1)}, bf16[2,512,128]{2,1,0:T(8,128)(2,1)S(1)}, u32[]{:S(2)}, u32[]{:S(2)}) collective-permute-start(bf16[2,512,128]{2,1,0:T(8,128)(2,1)S(1)} %cast_kernel.1.refs_0_.refs_4_), channel_id=1, source_target_pairs={{0,2},{1,3},{2,0},{3,1},{4,6},{5,7},{6,4},{7,5},{8,10},{9,11},{10,... | collective-permute-start | bytes 786440 | tf_op jit(solution)/shard_map/ppermute | solution.py:496
  9.7 7.0 %collective-permute-done.refs_1_.refs_5_ = bf16[2,512,128]{2,1,0:T(8,128)(2,1)S(1)} collective-permute-done((bf16[2,512,128]{2,1,0:T(8,128)(2,1)S(1)}, bf16[2,512,128]{2,1,0:T(8,128)(2,1)S(1)}, u32[]{:S(2)}, u32[]{:S(2)}) %collective-permute-start) | collective-permute-done | bytes 262176 | tf_op jit(solution)/shard_map/ppermute | solution.py:496
  16.7 0.7 copy-done.14
  17.4 3.3 %pre_kernel.1 = (bf16[2,49,16,512]{3,2,1,0:T(8,128)(2,1)S(1)}, f32[4,16,128]{2,1,0:T(8,128)S(1)}) custom-call(s32[1]{0:T(128)S(6)} %copy.29.counts_ref, f32[49,16,512]{2,1,0:T(8,128)} %bitcast.22, bf16[49,16,512]{2,1,0:T(8,128)(2,1)} %bitcast.24, f32[7,512]{1,0:T(8,128)} %refs_9_.1), custom_call_target="tpu_custom_call" | custom-call | bytes 4061188 | tf_op jit(solution)/shard_map/pre_kernel/pallas_call | solution.py:471
  20.7 0.0 collective-permute-done.1.refs_2_.refs_6_
  20.8 0.0 collective-permute-done.2.refs_3_.refs_7_
  20.8 0.0 copy-start.16
  20.8 0.7 copy-done.16
  21.5 0.0 collective-permute-start.3
  21.5 1.7 %collective-permute-start.6 = (bf16[2,512,128]{2,1,0:T(8,128)(2,1)}, bf16[2,512,128]{2,1,0:T(8,128)(2,1)}, u32[]{:S(2)}, u32[]{:S(2)}) collective-permute-start(bf16[2,512,128]{2,1,0:T(8,128)(2,1)} %collective-permute-done.1.refs_2_.refs_6_), channel_id=1, source_target_pairs={{0,2},{1,3},{2,0},{3,1},{4,6},{5,7},{6,4},{7,5},{8,10},{9,11},{10,... | collective-permute-start | bytes 786440 | tf_op jit(solution)/shard_map/ppermute | solution.py:496
  23.2 0.0 collective-permute-start.7
  23.2 0.1 stack.19
  23.3 1.9 %collective-permute-start.4 = (bf16[2,512,128]{2,1,0:T(8,128)(2,1)}, bf16[2,512,128]{2,1,0:T(8,128)(2,1)S(1)}, u32[]{:S(2)}, u32[]{:S(2)}) collective-permute-start(bf16[2,512,128]{2,1,0:T(8,128)(2,1)} %collective-permute-done.1.refs_2_.refs_6_), channel_id=1, source_target_pairs={{0,18},{1,19},{2,16},{3,17},{4,22},{5,23},{6,20},{7,21},{8,26},{9,... | collective-permute-start | bytes 786440 | tf_op jit(solution)/shard_map/ppermute | solution.py:492
  25.1 0.0 collective-permute-done.3.oth_ref
  25.1 7.0 %block_kernel.3 = (bf16[2,784,512]{2,1,0:T(8,128)(2,1)S(1)}, bf16[2,784,512]{2,1,0:T(8,128)(2,1)S(1)}, f32[16,128]{1,0:T(8,128)S(1)}, f32[2,512,128]{2,1,0:T(8,1...) custom-call(s32[8]{0:T(128)S(1)} %broadcast_xor_fusion.place_ref, ...), custom_call_target="tpu_custom_call" | custom-call | bytes 9060384 | tf_op jit(solution)/shard_map/block_kernel/pallas_call | solution.py:471
  32.2 1.8 %collective-permute-start.5 = (bf16[2,512,128]{2,1,0:T(8,128)(2,1)S(1)}, bf16[2,512,128]{2,1,0:T(8,128)(2,1)S(1)}, u32[]{:S(2)}, u32[]{:S(2)}) collective-permute-start(bf16[2,512,128]{2,1,0:T(8,128)(2,1)S(1)} %copy-done.15), channel_id=1, source_target_pairs={{0,2},{1,3},{2,0},{3,1},{4,6},{5,7},{6,4},{7,5},{8,10},{9,11},{10,... | collective-permute-start | bytes 786440 | tf_op jit(solution)/shard_map/ppermute | solution.py:496
  33.9 4.2 %block_kernel.4 = (bf16[2,784,256]{2,1,0:T(8,128)(2,1)S(1)}, bf16[2,784,256]{2,1,0:T(8,128)(2,1)S(1)}, f32[16,128]{1,0:T(8,128)S(1)}, bf16[2,512,128]{2,1,0:T(8,128)(2,1)S(1)}, bf16[2,512,128]{2,1,0:T(8,128)(2,1)S(1)}) custom-call(s32[8]{0:T(128)S(1)} %broadcast_xor_fusion.place_ref, bf16[2,784,512]{2,1,0:T(8,128)(2,1)S(1)} %bitcast.19, ...), custom_call_target="tpu_custom_call" | custom-call | bytes 5881888 | tf_op jit(solution)/shard_map/block_kernel/pallas_call | solution.py:471
  38.2 0.4 collective-permute-start.8
  38.6 0.3 collective-permute-start.9
  38.8 0.2 collective-permute-start.10
  39.1 4.0 %back_kernel.3 = (f32[2,784,512]{2,1,0:T(8,128)S(1)}, f32[2,784,512]{2,1,0:T(8,128)S(1)}) custom-call(bf16[2,784,512]{2,1,0:T(8,128)(2,1)S(1)} %get-tuple-element.73.refs_0_, bf16[2,784,256]{2,1,0:T(8,128)(2,1)S(1)} %get-tuple-element.76.refs_1_, bf16[2,784,512]{2,1,0:T(8,128)(2,1)S(1)} %get-tuple-element.77.refs_2_, ...), custom_call_target="tpu_custom_call" | custom-call | bytes 12812288 | tf_op jit(solution)/shard_map/back_kernel/pallas_call | solution.py:471
  43.1 0.0 collective-permute-done.5.refs_1_.refs_3_
  43.1 3.9 %block_kernel.5 = (bf16[2,784,256]{2,1,0:T(8,128)(2,1)S(1)}, bf16[2,784,256]{2,1,0:T(8,128)(2,1)S(1)}, f32[16,128]{1,0:T(8,128)S(1)}, bf16[2,512,128]{2,1,0:T(8,128)(2,1)S(1)}, bf16[2,512,128]{2,1,0:T(8,128)(2,1)S(1)}) custom-call(s32[8]{0:T(128)S(1)} %broadcast_xor_fusion.place_ref, bf16[2,784,512]{2,1,0:T(8,128)(2,1)S(1)} %bitcast.20, ...), custom_call_target="tpu_custom_call" | custom-call | bytes 5881888 | tf_op jit(solution)/shard_map/block_kernel/pallas_call | solution.py:471
  47.0 0.7 back_kernel.5
  47.6 0.8 collective-permute-done.8
  48.4 0.0 collective-permute-start.11
  48.5 2.0 %collective-permute-start.12 = (bf16[2,512,128]{2,1,0:T(8,128)(2,1)S(1)}, bf16[2,512,128]{2,1,0:T(8,128)(2,1)S(1)}, u32[]{:S(2)}, u32[]{:S(2)}) collective-permute-start(bf16[2,512,128]{2,1,0:T(8,128)(2,1)S(1)} %get-tuple-element.95), channel_id=1, source_target_pairs={{0,18},{1,19},{2,16},{3,17},{4,22},{5,23},{6,20},{7,21},{8,26},{9,... | collective-permute-start | bytes 786440 | tf_op jit(solution)/shard_map/ppermute | solution.py:492
  50.5 2.0 %collective-permute-start.13 = (bf16[2,512,128]{2,1,0:T(8,128)(2,1)S(1)}, bf16[2,512,128]{2,1,0:T(8,128)(2,1)S(1)}, u32[]{:S(2)}, u32[]{:S(2)}) collective-permute-start(bf16[2,512,128]{2,1,0:T(8,128)(2,1)S(1)} %get-tuple-element.96), channel_id=1, source_target_pairs={{0,4},{1,5},{2,6},{3,7},{4,0},{5,1},{6,2},{7,3},{8,12},{9,13},{10,... | collective-permute-start | bytes 786440 | tf_op jit(solution)/shard_map/ppermute | solution.py:496
  52.5 0.6 back_kernel.4
  53.1 5.8 %post_kernel.1 = (f32[49,16,512]{2,1,0:T(8,128)}, f32[49,16,512]{2,1,0:T(8,128)}, f32[44,128]{1,0:T(8,128)S(1)}) custom-call(s32[1]{0:T(128)S(6)} %copy.29.counts_ref, f32[49,16,512]{2,1,0:T(8,128)S(1)} %bitcast.23, bf16[49,16,512]{2,1,0:T(8,128)(2,1)S(1)} %bitcast.25, f32[7,512]{1,0:T(8,128)S(1)} %copy-done.8, ...), custom_call_target="tpu_custom_call" | custom-call | bytes 10530820 | tf_op jit(solution)/shard_map/post_kernel/pallas_call | solution.py:471
  58.9 0.2 collective-permute-done.13
  59.1 0.1 add_convert_fusion.2
  59.2 0.0 copy-start.2
  59.2 0.0 copy-start.3
  59.2 0.0 copy-start.4
  59.2 0.0 copy-start.5
  59.2 0.0 copy-start.6
  59.2 0.0 copy-start.7
  59.3 0.0 copy-start.10
  59.3 0.0 copy-start.11
  59.3 0.0 copy-start.12
  59.3 0.0 copy-start.13
  59.3 0.1 add_convert_fusion.1
  59.4 0.7 collective-permute-start.14
  60.2 4.6 %collective-permute-start.15 = (bf16[2,512,128]{2,1,0:T(8,128)(2,1)S(1)}, bf16[2,512,128]{2,1,0:T(8,128)(2,1)S(1)}, u32[]{:S(2)}, u32[]{:S(2)}) collective-permute-start(bf16[2,512,128]{2,1,0:T(8,128)(2,1)S(1)} %add_convert_fusion.1), channel_id=1, source_target_pairs={{0,8},{1,9},{2,10},{3,11},{4,12},{5,13},{6,14},{7,15},{8,0},{9,1},... | collective-permute-start | bytes 786440 | tf_op jit(solution)/shard_map/ppermute | solution.py:492
  64.7 0.0 collective-permute-start.16
  64.7 1.2 %collective-permute-done.16 = f32[44,128]{1,0:T(8,128)S(1)} collective-permute-done((f32[44,128]{1,0:T(8,128)S(1)}, f32[44,128]{1,0:T(8,128)S(1)}, u32[]{:S(2)}, u32[]{:S(2)}) %collective-permute-start.16) | collective-permute-done | bytes 22560 | tf_op jit(solution)/shard_map/ppermute | solution.py:496
  65.9 0.7 collective-permute-start.17
  66.6 3.2 %collective-permute-done.17 = f32[44,128]{1,0:T(8,128)S(1)} collective-permute-done((f32[44,128]{1,0:T(8,128)S(1)}, f32[44,128]{1,0:T(8,128)S(1)}, u32[]{:S(2)}, u32[]{:S(2)}) %collective-permute-start.17) | collective-permute-done | bytes 22560 | tf_op jit(solution)/shard_map/ppermute | solution.py:504
  69.7 0.5 collective-permute-start.18
  70.2 3.3 %collective-permute-done.18 = f32[44,128]{1,0:T(8,128)S(1)} collective-permute-done((f32[44,128]{1,0:T(8,128)S(1)}, f32[44,128]{1,0:T(8,128)S(1)}, u32[]{:S(2)}, u32[]{:S(2)}) %collective-permute-start.18) | collective-permute-done | bytes 22560 | tf_op jit(solution)/shard_map/ppermute | solution.py:496
  73.6 0.0 collective-permute-done.14
  73.6 2.1 %collective-permute-done.15 = bf16[2,512,128]{2,1,0:T(8,128)(2,1)S(1)} collective-permute-done((bf16[2,512,128]{2,1,0:T(8,128)(2,1)S(1)}, bf16[2,512,128]{2,1,0:T(8,128)(2,1)S(1)}, u32[]{:S(2)}, u32[]{:S(2)}) %collective-permute-start.15) | collective-permute-done | bytes 262176 | tf_op jit(solution)/shard_map/ppermute | solution.py:492
  75.7 0.1 add_convert_fusion.own_ref
  75.8 0.1 collective-permute-start.19
  75.9 1.5 %collective-permute-start.20 = (f32[44,128]{1,0:T(8,128)S(1)}, f32[44,128]{1,0:T(8,128)S(1)}, u32[]{:S(2)}, u32[]{:S(2)}) collective-permute-start(f32[44,128]{1,0:T(8,128)S(1)} %add.45), channel_id=1, source_target_pairs={{0,4},{1,5},{2,6},{3,7},{4,0},{5,1},{6,2},{7,3},{8,12},{9,13},{10,... | collective-permute-start | bytes 67592 | tf_op jit(solution)/shard_map/ppermute | solution.py:496
  77.4 2.4 %collective-permute-done.20 = f32[44,128]{1,0:T(8,128)S(1)} collective-permute-done((f32[44,128]{1,0:T(8,128)S(1)}, f32[44,128]{1,0:T(8,128)S(1)}, u32[]{:S(2)}, u32[]{:S(2)}) %collective-permute-start.20) | collective-permute-done | bytes 22560 | tf_op jit(solution)/shard_map/ppermute | solution.py:496
  79.8 2.6 %collective-permute-start.21 = (f32[44,128]{1,0:T(8,128)S(1)}, f32[44,128]{1,0:T(8,128)S(1)}, u32[]{:S(2)}, u32[]{:S(2)}) collective-permute-start(f32[44,128]{1,0:T(8,128)S(1)} %add.46), channel_id=1, source_target_pairs={{0,8},{1,9},{2,10},{3,11},{4,12},{5,13},{6,14},{7,15},{8,0},{9,1},... | collective-permute-start | bytes 67592 | tf_op jit(solution)/shard_map/ppermute | solution.py:496
  82.4 2.1 %collective-permute-done.21 = f32[44,128]{1,0:T(8,128)S(1)} collective-permute-done((f32[44,128]{1,0:T(8,128)S(1)}, f32[44,128]{1,0:T(8,128)S(1)}, u32[]{:S(2)}, u32[]{:S(2)}) %collective-permute-start.21) | collective-permute-done | bytes 22560 | tf_op jit(solution)/shard_map/ppermute | solution.py:496
  84.5 0.0 collective-permute-done.19.got_ref
  84.7 1.6 %update_kernel.1 = (f32[512,128]{1,0:T(8,128)}, f32[512,128]{1,0:T(8,128)}, f32[512,128]{1,0:T(8,128)}, f32[16,128]{1,0:T(8,128)}, f32[16,128]{1,0:T(8,128)}, /*...) custom-call(bf16[2,512,128]{2,1,0:T(8,128)(2,1)S(1)} %add_convert_fu, ...), custom_call_target="tpu_custom_call" | custom-call | bytes 3827712 | tf_op jit(solution)/shard_map/update_kernel/pallas_call | solution.py:471
  (34 shorter events, 0.1 us)
Async XLA Ops:
  0.6 24.5 %copy-start.9 = (f32[2048]{0:T(1024)S(1)}, f32[2048]{0:T(1024)}, u32[]{:S(2)}) copy-start(f32[2048]{0:T(1024)} %param.19) | copy-start | bytes 24580
  1.8 14.9 %collective-permute-start = (bf16[2,512,128]{2,1,0:T(8,128)(2,1)S(1)}, bf16[2,512,128]{2,1,0:T(8,128)(2,1)S(1)}, u32[]{:S(2)}, u32[]{:S(2)}) collective-permute-start(bf16[2,512,128]{2,1,0:T(8,128)(2,1)S(1)} %cast_kernel.1.refs_0_.refs_4_), channel_id=1, source_target_pairs={{0,4},{1,5},{2,6},{3,7},{4,0},{5,1},{6,2},{7,3},{8,12},{9,13},{10,... | collective-permute-start | bytes 786440 | tf_op jit(solution)/shard_map/ppermute | solution.py:496
  4.9 15.9 %collective-permute-start.1 = (bf16[2,512,128]{2,1,0:T(8,128)(2,1)S(1)}, bf16[2,512,128]{2,1,0:T(8,128)(2,1)}, u32[]{:S(2)}, u32[]{:S(2)}) collective-permute-start(bf16[2,512,128]{2,1,0:T(8,128)(2,1)S(1)} %cast_kernel.1.refs_0_.refs_4_), channel_id=1, source_target_pairs={{0,8},{1,9},{2,10},{3,11},{4,12},{5,13},{6,14},{7,15},{8,0},{9,1},... | collective-permute-start | bytes 786440 | tf_op jit(solution)/shard_map/ppermute | solution.py:492
  7.5 13.3 %collective-permute-start.2 = (bf16[2,512,128]{2,1,0:T(8,128)(2,1)S(1)}, bf16[2,512,128]{2,1,0:T(8,128)(2,1)S(1)}, u32[]{:S(2)}, u32[]{:S(2)}) collective-permute-start(bf16[2,512,128]{2,1,0:T(8,128)(2,1)S(1)} %cast_kernel.1.refs_0_.refs_4_), channel_id=1, source_target_pairs={{0,2},{1,3},{2,0},{3,1},{4,6},{5,7},{6,4},{7,5},{8,10},{9,11},{10,... | collective-permute-start | bytes 786440 | tf_op jit(solution)/shard_map/ppermute | solution.py:496
  16.7 0.7 copy-start.14
  20.8 0.7 copy-start.16
  21.5 3.6 %collective-permute-start.3 = (bf16[2,784,512]{2,1,0:T(8,128)(2,1)S(1)}, bf16[2,784,512]{2,1,0:T(8,128)(2,1)S(1)}, u32[]{:S(2)}, u32[]{:S(2)}) collective-permute-start(bf16[2,784,512]{2,1,0:T(8,128)(2,1)S(1)} %bitcast.17), channel_id=1, source_target_pairs={{0,1},{1,0},{2,3},{3,2},{4,5},{5,4},{6,7},{7,6},{8,9},{9,8},{10,11... | collective-permute-start | bytes 4816904 | tf_op jit(solution)/shard_map/ppermute | solution.py:496
  21.5 12.5 %collective-permute-start.6 = (bf16[2,512,128]{2,1,0:T(8,128)(2,1)}, bf16[2,512,128]{2,1,0:T(8,128)(2,1)}, u32[]{:S(2)}, u32[]{:S(2)}) collective-permute-start(bf16[2,512,128]{2,1,0:T(8,128)(2,1)} %collective-permute-done.1.refs_2_.refs_6_), channel_id=1, source_target_pairs={{0,2},{1,3},{2,0},{3,1},{4,6},{5,7},{6,4},{7,5},{8,10},{9,11},{10,... | collective-permute-start | bytes 786440 | tf_op jit(solution)/shard_map/ppermute | solution.py:496
  23.2 10.8 %collective-permute-start.7 = (bf16[2,512,128]{2,1,0:T(8,128)(2,1)}, bf16[2,512,128]{2,1,0:T(8,128)(2,1)}, u32[]{:S(2)}, u32[]{:S(2)}) collective-permute-start(bf16[2,512,128]{2,1,0:T(8,128)(2,1)} %collective-permute-done.1.refs_2_.refs_6_), channel_id=1, source_target_pairs={{0,16},{16,0},{1,17},{17,1},{2,18},{18,2},{3,19},{19,3},{4,20},{20... | collective-permute-start | bytes 786440 | tf_op jit(solution)/shard_map/ppermute | solution.py:504
  23.3 19.8 %collective-permute-start.4 = (bf16[2,512,128]{2,1,0:T(8,128)(2,1)}, bf16[2,512,128]{2,1,0:T(8,128)(2,1)S(1)}, u32[]{:S(2)}, u32[]{:S(2)}) collective-permute-start(bf16[2,512,128]{2,1,0:T(8,128)(2,1)} %collective-permute-done.1.refs_2_.refs_6_), channel_id=1, source_target_pairs={{0,18},{1,19},{2,16},{3,17},{4,22},{5,23},{6,20},{7,21},{8,26},{9,... | collective-permute-start | bytes 786440 | tf_op jit(solution)/shard_map/ppermute | solution.py:492
  25.1 7.1 %copy-start.15 = (bf16[2,512,128]{2,1,0:T(8,128)(2,1)S(1)}, bf16[2,512,128]{2,1,0:T(8,128)(2,1)}, u32[]{:S(2)}) copy-start(bf16[2,512,128]{2,1,0:T(8,128)(2,1)} %copy-done.14) | copy-start | bytes 786436
  32.2 10.9 %collective-permute-start.5 = (bf16[2,512,128]{2,1,0:T(8,128)(2,1)S(1)}, bf16[2,512,128]{2,1,0:T(8,128)(2,1)S(1)}, u32[]{:S(2)}, u32[]{:S(2)}) collective-permute-start(bf16[2,512,128]{2,1,0:T(8,128)(2,1)S(1)} %copy-done.15), channel_id=1, source_target_pairs={{0,2},{1,3},{2,0},{3,1},{4,6},{5,7},{6,4},{7,5},{8,10},{9,11},{10,... | collective-permute-start | bytes 786440 | tf_op jit(solution)/shard_map/ppermute | solution.py:496
  38.2 10.3 %collective-permute-start.8 = (bf16[2,512,128]{2,1,0:T(8,128)(2,1)S(1)}, bf16[2,512,128]{2,1,0:T(8,128)(2,1)S(1)}, u32[]{:S(2)}, u32[]{:S(2)}) collective-permute-start(bf16[2,512,128]{2,1,0:T(8,128)(2,1)S(1)} %get-tuple-element.85), channel_id=1, source_target_pairs={{0,2},{1,3},{2,0},{3,1},{4,6},{5,7},{6,4},{7,5},{8,10},{9,11},{10,... | collective-permute-start | bytes 786440 | tf_op jit(solution)/shard_map/ppermute | solution.py:496
  38.6 9.9 %collective-permute-start.9 = (bf16[2,512,128]{2,1,0:T(8,128)(2,1)S(1)}, bf16[2,512,128]{2,1,0:T(8,128)(2,1)S(1)}, u32[]{:S(2)}, u32[]{:S(2)}) collective-permute-start(bf16[2,512,128]{2,1,0:T(8,128)(2,1)S(1)} %get-tuple-element.86), channel_id=1, source_target_pairs={{0,16},{16,0},{1,17},{17,1},{2,18},{18,2},{3,19},{19,3},{4,20},{20... | collective-permute-start | bytes 786440 | tf_op jit(solution)/shard_map/ppermute | solution.py:504
  38.8 9.6 %collective-permute-start.10 = (bf16[2,512,128]{2,1,0:T(8,128)(2,1)S(1)}, bf16[2,512,128]{2,1,0:T(8,128)(2,1)S(1)}, u32[]{:S(2)}, u32[]{:S(2)}) collective-permute-start(bf16[2,512,128]{2,1,0:T(8,128)(2,1)S(1)} %get-tuple-element.87), channel_id=1, source_target_pairs={{0,4},{1,5},{2,6},{3,7},{4,0},{5,1},{6,2},{7,3},{8,12},{9,13},{10,... | collective-permute-start | bytes 786440 | tf_op jit(solution)/shard_map/ppermute | solution.py:496
  48.4 4.6 %collective-permute-start.11 = (bf16[2,784,512]{2,1,0:T(8,128)(2,1)S(1)}, bf16[2,784,512]{2,1,0:T(8,128)(2,1)S(1)}, u32[]{:S(2)}, u32[]{:S(2)}) collective-permute-start(bf16[2,784,512]{2,1,0:T(8,128)(2,1)S(1)} %back_kernel.5), channel_id=1, source_target_pairs={{0,1},{1,0},{2,3},{3,2},{4,5},{5,4},{6,7},{7,6},{8,9},{9,8},{10,11... | collective-permute-start | bytes 4816904 | tf_op jit(solution)/shard_map/ppermute | solution.py:496
  48.5 10.5 %collective-permute-start.12 = (bf16[2,512,128]{2,1,0:T(8,128)(2,1)S(1)}, bf16[2,512,128]{2,1,0:T(8,128)(2,1)S(1)}, u32[]{:S(2)}, u32[]{:S(2)}) collective-permute-start(bf16[2,512,128]{2,1,0:T(8,128)(2,1)S(1)} %get-tuple-element.95), channel_id=1, source_target_pairs={{0,18},{1,19},{2,16},{3,17},{4,22},{5,23},{6,20},{7,21},{8,26},{9,... | collective-permute-start | bytes 786440 | tf_op jit(solution)/shard_map/ppermute | solution.py:492
  50.4 2.7 %copy-start = (f32[16,49,512]{2,0,1:T(8,128)S(1)}, f32[16,49,512]{2,0,1:T(8,128)}, u32[]{:S(2)}) copy-start(f32[16,49,512]{2,0,1:T(8,128)} %param.15) | copy-start | bytes 4816900
  50.5 2.7 %copy-start.1 = (bf16[16,49,512]{2,0,1:T(8,128)(2,1)S(1)}, bf16[16,49,512]{2,0,1:T(8,128)(2,1)}, u32[]{:S(2)}) copy-start(bf16[16,49,512]{2,0,1:T(8,128)(2,1)} %param.16) | copy-start | bytes 2408452
  50.5 2.7 %copy-start.8 = (f32[7,512]{1,0:T(8,128)S(1)}, f32[7,512]{1,0:T(8,128)}, u32[]{:S(2)}) copy-start(f32[7,512]{1,0:T(8,128)} %refs_9_.1) | copy-start | bytes 43012
  50.5 8.7 %collective-permute-start.13 = (bf16[2,512,128]{2,1,0:T(8,128)(2,1)S(1)}, bf16[2,512,128]{2,1,0:T(8,128)(2,1)S(1)}, u32[]{:S(2)}, u32[]{:S(2)}) collective-permute-start(bf16[2,512,128]{2,1,0:T(8,128)(2,1)S(1)} %get-tuple-element.96), channel_id=1, source_target_pairs={{0,4},{1,5},{2,6},{3,7},{4,0},{5,1},{6,2},{7,3},{8,12},{9,13},{10,... | collective-permute-start | bytes 786440 | tf_op jit(solution)/shard_map/ppermute | solution.py:496
  59.2 25.4 %copy-start.2 = (f32[512,128]{1,0:T(8,128)S(1)}, f32[512,128]{1,0:T(8,128)}, u32[]{:S(2)}) copy-start(f32[512,128]{1,0:T(8,128)} %refs_0_.1) | copy-start | bytes 786436
  59.2 25.4 %copy-start.3 = (f32[128,512]{1,0:T(8,128)S(1)}, f32[128,512]{1,0:T(8,128)}, u32[]{:S(2)}) copy-start(f32[128,512]{1,0:T(8,128)} %refs_6_.1) | copy-start | bytes 786436
  59.2 25.4 %copy-start.4 = (f32[512,128]{1,0:T(8,128)S(1)}, f32[512,128]{1,0:T(8,128)}, u32[]{:S(2)}) copy-start(f32[512,128]{1,0:T(8,128)} %refs_1_.1) | copy-start | bytes 786436
  59.2 25.4 %copy-start.5 = (f32[512,128]{1,0:T(8,128)S(1)}, f32[512,128]{1,0:T(8,128)}, u32[]{:S(2)}) copy-start(f32[512,128]{1,0:T(8,128)} %refs_2_.1) | copy-start | bytes 786436
  59.2 25.4 %copy-start.6 = (f32[128,512]{1,0:T(8,128)S(1)}, f32[128,512]{1,0:T(8,128)}, u32[]{:S(2)}) copy-start(f32[128,512]{1,0:T(8,128)} %refs_7_.1) | copy-start | bytes 786436
  59.2 25.4 %copy-start.7 = (f32[128,512]{1,0:T(8,128)S(1)}, f32[128,512]{1,0:T(8,128)}, u32[]{:S(2)}) copy-start(f32[128,512]{1,0:T(8,128)} %refs_8_.1) | copy-start | bytes 786436
  59.3 25.4 %copy-start.10 = (f32[7,512]{1,0:T(8,128)S(1)}, f32[7,512]{1,0:T(8,128)}, u32[]{:S(2)}) copy-start(f32[7,512]{1,0:T(8,128)} %refs_10_.1) | copy-start | bytes 43012
  59.3 25.4 %copy-start.11 = (f32[7,512]{1,0:T(8,128)S(1)}, f32[7,512]{1,0:T(8,128)}, u32[]{:S(2)}) copy-start(f32[7,512]{1,0:T(8,128)} %refs_11_.1) | copy-start | bytes 43012
  59.3 25.4 %copy-start.12 = (f32[2048]{0:T(1024)S(1)}, f32[2048]{0:T(1024)}, u32[]{:S(2)}) copy-start(f32[2048]{0:T(1024)} %param.24) | copy-start | bytes 24580
  59.3 25.4 %copy-start.13 = (f32[2048]{0:T(1024)S(1)}, f32[2048]{0:T(1024)}, u32[]{:S(2)}) copy-start(f32[2048]{0:T(1024)} %param.25) | copy-start | bytes 24580
  59.4 14.1 %collective-permute-start.14 = (bf16[2,512,128]{2,1,0:T(8,128)(2,1)S(1)}, bf16[2,512,128]{2,1,0:T(8,128)(2,1)S(1)}, u32[]{:S(2)}, u32[]{:S(2)}) collective-permute-start(bf16[2,512,128]{2,1,0:T(8,128)(2,1)S(1)} %add_convert_fusion.2), channel_id=1, source_target_pairs={{0,2},{1,3},{2,0},{3,1},{4,6},{5,7},{6,4},{7,5},{8,10},{9,11},{10,... | collective-permute-start | bytes 786440 | tf_op jit(solution)/shard_map/ppermute | solution.py:496
  60.2 15.6 %collective-permute-start.15 = (bf16[2,512,128]{2,1,0:T(8,128)(2,1)S(1)}, bf16[2,512,128]{2,1,0:T(8,128)(2,1)S(1)}, u32[]{:S(2)}, u32[]{:S(2)}) collective-permute-start(bf16[2,512,128]{2,1,0:T(8,128)(2,1)S(1)} %add_convert_fusion.1), channel_id=1, source_target_pairs={{0,8},{1,9},{2,10},{3,11},{4,12},{5,13},{6,14},{7,15},{8,0},{9,1},... | collective-permute-start | bytes 786440 | tf_op jit(solution)/shard_map/ppermute | solution.py:492
  64.7 1.2 %collective-permute-start.16 = (f32[44,128]{1,0:T(8,128)S(1)}, f32[44,128]{1,0:T(8,128)S(1)}, u32[]{:S(2)}, u32[]{:S(2)}) collective-permute-start(f32[44,128]{1,0:T(8,128)S(1)} %get-tuple-element.97), channel_id=1, source_target_pairs={{0,1},{1,0},{2,3},{3,2},{4,5},{5,4},{6,7},{7,6},{8,9},{9,8},{10,11... | collective-permute-start | bytes 67592 | tf_op jit(solution)/shard_map/ppermute | solution.py:496
  65.9 3.8 %collective-permute-start.17 = (f32[44,128]{1,0:T(8,128)S(1)}, f32[44,128]{1,0:T(8,128)S(1)}, u32[]{:S(2)}, u32[]{:S(2)}) collective-permute-start(f32[44,128]{1,0:T(8,128)S(1)} %add.43), channel_id=1, source_target_pairs={{0,16},{16,0},{1,17},{17,1},{2,18},{18,2},{3,19},{19,3},{4,20},{20... | collective-permute-start | bytes 67592 | tf_op jit(solution)/shard_map/ppermute | solution.py:504
  69.7 3.8 %collective-permute-start.18 = (f32[44,128]{1,0:T(8,128)S(1)}, f32[44,128]{1,0:T(8,128)S(1)}, u32[]{:S(2)}, u32[]{:S(2)}) collective-permute-start(f32[44,128]{1,0:T(8,128)S(1)} %add.44), channel_id=1, source_target_pairs={{0,2},{1,3},{2,0},{3,1},{4,6},{5,7},{6,4},{7,5},{8,10},{9,11},{10,... | collective-permute-start | bytes 67592 | tf_op jit(solution)/shard_map/ppermute | solution.py:496
  75.8 8.7 %collective-permute-start.19 = (bf16[2,512,128]{2,1,0:T(8,128)(2,1)S(1)}, bf16[2,512,128]{2,1,0:T(8,128)(2,1)S(1)}, u32[]{:S(2)}, u32[]{:S(2)}) collective-permute-start(bf16[2,512,128]{2,1,0:T(8,128)(2,1)S(1)} %add_convert_fusion.own_ref), channel_id=1, source_target_pairs={{0,16},{16,0},{1,17},{17,1},{2,18},{18,2},{3,19},{19,3},{4,20},{20... | collective-permute-start | bytes 786440 | tf_op jit(solution)/shard_map/ppermute | solution.py:504
  75.9 3.9 %collective-permute-start.20 = (f32[44,128]{1,0:T(8,128)S(1)}, f32[44,128]{1,0:T(8,128)S(1)}, u32[]{:S(2)}, u32[]{:S(2)}) collective-permute-start(f32[44,128]{1,0:T(8,128)S(1)} %add.45), channel_id=1, source_target_pairs={{0,4},{1,5},{2,6},{3,7},{4,0},{5,1},{6,2},{7,3},{8,12},{9,13},{10,... | collective-permute-start | bytes 67592 | tf_op jit(solution)/shard_map/ppermute | solution.py:496
  79.8 4.7 %collective-permute-start.21 = (f32[44,128]{1,0:T(8,128)S(1)}, f32[44,128]{1,0:T(8,128)S(1)}, u32[]{:S(2)}, u32[]{:S(2)}) collective-permute-start(f32[44,128]{1,0:T(8,128)S(1)} %add.46), channel_id=1, source_target_pairs={{0,8},{1,9},{2,10},{3,11},{4,12},{5,13},{6,14},{7,15},{8,0},{9,1},... | collective-permute-start | bytes 67592 | tf_op jit(solution)/shard_map/ppermute | solution.py:496

commit v5 on v4

--- a/solution.py
+++ b/solution.py
@@ -319,11 +319,19 @@
     return jnp.concatenate([refs[0][i], refs[1][i]], axis=1)
 
 
-def block_kernel(first, count, place_ref, own_ref, oth_ref, bias_ref, *refs):
+def block_places():
+    near, wide = lax.axis_index("narrow"), lax.axis_index("wide")
+    far_step = 8 + 4 * near
+    other_step = 12 - 4 * near
+    return [wide ^ step for step in (0, 4, far_step, 2, far_step ^ 2, other_step, other_step ^ 2, 6)]
+
+
+def block_kernel(first, count, own_ref, oth_ref, bias_ref, *refs):
     w_refs, (act_ref, low_ref, sums_ref), outs = refs[:count], refs[count : count + 3], refs[count + 3 :]
     sums_ref[...] = jnp.zeros_like(sums_ref)
+    places = block_places()
     for j in range(count // 2):
-        lines = [pl.ds(place_ref[first + 2 * j + k], 1) for k in range(2)]
+        lines = [pl.ds(places[first + 2 * j + k], 1) for k in range(2)]
         bias = jnp.concatenate([bias_ref[line, :] for line in lines], axis=1)
         a, b = (joined(w_refs[2 * j : 2 * j + 2], i) for i in range(2))
         columns = slice(j * 256, (j + 1) * 256)
@@ -539,17 +547,10 @@
     images, pixels, width = features.shape
     rows = images * pixels
     units = hidden_weight.shape[1]
-    near, wide = lax.axis_index("narrow"), lax.axis_index("wide")
-    first_far = jnp.where(near == 0, 8, 12)
-    last_far = 20 - first_far
-    zero = 0 * first_far
-    place = [zero, zero + 4, first_far, zero + 2, first_far ^ 2, last_far, last_far ^ 2, zero + 6]
-    place = (wide ^ jnp.stack(place)).astype(jnp.int32)
-
     pair, pair_f = struct((2, width, units), bf16), struct((2, width, units))
     w0 = call(cast_kernel, pair, (hidden_weight, output_weight), loose=(0, 1))
     wz1, wzf, wy0 = flip(w0, 4), far(w0), flip(w0, 2)
-    vectors_late = after(vectors, wz1)
+    vectors_late = after(vectors, wy0)
     x = features.transpose(1, 0, 2)
     cot = cotangent.transpose(1, 0, 2)
     big = struct((pixels, images, width))
@@ -562,9 +563,9 @@
         smem=1,
         loose=(1, 2, 3),
     )
-    sb = after(sb.reshape(2, rows, width), wzf, wy0)
+    sb = after(sb.reshape(2, rows, width), wzf, wz1, wy0)
     other = flip(sb, 1)
-    wyo, wyf, wzo = diagonal(wzf), flip(wzf, 2), across(wzf)
+    wyf, wzo = flip(wzf, 2), across(wzf)
     bias = hidden_bias.reshape(-1, 128)
     total, total_low = struct((2, rows, width)), struct((2, rows, width), bf16)
 
@@ -575,8 +576,7 @@
         return call(
             functools.partial(block_kernel, first, len(weights)),
             [tall, tall, lines, *results],
-            (place, sb, other, bias, *weights),
-            smem=1,
+            (sb, other, bias, *weights),
             vmem=20,
             **kw,
         )
@@ -588,13 +588,14 @@
         return call(kernel, results, (*acts, *lows, *weights, *old), loose=loose)
 
     w_near = [w0, wz1, wzf, wy0]
-    *near_hidden, sums1, g0, gz1, gzf, gy0 = blocks(0, w_near, [pair_f, pair, pair_f, pair], loose=(5, 6, 7))
+    *near_hidden, sums1, g0, gz1, gzf, gy0 = blocks(0, w_near, [pair_f, pair, pair_f, pair])
     z1 = flip(gz1, 4)
     wy1 = flip(after(wz1, sums1), 2)
     wyf, wzo, _ = lax.optimization_barrier((wyf, wzo, sums1))
+    wyo = across(wyf)
     *far_hidden, sums2, gyf, gzo = blocks(4, [wyf, wzo], [pair, pair])
     yf, xs = flip(gyf, 2), across(gzo)
-    old = back((0, 1), [total, total], (near_hidden, far_hidden), [*w_near, wyf, wzo], loose=(5, 6, 7))
+    old = back((0, 1), [total, total], (near_hidden, far_hidden), [*w_near, wyf, wzo])
     wyo, wy1, _ = lax.optimization_barrier((wyo, wy1, old[0]))
     *last_hidden, sums3, gyo, gy1 = blocks(6, [wyo, wy1], [pair, pair])
     ds, zy = diagonal(gyo), flip(gy1, 4)

time: 86.6 us -> 82.1 us (0.948)
  Pallas kernels: 32.2 us -> 28 us
  waiting for transfers between devices: 22.5 us -> 26.6 us
  starting transfers between devices: 28 us -> 24.4 us
    ppermute x4 -> x3, waiting for transfers between devices: 2.14 us -> 9.09 us  [joint(): return lax.ppermute(values, BOTH, [(s, n * 16 + w) for s, (n, w) in pairs])]
    ppermute x4 -> x3, starting transfers between devices: 11 us -> 5.62 us  [joint(): return lax.ppermute(values, BOTH, [(s, n * 16 + w) for s, (n, w) in pairs])]
    ppermute x4 -> x5, starting transfers between devices: 1.01 us -> 5.87 us  [across(): return lax.ppermute(values, 'narrow', [(0, 1), (1, 0)])]
    pallas_call x10, Pallas kernels: 32.2 us -> 28 us  [call(): pl.pallas_call(kernel, out_shape=outs, in_specs=[SMEM] * smem + [VMEM] *...]
    ppermute x14, starting transfers between devices: 16 us -> 12.9 us  [flip(): return lax.ppermute(values, 'wide', [(w, w ^ bit) for w in range(16)])]
    ppermute x14, waiting for transfers between devices: 17.1 us -> 14.7 us  [flip(): return lax.ppermute(values, 'wide', [(w, w ^ bit) for w in range(16)])]
    ppermute x4 -> x5, waiting for transfers between devices: 3.18 us -> 2.76 us  [across(): return lax.ppermute(values, 'narrow', [(0, 1), (1, 0)])]
  transfers between devices with their start and end apart: 22 -> 22, of which waited for: 9 -> 12; matrix products, arithmetic and copies ran while one was open for 0% -> 0% of each run, Pallas kernels for 34% -> 31%
where the time goes in v5:
time: 82.1 us; the launch traced here: 81.9 us
  Pallas kernels  28 us (34%)
  waiting for transfers between devices  26.6 us (32%)
  starting transfers between devices  24.4 us (30%)
  between operations  1.79 us (2%)
    pallas_call x10, Pallas kernels, call(): pl.pallas_call(kernel, out_shape=outs, in_specs=[SMEM] * smem + [VMEM] *...  28 us
    ppermute x14, waiting for transfers between devices, flip(): return lax.ppermute(values, 'wide', [(w, w ^ bit) for w in range(16)])  14.7 us
    ppermute x14, starting transfers between devices, flip(): return lax.ppermute(values, 'wide', [(w, w ^ bit) for w in range(16)])  12.9 us
    ppermute x3, waiting for transfers between devices, joint(): return lax.ppermute(values, BOTH, [(s, n * 16 + w) for s, (n, w) in pairs])  9.09 us
    ppermute x5, starting transfers between devices, across(): return lax.ppermute(values, 'narrow', [(0, 1), (1, 0)])  5.87 us
    ppermute x3, starting transfers between devices, joint(): return lax.ppermute(values, BOTH, [(s, n * 16 + w) for s, (n, w) in pairs])  5.62 us
    ppermute x5, waiting for transfers between devices, across(): return lax.ppermute(values, 'narrow', [(0, 1), (1, 0)])  2.76 us
  transfers between devices with their start and end apart: 22, of which 12 were waited for; matrix products, arithmetic and copies ran while one was open for 0% of the time, Pallas kernels for 31%

profile of v5, /device:TPU:0, one launch (start us, length us, event | category | flops | bytes accessed | tf_op | source)
XLA Modules:
  0.0 81.9 jit_solution(4174854769931641307)
XLA Ops:
  0.7 1.1 %cast_kernel.1.refs_0_.refs_4_ = bf16[2,512,128]{2,1,0:T(8,128)(2,1)S(1)} custom-call(f32[512,128]{1,0:T(8,128)} %refs_0_.1, f32[128,512]{1,0:T(8,128)} %refs_6_.1), custom_call_target="tpu_custom_call" | custom-call | bytes 786432 | tf_op jit(solution)/shard_map/cast_kernel/pallas_call | solution.py:479
  1.8 3.0 %collective-permute-start = (bf16[2,512,128]{2,1,0:T(8,128)(2,1)S(1)}, bf16[2,512,128]{2,1,0:T(8,128)(2,1)S(1)}, u32[]{:S(2)}, u32[]{:S(2)}) collective-permute-start(bf16[2,512,128]{2,1,0:T(8,128)(2,1)S(1)} %cast_kernel.1.refs_0_.refs_4_), channel_id=1, source_target_pairs={{0,2},{1,3},{2,0},{3,1},{4,6},{5,7},{6,4},{7,5},{8,10},{9,11},{10,... | collective-permute-start | bytes 786440 | tf_op jit(solution)/shard_map/ppermute | solution.py:504
  4.8 2.6 %collective-permute-start.1 = (bf16[2,512,128]{2,1,0:T(8,128)(2,1)S(1)}, bf16[2,512,128]{2,1,0:T(8,128)(2,1)S(1)}, u32[]{:S(2)}, u32[]{:S(2)}) collective-permute-start(bf16[2,512,128]{2,1,0:T(8,128)(2,1)S(1)} %cast_kernel.1.refs_0_.refs_4_), channel_id=1, source_target_pairs={{0,8},{1,9},{2,10},{3,11},{4,12},{5,13},{6,14},{7,15},{8,0},{9,1},... | collective-permute-start | bytes 786440 | tf_op jit(solution)/shard_map/ppermute | solution.py:500
  7.4 1.6 %collective-permute-start.2 = (bf16[2,512,128]{2,1,0:T(8,128)(2,1)S(1)}, bf16[2,512,128]{2,1,0:T(8,128)(2,1)S(1)}, u32[]{:S(2)}, u32[]{:S(2)}) collective-permute-start(bf16[2,512,128]{2,1,0:T(8,128)(2,1)S(1)} %cast_kernel.1.refs_0_.refs_4_), channel_id=1, source_target_pairs={{0,4},{1,5},{2,6},{3,7},{4,0},{5,1},{6,2},{7,3},{8,12},{9,13},{10,... | collective-permute-start | bytes 786440 | tf_op jit(solution)/shard_map/ppermute | solution.py:504
  9.7 1.5 %collective-permute-done.refs_3_.refs_7_ = bf16[2,512,128]{2,1,0:T(8,128)(2,1)S(1)} collective-permute-done((bf16[2,512,128]{2,1,0:T(8,128)(2,1)S(1)}, bf16[2,512,128]{2,1,0:T(8,128)(2,1)S(1)}, u32[]{:S(2)}, u32[]{:S(2)}) %collective-permute-start) | collective-permute-done | bytes 262176 | tf_op jit(solution)/shard_map/ppermute | solution.py:504
  11.1 3.3 %pre_kernel.1 = (bf16[2,49,16,512]{3,2,1,0:T(8,128)(2,1)S(1)}, f32[4,16,128]{2,1,0:T(8,128)S(1)}) custom-call(s32[1]{0:T(128)S(6)} %copy.29.counts_ref, f32[49,16,512]{2,1,0:T(8,128)} %bitcast.18, bf16[49,16,512]{2,1,0:T(8,128)(2,1)} %bitcast.20, f32[7,512]{1,0:T(8,128)} %refs_9_.1), custom_call_target="tpu_custom_call" | custom-call | bytes 4061188 | tf_op jit(solution)/shard_map/pre_kernel/pallas_call | solution.py:479
  14.5 4.7 %collective-permute-done.1.refs_2_.refs_6_ = bf16[2,512,128]{2,1,0:T(8,128)(2,1)S(1)} collective-permute-done((bf16[2,512,128]{2,1,0:T(8,128)(2,1)S(1)}, bf16[2,512,128]{2,1,0:T(8,128)(2,1)S(1)}, u32[]{:S(2)}, u32[]{:S(2)}) %collective-permute-start.1) | collective-permute-done | bytes 262176 | tf_op jit(solution)/shard_map/ppermute | solution.py:500
  19.2 0.2 collective-permute-done.2.refs_1_.refs_5_
  19.4 0.0 collective-permute-start.3
  19.4 0.5 collective-permute-start.4
  19.9 2.3 %collective-permute-start.5 = (bf16[2,512,128]{2,1,0:T(8,128)(2,1)S(1)}, bf16[2,512,128]{2,1,0:T(8,128)(2,1)S(1)}, u32[]{:S(2)}, u32[]{:S(2)}) collective-permute-start(bf16[2,512,128]{2,1,0:T(8,128)(2,1)S(1)} %collective-permute-done.1.refs_2_.refs_6_), channel_id=1, source_target_pairs={{0,16},{16,0},{1,17},{17,1},{2,18},{18,2},{3,19},{19,3},{4,20},{20... | collective-permute-start | bytes 786440 | tf_op jit(solution)/shard_map/ppermute | solution.py:512
  22.2 0.7 collective-permute-done.3.oth_ref
  22.9 5.9 %block_kernel.3 = (bf16[2,784,512]{2,1,0:T(8,128)(2,1)S(1)}, bf16[2,784,512]{2,1,0:T(8,128)(2,1)S(1)}, f32[16,128]{1,0:T(8,128)S(1)}, f32[2,512,128]{2,1,0:T(8,1...) custom-call(bf16[2,784,512]{2,1,0:T(8,128)(2,1)S(1)} %bitcast.14, ...), custom_call_target="tpu_custom_call" | custom-call | bytes 9060352 | tf_op jit(solution)/shard_map/block_kernel/pallas_call | solution.py:479
  28.8 0.1 collective-permute-done.5.refs_1_.refs_9_
  28.9 2.2 %collective-permute-start.6 = (bf16[2,512,128]{2,1,0:T(8,128)(2,1)S(1)}, bf16[2,512,128]{2,1,0:T(8,128)(2,1)S(1)}, u32[]{:S(2)}, u32[]{:S(2)}) collective-permute-start(bf16[2,512,128]{2,1,0:T(8,128)(2,1)S(1)} %collective-permute-done.4.refs_0_.refs_8_), channel_id=1, source_target_pairs={{0,16},{16,0},{1,17},{17,1},{2,18},{18,2},{3,19},{19,3},{4,20},{20... | collective-permute-start | bytes 786440 | tf_op jit(solution)/shard_map/ppermute | solution.py:512
  31.1 1.0 %collective-permute-start.7 = (bf16[2,512,128]{2,1,0:T(8,128)(2,1)S(1)}, bf16[2,512,128]{2,1,0:T(8,128)(2,1)S(1)}, u32[]{:S(2)}, u32[]{:S(2)}) collective-permute-start(bf16[2,512,128]{2,1,0:T(8,128)(2,1)S(1)} %collective-permute-done.2.refs_1_.refs_5_), channel_id=1, source_target_pairs={{0,2},{1,3},{2,0},{3,1},{4,6},{5,7},{6,4},{7,5},{8,10},{9,11},{10,... | collective-permute-start | bytes 786440 | tf_op jit(solution)/shard_map/ppermute | solution.py:504
  32.1 3.2 %block_kernel.4 = (bf16[2,784,256]{2,1,0:T(8,128)(2,1)S(1)}, bf16[2,784,256]{2,1,0:T(8,128)(2,1)S(1)}, f32[16,128]{1,0:T(8,128)S(1)}, bf16[2,512,128]{2,1,0:T(8,128)(2,1)S(1)}, bf16[2,512,128]{2,1,0:T(8,128)(2,1)S(1)}) custom-call(bf16[2,784,512]{2,1,0:T(8,128)(2,1)S(1)} %bitcast.15, bf16[2,784,512]{2,1,0:T(8,128)(2,1)S(1)} %collective-permute-done.3.oth_ref, ...), custom_call_target="tpu_custom_call" | custom-call | bytes 5881856 | tf_op jit(solution)/shard_map/block_kernel/pallas_call | solution.py:479
  35.3 1.1 %collective-permute-start.8 = (bf16[2,512,128]{2,1,0:T(8,128)(2,1)S(1)}, bf16[2,512,128]{2,1,0:T(8,128)(2,1)S(1)}, u32[]{:S(2)}, u32[]{:S(2)}) collective-permute-start(bf16[2,512,128]{2,1,0:T(8,128)(2,1)S(1)} %get-tuple-element.85), channel_id=1, source_target_pairs={{0,2},{1,3},{2,0},{3,1},{4,6},{5,7},{6,4},{7,5},{8,10},{9,11},{10,... | collective-permute-start | bytes 786440 | tf_op jit(solution)/shard_map/ppermute | solution.py:504
  36.4 0.1 collective-permute-start.9
  36.4 1.7 %collective-permute-start.10 = (bf16[2,512,128]{2,1,0:T(8,128)(2,1)S(1)}, bf16[2,512,128]{2,1,0:T(8,128)(2,1)S(1)}, u32[]{:S(2)}, u32[]{:S(2)}) collective-permute-start(bf16[2,512,128]{2,1,0:T(8,128)(2,1)S(1)} %get-tuple-element.87), channel_id=1, source_target_pairs={{0,4},{1,5},{2,6},{3,7},{4,0},{5,1},{6,2},{7,3},{8,12},{9,13},{10,... | collective-permute-start | bytes 786440 | tf_op jit(solution)/shard_map/ppermute | solution.py:504
  38.1 2.7 %back_kernel.3 = (f32[2,784,512]{2,1,0:T(8,128)S(1)}, f32[2,784,512]{2,1,0:T(8,128)S(1)}) custom-call(bf16[2,784,512]{2,1,0:T(8,128)(2,1)S(1)} %get-tuple-element.74.refs_0_, bf16[2,784,256]{2,1,0:T(8,128)(2,1)S(1)} %get-tuple-element.76.refs_1_, bf16[2,784,512]{2,1,0:T(8,128)(2,1)S(1)} %get-tuple-element.77.refs_2_, ...), custom_call_target="tpu_custom_call" | custom-call | bytes 12812288 | tf_op jit(solution)/shard_map/back_kernel/pallas_call | solution.py:479
  40.8 0.0 collective-permute-done.6.refs_0_.refs_2_
  40.8 0.0 collective-permute-done.7.refs_1_.refs_3_
  40.8 3.3 %block_kernel.5 = (bf16[2,784,256]{2,1,0:T(8,128)(2,1)S(1)}, bf16[2,784,256]{2,1,0:T(8,128)(2,1)S(1)}, f32[16,128]{1,0:T(8,128)S(1)}, bf16[2,512,128]{2,1,0:T(8,128)(2,1)S(1)}, bf16[2,512,128]{2,1,0:T(8,128)(2,1)S(1)}) custom-call(bf16[2,784,512]{2,1,0:T(8,128)(2,1)S(1)} %bitcast.16, bf16[2,784,512]{2,1,0:T(8,128)(2,1)S(1)} %collective-permute-done.3.oth_ref, ...), custom_call_target="tpu_custom_call" | custom-call | bytes 5881856 | tf_op jit(solution)/shard_map/block_kernel/pallas_call | solution.py:479
  44.2 0.6 back_kernel.5
  44.8 0.0 collective-permute-done.9
  44.8 0.0 collective-permute-done.10
  44.8 0.1 collective-permute-start.11
  44.9 2.5 %collective-permute-start.12 = (bf16[2,512,128]{2,1,0:T(8,128)(2,1)S(1)}, bf16[2,512,128]{2,1,0:T(8,128)(2,1)S(1)}, u32[]{:S(2)}, u32[]{:S(2)}) collective-permute-start(bf16[2,512,128]{2,1,0:T(8,128)(2,1)S(1)} %get-tuple-element.95), channel_id=1, source_target_pairs={{0,18},{1,19},{2,16},{3,17},{4,22},{5,23},{6,20},{7,21},{8,26},{9,... | collective-permute-start | bytes 786440 | tf_op jit(solution)/shard_map/ppermute | solution.py:500
  47.4 0.3 collective-permute-start.13
  47.7 0.6 back_kernel.4
  48.4 0.0 collective-permute-done.11
  48.4 0.4 copy-done
  48.8 0.2 copy-done.1
  49.0 5.7 %post_kernel.1 = (f32[49,16,512]{2,1,0:T(8,128)}, f32[49,16,512]{2,1,0:T(8,128)}, f32[44,128]{1,0:T(8,128)S(1)}) custom-call(s32[1]{0:T(128)S(6)} %copy.29.counts_ref, f32[49,16,512]{2,1,0:T(8,128)S(1)} %bitcast.19, bf16[49,16,512]{2,1,0:T(8,128)(2,1)S(1)} %bitcast.21, f32[7,512]{1,0:T(8,128)S(1)} %copy-done.8, ...), custom_call_target="tpu_custom_call" | custom-call | bytes 10530820 | tf_op jit(solution)/shard_map/post_kernel/pallas_call | solution.py:479
  54.7 0.0 collective-permute-done.12
  54.7 1.1 %collective-permute-done.13 = bf16[2,512,128]{2,1,0:T(8,128)(2,1)S(1)} collective-permute-done((bf16[2,512,128]{2,1,0:T(8,128)(2,1)S(1)}, bf16[2,512,128]{2,1,0:T(8,128)(2,1)S(1)}, u32[]{:S(2)}, u32[]{:S(2)}) %collective-permute-start.13) | collective-permute-done | bytes 262176 | tf_op jit(solution)/shard_map/ppermute | solution.py:504
  55.8 0.1 add_convert_fusion.2
  55.9 0.0 copy-start.2
  55.9 0.0 copy-start.3
  55.9 0.0 copy-start.4
  55.9 0.0 copy-start.5
  55.9 0.0 copy-start.6
  55.9 0.0 copy-start.7
  55.9 0.0 copy-start.10
  55.9 0.0 copy-start.11
  56.0 0.0 copy-start.12
  56.0 0.0 copy-start.13
  56.0 0.1 add_convert_fusion.1
  56.1 1.1 %collective-permute-start.14 = (bf16[2,512,128]{2,1,0:T(8,128)(2,1)S(1)}, bf16[2,512,128]{2,1,0:T(8,128)(2,1)S(1)}, u32[]{:S(2)}, u32[]{:S(2)}) collective-permute-start(bf16[2,512,128]{2,1,0:T(8,128)(2,1)S(1)} %add_convert_fusion.2), channel_id=1, source_target_pairs={{0,2},{1,3},{2,0},{3,1},{4,6},{5,7},{6,4},{7,5},{8,10},{9,11},{10,... | collective-permute-start | bytes 786440 | tf_op jit(solution)/shard_map/ppermute | solution.py:504
  57.2 0.6 collective-permute-start.15
  57.7 1.2 %collective-permute-done.16 = f32[44,128]{1,0:T(8,128)S(1)} collective-permute-done((f32[44,128]{1,0:T(8,128)S(1)}, f32[44,128]{1,0:T(8,128)S(1)}, u32[]{:S(2)}, u32[]{:S(2)}) %collective-permute-start.16) | collective-permute-done | bytes 22560 | tf_op jit(solution)/shard_map/ppermute | solution.py:504
  58.9 1.2 %collective-permute-start.17 = (f32[44,128]{1,0:T(8,128)S(1)}, f32[44,128]{1,0:T(8,128)S(1)}, u32[]{:S(2)}, u32[]{:S(2)}) collective-permute-start(f32[44,128]{1,0:T(8,128)S(1)} %add.43), channel_id=1, source_target_pairs={{0,16},{16,0},{1,17},{17,1},{2,18},{18,2},{3,19},{19,3},{4,20},{20... | collective-permute-start | bytes 67592 | tf_op jit(solution)/shard_map/ppermute | solution.py:512
  60.1 2.7 %collective-permute-done.17 = f32[44,128]{1,0:T(8,128)S(1)} collective-permute-done((f32[44,128]{1,0:T(8,128)S(1)}, f32[44,128]{1,0:T(8,128)S(1)}, u32[]{:S(2)}, u32[]{:S(2)}) %collective-permute-start.17) | collective-permute-done | bytes 22560 | tf_op jit(solution)/shard_map/ppermute | solution.py:512
  62.8 1.0 %collective-permute-start.18 = (f32[44,128]{1,0:T(8,128)S(1)}, f32[44,128]{1,0:T(8,128)S(1)}, u32[]{:S(2)}, u32[]{:S(2)}) collective-permute-start(f32[44,128]{1,0:T(8,128)S(1)} %add.44), channel_id=1, source_target_pairs={{0,2},{1,3},{2,0},{3,1},{4,6},{5,7},{6,4},{7,5},{8,10},{9,11},{10,... | collective-permute-start | bytes 67592 | tf_op jit(solution)/shard_map/ppermute | solution.py:504
  63.8 2.8 %collective-permute-done.18 = f32[44,128]{1,0:T(8,128)S(1)} collective-permute-done((f32[44,128]{1,0:T(8,128)S(1)}, f32[44,128]{1,0:T(8,128)S(1)}, u32[]{:S(2)}, u32[]{:S(2)}) %collective-permute-start.18) | collective-permute-done | bytes 22560 | tf_op jit(solution)/shard_map/ppermute | solution.py:504
  66.6 4.3 %collective-permute-done.15 = bf16[2,512,128]{2,1,0:T(8,128)(2,1)S(1)} collective-permute-done((bf16[2,512,128]{2,1,0:T(8,128)(2,1)S(1)}, bf16[2,512,128]{2,1,0:T(8,128)(2,1)S(1)}, u32[]{:S(2)}, u32[]{:S(2)}) %collective-permute-start.15) | collective-permute-done | bytes 262176 | tf_op jit(solution)/shard_map/ppermute | solution.py:500
  71.0 0.1 add_convert_fusion.own_ref
  71.1 0.1 collective-permute-start.19
  71.2 0.7 collective-permute-start.20
  71.9 3.1 %collective-permute-done.20 = f32[44,128]{1,0:T(8,128)S(1)} collective-permute-done((f32[44,128]{1,0:T(8,128)S(1)}, f32[44,128]{1,0:T(8,128)S(1)}, u32[]{:S(2)}, u32[]{:S(2)}) %collective-permute-start.20) | collective-permute-done | bytes 22560 | tf_op jit(solution)/shard_map/ppermute | solution.py:504
  75.1 0.9 %collective-permute-start.21 = (f32[44,128]{1,0:T(8,128)S(1)}, f32[44,128]{1,0:T(8,128)S(1)}, u32[]{:S(2)}, u32[]{:S(2)}) collective-permute-start(f32[44,128]{1,0:T(8,128)S(1)} %add.46), channel_id=1, source_target_pairs={{0,8},{1,9},{2,10},{3,11},{4,12},{5,13},{6,14},{7,15},{8,0},{9,1},... | collective-permute-start | bytes 67592 | tf_op jit(solution)/shard_map/ppermute | solution.py:504
  75.9 4.1 %collective-permute-done.21 = f32[44,128]{1,0:T(8,128)S(1)} collective-permute-done((f32[44,128]{1,0:T(8,128)S(1)}, f32[44,128]{1,0:T(8,128)S(1)}, u32[]{:S(2)}, u32[]{:S(2)}) %collective-permute-start.21) | collective-permute-done | bytes 22560 | tf_op jit(solution)/shard_map/ppermute | solution.py:504
  80.2 1.6 %update_kernel.1 = (f32[512,128]{1,0:T(8,128)}, f32[512,128]{1,0:T(8,128)}, f32[512,128]{1,0:T(8,128)}, f32[16,128]{1,0:T(8,128)}, f32[16,128]{1,0:T(8,128)}, /*...) custom-call(bf16[2,512,128]{2,1,0:T(8,128)(2,1)S(1)} %add_convert_fu, ...), custom_call_target="tpu_custom_call" | custom-call | bytes 3827712 | tf_op jit(solution)/shard_map/update_kernel/pallas_call | solution.py:479
  (26 shorter events, 0.1 us)
Async XLA Ops:
  0.6 22.2 %copy-start.9 = (f32[2048]{0:T(1024)S(1)}, f32[2048]{0:T(1024)}, u32[]{:S(2)}) copy-start(f32[2048]{0:T(1024)} %param.19) | copy-start | bytes 24580
  1.8 9.3 %collective-permute-start = (bf16[2,512,128]{2,1,0:T(8,128)(2,1)S(1)}, bf16[2,512,128]{2,1,0:T(8,128)(2,1)S(1)}, u32[]{:S(2)}, u32[]{:S(2)}) collective-permute-start(bf16[2,512,128]{2,1,0:T(8,128)(2,1)S(1)} %cast_kernel.1.refs_0_.refs_4_), channel_id=1, source_target_pairs={{0,2},{1,3},{2,0},{3,1},{4,6},{5,7},{6,4},{7,5},{8,10},{9,11},{10,... | collective-permute-start | bytes 786440 | tf_op jit(solution)/shard_map/ppermute | solution.py:504
  4.8 14.4 %collective-permute-start.1 = (bf16[2,512,128]{2,1,0:T(8,128)(2,1)S(1)}, bf16[2,512,128]{2,1,0:T(8,128)(2,1)S(1)}, u32[]{:S(2)}, u32[]{:S(2)}) collective-permute-start(bf16[2,512,128]{2,1,0:T(8,128)(2,1)S(1)} %cast_kernel.1.refs_0_.refs_4_), channel_id=1, source_target_pairs={{0,8},{1,9},{2,10},{3,11},{4,12},{5,13},{6,14},{7,15},{8,0},{9,1},... | collective-permute-start | bytes 786440 | tf_op jit(solution)/shard_map/ppermute | solution.py:500
  7.4 12.0 %collective-permute-start.2 = (bf16[2,512,128]{2,1,0:T(8,128)(2,1)S(1)}, bf16[2,512,128]{2,1,0:T(8,128)(2,1)S(1)}, u32[]{:S(2)}, u32[]{:S(2)}) collective-permute-start(bf16[2,512,128]{2,1,0:T(8,128)(2,1)S(1)} %cast_kernel.1.refs_0_.refs_4_), channel_id=1, source_target_pairs={{0,4},{1,5},{2,6},{3,7},{4,0},{5,1},{6,2},{7,3},{8,12},{9,13},{10,... | collective-permute-start | bytes 786440 | tf_op jit(solution)/shard_map/ppermute | solution.py:504
  19.4 3.5 %collective-permute-start.3 = (bf16[2,784,512]{2,1,0:T(8,128)(2,1)S(1)}, bf16[2,784,512]{2,1,0:T(8,128)(2,1)S(1)}, u32[]{:S(2)}, u32[]{:S(2)}) collective-permute-start(bf16[2,784,512]{2,1,0:T(8,128)(2,1)S(1)} %bitcast.13), channel_id=1, source_target_pairs={{0,1},{1,0},{2,3},{3,2},{4,5},{5,4},{6,7},{7,6},{8,9},{9,8},{10,11... | collective-permute-start | bytes 4816904 | tf_op jit(solution)/shard_map/ppermute | solution.py:504
  19.4 9.4 %collective-permute-start.4 = (bf16[2,512,128]{2,1,0:T(8,128)(2,1)S(1)}, bf16[2,512,128]{2,1,0:T(8,128)(2,1)S(1)}, u32[]{:S(2)}, u32[]{:S(2)}) collective-permute-start(bf16[2,512,128]{2,1,0:T(8,128)(2,1)S(1)} %collective-permute-done.1.refs_2_.refs_6_), channel_id=1, source_target_pairs={{0,2},{1,3},{2,0},{3,1},{4,6},{5,7},{6,4},{7,5},{8,10},{9,11},{10,... | collective-permute-start | bytes 786440 | tf_op jit(solution)/shard_map/ppermute | solution.py:504
  19.9 9.0 %collective-permute-start.5 = (bf16[2,512,128]{2,1,0:T(8,128)(2,1)S(1)}, bf16[2,512,128]{2,1,0:T(8,128)(2,1)S(1)}, u32[]{:S(2)}, u32[]{:S(2)}) collective-permute-start(bf16[2,512,128]{2,1,0:T(8,128)(2,1)S(1)} %collective-permute-done.1.refs_2_.refs_6_), channel_id=1, source_target_pairs={{0,16},{16,0},{1,17},{17,1},{2,18},{18,2},{3,19},{19,3},{4,20},{20... | collective-permute-start | bytes 786440 | tf_op jit(solution)/shard_map/ppermute | solution.py:512
  28.9 11.9 %collective-permute-start.6 = (bf16[2,512,128]{2,1,0:T(8,128)(2,1)S(1)}, bf16[2,512,128]{2,1,0:T(8,128)(2,1)S(1)}, u32[]{:S(2)}, u32[]{:S(2)}) collective-permute-start(bf16[2,512,128]{2,1,0:T(8,128)(2,1)S(1)} %collective-permute-done.4.refs_0_.refs_8_), channel_id=1, source_target_pairs={{0,16},{16,0},{1,17},{17,1},{2,18},{18,2},{3,19},{19,3},{4,20},{20... | collective-permute-start | bytes 786440 | tf_op jit(solution)/shard_map/ppermute | solution.py:512
  31.1 9.7 %collective-permute-start.7 = (bf16[2,512,128]{2,1,0:T(8,128)(2,1)S(1)}, bf16[2,512,128]{2,1,0:T(8,128)(2,1)S(1)}, u32[]{:S(2)}, u32[]{:S(2)}) collective-permute-start(bf16[2,512,128]{2,1,0:T(8,128)(2,1)S(1)} %collective-permute-done.2.refs_1_.refs_5_), channel_id=1, source_target_pairs={{0,2},{1,3},{2,0},{3,1},{4,6},{5,7},{6,4},{7,5},{8,10},{9,11},{10,... | collective-permute-start | bytes 786440 | tf_op jit(solution)/shard_map/ppermute | solution.py:504
  35.3 9.5 %collective-permute-start.8 = (bf16[2,512,128]{2,1,0:T(8,128)(2,1)S(1)}, bf16[2,512,128]{2,1,0:T(8,128)(2,1)S(1)}, u32[]{:S(2)}, u32[]{:S(2)}) collective-permute-start(bf16[2,512,128]{2,1,0:T(8,128)(2,1)S(1)} %get-tuple-element.85), channel_id=1, source_target_pairs={{0,2},{1,3},{2,0},{3,1},{4,6},{5,7},{6,4},{7,5},{8,10},{9,11},{10,... | collective-permute-start | bytes 786440 | tf_op jit(solution)/shard_map/ppermute | solution.py:504
  36.4 8.4 %collective-permute-start.9 = (bf16[2,512,128]{2,1,0:T(8,128)(2,1)S(1)}, bf16[2,512,128]{2,1,0:T(8,128)(2,1)S(1)}, u32[]{:S(2)}, u32[]{:S(2)}) collective-permute-start(bf16[2,512,128]{2,1,0:T(8,128)(2,1)S(1)} %get-tuple-element.86), channel_id=1, source_target_pairs={{0,16},{16,0},{1,17},{17,1},{2,18},{18,2},{3,19},{19,3},{4,20},{20... | collective-permute-start | bytes 786440 | tf_op jit(solution)/shard_map/ppermute | solution.py:512
  36.4 8.4 %collective-permute-start.10 = (bf16[2,512,128]{2,1,0:T(8,128)(2,1)S(1)}, bf16[2,512,128]{2,1,0:T(8,128)(2,1)S(1)}, u32[]{:S(2)}, u32[]{:S(2)}) collective-permute-start(bf16[2,512,128]{2,1,0:T(8,128)(2,1)S(1)} %get-tuple-element.87), channel_id=1, source_target_pairs={{0,4},{1,5},{2,6},{3,7},{4,0},{5,1},{6,2},{7,3},{8,12},{9,13},{10,... | collective-permute-start | bytes 786440 | tf_op jit(solution)/shard_map/ppermute | solution.py:504
  44.8 3.5 %collective-permute-start.11 = (bf16[2,784,512]{2,1,0:T(8,128)(2,1)S(1)}, bf16[2,784,512]{2,1,0:T(8,128)(2,1)S(1)}, u32[]{:S(2)}, u32[]{:S(2)}) collective-permute-start(bf16[2,784,512]{2,1,0:T(8,128)(2,1)S(1)} %back_kernel.5), channel_id=1, source_target_pairs={{0,1},{1,0},{2,3},{3,2},{4,5},{5,4},{6,7},{7,6},{8,9},{9,8},{10,11... | collective-permute-start | bytes 4816904 | tf_op jit(solution)/shard_map/ppermute | solution.py:504
  44.9 9.8 %collective-permute-start.12 = (bf16[2,512,128]{2,1,0:T(8,128)(2,1)S(1)}, bf16[2,512,128]{2,1,0:T(8,128)(2,1)S(1)}, u32[]{:S(2)}, u32[]{:S(2)}) collective-permute-start(bf16[2,512,128]{2,1,0:T(8,128)(2,1)S(1)} %get-tuple-element.95), channel_id=1, source_target_pairs={{0,18},{1,19},{2,16},{3,17},{4,22},{5,23},{6,20},{7,21},{8,26},{9,... | collective-permute-start | bytes 786440 | tf_op jit(solution)/shard_map/ppermute | solution.py:500
  47.4 1.4 %copy-start = (f32[16,49,512]{2,0,1:T(8,128)S(1)}, f32[16,49,512]{2,0,1:T(8,128)}, u32[]{:S(2)}) copy-start(f32[16,49,512]{2,0,1:T(8,128)} %param.15) | copy-start | bytes 4816900
  47.4 1.6 %copy-start.1 = (bf16[16,49,512]{2,0,1:T(8,128)(2,1)S(1)}, bf16[16,49,512]{2,0,1:T(8,128)(2,1)}, u32[]{:S(2)}) copy-start(bf16[16,49,512]{2,0,1:T(8,128)(2,1)} %param.16) | copy-start | bytes 2408452
  47.4 1.6 %copy-start.8 = (f32[7,512]{1,0:T(8,128)S(1)}, f32[7,512]{1,0:T(8,128)}, u32[]{:S(2)}) copy-start(f32[7,512]{1,0:T(8,128)} %refs_9_.1) | copy-start | bytes 43012
  47.4 8.4 %collective-permute-start.13 = (bf16[2,512,128]{2,1,0:T(8,128)(2,1)S(1)}, bf16[2,512,128]{2,1,0:T(8,128)(2,1)S(1)}, u32[]{:S(2)}, u32[]{:S(2)}) collective-permute-start(bf16[2,512,128]{2,1,0:T(8,128)(2,1)S(1)} %get-tuple-element.96), channel_id=1, source_target_pairs={{0,4},{1,5},{2,6},{3,7},{4,0},{5,1},{6,2},{7,3},{8,12},{9,13},{10,... | collective-permute-start | bytes 786440 | tf_op jit(solution)/shard_map/ppermute | solution.py:504
  55.9 24.2 %copy-start.2 = (f32[512,128]{1,0:T(8,128)S(1)}, f32[512,128]{1,0:T(8,128)}, u32[]{:S(2)}) copy-start(f32[512,128]{1,0:T(8,128)} %refs_0_.1) | copy-start | bytes 786436
  55.9 24.2 %copy-start.3 = (f32[128,512]{1,0:T(8,128)S(1)}, f32[128,512]{1,0:T(8,128)}, u32[]{:S(2)}) copy-start(f32[128,512]{1,0:T(8,128)} %refs_6_.1) | copy-start | bytes 786436
  55.9 24.2 %copy-start.4 = (f32[512,128]{1,0:T(8,128)S(1)}, f32[512,128]{1,0:T(8,128)}, u32[]{:S(2)}) copy-start(f32[512,128]{1,0:T(8,128)} %refs_1_.1) | copy-start | bytes 786436
  55.9 24.2 %copy-start.5 = (f32[512,128]{1,0:T(8,128)S(1)}, f32[512,128]{1,0:T(8,128)}, u32[]{:S(2)}) copy-start(f32[512,128]{1,0:T(8,128)} %refs_2_.1) | copy-start | bytes 786436
  55.9 24.2 %copy-start.6 = (f32[128,512]{1,0:T(8,128)S(1)}, f32[128,512]{1,0:T(8,128)}, u32[]{:S(2)}) copy-start(f32[128,512]{1,0:T(8,128)} %refs_7_.1) | copy-start | bytes 786436
  55.9 24.2 %copy-start.7 = (f32[128,512]{1,0:T(8,128)S(1)}, f32[128,512]{1,0:T(8,128)}, u32[]{:S(2)}) copy-start(f32[128,512]{1,0:T(8,128)} %refs_8_.1) | copy-start | bytes 786436
  55.9 24.2 %copy-start.10 = (f32[7,512]{1,0:T(8,128)S(1)}, f32[7,512]{1,0:T(8,128)}, u32[]{:S(2)}) copy-start(f32[7,512]{1,0:T(8,128)} %refs_10_.1) | copy-start | bytes 43012
  55.9 24.2 %copy-start.11 = (f32[7,512]{1,0:T(8,128)S(1)}, f32[7,512]{1,0:T(8,128)}, u32[]{:S(2)}) copy-start(f32[7,512]{1,0:T(8,128)} %refs_11_.1) | copy-start | bytes 43012
  56.0 24.2 %copy-start.12 = (f32[2048]{0:T(1024)S(1)}, f32[2048]{0:T(1024)}, u32[]{:S(2)}) copy-start(f32[2048]{0:T(1024)} %param.24) | copy-start | bytes 24580
  56.0 24.2 %copy-start.13 = (f32[2048]{0:T(1024)S(1)}, f32[2048]{0:T(1024)}, u32[]{:S(2)}) copy-start(f32[2048]{0:T(1024)} %param.25) | copy-start | bytes 24580
  56.1 10.5 %collective-permute-start.14 = (bf16[2,512,128]{2,1,0:T(8,128)(2,1)S(1)}, bf16[2,512,128]{2,1,0:T(8,128)(2,1)S(1)}, u32[]{:S(2)}, u32[]{:S(2)}) collective-permute-start(bf16[2,512,128]{2,1,0:T(8,128)(2,1)S(1)} %add_convert_fusion.2), channel_id=1, source_target_pairs={{0,2},{1,3},{2,0},{3,1},{4,6},{5,7},{6,4},{7,5},{8,10},{9,11},{10,... | collective-permute-start | bytes 786440 | tf_op jit(solution)/shard_map/ppermute | solution.py:504
  57.2 13.8 %collective-permute-start.15 = (bf16[2,512,128]{2,1,0:T(8,128)(2,1)S(1)}, bf16[2,512,128]{2,1,0:T(8,128)(2,1)S(1)}, u32[]{:S(2)}, u32[]{:S(2)}) collective-permute-start(bf16[2,512,128]{2,1,0:T(8,128)(2,1)S(1)} %add_convert_fusion.1), channel_id=1, source_target_pairs={{0,8},{1,9},{2,10},{3,11},{4,12},{5,13},{6,14},{7,15},{8,0},{9,1},... | collective-permute-start | bytes 786440 | tf_op jit(solution)/shard_map/ppermute | solution.py:500
  57.7 1.2 %collective-permute-start.16 = (f32[44,128]{1,0:T(8,128)S(1)}, f32[44,128]{1,0:T(8,128)S(1)}, u32[]{:S(2)}, u32[]{:S(2)}) collective-permute-start(f32[44,128]{1,0:T(8,128)S(1)} %get-tuple-element.97), channel_id=1, source_target_pairs={{0,1},{1,0},{2,3},{3,2},{4,5},{5,4},{6,7},{7,6},{8,9},{9,8},{10,11... | collective-permute-start | bytes 67592 | tf_op jit(solution)/shard_map/ppermute | solution.py:504
  58.9 3.8 %collective-permute-start.17 = (f32[44,128]{1,0:T(8,128)S(1)}, f32[44,128]{1,0:T(8,128)S(1)}, u32[]{:S(2)}, u32[]{:S(2)}) collective-permute-start(f32[44,128]{1,0:T(8,128)S(1)} %add.43), channel_id=1, source_target_pairs={{0,16},{16,0},{1,17},{17,1},{2,18},{18,2},{3,19},{19,3},{4,20},{20... | collective-permute-start | bytes 67592 | tf_op jit(solution)/shard_map/ppermute | solution.py:512
  62.8 3.8 %collective-permute-start.18 = (f32[44,128]{1,0:T(8,128)S(1)}, f32[44,128]{1,0:T(8,128)S(1)}, u32[]{:S(2)}, u32[]{:S(2)}) collective-permute-start(f32[44,128]{1,0:T(8,128)S(1)} %add.44), channel_id=1, source_target_pairs={{0,2},{1,3},{2,0},{3,1},{4,6},{5,7},{6,4},{7,5},{8,10},{9,11},{10,... | collective-permute-start | bytes 67592 | tf_op jit(solution)/shard_map/ppermute | solution.py:504
  71.1 9.0 %collective-permute-start.19 = (bf16[2,512,128]{2,1,0:T(8,128)(2,1)S(1)}, bf16[2,512,128]{2,1,0:T(8,128)(2,1)S(1)}, u32[]{:S(2)}, u32[]{:S(2)}) collective-permute-start(bf16[2,512,128]{2,1,0:T(8,128)(2,1)S(1)} %add_convert_fusion.own_ref), channel_id=1, source_target_pairs={{0,16},{16,0},{1,17},{17,1},{2,18},{18,2},{3,19},{19,3},{4,20},{20... | collective-permute-start | bytes 786440 | tf_op jit(solution)/shard_map/ppermute | solution.py:512
  71.2 3.9 %collective-permute-start.20 = (f32[44,128]{1,0:T(8,128)S(1)}, f32[44,128]{1,0:T(8,128)S(1)}, u32[]{:S(2)}, u32[]{:S(2)}) collective-permute-start(f32[44,128]{1,0:T(8,128)S(1)} %add.45), channel_id=1, source_target_pairs={{0,4},{1,5},{2,6},{3,7},{4,0},{5,1},{6,2},{7,3},{8,12},{9,13},{10,... | collective-permute-start | bytes 67592 | tf_op jit(solution)/shard_map/ppermute | solution.py:504
  75.1 5.0 %collective-permute-start.21 = (f32[44,128]{1,0:T(8,128)S(1)}, f32[44,128]{1,0:T(8,128)S(1)}, u32[]{:S(2)}, u32[]{:S(2)}) collective-permute-start(f32[44,128]{1,0:T(8,128)S(1)} %add.46), channel_id=1, source_target_pairs={{0,8},{1,9},{2,10},{3,11},{4,12},{5,13},{6,14},{7,15},{8,0},{9,1},... | collective-permute-start | bytes 67592 | tf_op jit(solution)/shard_map/ppermute | solution.py:504

commit v6 on v5

--- a/solution.py
+++ b/solution.py
@@ -243,51 +243,6 @@
     return vec_ref[2:3, :] * (r1 * vec_ref[0:1, :])
 
 
-def pre_kernel(counts_ref, x_ref, cot_ref, vec_ref, sb_ref, stat_ref, d_ref, h_ref):
-    pixels, images, width = x_ref.shape
-    size = pixels * width
-    zero = jnp.zeros((images, width), f32)
-
-    def loop(body, init):
-        return lax.fori_loop(0, pixels, body, init, unroll=7)
-
-    mu1 = row_total(loop(lambda p, s: s + x_ref[p], zero)) / size
-
-    def centre(p, s):
-        d = x_ref[p] - mu1
-        return s + d * d
-
-    r1 = lax.rsqrt(row_total(loop(centre, zero)) / size + norm_epsilon)
-    lift = mixed_parts(x_ref, mu1, r1, vec_ref, h_ref, d_ref)
-
-    def middle(p, s):
-        m = x_ref[p] + lift * d_ref[p]
-        h_ref[p] = m
-        return s + m
-
-    total = loop(middle, zero)
-    mu2 = row_total(total) / size
-
-    def spread(p, s):
-        d = h_ref[p] - mu2
-        d_ref[p] = d
-        return s + d * d
-
-    r2 = lax.rsqrt(row_total(loop(spread, zero)) / size + norm_epsilon)
-    scale = r2 * vec_ref[3:4, :]
-    shift = jnp.broadcast_to(vec_ref[4:5, :], (images, width))
-    gate = valid_gate(counts_ref, (images, width)) * vec_ref[5:6, :]
-
-    def finish(p, carry):
-        sb_ref[0, p] = (d_ref[p] * scale + shift).astype(bf16)
-        sb_ref[1, p] = (cot_ref[p].astype(f32) * gate).astype(bf16)
-        return carry
-
-    loop(finish, 0)
-    for i, stat in enumerate((mu1, r1, mu2, r2)):
-        stat_ref[i] = jnp.broadcast_to(stat, (images, 128))
-
-
 def normal_parts(h):
     d = 1.0 + (0.3275911 / math.sqrt(2.0)) * jnp.abs(h)
     t = pl.reciprocal(d, approx=True)
@@ -305,16 +260,6 @@
     return lax.dot_general(left, right, (dims, ((), ())), preferred_element_type=f32)
 
 
-def side_by_side(refs, j):
-    left, right = refs[2 * j], refs[2 * j + 1]
-    return jnp.concatenate([left[...], right[...]], axis=1)
-
-
-def cast_kernel(a_ref, b_ref, out_ref):
-    out_ref[0] = a_ref[...].astype(bf16)
-    out_ref[1] = b_ref[...].T.astype(bf16)
-
-
 def joined(refs, i):
     return jnp.concatenate([refs[0][i], refs[1][i]], axis=1)
 
@@ -323,36 +268,111 @@
     near, wide = lax.axis_index("narrow"), lax.axis_index("wide")
     far_step = 8 + 4 * near
     other_step = 12 - 4 * near
-    return [wide ^ step for step in (0, 4, far_step, 2, far_step ^ 2, other_step, other_step ^ 2, 6)]
+    return [wide ^ step for step in (0, 2, 4, far_step, far_step ^ 2, other_step, other_step ^ 2, 6)]
+
+
+def block_bias(bias_ref, places, at):
+    return jnp.concatenate([bias_ref[pl.ds(places[at + k], 1), :] for k in range(2)], axis=1)
+
+
+def block_rows(second, upstream, a, b, bias):
+    h = dot(second, a, ((1,), (0,))) + bias
+    back = dot(upstream, b, ((1,), (0,)))
+    phi, slope = normal_parts(h)
+    active = (h * phi).astype(bf16)
+    low = (back * slope).astype(bf16)
+    column = jnp.sum(low.astype(f32), axis=0, keepdims=True)
+    grads = [dot(left, right, ((0,), (0,))) for left, right in ((second, low), (upstream, active))]
+    return active, low, column, grads
+
+
+def pre_kernel(
+    counts_ref, x_ref, cot_ref, vec_ref, bias_ref, w0_ref, w1_ref,
+    sb_ref, stat_ref, act_ref, low_ref, column_ref, part_ref, d_ref, h_ref,
+):
+    pixels, images, width = x_ref.shape
+    size = pixels * width
+    zero = jnp.zeros((images, width), f32)
+
+    def loop(body, init):
+        return lax.fori_loop(0, pixels, body, init, unroll=7)
+
+    mu1 = row_total(loop(lambda p, s: s + x_ref[p], zero)) / size
+
+    def centre(p, s):
+        d = x_ref[p] - mu1
+        return s + d * d
+
+    r1 = lax.rsqrt(row_total(loop(centre, zero)) / size + norm_epsilon)
+    lift = mixed_parts(x_ref, mu1, r1, vec_ref, h_ref, d_ref)
+
+    def middle(p, s):
+        m = x_ref[p] + lift * d_ref[p]
+        h_ref[p] = m
+        return s + m
+
+    total = loop(middle, zero)
+    mu2 = row_total(total) / size
+
+    def spread(p, s):
+        d = h_ref[p] - mu2
+        d_ref[p] = d
+        return s + d * d
+
+    r2 = lax.rsqrt(row_total(loop(spread, zero)) / size + norm_epsilon)
+    scale = r2 * vec_ref[3:4, :]
+    shift = jnp.broadcast_to(vec_ref[4:5, :], (images, width))
+    gate = valid_gate(counts_ref, (images, width)) * vec_ref[5:6, :]
+
+    def finish(p, carry):
+        sb_ref[0, p] = (d_ref[p] * scale + shift).astype(bf16)
+        sb_ref[1, p] = (cot_ref[p].astype(f32) * gate).astype(bf16)
+        return carry
+
+    loop(finish, 0)
+    for i, stat in enumerate((mu1, r1, mu2, r2)):
+        stat_ref[i] = jnp.broadcast_to(stat, (images, 128))
+    second, upstream = (sb_ref[i].reshape(pixels * images, width) for i in range(2))
+    a, b = (joined((w0_ref, w1_ref), i) for i in range(2))
+    bias = block_bias(bias_ref, block_places(), 0)
+    act_ref[...], low_ref[...], column_ref[...], grads = block_rows(second, upstream, a, b, bias)
+    for i, grad in enumerate(grads):
+        part_ref[i] = grad
+
+
+def side_by_side(refs, j):
+    left, right = refs[2 * j], refs[2 * j + 1]
+    return jnp.concatenate([left[...], right[...]], axis=1)
+
+
+def cast_kernel(a_ref, b_ref, out_ref):
+    out_ref[0] = a_ref[...].astype(bf16)
+    out_ref[1] = b_ref[...].T.astype(bf16)
 
 
 def block_kernel(first, count, own_ref, oth_ref, bias_ref, *refs):
-    w_refs, (act_ref, low_ref, sums_ref), outs = refs[:count], refs[count : count + 3], refs[count + 3 :]
+    w_refs, refs = refs[:count], refs[count:]
+    begun, refs = (refs[:4], refs[4:]) if first == 0 else (None, refs)
+    act_ref, low_ref, sums_ref, *outs = refs
     sums_ref[...] = jnp.zeros_like(sums_ref)
     places = block_places()
     for j in range(count // 2):
-        lines = [pl.ds(places[first + 2 * j + k], 1) for k in range(2)]
-        bias = jnp.concatenate([bias_ref[line, :] for line in lines], axis=1)
+        bias = block_bias(bias_ref, places, first + 2 * j)
         a, b = (joined(w_refs[2 * j : 2 * j + 2], i) for i in range(2))
         columns = slice(j * 256, (j + 1) * 256)
-        grads = [None, None]
-        sums = None
+        grads = sums = None
         for r, sb_ref in enumerate((own_ref, oth_ref)):
-            h = dot(sb_ref[0], a, ((1,), (0,))) + bias
-            back = dot(sb_ref[1], b, ((1,), (0,)))
-            phi, slope = normal_parts(h)
-            active = (h * phi).astype(bf16)
-            low = (back * slope).astype(bf16)
+            if begun is not None and j == r == 0:
+                active, low, column, parts = begun[0][...], begun[1][...], begun[2][...], begun[3]
+            else:
+                active, low, column, parts = block_rows(sb_ref[0], sb_ref[1], a, b, bias)
             act_ref[r, :, columns] = active
             low_ref[r, :, columns] = low
-            column = jnp.sum(low.astype(f32), axis=0, keepdims=True)
             sums = column if r == 0 else sums + column
-            for i, (left, right) in enumerate(((sb_ref[0], low), (sb_ref[1], active))):
-                part = dot(left, right, ((0,), (0,)))
-                grads[i] = part if r == 0 else grads[i] + part
+            grads = [parts[0], parts[1]] if r == 0 else [total + part for total, part in zip(grads, parts)]
         for k in range(2):
             half = slice(k * 128, (k + 1) * 128)
-            sums_ref[lines[k], :] = sums[:, half]
+            sums_ref[pl.ds(places[first + 2 * j + k], 1), :] = sums[:, half]
             for i, grad in enumerate(grads):
                 outs[2 * j + k][i] = grad[:, half].astype(outs[2 * j + k].dtype)
 
@@ -550,35 +570,43 @@
     pair, pair_f = struct((2, width, units), bf16), struct((2, width, units))
     w0 = call(cast_kernel, pair, (hidden_weight, output_weight), loose=(0, 1))
     wz1, wzf, wy0 = flip(w0, 4), far(w0), flip(w0, 2)
-    vectors_late = after(vectors, wy0)
+    vectors_late, wy0 = lax.optimization_barrier((vectors, wy0))
+    bias = hidden_bias.reshape(-1, 128)
     x = features.transpose(1, 0, 2)
     cot = cotangent.transpose(1, 0, 2)
     big = struct((pixels, images, width))
     keep = pltpu.VMEM((pixels, images, width), f32)
-    sb, stat = call(
+    tile = struct((rows, 256), bf16)
+    sb, stat, *begun = call(
         pre_kernel,
-        [struct((2, pixels, images, width), bf16), struct((4, images, 128))],
-        (counts, x, cot, vectors_late),
+        [
+            struct((2, pixels, images, width), bf16),
+            struct((4, images, 128)),
+            tile,
+            tile,
+            struct((1, 256)),
+            struct((2, width, 256)),
+        ],
+        (counts, x, cot, vectors_late, bias, w0, wy0),
         [keep, keep],
         smem=1,
         loose=(1, 2, 3),
+        vmem=20,
     )
     sb = after(sb.reshape(2, rows, width), wzf, wz1, wy0)
     other = flip(sb, 1)
     wyf, wzo = flip(wzf, 2), across(wzf)
-    bias = hidden_bias.reshape(-1, 128)
     total, total_low = struct((2, rows, width)), struct((2, rows, width), bf16)
 
     lines = struct(bias.shape)
 
-    def blocks(first, weights, results, **kw):
+    def blocks(first, weights, results, begun=()):
         tall = struct((2, rows, 128 * len(weights)), bf16)
         return call(
             functools.partial(block_kernel, first, len(weights)),
             [tall, tall, lines, *results],
-            (sb, other, bias, *weights),
+            (sb, other, bias, *weights, *begun),
             vmem=20,
-            **kw,
         )
 
     def back(sides, results, hidden, weights, old=(), loose=()):
@@ -587,11 +615,11 @@
         kernel = functools.partial(back_kernel, sides, counts, bool(old))
         return call(kernel, results, (*acts, *lows, *weights, *old), loose=loose)
 
-    w_near = [w0, wz1, wzf, wy0]
-    *near_hidden, sums1, g0, gz1, gzf, gy0 = blocks(0, w_near, [pair_f, pair, pair_f, pair])
+    w_near = [w0, wy0, wz1, wzf]
+    *near_hidden, sums1, g0, gy0, gz1, gzf = blocks(0, w_near, [pair_f, pair, pair, pair_f], begun)
     z1 = flip(gz1, 4)
     wy1 = flip(after(wz1, sums1), 2)
-    wyf, wzo, _ = lax.optimization_barrier((wyf, wzo, sums1))
+    wyf = after(wyf, sums1)
     wyo = across(wyf)
     *far_hidden, sums2, gyf, gzo = blocks(4, [wyf, wzo], [pair, pair])
     yf, xs = flip(gyf, 2), across(gzo)

time: 82.1 us -> 81.5 us (level)
  waiting for transfers between devices: 26.6 us -> 24.8 us
  Pallas kernels: 28 us -> 29.1 us
    ppermute x3, waiting for transfers between devices: 9.09 us -> 6.8 us  [joint(): return lax.ppermute(values, BOTH, [(s, n * 16 + w) for s, (n, w) in pairs])]
    pallas_call x10, Pallas kernels: 28 us -> 29.1 us  [call(): pl.pallas_call(kernel, out_shape=outs, in_specs=[SMEM] * smem + [VMEM] *...]
  transfers between devices with their start and end apart: 22 -> 22, of which waited for: 12 -> 14; matrix products, arithmetic and copies ran while one was open for 0% -> 0% of each run, Pallas kernels for 31% -> 32%
where the time goes in v6:
time: 81.5 us; the launch traced here: 81.2 us
  Pallas kernels  29.1 us (36%)
  waiting for transfers between devices  24.8 us (30%)
  starting transfers between devices  24.3 us (30%)
  between operations  1.77 us (2%)
  local copies, waits for them, and re-layouts  0.97 us (1%)
    pallas_call x10, Pallas kernels, call(): pl.pallas_call(kernel, out_shape=outs, in_specs=[SMEM] * smem + [VMEM] *...  29.1 us
    ppermute x14, waiting for transfers between devices, flip(): return lax.ppermute(values, 'wide', [(w, w ^ bit) for w in range(16)])  15.2 us
    ppermute x14, starting transfers between devices, flip(): return lax.ppermute(values, 'wide', [(w, w ^ bit) for w in range(16)])  13.4 us
    ppermute x3, waiting for transfers between devices, joint(): return lax.ppermute(values, BOTH, [(s, n * 16 + w) for s, (n, w) in pairs])  6.8 us
    ppermute x5, starting transfers between devices, across(): return lax.ppermute(values, 'narrow', [(0, 1), (1, 0)])  5.75 us
    ppermute x3, starting transfers between devices, joint(): return lax.ppermute(values, BOTH, [(s, n * 16 + w) for s, (n, w) in pairs])  5.12 us
    ppermute x5, waiting for transfers between devices, across(): return lax.ppermute(values, 'narrow', [(0, 1), (1, 0)])  2.8 us
  transfers between devices with their start and end apart: 22, of which 14 were waited for; matrix products, arithmetic and copies ran while one was open for 0% of the time, Pallas kernels for 32%

profile of v6, /device:TPU:0, one launch (start us, length us, event | category | flops | bytes accessed | tf_op | source)
XLA Modules:
  0.0 81.2 jit_solution(16787768179824651475)
XLA Ops:
  0.6 1.1 %cast_kernel.1.w0_ref.refs_0_.refs_4_ = bf16[2,512,128]{2,1,0:T(8,128)(2,1)S(1)} custom-call(f32[512,128]{1,0:T(8,128)} %refs_0_.1, f32[128,512]{1,0:T(8,128)} %refs_6_.1), custom_call_target="tpu_custom_call" | custom-call | bytes 786432 | tf_op jit(solution)/shard_map/cast_kernel/pallas_call | solution.py:499
  1.8 3.0 %collective-permute-start = (bf16[2,512,128]{2,1,0:T(8,128)(2,1)S(1)}, bf16[2,512,128]{2,1,0:T(8,128)(2,1)S(1)}, u32[]{:S(2)}, u32[]{:S(2)}) collective-permute-start(bf16[2,512,128]{2,1,0:T(8,128)(2,1)S(1)} %cast_kernel.1.w0_ref.refs_0_.refs_4_), channel_id=1, source_target_pairs={{0,2},{1,3},{2,0},{3,1},{4,6},{5,7},{6,4},{7,5},{8,10},{9,11},{10,... | collective-permute-start | bytes 786440 | tf_op jit(solution)/shard_map/ppermute | solution.py:524
  4.8 2.6 %collective-permute-start.1 = (bf16[2,512,128]{2,1,0:T(8,128)(2,1)S(1)}, bf16[2,512,128]{2,1,0:T(8,128)(2,1)S(1)}, u32[]{:S(2)}, u32[]{:S(2)}) collective-permute-start(bf16[2,512,128]{2,1,0:T(8,128)(2,1)S(1)} %cast_kernel.1.w0_ref.refs_0_.refs_4_), channel_id=1, source_target_pairs={{0,8},{1,9},{2,10},{3,11},{4,12},{5,13},{6,14},{7,15},{8,0},{9,1},... | collective-permute-start | bytes 786440 | tf_op jit(solution)/shard_map/ppermute | solution.py:520
  7.4 1.6 %collective-permute-start.2 = (bf16[2,512,128]{2,1,0:T(8,128)(2,1)S(1)}, bf16[2,512,128]{2,1,0:T(8,128)(2,1)S(1)}, u32[]{:S(2)}, u32[]{:S(2)}) collective-permute-start(bf16[2,512,128]{2,1,0:T(8,128)(2,1)S(1)} %cast_kernel.1.w0_ref.refs_0_.refs_4_), channel_id=1, source_target_pairs={{0,4},{1,5},{2,6},{3,7},{4,0},{5,1},{6,2},{7,3},{8,12},{9,13},{10,... | collective-permute-start | bytes 786440 | tf_op jit(solution)/shard_map/ppermute | solution.py:524
  9.6 1.5 %collective-permute-done.w1_ref.refs_1_.refs_5_ = bf16[2,512,128]{2,1,0:T(8,128)(2,1)S(1)} collective-permute-done((bf16[2,512,128]{2,1,0:T(8,128)(2,1)S(1)}, bf16[2,512,128]{2,1,0:T(8,128)(2,1)S(1)}, u32[]{:S(2)}, u32[]{:S(2)}) %collective-permute-start) | collective-permute-done | bytes 262176 | tf_op jit(solution)/shard_map/ppermute | solution.py:524
  11.1 0.7 copy-done.8
  11.8 5.2 %pre_kernel.1 = (bf16[2,49,16,512]{3,2,1,0:T(8,128)(2,1)S(1)}, f32[4,16,128]{2,1,0:T(8,128)S(1)}, bf16[784,256]{1,0:T(8,128)(2,1)S(1)}, bf16[784,256]{1,0:T(8,12...) custom-call(s32[1]{0:T(128)S(6)} %copy.29.counts_ref, f32[49,16,512]{2,1,0:T(8,128)} %bitcast.18, ...), custom_call_target="tpu_custom_call" | custom-call | bytes 6446084 | tf_op jit(solution)/shard_map/pre_kernel/pallas_call | solution.py:499
  17.0 2.2 %collective-permute-done.1.refs_3_.refs_7_ = bf16[2,512,128]{2,1,0:T(8,128)(2,1)S(1)} collective-permute-done((bf16[2,512,128]{2,1,0:T(8,128)(2,1)S(1)}, bf16[2,512,128]{2,1,0:T(8,128)(2,1)S(1)}, u32[]{:S(2)}, u32[]{:S(2)}) %collective-permute-start.1) | collective-permute-done | bytes 262176 | tf_op jit(solution)/shard_map/ppermute | solution.py:520
  19.2 0.2 collective-permute-done.2.refs_2_.refs_6_
  19.4 0.0 collective-permute-start.3
  19.4 0.5 collective-permute-start.4
  19.9 2.3 %collective-permute-start.7 = (bf16[2,512,128]{2,1,0:T(8,128)(2,1)S(1)}, bf16[2,512,128]{2,1,0:T(8,128)(2,1)S(1)}, u32[]{:S(2)}, u32[]{:S(2)}) collective-permute-start(bf16[2,512,128]{2,1,0:T(8,128)(2,1)S(1)} %collective-permute-done.1.refs_3_.refs_7_), channel_id=1, source_target_pairs={{0,16},{16,0},{1,17},{17,1},{2,18},{18,2},{3,19},{19,3},{4,20},{20... | collective-permute-start | bytes 786440 | tf_op jit(solution)/shard_map/ppermute | solution.py:532
  22.2 0.7 collective-permute-done.3.oth_ref
  22.9 4.7 %block_kernel.3 = (bf16[2,784,512]{2,1,0:T(8,128)(2,1)S(1)}, bf16[2,784,512]{2,1,0:T(8,128)(2,1)S(1)}, f32[16,128]{1,0:T(8,128)S(1)}, f32[2,512,128]{2,1,0:T(8,1...) custom-call(bf16[2,784,512]{2,1,0:T(8,128)(2,1)S(1)} %bitcast.14, ...), custom_call_target="tpu_custom_call" | custom-call | bytes 10912768 | tf_op jit(solution)/shard_map/block_kernel/pallas_call | solution.py:499
  27.6 0.5 collective-permute-done.4.refs_0_.refs_8_
  28.1 0.5 collective-permute-start.6
  28.6 2.3 %collective-permute-start.5 = (bf16[2,512,128]{2,1,0:T(8,128)(2,1)S(1)}, bf16[2,512,128]{2,1,0:T(8,128)(2,1)S(1)}, u32[]{:S(2)}, u32[]{:S(2)}) collective-permute-start(bf16[2,512,128]{2,1,0:T(8,128)(2,1)S(1)} %collective-permute-done.4.refs_0_.refs_8_), channel_id=1, source_target_pairs={{0,16},{16,0},{1,17},{17,1},{2,18},{18,2},{3,19},{19,3},{4,20},{20... | collective-permute-start | bytes 786440 | tf_op jit(solution)/shard_map/ppermute | solution.py:532
  30.9 3.3 %block_kernel.4 = (bf16[2,784,256]{2,1,0:T(8,128)(2,1)S(1)}, bf16[2,784,256]{2,1,0:T(8,128)(2,1)S(1)}, f32[16,128]{1,0:T(8,128)S(1)}, bf16[2,512,128]{2,1,0:T(8,128)(2,1)S(1)}, bf16[2,512,128]{2,1,0:T(8,128)(2,1)S(1)}) custom-call(bf16[2,784,512]{2,1,0:T(8,128)(2,1)S(1)} %bitcast.15, bf16[2,784,512]{2,1,0:T(8,128)(2,1)S(1)} %collective-permute-done.3.oth_ref, ...), custom_call_target="tpu_custom_call" | custom-call | bytes 5881856 | tf_op jit(solution)/shard_map/block_kernel/pallas_call | solution.py:499
  34.2 1.6 %collective-permute-start.8 = (bf16[2,512,128]{2,1,0:T(8,128)(2,1)S(1)}, bf16[2,512,128]{2,1,0:T(8,128)(2,1)S(1)}, u32[]{:S(2)}, u32[]{:S(2)}) collective-permute-start(bf16[2,512,128]{2,1,0:T(8,128)(2,1)S(1)} %get-tuple-element.93), channel_id=1, source_target_pairs={{0,2},{1,3},{2,0},{3,1},{4,6},{5,7},{6,4},{7,5},{8,10},{9,11},{10,... | collective-permute-start | bytes 786440 | tf_op jit(solution)/shard_map/ppermute | solution.py:524
  35.7 0.0 collective-permute-start.9
  35.8 1.7 %collective-permute-start.10 = (bf16[2,512,128]{2,1,0:T(8,128)(2,1)S(1)}, bf16[2,512,128]{2,1,0:T(8,128)(2,1)S(1)}, u32[]{:S(2)}, u32[]{:S(2)}) collective-permute-start(bf16[2,512,128]{2,1,0:T(8,128)(2,1)S(1)} %get-tuple-element.95), channel_id=1, source_target_pairs={{0,4},{1,5},{2,6},{3,7},{4,0},{5,1},{6,2},{7,3},{8,12},{9,13},{10,... | collective-permute-start | bytes 786440 | tf_op jit(solution)/shard_map/ppermute | solution.py:524
  37.4 2.7 %back_kernel.3 = (f32[2,784,512]{2,1,0:T(8,128)S(1)}, f32[2,784,512]{2,1,0:T(8,128)S(1)}) custom-call(bf16[2,784,512]{2,1,0:T(8,128)(2,1)S(1)} %get-tuple-element.83.refs_0_, bf16[2,784,256]{2,1,0:T(8,128)(2,1)S(1)} %get-tuple-element.84.refs_1_, bf16[2,784,512]{2,1,0:T(8,128)(2,1)S(1)} %get-tuple-element.85.refs_2_, ...), custom_call_target="tpu_custom_call" | custom-call | bytes 12812288 | tf_op jit(solution)/shard_map/back_kernel/pallas_call | solution.py:499
  40.1 0.0 collective-permute-done.6.refs_1_.refs_3_
  40.1 0.0 collective-permute-done.5.refs_0_.refs_2_
  40.2 3.4 %block_kernel.5 = (bf16[2,784,256]{2,1,0:T(8,128)(2,1)S(1)}, bf16[2,784,256]{2,1,0:T(8,128)(2,1)S(1)}, f32[16,128]{1,0:T(8,128)S(1)}, bf16[2,512,128]{2,1,0:T(8,128)(2,1)S(1)}, bf16[2,512,128]{2,1,0:T(8,128)(2,1)S(1)}) custom-call(bf16[2,784,512]{2,1,0:T(8,128)(2,1)S(1)} %bitcast.16, bf16[2,784,512]{2,1,0:T(8,128)(2,1)S(1)} %collective-permute-done.3.oth_ref, ...), custom_call_target="tpu_custom_call" | custom-call | bytes 5881856 | tf_op jit(solution)/shard_map/block_kernel/pallas_call | solution.py:499
  43.6 0.7 back_kernel.5
  44.3 0.0 collective-permute-done.8
  44.3 0.0 collective-permute-done.10
  44.3 0.1 collective-permute-start.11
  44.4 2.0 %collective-permute-start.12 = (bf16[2,512,128]{2,1,0:T(8,128)(2,1)S(1)}, bf16[2,512,128]{2,1,0:T(8,128)(2,1)S(1)}, u32[]{:S(2)}, u32[]{:S(2)}) collective-permute-start(bf16[2,512,128]{2,1,0:T(8,128)(2,1)S(1)} %get-tuple-element.103), channel_id=1, source_target_pairs={{0,18},{1,19},{2,16},{3,17},{4,22},{5,23},{6,20},{7,21},{8,26},{9,... | collective-permute-start | bytes 786440 | tf_op jit(solution)/shard_map/ppermute | solution.py:520
  46.4 0.7 collective-permute-start.13
  47.1 0.6 back_kernel.4
  47.7 0.1 collective-permute-done.11
  47.9 0.2 copy-done.1
  48.1 5.8 %post_kernel.1 = (f32[49,16,512]{2,1,0:T(8,128)}, f32[49,16,512]{2,1,0:T(8,128)}, f32[44,128]{1,0:T(8,128)S(1)}) custom-call(s32[1]{0:T(128)S(6)} %copy.29.counts_ref, f32[49,16,512]{2,1,0:T(8,128)S(1)} %bitcast.19, bf16[49,16,512]{2,1,0:T(8,128)(2,1)S(1)} %bitcast.21, f32[7,512]{1,0:T(8,128)S(1)} %copy-done.9, ...), custom_call_target="tpu_custom_call" | custom-call | bytes 10530820 | tf_op jit(solution)/shard_map/post_kernel/pallas_call | solution.py:499
  53.8 0.2 collective-permute-done.12
  54.0 0.8 collective-permute-done.13
  54.8 0.1 add_convert_fusion.2
  54.9 0.0 copy-start.2
  54.9 0.0 copy-start.3
  54.9 0.0 copy-start.4
  54.9 0.0 copy-start.5
  54.9 0.0 copy-start.6
  55.0 0.0 copy-start.7
  55.0 0.0 copy-start.10
  55.0 0.0 copy-start.11
  55.0 0.0 copy-start.12
  55.0 0.0 copy-start.13
  55.0 0.1 add_convert_fusion.1
  55.1 1.6 %collective-permute-start.14 = (bf16[2,512,128]{2,1,0:T(8,128)(2,1)S(1)}, bf16[2,512,128]{2,1,0:T(8,128)(2,1)S(1)}, u32[]{:S(2)}, u32[]{:S(2)}) collective-permute-start(bf16[2,512,128]{2,1,0:T(8,128)(2,1)S(1)} %add_convert_fusion.2), channel_id=1, source_target_pairs={{0,2},{1,3},{2,0},{3,1},{4,6},{5,7},{6,4},{7,5},{8,10},{9,11},{10,... | collective-permute-start | bytes 786440 | tf_op jit(solution)/shard_map/ppermute | solution.py:524
  56.7 0.5 collective-permute-start.15
  57.2 1.2 %collective-permute-done.16 = f32[44,128]{1,0:T(8,128)S(1)} collective-permute-done((f32[44,128]{1,0:T(8,128)S(1)}, f32[44,128]{1,0:T(8,128)S(1)}, u32[]{:S(2)}, u32[]{:S(2)}) %collective-permute-start.16) | collective-permute-done | bytes 22560 | tf_op jit(solution)/shard_map/ppermute | solution.py:524
  58.4 1.0 %collective-permute-start.17 = (f32[44,128]{1,0:T(8,128)S(1)}, f32[44,128]{1,0:T(8,128)S(1)}, u32[]{:S(2)}, u32[]{:S(2)}) collective-permute-start(f32[44,128]{1,0:T(8,128)S(1)} %add.43), channel_id=1, source_target_pairs={{0,16},{16,0},{1,17},{17,1},{2,18},{18,2},{3,19},{19,3},{4,20},{20... | collective-permute-start | bytes 67592 | tf_op jit(solution)/shard_map/ppermute | solution.py:532
  59.5 2.8 %collective-permute-done.17 = f32[44,128]{1,0:T(8,128)S(1)} collective-permute-done((f32[44,128]{1,0:T(8,128)S(1)}, f32[44,128]{1,0:T(8,128)S(1)}, u32[]{:S(2)}, u32[]{:S(2)}) %collective-permute-start.17) | collective-permute-done | bytes 22560 | tf_op jit(solution)/shard_map/ppermute | solution.py:532
  62.3 1.0 %collective-permute-start.18 = (f32[44,128]{1,0:T(8,128)S(1)}, f32[44,128]{1,0:T(8,128)S(1)}, u32[]{:S(2)}, u32[]{:S(2)}) collective-permute-start(f32[44,128]{1,0:T(8,128)S(1)} %add.44), channel_id=1, source_target_pairs={{0,2},{1,3},{2,0},{3,1},{4,6},{5,7},{6,4},{7,5},{8,10},{9,11},{10,... | collective-permute-start | bytes 67592 | tf_op jit(solution)/shard_map/ppermute | solution.py:524
  63.3 2.8 %collective-permute-done.18 = f32[44,128]{1,0:T(8,128)S(1)} collective-permute-done((f32[44,128]{1,0:T(8,128)S(1)}, f32[44,128]{1,0:T(8,128)S(1)}, u32[]{:S(2)}, u32[]{:S(2)}) %collective-permute-start.18) | collective-permute-done | bytes 22560 | tf_op jit(solution)/shard_map/ppermute | solution.py:524
  66.1 4.4 %collective-permute-done.15 = bf16[2,512,128]{2,1,0:T(8,128)(2,1)S(1)} collective-permute-done((bf16[2,512,128]{2,1,0:T(8,128)(2,1)S(1)}, bf16[2,512,128]{2,1,0:T(8,128)(2,1)S(1)}, u32[]{:S(2)}, u32[]{:S(2)}) %collective-permute-start.15) | collective-permute-done | bytes 262176 | tf_op jit(solution)/shard_map/ppermute | solution.py:520
  70.5 0.1 add_convert_fusion.own_ref
  70.6 0.1 collective-permute-start.19
  70.7 0.4 collective-permute-start.20
  71.1 3.5 %collective-permute-done.20 = f32[44,128]{1,0:T(8,128)S(1)} collective-permute-done((f32[44,128]{1,0:T(8,128)S(1)}, f32[44,128]{1,0:T(8,128)S(1)}, u32[]{:S(2)}, u32[]{:S(2)}) %collective-permute-start.20) | collective-permute-done | bytes 22560 | tf_op jit(solution)/shard_map/ppermute | solution.py:524
  74.6 0.9 %collective-permute-start.21 = (f32[44,128]{1,0:T(8,128)S(1)}, f32[44,128]{1,0:T(8,128)S(1)}, u32[]{:S(2)}, u32[]{:S(2)}) collective-permute-start(f32[44,128]{1,0:T(8,128)S(1)} %add.46), channel_id=1, source_target_pairs={{0,8},{1,9},{2,10},{3,11},{4,12},{5,13},{6,14},{7,15},{8,0},{9,1},... | collective-permute-start | bytes 67592 | tf_op jit(solution)/shard_map/ppermute | solution.py:524
  75.5 3.9 %collective-permute-done.21 = f32[44,128]{1,0:T(8,128)S(1)} collective-permute-done((f32[44,128]{1,0:T(8,128)S(1)}, f32[44,128]{1,0:T(8,128)S(1)}, u32[]{:S(2)}, u32[]{:S(2)}) %collective-permute-start.21) | collective-permute-done | bytes 22560 | tf_op jit(solution)/shard_map/ppermute | solution.py:524
  79.5 1.6 %update_kernel.1 = (f32[512,128]{1,0:T(8,128)}, f32[512,128]{1,0:T(8,128)}, f32[512,128]{1,0:T(8,128)}, f32[16,128]{1,0:T(8,128)}, f32[16,128]{1,0:T(8,128)}, /*...) custom-call(bf16[2,512,128]{2,1,0:T(8,128)(2,1)S(1)} %add_convert_fu, ...), custom_call_target="tpu_custom_call" | custom-call | bytes 3827712 | tf_op jit(solution)/shard_map/update_kernel/pallas_call | solution.py:499
  (26 shorter events, 0.1 us)
Async XLA Ops:
  1.8 9.3 %collective-permute-start = (bf16[2,512,128]{2,1,0:T(8,128)(2,1)S(1)}, bf16[2,512,128]{2,1,0:T(8,128)(2,1)S(1)}, u32[]{:S(2)}, u32[]{:S(2)}) collective-permute-start(bf16[2,512,128]{2,1,0:T(8,128)(2,1)S(1)} %cast_kernel.1.w0_ref.refs_0_.refs_4_), channel_id=1, source_target_pairs={{0,2},{1,3},{2,0},{3,1},{4,6},{5,7},{6,4},{7,5},{8,10},{9,11},{10,... | collective-permute-start | bytes 786440 | tf_op jit(solution)/shard_map/ppermute | solution.py:524
  4.8 14.4 %collective-permute-start.1 = (bf16[2,512,128]{2,1,0:T(8,128)(2,1)S(1)}, bf16[2,512,128]{2,1,0:T(8,128)(2,1)S(1)}, u32[]{:S(2)}, u32[]{:S(2)}) collective-permute-start(bf16[2,512,128]{2,1,0:T(8,128)(2,1)S(1)} %cast_kernel.1.w0_ref.refs_0_.refs_4_), channel_id=1, source_target_pairs={{0,8},{1,9},{2,10},{3,11},{4,12},{5,13},{6,14},{7,15},{8,0},{9,1},... | collective-permute-start | bytes 786440 | tf_op jit(solution)/shard_map/ppermute | solution.py:520
  7.4 12.0 %collective-permute-start.2 = (bf16[2,512,128]{2,1,0:T(8,128)(2,1)S(1)}, bf16[2,512,128]{2,1,0:T(8,128)(2,1)S(1)}, u32[]{:S(2)}, u32[]{:S(2)}) collective-permute-start(bf16[2,512,128]{2,1,0:T(8,128)(2,1)S(1)} %cast_kernel.1.w0_ref.refs_0_.refs_4_), channel_id=1, source_target_pairs={{0,4},{1,5},{2,6},{3,7},{4,0},{5,1},{6,2},{7,3},{8,12},{9,13},{10,... | collective-permute-start | bytes 786440 | tf_op jit(solution)/shard_map/ppermute | solution.py:524
  11.1 0.7 copy-start.8
  19.4 3.5 %collective-permute-start.3 = (bf16[2,784,512]{2,1,0:T(8,128)(2,1)S(1)}, bf16[2,784,512]{2,1,0:T(8,128)(2,1)S(1)}, u32[]{:S(2)}, u32[]{:S(2)}) collective-permute-start(bf16[2,784,512]{2,1,0:T(8,128)(2,1)S(1)} %bitcast.13), channel_id=1, source_target_pairs={{0,1},{1,0},{2,3},{3,2},{4,5},{5,4},{6,7},{7,6},{8,9},{9,8},{10,11... | collective-permute-start | bytes 4816904 | tf_op jit(solution)/shard_map/ppermute | solution.py:524
  19.4 8.7 %collective-permute-start.4 = (bf16[2,512,128]{2,1,0:T(8,128)(2,1)S(1)}, bf16[2,512,128]{2,1,0:T(8,128)(2,1)S(1)}, u32[]{:S(2)}, u32[]{:S(2)}) collective-permute-start(bf16[2,512,128]{2,1,0:T(8,128)(2,1)S(1)} %collective-permute-done.1.refs_3_.refs_7_), channel_id=1, source_target_pairs={{0,2},{1,3},{2,0},{3,1},{4,6},{5,7},{6,4},{7,5},{8,10},{9,11},{10,... | collective-permute-start | bytes 786440 | tf_op jit(solution)/shard_map/ppermute | solution.py:524
  19.9 11.0 %collective-permute-start.7 = (bf16[2,512,128]{2,1,0:T(8,128)(2,1)S(1)}, bf16[2,512,128]{2,1,0:T(8,128)(2,1)S(1)}, u32[]{:S(2)}, u32[]{:S(2)}) collective-permute-start(bf16[2,512,128]{2,1,0:T(8,128)(2,1)S(1)} %collective-permute-done.1.refs_3_.refs_7_), channel_id=1, source_target_pairs={{0,16},{16,0},{1,17},{17,1},{2,18},{18,2},{3,19},{19,3},{4,20},{20... | collective-permute-start | bytes 786440 | tf_op jit(solution)/shard_map/ppermute | solution.py:532
  28.1 12.0 %collective-permute-start.6 = (bf16[2,512,128]{2,1,0:T(8,128)(2,1)S(1)}, bf16[2,512,128]{2,1,0:T(8,128)(2,1)S(1)}, u32[]{:S(2)}, u32[]{:S(2)}) collective-permute-start(bf16[2,512,128]{2,1,0:T(8,128)(2,1)S(1)} %collective-permute-done.2.refs_2_.refs_6_), channel_id=1, source_target_pairs={{0,2},{1,3},{2,0},{3,1},{4,6},{5,7},{6,4},{7,5},{8,10},{9,11},{10,... | collective-permute-start | bytes 786440 | tf_op jit(solution)/shard_map/ppermute | solution.py:524
  28.6 11.6 %collective-permute-start.5 = (bf16[2,512,128]{2,1,0:T(8,128)(2,1)S(1)}, bf16[2,512,128]{2,1,0:T(8,128)(2,1)S(1)}, u32[]{:S(2)}, u32[]{:S(2)}) collective-permute-start(bf16[2,512,128]{2,1,0:T(8,128)(2,1)S(1)} %collective-permute-done.4.refs_0_.refs_8_), channel_id=1, source_target_pairs={{0,16},{16,0},{1,17},{17,1},{2,18},{18,2},{3,19},{19,3},{4,20},{20... | collective-permute-start | bytes 786440 | tf_op jit(solution)/shard_map/ppermute | solution.py:532
  34.2 10.1 %collective-permute-start.8 = (bf16[2,512,128]{2,1,0:T(8,128)(2,1)S(1)}, bf16[2,512,128]{2,1,0:T(8,128)(2,1)S(1)}, u32[]{:S(2)}, u32[]{:S(2)}) collective-permute-start(bf16[2,512,128]{2,1,0:T(8,128)(2,1)S(1)} %get-tuple-element.93), channel_id=1, source_target_pairs={{0,2},{1,3},{2,0},{3,1},{4,6},{5,7},{6,4},{7,5},{8,10},{9,11},{10,... | collective-permute-start | bytes 786440 | tf_op jit(solution)/shard_map/ppermute | solution.py:524
  35.7 8.6 %collective-permute-start.9 = (bf16[2,512,128]{2,1,0:T(8,128)(2,1)S(1)}, bf16[2,512,128]{2,1,0:T(8,128)(2,1)S(1)}, u32[]{:S(2)}, u32[]{:S(2)}) collective-permute-start(bf16[2,512,128]{2,1,0:T(8,128)(2,1)S(1)} %get-tuple-element.94), channel_id=1, source_target_pairs={{0,16},{16,0},{1,17},{17,1},{2,18},{18,2},{3,19},{19,3},{4,20},{20... | collective-permute-start | bytes 786440 | tf_op jit(solution)/shard_map/ppermute | solution.py:532
  35.8 8.6 %collective-permute-start.10 = (bf16[2,512,128]{2,1,0:T(8,128)(2,1)S(1)}, bf16[2,512,128]{2,1,0:T(8,128)(2,1)S(1)}, u32[]{:S(2)}, u32[]{:S(2)}) collective-permute-start(bf16[2,512,128]{2,1,0:T(8,128)(2,1)S(1)} %get-tuple-element.95), channel_id=1, source_target_pairs={{0,4},{1,5},{2,6},{3,7},{4,0},{5,1},{6,2},{7,3},{8,12},{9,13},{10,... | collective-permute-start | bytes 786440 | tf_op jit(solution)/shard_map/ppermute | solution.py:524
  44.3 3.5 %collective-permute-start.11 = (bf16[2,784,512]{2,1,0:T(8,128)(2,1)S(1)}, bf16[2,784,512]{2,1,0:T(8,128)(2,1)S(1)}, u32[]{:S(2)}, u32[]{:S(2)}) collective-permute-start(bf16[2,784,512]{2,1,0:T(8,128)(2,1)S(1)} %back_kernel.5), channel_id=1, source_target_pairs={{0,1},{1,0},{2,3},{3,2},{4,5},{5,4},{6,7},{7,6},{8,9},{9,8},{10,11... | collective-permute-start | bytes 4816904 | tf_op jit(solution)/shard_map/ppermute | solution.py:524
  44.4 9.6 %collective-permute-start.12 = (bf16[2,512,128]{2,1,0:T(8,128)(2,1)S(1)}, bf16[2,512,128]{2,1,0:T(8,128)(2,1)S(1)}, u32[]{:S(2)}, u32[]{:S(2)}) collective-permute-start(bf16[2,512,128]{2,1,0:T(8,128)(2,1)S(1)} %get-tuple-element.103), channel_id=1, source_target_pairs={{0,18},{1,19},{2,16},{3,17},{4,22},{5,23},{6,20},{7,21},{8,26},{9,... | collective-permute-start | bytes 786440 | tf_op jit(solution)/shard_map/ppermute | solution.py:520
  46.4 1.4 %copy-start = (f32[16,49,512]{2,0,1:T(8,128)S(1)}, f32[16,49,512]{2,0,1:T(8,128)}, u32[]{:S(2)}) copy-start(f32[16,49,512]{2,0,1:T(8,128)} %param.15) | copy-start | bytes 4816900
  46.4 1.6 %copy-start.1 = (bf16[16,49,512]{2,0,1:T(8,128)(2,1)S(1)}, bf16[16,49,512]{2,0,1:T(8,128)(2,1)}, u32[]{:S(2)}) copy-start(bf16[16,49,512]{2,0,1:T(8,128)(2,1)} %param.16) | copy-start | bytes 2408452
  46.4 1.6 %copy-start.9 = (f32[7,512]{1,0:T(8,128)S(1)}, f32[7,512]{1,0:T(8,128)}, u32[]{:S(2)}) copy-start(f32[7,512]{1,0:T(8,128)} %refs_9_.1) | copy-start | bytes 43012
  46.4 8.4 %collective-permute-start.13 = (bf16[2,512,128]{2,1,0:T(8,128)(2,1)S(1)}, bf16[2,512,128]{2,1,0:T(8,128)(2,1)S(1)}, u32[]{:S(2)}, u32[]{:S(2)}) collective-permute-start(bf16[2,512,128]{2,1,0:T(8,128)(2,1)S(1)} %get-tuple-element.104), channel_id=1, source_target_pairs={{0,4},{1,5},{2,6},{3,7},{4,0},{5,1},{6,2},{7,3},{8,12},{9,13},{10,... | collective-permute-start | bytes 786440 | tf_op jit(solution)/shard_map/ppermute | solution.py:524
  54.9 24.5 %copy-start.2 = (f32[512,128]{1,0:T(8,128)S(1)}, f32[512,128]{1,0:T(8,128)}, u32[]{:S(2)}) copy-start(f32[512,128]{1,0:T(8,128)} %refs_0_.1) | copy-start | bytes 786436
  54.9 24.5 %copy-start.3 = (f32[128,512]{1,0:T(8,128)S(1)}, f32[128,512]{1,0:T(8,128)}, u32[]{:S(2)}) copy-start(f32[128,512]{1,0:T(8,128)} %refs_6_.1) | copy-start | bytes 786436
  54.9 24.5 %copy-start.4 = (f32[512,128]{1,0:T(8,128)S(1)}, f32[512,128]{1,0:T(8,128)}, u32[]{:S(2)}) copy-start(f32[512,128]{1,0:T(8,128)} %refs_1_.1) | copy-start | bytes 786436
  54.9 24.5 %copy-start.5 = (f32[512,128]{1,0:T(8,128)S(1)}, f32[512,128]{1,0:T(8,128)}, u32[]{:S(2)}) copy-start(f32[512,128]{1,0:T(8,128)} %refs_2_.1) | copy-start | bytes 786436
  54.9 24.5 %copy-start.6 = (f32[128,512]{1,0:T(8,128)S(1)}, f32[128,512]{1,0:T(8,128)}, u32[]{:S(2)}) copy-start(f32[128,512]{1,0:T(8,128)} %refs_7_.1) | copy-start | bytes 786436
  55.0 24.5 %copy-start.7 = (f32[128,512]{1,0:T(8,128)S(1)}, f32[128,512]{1,0:T(8,128)}, u32[]{:S(2)}) copy-start(f32[128,512]{1,0:T(8,128)} %refs_8_.1) | copy-start | bytes 786436
  55.0 24.5 %copy-start.10 = (f32[7,512]{1,0:T(8,128)S(1)}, f32[7,512]{1,0:T(8,128)}, u32[]{:S(2)}) copy-start(f32[7,512]{1,0:T(8,128)} %refs_10_.1) | copy-start | bytes 43012
  55.0 24.5 %copy-start.11 = (f32[7,512]{1,0:T(8,128)S(1)}, f32[7,512]{1,0:T(8,128)}, u32[]{:S(2)}) copy-start(f32[7,512]{1,0:T(8,128)} %refs_11_.1) | copy-start | bytes 43012
  55.0 24.5 %copy-start.12 = (f32[2048]{0:T(1024)S(1)}, f32[2048]{0:T(1024)}, u32[]{:S(2)}) copy-start(f32[2048]{0:T(1024)} %param.24) | copy-start | bytes 24580
  55.0 24.5 %copy-start.13 = (f32[2048]{0:T(1024)S(1)}, f32[2048]{0:T(1024)}, u32[]{:S(2)}) copy-start(f32[2048]{0:T(1024)} %param.25) | copy-start | bytes 24580
  55.1 11.0 %collective-permute-start.14 = (bf16[2,512,128]{2,1,0:T(8,128)(2,1)S(1)}, bf16[2,512,128]{2,1,0:T(8,128)(2,1)S(1)}, u32[]{:S(2)}, u32[]{:S(2)}) collective-permute-start(bf16[2,512,128]{2,1,0:T(8,128)(2,1)S(1)} %add_convert_fusion.2), channel_id=1, source_target_pairs={{0,2},{1,3},{2,0},{3,1},{4,6},{5,7},{6,4},{7,5},{8,10},{9,11},{10,... | collective-permute-start | bytes 786440 | tf_op jit(solution)/shard_map/ppermute | solution.py:524
  56.7 13.8 %collective-permute-start.15 = (bf16[2,512,128]{2,1,0:T(8,128)(2,1)S(1)}, bf16[2,512,128]{2,1,0:T(8,128)(2,1)S(1)}, u32[]{:S(2)}, u32[]{:S(2)}) collective-permute-start(bf16[2,512,128]{2,1,0:T(8,128)(2,1)S(1)} %add_convert_fusion.1), channel_id=1, source_target_pairs={{0,8},{1,9},{2,10},{3,11},{4,12},{5,13},{6,14},{7,15},{8,0},{9,1},... | collective-permute-start | bytes 786440 | tf_op jit(solution)/shard_map/ppermute | solution.py:520
  57.2 1.2 %collective-permute-start.16 = (f32[44,128]{1,0:T(8,128)S(1)}, f32[44,128]{1,0:T(8,128)S(1)}, u32[]{:S(2)}, u32[]{:S(2)}) collective-permute-start(f32[44,128]{1,0:T(8,128)S(1)} %get-tuple-element.105), channel_id=1, source_target_pairs={{0,1},{1,0},{2,3},{3,2},{4,5},{5,4},{6,7},{7,6},{8,9},{9,8},{10,11... | collective-permute-start | bytes 67592 | tf_op jit(solution)/shard_map/ppermute | solution.py:524
  58.4 3.8 %collective-permute-start.17 = (f32[44,128]{1,0:T(8,128)S(1)}, f32[44,128]{1,0:T(8,128)S(1)}, u32[]{:S(2)}, u32[]{:S(2)}) collective-permute-start(f32[44,128]{1,0:T(8,128)S(1)} %add.43), channel_id=1, source_target_pairs={{0,16},{16,0},{1,17},{17,1},{2,18},{18,2},{3,19},{19,3},{4,20},{20... | collective-permute-start | bytes 67592 | tf_op jit(solution)/shard_map/ppermute | solution.py:532
  62.3 3.8 %collective-permute-start.18 = (f32[44,128]{1,0:T(8,128)S(1)}, f32[44,128]{1,0:T(8,128)S(1)}, u32[]{:S(2)}, u32[]{:S(2)}) collective-permute-start(f32[44,128]{1,0:T(8,128)S(1)} %add.44), channel_id=1, source_target_pairs={{0,2},{1,3},{2,0},{3,1},{4,6},{5,7},{6,4},{7,5},{8,10},{9,11},{10,... | collective-permute-start | bytes 67592 | tf_op jit(solution)/shard_map/ppermute | solution.py:524
  70.6 8.7 %collective-permute-start.19 = (bf16[2,512,128]{2,1,0:T(8,128)(2,1)S(1)}, bf16[2,512,128]{2,1,0:T(8,128)(2,1)S(1)}, u32[]{:S(2)}, u32[]{:S(2)}) collective-permute-start(bf16[2,512,128]{2,1,0:T(8,128)(2,1)S(1)} %add_convert_fusion.own_ref), channel_id=1, source_target_pairs={{0,16},{16,0},{1,17},{17,1},{2,18},{18,2},{3,19},{19,3},{4,20},{20... | collective-permute-start | bytes 786440 | tf_op jit(solution)/shard_map/ppermute | solution.py:532
  70.7 3.9 %collective-permute-start.20 = (f32[44,128]{1,0:T(8,128)S(1)}, f32[44,128]{1,0:T(8,128)S(1)}, u32[]{:S(2)}, u32[]{:S(2)}) collective-permute-start(f32[44,128]{1,0:T(8,128)S(1)} %add.45), channel_id=1, source_target_pairs={{0,4},{1,5},{2,6},{3,7},{4,0},{5,1},{6,2},{7,3},{8,12},{9,13},{10,... | collective-permute-start | bytes 67592 | tf_op jit(solution)/shard_map/ppermute | solution.py:524
  74.6 4.7 %collective-permute-start.21 = (f32[44,128]{1,0:T(8,128)S(1)}, f32[44,128]{1,0:T(8,128)S(1)}, u32[]{:S(2)}, u32[]{:S(2)}) collective-permute-start(f32[44,128]{1,0:T(8,128)S(1)} %add.46), channel_id=1, source_target_pairs={{0,8},{1,9},{2,10},{3,11},{4,12},{5,13},{6,14},{7,15},{8,0},{9,1},... | collective-permute-start | bytes 67592 | tf_op jit(solution)/shard_map/ppermute | solution.py:524

commit v7 on v6

--- a/solution.py
+++ b/solution.py
@@ -260,8 +260,12 @@
     return lax.dot_general(left, right, (dims, ((), ())), preferred_element_type=f32)
 
 
-def joined(refs, i):
-    return jnp.concatenate([refs[0][i], refs[1][i]], axis=1)
+def joined(refs):
+    chunks = [[ref[1, c * 128 : (c + 1) * 128, :] for c in range(4)] for ref in refs]
+    return (
+        jnp.concatenate([ref[0] for ref in refs], axis=1),
+        jnp.concatenate([jnp.concatenate(row, axis=1) for row in chunks], axis=0),
+    )
 
 
 def block_places():
@@ -277,18 +281,18 @@
 
 def block_rows(second, upstream, a, b, bias):
     h = dot(second, a, ((1,), (0,))) + bias
-    back = dot(upstream, b, ((1,), (0,)))
+    back = dot(upstream, b, ((1,), (1,)))
     phi, slope = normal_parts(h)
     active = (h * phi).astype(bf16)
     low = (back * slope).astype(bf16)
     column = jnp.sum(low.astype(f32), axis=0, keepdims=True)
-    grads = [dot(left, right, ((0,), (0,))) for left, right in ((second, low), (upstream, active))]
+    grads = [dot(left, right, ((0,), (0,))) for left, right in ((second, low), (active, upstream))]
     return active, low, column, grads
 
 
 def pre_kernel(
     counts_ref, x_ref, cot_ref, vec_ref, bias_ref, w0_ref, w1_ref,
-    sb_ref, stat_ref, act_ref, low_ref, column_ref, part_ref, d_ref, h_ref,
+    sb_ref, stat_ref, act_ref, low_ref, column_ref, part_a, part_b, d_ref, h_ref,
 ):
     pixels, images, width = x_ref.shape
     size = pixels * width
@@ -333,11 +337,10 @@
     for i, stat in enumerate((mu1, r1, mu2, r2)):
         stat_ref[i] = jnp.broadcast_to(stat, (images, 128))
     second, upstream = (sb_ref[i].reshape(pixels * images, width) for i in range(2))
-    a, b = (joined((w0_ref, w1_ref), i) for i in range(2))
+    a, b = joined((w0_ref, w1_ref))
     bias = block_bias(bias_ref, block_places(), 0)
     act_ref[...], low_ref[...], column_ref[...], grads = block_rows(second, upstream, a, b, bias)
-    for i, grad in enumerate(grads):
-        part_ref[i] = grad
+    part_a[...], part_b[...] = grads
 
 
 def side_by_side(refs, j):
@@ -347,34 +350,39 @@
 
 def cast_kernel(a_ref, b_ref, out_ref):
     out_ref[0] = a_ref[...].astype(bf16)
-    out_ref[1] = b_ref[...].T.astype(bf16)
+    low = b_ref[...].astype(bf16)
+    for c in range(4):
+        out_ref[1, c * 128 : (c + 1) * 128, :] = low[:, c * 128 : (c + 1) * 128]
 
 
 def block_kernel(first, count, own_ref, oth_ref, bias_ref, *refs):
     w_refs, refs = refs[:count], refs[count:]
-    begun, refs = (refs[:4], refs[4:]) if first == 0 else (None, refs)
+    begun, refs = (refs[:5], refs[5:]) if first == 0 else (None, refs)
     act_ref, low_ref, sums_ref, *outs = refs
     sums_ref[...] = jnp.zeros_like(sums_ref)
     places = block_places()
     for j in range(count // 2):
         bias = block_bias(bias_ref, places, first + 2 * j)
-        a, b = (joined(w_refs[2 * j : 2 * j + 2], i) for i in range(2))
+        a, b = joined(w_refs[2 * j : 2 * j + 2])
         columns = slice(j * 256, (j + 1) * 256)
         grads = sums = None
         for r, sb_ref in enumerate((own_ref, oth_ref)):
             if begun is not None and j == r == 0:
-                active, low, column, parts = begun[0][...], begun[1][...], begun[2][...], begun[3]
+                active, low, column, *parts = (ref[...] for ref in begun)
             else:
                 active, low, column, parts = block_rows(sb_ref[0], sb_ref[1], a, b, bias)
             act_ref[r, :, columns] = active
             low_ref[r, :, columns] = low
             sums = column if r == 0 else sums + column
-            grads = [parts[0], parts[1]] if r == 0 else [total + part for total, part in zip(grads, parts)]
+            grads = parts if r == 0 else [total + part for total, part in zip(grads, parts)]
         for k in range(2):
             half = slice(k * 128, (k + 1) * 128)
             sums_ref[pl.ds(places[first + 2 * j + k], 1), :] = sums[:, half]
-            for i, grad in enumerate(grads):
-                outs[2 * j + k][i] = grad[:, half].astype(outs[2 * j + k].dtype)
+            out_ref = outs[2 * j + k]
+            out_ref[0] = grads[0][:, half].astype(out_ref.dtype)
+            for c in range(4):
+                chunk = slice(c * 128, (c + 1) * 128)
+                out_ref[1, chunk, :] = grads[1][half, chunk].astype(out_ref.dtype)
 
 
 def back_kernel(sides, counts, started, *refs):
@@ -389,7 +397,8 @@
             for left_ref in lefts:
                 for j in range(left_ref.shape[2] // 256):
                     left = left_ref[r, :, j * 256 : (j + 1) * 256]
-                    part = dot(left, joined(w_refs[w : w + 2], 1 - i), ((1,), (1,)))
+                    weight = joined(w_refs[w : w + 2])[1 - i]
+                    part = dot(left, weight, ((1,), (i,)))
                     total = part if total is None else total + part
                     w += 2
             totals[at][i] = total.astype(totals[at].dtype)
@@ -406,7 +415,7 @@
     settings = (
         (grads[0], 0.04, weight_shrink),
         (sums_ref[:lines, :], 0.2, 0.0),
-        (grads[1].T, 0.02, weight_shrink),
+        (jnp.concatenate([grads[1, c * 128 : (c + 1) * 128, :] for c in range(4)], axis=1), 0.02, weight_shrink),
         (jnp.concatenate(wide, axis=0), 0.3, 0.0),
     )
     for n, (grad, rate, shrink) in enumerate(settings):
@@ -585,7 +594,8 @@
             tile,
             tile,
             struct((1, 256)),
-            struct((2, width, 256)),
+            struct((width, 256)),
+            struct((256, width)),
         ],
         (counts, x, cot, vectors_late, bias, w0, wy0),
         [keep, keep],
@@ -644,10 +654,10 @@
     )
     ds, zy, _ = lax.optimization_barrier((ds, zy, sums))
     sum_f = wide_sum(gzf, xs, yf, ds).astype(bf16)
-    y0 = flip(after(wide_sum(gy0, zy).astype(bf16), sum_f), 2)
     zf = far(sum_f)
     sums = sums + flip(sums, 1)
     sums = after(sums, sum_f)
+    y0 = flip(after(wide_sum(gy0, zy).astype(bf16), sums), 2)
     sums = sums + across(sums)
     sums = sums + flip(sums, 2)
     own = wide_sum(g0, y0, z1, zf).astype(bf16)

time: 81.5 us -> 80 us (0.982)
  waiting for transfers between devices: 24.8 us -> 21.8 us
  starting transfers between devices: 24.3 us -> 25.9 us
    ppermute x14, waiting for transfers between devices: 15.2 us -> 12.4 us  [flip(): return lax.ppermute(values, 'wide', [(w, w ^ bit) for w in range(16)])]
    ppermute x14, starting transfers between devices: 13.4 us -> 14.6 us  [flip(): return lax.ppermute(values, 'wide', [(w, w ^ bit) for w in range(16)])]
  transfers between devices with their start and end apart: 22 -> 22, of which waited for: 14 -> 12; matrix products, arithmetic and copies ran while one was open for 0% -> 0% of each run, Pallas kernels for 32% -> 33%
where the time goes in v7:
time: 80 us; the launch traced here: 79.7 us
  Pallas kernels  29 us (36%)
  starting transfers between devices  25.9 us (32%)
  waiting for transfers between devices  21.8 us (27%)
  between operations  1.62 us (2%)
  local copies, waits for them, and re-layouts  0.98 us (1%)
    pallas_call x10, Pallas kernels, call(): pl.pallas_call(kernel, out_shape=outs, in_specs=[SMEM] * smem + [VMEM] *...  29 us
    ppermute x14, starting transfers between devices, flip(): return lax.ppermute(values, 'wide', [(w, w ^ bit) for w in range(16)])  14.6 us
    ppermute x14, waiting for transfers between devices, flip(): return lax.ppermute(values, 'wide', [(w, w ^ bit) for w in range(16)])  12.4 us
    ppermute x3, waiting for transfers between devices, joint(): return lax.ppermute(values, BOTH, [(s, n * 16 + w) for s, (n, w) in pairs])  6.64 us
    ppermute x3, starting transfers between devices, joint(): return lax.ppermute(values, BOTH, [(s, n * 16 + w) for s, (n, w) in pairs])  5.74 us
    ppermute x5, starting transfers between devices, across(): return lax.ppermute(values, 'narrow', [(0, 1), (1, 0)])  5.6 us
    ppermute x5, waiting for transfers between devices, across(): return lax.ppermute(values, 'narrow', [(0, 1), (1, 0)])  2.79 us
  transfers between devices with their start and end apart: 22, of which 12 were waited for; matrix products, arithmetic and copies ran while one was open for 0% of the time, Pallas kernels for 33%

profile of v7, /device:TPU:0, one launch (start us, length us, event | category | flops | bytes accessed | tf_op | source)
XLA Modules:
  0.0 79.7 jit_solution(17306120189960891213)
XLA Ops:
  0.6 1.1 %cast_kernel.1.w0_ref.refs_0_.refs_4_ = bf16[2,512,128]{2,1,0:T(8,128)(2,1)S(1)} custom-call(f32[512,128]{1,0:T(8,128)} %refs_0_.1, f32[128,512]{1,0:T(8,128)} %refs_6_.1), custom_call_target="tpu_custom_call" | custom-call | bytes 786432 | tf_op jit(solution)/shard_map/cast_kernel/pallas_call | solution.py:508
  1.7 3.0 %collective-permute-start = (bf16[2,512,128]{2,1,0:T(8,128)(2,1)S(1)}, bf16[2,512,128]{2,1,0:T(8,128)(2,1)S(1)}, u32[]{:S(2)}, u32[]{:S(2)}) collective-permute-start(bf16[2,512,128]{2,1,0:T(8,128)(2,1)S(1)} %cast_kernel.1.w0_ref.refs_0_.refs_4_), channel_id=1, source_target_pairs={{0,2},{1,3},{2,0},{3,1},{4,6},{5,7},{6,4},{7,5},{8,10},{9,11},{10,... | collective-permute-start | bytes 786440 | tf_op jit(solution)/shard_map/ppermute | solution.py:533
  4.7 2.6 %collective-permute-start.1 = (bf16[2,512,128]{2,1,0:T(8,128)(2,1)S(1)}, bf16[2,512,128]{2,1,0:T(8,128)(2,1)S(1)}, u32[]{:S(2)}, u32[]{:S(2)}) collective-permute-start(bf16[2,512,128]{2,1,0:T(8,128)(2,1)S(1)} %cast_kernel.1.w0_ref.refs_0_.refs_4_), channel_id=1, source_target_pairs={{0,8},{1,9},{2,10},{3,11},{4,12},{5,13},{6,14},{7,15},{8,0},{9,1},... | collective-permute-start | bytes 786440 | tf_op jit(solution)/shard_map/ppermute | solution.py:529
  7.3 1.6 %collective-permute-start.2 = (bf16[2,512,128]{2,1,0:T(8,128)(2,1)S(1)}, bf16[2,512,128]{2,1,0:T(8,128)(2,1)S(1)}, u32[]{:S(2)}, u32[]{:S(2)}) collective-permute-start(bf16[2,512,128]{2,1,0:T(8,128)(2,1)S(1)} %cast_kernel.1.w0_ref.refs_0_.refs_4_), channel_id=1, source_target_pairs={{0,4},{1,5},{2,6},{3,7},{4,0},{5,1},{6,2},{7,3},{8,12},{9,13},{10,... | collective-permute-start | bytes 786440 | tf_op jit(solution)/shard_map/ppermute | solution.py:533
  9.6 1.5 %collective-permute-done.w1_ref.refs_1_.refs_5_ = bf16[2,512,128]{2,1,0:T(8,128)(2,1)S(1)} collective-permute-done((bf16[2,512,128]{2,1,0:T(8,128)(2,1)S(1)}, bf16[2,512,128]{2,1,0:T(8,128)(2,1)S(1)}, u32[]{:S(2)}, u32[]{:S(2)}) %collective-permute-start) | collective-permute-done | bytes 262176 | tf_op jit(solution)/shard_map/ppermute | solution.py:533
  11.0 0.7 copy-done.8
  11.7 5.2 %pre_kernel.1 = (bf16[2,49,16,512]{3,2,1,0:T(8,128)(2,1)S(1)}, f32[4,16,128]{2,1,0:T(8,128)S(1)}, bf16[784,256]{1,0:T(8,128)(2,1)S(1)}, bf16[784,256]{1,0:T(8,12...) custom-call(s32[1]{0:T(128)S(6)} %copy.29.counts_ref, f32[49,16,512]{2,1,0:T(8,128)} %bitcast.18, ...), custom_call_target="tpu_custom_call" | custom-call | bytes 6446084 | tf_op jit(solution)/shard_map/pre_kernel/pallas_call | solution.py:508
  16.9 2.2 %collective-permute-done.1.refs_3_.refs_7_ = bf16[2,512,128]{2,1,0:T(8,128)(2,1)S(1)} collective-permute-done((bf16[2,512,128]{2,1,0:T(8,128)(2,1)S(1)}, bf16[2,512,128]{2,1,0:T(8,128)(2,1)S(1)}, u32[]{:S(2)}, u32[]{:S(2)}) %collective-permute-start.1) | collective-permute-done | bytes 262176 | tf_op jit(solution)/shard_map/ppermute | solution.py:529
  19.1 0.2 collective-permute-done.2.refs_2_.refs_6_
  19.3 0.5 collective-permute-start.4
  19.8 2.3 %collective-permute-start.7 = (bf16[2,512,128]{2,1,0:T(8,128)(2,1)S(1)}, bf16[2,512,128]{2,1,0:T(8,128)(2,1)S(1)}, u32[]{:S(2)}, u32[]{:S(2)}) collective-permute-start(bf16[2,512,128]{2,1,0:T(8,128)(2,1)S(1)} %collective-permute-done.1.refs_3_.refs_7_), channel_id=1, source_target_pairs={{0,16},{16,0},{1,17},{17,1},{2,18},{18,2},{3,19},{19,3},{4,20},{20... | collective-permute-start | bytes 786440 | tf_op jit(solution)/shard_map/ppermute | solution.py:541
  22.1 0.7 collective-permute-done.3.oth_ref
  22.8 5.0 %block_kernel.3 = (bf16[2,784,512]{2,1,0:T(8,128)(2,1)S(1)}, bf16[2,784,512]{2,1,0:T(8,128)(2,1)S(1)}, f32[16,128]{1,0:T(8,128)S(1)}, f32[2,512,128]{2,1,0:T(8,1...) custom-call(bf16[2,784,512]{2,1,0:T(8,128)(2,1)S(1)} %bitcast.14, ...), custom_call_target="tpu_custom_call" | custom-call | bytes 10912768 | tf_op jit(solution)/shard_map/block_kernel/pallas_call | solution.py:508
  27.7 0.3 collective-permute-done.4.refs_0_.refs_8_
  28.0 0.6 collective-permute-start.6
  28.7 2.1 %collective-permute-start.5 = (bf16[2,512,128]{2,1,0:T(8,128)(2,1)S(1)}, bf16[2,512,128]{2,1,0:T(8,128)(2,1)S(1)}, u32[]{:S(2)}, u32[]{:S(2)}) collective-permute-start(bf16[2,512,128]{2,1,0:T(8,128)(2,1)S(1)} %collective-permute-done.4.refs_0_.refs_8_), channel_id=1, source_target_pairs={{0,16},{16,0},{1,17},{17,1},{2,18},{18,2},{3,19},{19,3},{4,20},{20... | collective-permute-start | bytes 786440 | tf_op jit(solution)/shard_map/ppermute | solution.py:541
  30.8 0.0 collective-permute-done.7.refs_1_.refs_9_
  30.8 3.2 %block_kernel.4 = (bf16[2,784,256]{2,1,0:T(8,128)(2,1)S(1)}, bf16[2,784,256]{2,1,0:T(8,128)(2,1)S(1)}, f32[16,128]{1,0:T(8,128)S(1)}, bf16[2,512,128]{2,1,0:T(8,128)(2,1)S(1)}, bf16[2,512,128]{2,1,0:T(8,128)(2,1)S(1)}) custom-call(bf16[2,784,512]{2,1,0:T(8,128)(2,1)S(1)} %bitcast.15, bf16[2,784,512]{2,1,0:T(8,128)(2,1)S(1)} %collective-permute-done.3.oth_ref, ...), custom_call_target="tpu_custom_call" | custom-call | bytes 5881856 | tf_op jit(solution)/shard_map/block_kernel/pallas_call | solution.py:508
  34.1 1.6 %collective-permute-start.8 = (bf16[2,512,128]{2,1,0:T(8,128)(2,1)S(1)}, bf16[2,512,128]{2,1,0:T(8,128)(2,1)S(1)}, u32[]{:S(2)}, u32[]{:S(2)}) collective-permute-start(bf16[2,512,128]{2,1,0:T(8,128)(2,1)S(1)} %get-tuple-element.95), channel_id=1, source_target_pairs={{0,2},{1,3},{2,0},{3,1},{4,6},{5,7},{6,4},{7,5},{8,10},{9,11},{10,... | collective-permute-start | bytes 786440 | tf_op jit(solution)/shard_map/ppermute | solution.py:533
  35.6 0.0 collective-permute-start.9
  35.7 1.7 %collective-permute-start.10 = (bf16[2,512,128]{2,1,0:T(8,128)(2,1)S(1)}, bf16[2,512,128]{2,1,0:T(8,128)(2,1)S(1)}, u32[]{:S(2)}, u32[]{:S(2)}) collective-permute-start(bf16[2,512,128]{2,1,0:T(8,128)(2,1)S(1)} %get-tuple-element.97), channel_id=1, source_target_pairs={{0,4},{1,5},{2,6},{3,7},{4,0},{5,1},{6,2},{7,3},{8,12},{9,13},{10,... | collective-permute-start | bytes 786440 | tf_op jit(solution)/shard_map/ppermute | solution.py:533
  37.3 2.6 %back_kernel.3 = (f32[2,784,512]{2,1,0:T(8,128)S(1)}, f32[2,784,512]{2,1,0:T(8,128)S(1)}) custom-call(bf16[2,784,512]{2,1,0:T(8,128)(2,1)S(1)} %get-tuple-element.85.refs_0_, bf16[2,784,256]{2,1,0:T(8,128)(2,1)S(1)} %get-tuple-element.86.refs_1_, bf16[2,784,512]{2,1,0:T(8,128)(2,1)S(1)} %get-tuple-element.87.refs_2_, ...), custom_call_target="tpu_custom_call" | custom-call | bytes 12812288 | tf_op jit(solution)/shard_map/back_kernel/pallas_call | solution.py:508
  40.0 0.0 collective-permute-done.5.refs_0_.refs_2_
  40.0 3.4 %block_kernel.5 = (bf16[2,784,256]{2,1,0:T(8,128)(2,1)S(1)}, bf16[2,784,256]{2,1,0:T(8,128)(2,1)S(1)}, f32[16,128]{1,0:T(8,128)S(1)}, bf16[2,512,128]{2,1,0:T(8,128)(2,1)S(1)}, bf16[2,512,128]{2,1,0:T(8,128)(2,1)S(1)}) custom-call(bf16[2,784,512]{2,1,0:T(8,128)(2,1)S(1)} %bitcast.16, bf16[2,784,512]{2,1,0:T(8,128)(2,1)S(1)} %collective-permute-done.3.oth_ref, ...), custom_call_target="tpu_custom_call" | custom-call | bytes 5881856 | tf_op jit(solution)/shard_map/block_kernel/pallas_call | solution.py:508
  43.5 0.6 back_kernel.5
  44.1 0.0 collective-permute-done.9
  44.1 0.0 collective-permute-done.10
  44.1 0.1 collective-permute-start.11
  44.2 2.0 %collective-permute-start.12 = (bf16[2,512,128]{2,1,0:T(8,128)(2,1)S(1)}, bf16[2,512,128]{2,1,0:T(8,128)(2,1)S(1)}, u32[]{:S(2)}, u32[]{:S(2)}) collective-permute-start(bf16[2,512,128]{2,1,0:T(8,128)(2,1)S(1)} %get-tuple-element.105), channel_id=1, source_target_pairs={{0,18},{1,19},{2,16},{3,17},{4,22},{5,23},{6,20},{7,21},{8,26},{9,... | collective-permute-start | bytes 786440 | tf_op jit(solution)/shard_map/ppermute | solution.py:529
  46.3 0.7 collective-permute-start.13
  47.0 0.6 back_kernel.4
  47.5 0.1 collective-permute-done.11
  47.7 0.0 copy-done
  47.7 0.2 copy-done.1
  47.9 5.8 %post_kernel.1 = (f32[49,16,512]{2,1,0:T(8,128)}, f32[49,16,512]{2,1,0:T(8,128)}, f32[44,128]{1,0:T(8,128)S(1)}) custom-call(s32[1]{0:T(128)S(6)} %copy.29.counts_ref, f32[49,16,512]{2,1,0:T(8,128)S(1)} %bitcast.19, bf16[49,16,512]{2,1,0:T(8,128)(2,1)S(1)} %bitcast.21, f32[7,512]{1,0:T(8,128)S(1)} %copy-done.10, ...), custom_call_target="tpu_custom_call" | custom-call | bytes 10530820 | tf_op jit(solution)/shard_map/post_kernel/pallas_call | solution.py:508
  53.7 0.2 collective-permute-start.14
  53.8 0.0 collective-permute-done.12
  53.8 0.8 %collective-permute-done.13 = bf16[2,512,128]{2,1,0:T(8,128)(2,1)S(1)} collective-permute-done((bf16[2,512,128]{2,1,0:T(8,128)(2,1)S(1)}, bf16[2,512,128]{2,1,0:T(8,128)(2,1)S(1)}, u32[]{:S(2)}, u32[]{:S(2)}) %collective-permute-start.13) | collective-permute-done | bytes 262176 | tf_op jit(solution)/shard_map/ppermute | solution.py:533
  54.6 0.1 add_convert_fusion.1
  54.8 0.0 copy-start.2
  54.8 0.0 copy-start.3
  54.8 0.0 copy-start.4
  54.8 0.0 copy-start.5
  54.8 0.0 copy-start.6
  54.8 0.0 copy-start.7
  54.9 0.0 copy-start.11
  54.9 0.0 copy-start.12
  54.9 0.0 copy-start.13
  54.9 0.0 copy-start.14
  54.9 1.1 %collective-permute-start.16 = (bf16[2,512,128]{2,1,0:T(8,128)(2,1)S(1)}, bf16[2,512,128]{2,1,0:T(8,128)(2,1)S(1)}, u32[]{:S(2)}, u32[]{:S(2)}) collective-permute-start(bf16[2,512,128]{2,1,0:T(8,128)(2,1)S(1)} %add_convert_fusion.1), channel_id=1, source_target_pairs={{0,8},{1,9},{2,10},{3,11},{4,12},{5,13},{6,14},{7,15},{8,0},{9,1},... | collective-permute-start | bytes 786440 | tf_op jit(solution)/shard_map/ppermute | solution.py:529
  56.0 0.1 add_convert_fusion.2
  56.1 1.0 %collective-permute-start.15 = (bf16[2,512,128]{2,1,0:T(8,128)(2,1)S(1)}, bf16[2,512,128]{2,1,0:T(8,128)(2,1)S(1)}, u32[]{:S(2)}, u32[]{:S(2)}) collective-permute-start(bf16[2,512,128]{2,1,0:T(8,128)(2,1)S(1)} %add_convert_fusion.2), channel_id=1, source_target_pairs={{0,2},{1,3},{2,0},{3,1},{4,6},{5,7},{6,4},{7,5},{8,10},{9,11},{10,... | collective-permute-start | bytes 786440 | tf_op jit(solution)/shard_map/ppermute | solution.py:533
  57.2 1.0 %collective-permute-start.17 = (f32[44,128]{1,0:T(8,128)S(1)}, f32[44,128]{1,0:T(8,128)S(1)}, u32[]{:S(2)}, u32[]{:S(2)}) collective-permute-start(f32[44,128]{1,0:T(8,128)S(1)} %add.37), channel_id=1, source_target_pairs={{0,16},{16,0},{1,17},{17,1},{2,18},{18,2},{3,19},{19,3},{4,20},{20... | collective-permute-start | bytes 67592 | tf_op jit(solution)/shard_map/ppermute | solution.py:541
  58.2 2.8 %collective-permute-done.17 = f32[44,128]{1,0:T(8,128)S(1)} collective-permute-done((f32[44,128]{1,0:T(8,128)S(1)}, f32[44,128]{1,0:T(8,128)S(1)}, u32[]{:S(2)}, u32[]{:S(2)}) %collective-permute-start.17) | collective-permute-done | bytes 22560 | tf_op jit(solution)/shard_map/ppermute | solution.py:541
  61.0 1.0 %collective-permute-start.18 = (f32[44,128]{1,0:T(8,128)S(1)}, f32[44,128]{1,0:T(8,128)S(1)}, u32[]{:S(2)}, u32[]{:S(2)}) collective-permute-start(f32[44,128]{1,0:T(8,128)S(1)} %add.44), channel_id=1, source_target_pairs={{0,2},{1,3},{2,0},{3,1},{4,6},{5,7},{6,4},{7,5},{8,10},{9,11},{10,... | collective-permute-start | bytes 67592 | tf_op jit(solution)/shard_map/ppermute | solution.py:533
  62.0 2.8 %collective-permute-done.18 = f32[44,128]{1,0:T(8,128)S(1)} collective-permute-done((f32[44,128]{1,0:T(8,128)S(1)}, f32[44,128]{1,0:T(8,128)S(1)}, u32[]{:S(2)}, u32[]{:S(2)}) %collective-permute-start.18) | collective-permute-done | bytes 22560 | tf_op jit(solution)/shard_map/ppermute | solution.py:533
  64.8 4.4 %collective-permute-done.16 = bf16[2,512,128]{2,1,0:T(8,128)(2,1)S(1)} collective-permute-done((bf16[2,512,128]{2,1,0:T(8,128)(2,1)S(1)}, bf16[2,512,128]{2,1,0:T(8,128)(2,1)S(1)}, u32[]{:S(2)}, u32[]{:S(2)}) %collective-permute-start.16) | collective-permute-done | bytes 262176 | tf_op jit(solution)/shard_map/ppermute | solution.py:529
  69.2 0.1 add_convert_fusion.own_ref
  69.4 0.1 collective-permute-start.19
  69.5 1.3 %collective-permute-start.20 = (f32[44,128]{1,0:T(8,128)S(1)}, f32[44,128]{1,0:T(8,128)S(1)}, u32[]{:S(2)}, u32[]{:S(2)}) collective-permute-start(f32[44,128]{1,0:T(8,128)S(1)} %add.45), channel_id=1, source_target_pairs={{0,4},{1,5},{2,6},{3,7},{4,0},{5,1},{6,2},{7,3},{8,12},{9,13},{10,... | collective-permute-start | bytes 67592 | tf_op jit(solution)/shard_map/ppermute | solution.py:533
  70.7 2.6 %collective-permute-done.20 = f32[44,128]{1,0:T(8,128)S(1)} collective-permute-done((f32[44,128]{1,0:T(8,128)S(1)}, f32[44,128]{1,0:T(8,128)S(1)}, u32[]{:S(2)}, u32[]{:S(2)}) %collective-permute-start.20) | collective-permute-done | bytes 22560 | tf_op jit(solution)/shard_map/ppermute | solution.py:533
  73.4 1.4 %collective-permute-start.21 = (f32[44,128]{1,0:T(8,128)S(1)}, f32[44,128]{1,0:T(8,128)S(1)}, u32[]{:S(2)}, u32[]{:S(2)}) collective-permute-start(f32[44,128]{1,0:T(8,128)S(1)} %add.46), channel_id=1, source_target_pairs={{0,8},{1,9},{2,10},{3,11},{4,12},{5,13},{6,14},{7,15},{8,0},{9,1},... | collective-permute-start | bytes 67592 | tf_op jit(solution)/shard_map/ppermute | solution.py:533
  74.7 3.4 %collective-permute-done.21 = f32[44,128]{1,0:T(8,128)S(1)} collective-permute-done((f32[44,128]{1,0:T(8,128)S(1)}, f32[44,128]{1,0:T(8,128)S(1)}, u32[]{:S(2)}, u32[]{:S(2)}) %collective-permute-start.21) | collective-permute-done | bytes 22560 | tf_op jit(solution)/shard_map/ppermute | solution.py:533
  78.2 1.5 %update_kernel.1 = (f32[512,128]{1,0:T(8,128)}, f32[512,128]{1,0:T(8,128)}, f32[512,128]{1,0:T(8,128)}, f32[16,128]{1,0:T(8,128)}, f32[16,128]{1,0:T(8,128)}, /*...) custom-call(bf16[2,512,128]{2,1,0:T(8,128)(2,1)S(1)} %add_convert_fu, ...), custom_call_target="tpu_custom_call" | custom-call | bytes 3827712 | tf_op jit(solution)/shard_map/update_kernel/pallas_call | solution.py:508
  (28 shorter events, 0.1 us)
Async XLA Ops:
  1.7 9.3 %collective-permute-start = (bf16[2,512,128]{2,1,0:T(8,128)(2,1)S(1)}, bf16[2,512,128]{2,1,0:T(8,128)(2,1)S(1)}, u32[]{:S(2)}, u32[]{:S(2)}) collective-permute-start(bf16[2,512,128]{2,1,0:T(8,128)(2,1)S(1)} %cast_kernel.1.w0_ref.refs_0_.refs_4_), channel_id=1, source_target_pairs={{0,2},{1,3},{2,0},{3,1},{4,6},{5,7},{6,4},{7,5},{8,10},{9,11},{10,... | collective-permute-start | bytes 786440 | tf_op jit(solution)/shard_map/ppermute | solution.py:533
  4.7 14.4 %collective-permute-start.1 = (bf16[2,512,128]{2,1,0:T(8,128)(2,1)S(1)}, bf16[2,512,128]{2,1,0:T(8,128)(2,1)S(1)}, u32[]{:S(2)}, u32[]{:S(2)}) collective-permute-start(bf16[2,512,128]{2,1,0:T(8,128)(2,1)S(1)} %cast_kernel.1.w0_ref.refs_0_.refs_4_), channel_id=1, source_target_pairs={{0,8},{1,9},{2,10},{3,11},{4,12},{5,13},{6,14},{7,15},{8,0},{9,1},... | collective-permute-start | bytes 786440 | tf_op jit(solution)/shard_map/ppermute | solution.py:529
  7.3 12.0 %collective-permute-start.2 = (bf16[2,512,128]{2,1,0:T(8,128)(2,1)S(1)}, bf16[2,512,128]{2,1,0:T(8,128)(2,1)S(1)}, u32[]{:S(2)}, u32[]{:S(2)}) collective-permute-start(bf16[2,512,128]{2,1,0:T(8,128)(2,1)S(1)} %cast_kernel.1.w0_ref.refs_0_.refs_4_), channel_id=1, source_target_pairs={{0,4},{1,5},{2,6},{3,7},{4,0},{5,1},{6,2},{7,3},{8,12},{9,13},{10,... | collective-permute-start | bytes 786440 | tf_op jit(solution)/shard_map/ppermute | solution.py:533
  11.0 0.7 copy-start.8
  19.3 3.5 %collective-permute-start.3 = (bf16[2,784,512]{2,1,0:T(8,128)(2,1)S(1)}, bf16[2,784,512]{2,1,0:T(8,128)(2,1)S(1)}, u32[]{:S(2)}, u32[]{:S(2)}) collective-permute-start(bf16[2,784,512]{2,1,0:T(8,128)(2,1)S(1)} %bitcast.13), channel_id=1, source_target_pairs={{0,1},{1,0},{2,3},{3,2},{4,5},{5,4},{6,7},{7,6},{8,9},{9,8},{10,11... | collective-permute-start | bytes 4816904 | tf_op jit(solution)/shard_map/ppermute | solution.py:533
  19.3 8.7 %collective-permute-start.4 = (bf16[2,512,128]{2,1,0:T(8,128)(2,1)S(1)}, bf16[2,512,128]{2,1,0:T(8,128)(2,1)S(1)}, u32[]{:S(2)}, u32[]{:S(2)}) collective-permute-start(bf16[2,512,128]{2,1,0:T(8,128)(2,1)S(1)} %collective-permute-done.1.refs_3_.refs_7_), channel_id=1, source_target_pairs={{0,2},{1,3},{2,0},{3,1},{4,6},{5,7},{6,4},{7,5},{8,10},{9,11},{10,... | collective-permute-start | bytes 786440 | tf_op jit(solution)/shard_map/ppermute | solution.py:533
  19.8 11.0 %collective-permute-start.7 = (bf16[2,512,128]{2,1,0:T(8,128)(2,1)S(1)}, bf16[2,512,128]{2,1,0:T(8,128)(2,1)S(1)}, u32[]{:S(2)}, u32[]{:S(2)}) collective-permute-start(bf16[2,512,128]{2,1,0:T(8,128)(2,1)S(1)} %collective-permute-done.1.refs_3_.refs_7_), channel_id=1, source_target_pairs={{0,16},{16,0},{1,17},{17,1},{2,18},{18,2},{3,19},{19,3},{4,20},{20... | collective-permute-start | bytes 786440 | tf_op jit(solution)/shard_map/ppermute | solution.py:541
  28.0 12.0 %collective-permute-start.6 = (bf16[2,512,128]{2,1,0:T(8,128)(2,1)S(1)}, bf16[2,512,128]{2,1,0:T(8,128)(2,1)S(1)}, u32[]{:S(2)}, u32[]{:S(2)}) collective-permute-start(bf16[2,512,128]{2,1,0:T(8,128)(2,1)S(1)} %collective-permute-done.2.refs_2_.refs_6_), channel_id=1, source_target_pairs={{0,2},{1,3},{2,0},{3,1},{4,6},{5,7},{6,4},{7,5},{8,10},{9,11},{10,... | collective-permute-start | bytes 786440 | tf_op jit(solution)/shard_map/ppermute | solution.py:533
  28.7 11.3 %collective-permute-start.5 = (bf16[2,512,128]{2,1,0:T(8,128)(2,1)S(1)}, bf16[2,512,128]{2,1,0:T(8,128)(2,1)S(1)}, u32[]{:S(2)}, u32[]{:S(2)}) collective-permute-start(bf16[2,512,128]{2,1,0:T(8,128)(2,1)S(1)} %collective-permute-done.4.refs_0_.refs_8_), channel_id=1, source_target_pairs={{0,16},{16,0},{1,17},{17,1},{2,18},{18,2},{3,19},{19,3},{4,20},{20... | collective-permute-start | bytes 786440 | tf_op jit(solution)/shard_map/ppermute | solution.py:541
  34.1 10.0 %collective-permute-start.8 = (bf16[2,512,128]{2,1,0:T(8,128)(2,1)S(1)}, bf16[2,512,128]{2,1,0:T(8,128)(2,1)S(1)}, u32[]{:S(2)}, u32[]{:S(2)}) collective-permute-start(bf16[2,512,128]{2,1,0:T(8,128)(2,1)S(1)} %get-tuple-element.95), channel_id=1, source_target_pairs={{0,2},{1,3},{2,0},{3,1},{4,6},{5,7},{6,4},{7,5},{8,10},{9,11},{10,... | collective-permute-start | bytes 786440 | tf_op jit(solution)/shard_map/ppermute | solution.py:533
  35.6 8.5 %collective-permute-start.9 = (bf16[2,512,128]{2,1,0:T(8,128)(2,1)S(1)}, bf16[2,512,128]{2,1,0:T(8,128)(2,1)S(1)}, u32[]{:S(2)}, u32[]{:S(2)}) collective-permute-start(bf16[2,512,128]{2,1,0:T(8,128)(2,1)S(1)} %get-tuple-element.96), channel_id=1, source_target_pairs={{0,16},{16,0},{1,17},{17,1},{2,18},{18,2},{3,19},{19,3},{4,20},{20... | collective-permute-start | bytes 786440 | tf_op jit(solution)/shard_map/ppermute | solution.py:541
  35.7 8.5 %collective-permute-start.10 = (bf16[2,512,128]{2,1,0:T(8,128)(2,1)S(1)}, bf16[2,512,128]{2,1,0:T(8,128)(2,1)S(1)}, u32[]{:S(2)}, u32[]{:S(2)}) collective-permute-start(bf16[2,512,128]{2,1,0:T(8,128)(2,1)S(1)} %get-tuple-element.97), channel_id=1, source_target_pairs={{0,4},{1,5},{2,6},{3,7},{4,0},{5,1},{6,2},{7,3},{8,12},{9,13},{10,... | collective-permute-start | bytes 786440 | tf_op jit(solution)/shard_map/ppermute | solution.py:533
  37.3 2.7 %copy-start.9 = (f32[2048]{0:T(1024)S(1)}, f32[2048]{0:T(1024)}, u32[]{:S(2)}) copy-start(f32[2048]{0:T(1024)} %param.19) | copy-start | bytes 24580
  44.1 3.5 %collective-permute-start.11 = (bf16[2,784,512]{2,1,0:T(8,128)(2,1)S(1)}, bf16[2,784,512]{2,1,0:T(8,128)(2,1)S(1)}, u32[]{:S(2)}, u32[]{:S(2)}) collective-permute-start(bf16[2,784,512]{2,1,0:T(8,128)(2,1)S(1)} %back_kernel.5), channel_id=1, source_target_pairs={{0,1},{1,0},{2,3},{3,2},{4,5},{5,4},{6,7},{7,6},{8,9},{9,8},{10,11... | collective-permute-start | bytes 4816904 | tf_op jit(solution)/shard_map/ppermute | solution.py:533
  44.2 9.6 %collective-permute-start.12 = (bf16[2,512,128]{2,1,0:T(8,128)(2,1)S(1)}, bf16[2,512,128]{2,1,0:T(8,128)(2,1)S(1)}, u32[]{:S(2)}, u32[]{:S(2)}) collective-permute-start(bf16[2,512,128]{2,1,0:T(8,128)(2,1)S(1)} %get-tuple-element.105), channel_id=1, source_target_pairs={{0,18},{1,19},{2,16},{3,17},{4,22},{5,23},{6,20},{7,21},{8,26},{9,... | collective-permute-start | bytes 786440 | tf_op jit(solution)/shard_map/ppermute | solution.py:529
  46.2 1.4 %copy-start = (f32[16,49,512]{2,0,1:T(8,128)S(1)}, f32[16,49,512]{2,0,1:T(8,128)}, u32[]{:S(2)}) copy-start(f32[16,49,512]{2,0,1:T(8,128)} %param.15) | copy-start | bytes 4816900
  46.2 1.6 %copy-start.1 = (bf16[16,49,512]{2,0,1:T(8,128)(2,1)S(1)}, bf16[16,49,512]{2,0,1:T(8,128)(2,1)}, u32[]{:S(2)}) copy-start(bf16[16,49,512]{2,0,1:T(8,128)(2,1)} %param.16) | copy-start | bytes 2408452
  46.3 1.6 %copy-start.10 = (f32[7,512]{1,0:T(8,128)S(1)}, f32[7,512]{1,0:T(8,128)}, u32[]{:S(2)}) copy-start(f32[7,512]{1,0:T(8,128)} %refs_9_.1) | copy-start | bytes 43012
  46.3 8.4 %collective-permute-start.13 = (bf16[2,512,128]{2,1,0:T(8,128)(2,1)S(1)}, bf16[2,512,128]{2,1,0:T(8,128)(2,1)S(1)}, u32[]{:S(2)}, u32[]{:S(2)}) collective-permute-start(bf16[2,512,128]{2,1,0:T(8,128)(2,1)S(1)} %get-tuple-element.106), channel_id=1, source_target_pairs={{0,4},{1,5},{2,6},{3,7},{4,0},{5,1},{6,2},{7,3},{8,12},{9,13},{10,... | collective-permute-start | bytes 786440 | tf_op jit(solution)/shard_map/ppermute | solution.py:533
  53.7 2.4 %collective-permute-start.14 = (f32[44,128]{1,0:T(8,128)S(1)}, f32[44,128]{1,0:T(8,128)S(1)}, u32[]{:S(2)}, u32[]{:S(2)}) collective-permute-start(f32[44,128]{1,0:T(8,128)S(1)} %get-tuple-element.107), channel_id=1, source_target_pairs={{0,1},{1,0},{2,3},{3,2},{4,5},{5,4},{6,7},{7,6},{8,9},{9,8},{10,11... | collective-permute-start | bytes 67592 | tf_op jit(solution)/shard_map/ppermute | solution.py:533
  54.8 23.3 %copy-start.2 = (f32[512,128]{1,0:T(8,128)S(1)}, f32[512,128]{1,0:T(8,128)}, u32[]{:S(2)}) copy-start(f32[512,128]{1,0:T(8,128)} %refs_0_.1) | copy-start | bytes 786436
  54.8 23.3 %copy-start.3 = (f32[128,512]{1,0:T(8,128)S(1)}, f32[128,512]{1,0:T(8,128)}, u32[]{:S(2)}) copy-start(f32[128,512]{1,0:T(8,128)} %refs_6_.1) | copy-start | bytes 786436
  54.8 23.3 %copy-start.4 = (f32[512,128]{1,0:T(8,128)S(1)}, f32[512,128]{1,0:T(8,128)}, u32[]{:S(2)}) copy-start(f32[512,128]{1,0:T(8,128)} %refs_1_.1) | copy-start | bytes 786436
  54.8 23.3 %copy-start.5 = (f32[512,128]{1,0:T(8,128)S(1)}, f32[512,128]{1,0:T(8,128)}, u32[]{:S(2)}) copy-start(f32[512,128]{1,0:T(8,128)} %refs_2_.1) | copy-start | bytes 786436
  54.8 23.3 %copy-start.6 = (f32[128,512]{1,0:T(8,128)S(1)}, f32[128,512]{1,0:T(8,128)}, u32[]{:S(2)}) copy-start(f32[128,512]{1,0:T(8,128)} %refs_7_.1) | copy-start | bytes 786436
  54.8 23.3 %copy-start.7 = (f32[128,512]{1,0:T(8,128)S(1)}, f32[128,512]{1,0:T(8,128)}, u32[]{:S(2)}) copy-start(f32[128,512]{1,0:T(8,128)} %refs_8_.1) | copy-start | bytes 786436
  54.9 23.3 %copy-start.11 = (f32[7,512]{1,0:T(8,128)S(1)}, f32[7,512]{1,0:T(8,128)}, u32[]{:S(2)}) copy-start(f32[7,512]{1,0:T(8,128)} %refs_10_.1) | copy-start | bytes 43012
  54.9 23.3 %copy-start.12 = (f32[7,512]{1,0:T(8,128)S(1)}, f32[7,512]{1,0:T(8,128)}, u32[]{:S(2)}) copy-start(f32[7,512]{1,0:T(8,128)} %refs_11_.1) | copy-start | bytes 43012
  54.9 23.3 %copy-start.13 = (f32[2048]{0:T(1024)S(1)}, f32[2048]{0:T(1024)}, u32[]{:S(2)}) copy-start(f32[2048]{0:T(1024)} %param.24) | copy-start | bytes 24580
  54.9 23.3 %copy-start.14 = (f32[2048]{0:T(1024)S(1)}, f32[2048]{0:T(1024)}, u32[]{:S(2)}) copy-start(f32[2048]{0:T(1024)} %param.25) | copy-start | bytes 24580
  54.9 14.3 %collective-permute-start.16 = (bf16[2,512,128]{2,1,0:T(8,128)(2,1)S(1)}, bf16[2,512,128]{2,1,0:T(8,128)(2,1)S(1)}, u32[]{:S(2)}, u32[]{:S(2)}) collective-permute-start(bf16[2,512,128]{2,1,0:T(8,128)(2,1)S(1)} %add_convert_fusion.1), channel_id=1, source_target_pairs={{0,8},{1,9},{2,10},{3,11},{4,12},{5,13},{6,14},{7,15},{8,0},{9,1},... | collective-permute-start | bytes 786440 | tf_op jit(solution)/shard_map/ppermute | solution.py:529
  56.1 13.1 %collective-permute-start.15 = (bf16[2,512,128]{2,1,0:T(8,128)(2,1)S(1)}, bf16[2,512,128]{2,1,0:T(8,128)(2,1)S(1)}, u32[]{:S(2)}, u32[]{:S(2)}) collective-permute-start(bf16[2,512,128]{2,1,0:T(8,128)(2,1)S(1)} %add_convert_fusion.2), channel_id=1, source_target_pairs={{0,2},{1,3},{2,0},{3,1},{4,6},{5,7},{6,4},{7,5},{8,10},{9,11},{10,... | collective-permute-start | bytes 786440 | tf_op jit(solution)/shard_map/ppermute | solution.py:533
  57.2 3.8 %collective-permute-start.17 = (f32[44,128]{1,0:T(8,128)S(1)}, f32[44,128]{1,0:T(8,128)S(1)}, u32[]{:S(2)}, u32[]{:S(2)}) collective-permute-start(f32[44,128]{1,0:T(8,128)S(1)} %add.37), channel_id=1, source_target_pairs={{0,16},{16,0},{1,17},{17,1},{2,18},{18,2},{3,19},{19,3},{4,20},{20... | collective-permute-start | bytes 67592 | tf_op jit(solution)/shard_map/ppermute | solution.py:541
  61.0 3.8 %collective-permute-start.18 = (f32[44,128]{1,0:T(8,128)S(1)}, f32[44,128]{1,0:T(8,128)S(1)}, u32[]{:S(2)}, u32[]{:S(2)}) collective-permute-start(f32[44,128]{1,0:T(8,128)S(1)} %add.44), channel_id=1, source_target_pairs={{0,2},{1,3},{2,0},{3,1},{4,6},{5,7},{6,4},{7,5},{8,10},{9,11},{10,... | collective-permute-start | bytes 67592 | tf_op jit(solution)/shard_map/ppermute | solution.py:533
  69.4 8.7 %collective-permute-start.19 = (bf16[2,512,128]{2,1,0:T(8,128)(2,1)S(1)}, bf16[2,512,128]{2,1,0:T(8,128)(2,1)S(1)}, u32[]{:S(2)}, u32[]{:S(2)}) collective-permute-start(bf16[2,512,128]{2,1,0:T(8,128)(2,1)S(1)} %add_convert_fusion.own_ref), channel_id=1, source_target_pairs={{0,16},{16,0},{1,17},{17,1},{2,18},{18,2},{3,19},{19,3},{4,20},{20... | collective-permute-start | bytes 786440 | tf_op jit(solution)/shard_map/ppermute | solution.py:541
  69.5 3.9 %collective-permute-start.20 = (f32[44,128]{1,0:T(8,128)S(1)}, f32[44,128]{1,0:T(8,128)S(1)}, u32[]{:S(2)}, u32[]{:S(2)}) collective-permute-start(f32[44,128]{1,0:T(8,128)S(1)} %add.45), channel_id=1, source_target_pairs={{0,4},{1,5},{2,6},{3,7},{4,0},{5,1},{6,2},{7,3},{8,12},{9,13},{10,... | collective-permute-start | bytes 67592 | tf_op jit(solution)/shard_map/ppermute | solution.py:533
  73.4 4.7 %collective-permute-start.21 = (f32[44,128]{1,0:T(8,128)S(1)}, f32[44,128]{1,0:T(8,128)S(1)}, u32[]{:S(2)}, u32[]{:S(2)}) collective-permute-start(f32[44,128]{1,0:T(8,128)S(1)} %add.46), channel_id=1, source_target_pairs={{0,8},{1,9},{2,10},{3,11},{4,12},{5,13},{6,14},{7,15},{8,0},{9,1},... | collective-permute-start | bytes 67592 | tf_op jit(solution)/shard_map/ppermute | solution.py:533

commit v8 on v7

--- a/solution.py
+++ b/solution.py
@@ -658,8 +658,8 @@
     sums = sums + flip(sums, 1)
     sums = after(sums, sum_f)
     y0 = flip(after(wide_sum(gy0, zy).astype(bf16), sums), 2)
+    sums = sums + flip(sums, 2)
     sums = sums + across(sums)
-    sums = sums + flip(sums, 2)
     own = wide_sum(g0, y0, z1, zf).astype(bf16)
     own, sums = lax.optimization_barrier((own, sums))
     got = across(own)

time: 80 us -> 80.1 us (level)
    ppermute x3, waiting for transfers between devices: 6.64 us -> 2.85 us  [joint(): return lax.ppermute(values, BOTH, [(s, n * 16 + w) for s, (n, w) in pairs])]
    ppermute x14, waiting for transfers between devices: 12.4 us -> 15.9 us  [flip(): return lax.ppermute(values, 'wide', [(w, w ^ bit) for w in range(16)])]
where the time goes in v8:
time: 80.1 us; the launch traced here: 79.8 us
  Pallas kernels  29 us (36%)
  starting transfers between devices  26.1 us (33%)
  waiting for transfers between devices  21.8 us (27%)
  between operations  1.61 us (2%)
  local copies, waits for them, and re-layouts  0.98 us (1%)
    pallas_call x10, Pallas kernels, call(): pl.pallas_call(kernel, out_shape=outs, in_specs=[SMEM] * smem + [VMEM] *...  29 us
    ppermute x14, waiting for transfers between devices, flip(): return lax.ppermute(values, 'wide', [(w, w ^ bit) for w in range(16)])  15.9 us
    ppermute x14, starting transfers between devices, flip(): return lax.ppermute(values, 'wide', [(w, w ^ bit) for w in range(16)])  14.8 us
    ppermute x3, starting transfers between devices, joint(): return lax.ppermute(values, BOTH, [(s, n * 16 + w) for s, (n, w) in pairs])  5.74 us
    ppermute x5, starting transfers between devices, across(): return lax.ppermute(values, 'narrow', [(0, 1), (1, 0)])  5.55 us
    ppermute x5, waiting for transfers between devices, across(): return lax.ppermute(values, 'narrow', [(0, 1), (1, 0)])  3.02 us
    ppermute x3, waiting for transfers between devices, joint(): return lax.ppermute(values, BOTH, [(s, n * 16 + w) for s, (n, w) in pairs])  2.85 us
  transfers between devices with their start and end apart: 22, of which 12 were waited for; matrix products, arithmetic and copies ran while one was open for 0% of the time, Pallas kernels for 33%

profile of v8, /device:TPU:0, one launch (start us, length us, event | category | flops | bytes accessed | tf_op | source)
XLA Modules:
  0.0 79.8 jit_solution(10920332908304240287)
XLA Ops:
  0.6 1.1 %cast_kernel.1.w0_ref.refs_0_.refs_4_ = bf16[2,512,128]{2,1,0:T(8,128)(2,1)S(1)} custom-call(f32[512,128]{1,0:T(8,128)} %refs_0_.1, f32[128,512]{1,0:T(8,128)} %refs_6_.1), custom_call_target="tpu_custom_call" | custom-call | bytes 786432 | tf_op jit(solution)/shard_map/cast_kernel/pallas_call | solution.py:508
  1.7 3.0 %collective-permute-start = (bf16[2,512,128]{2,1,0:T(8,128)(2,1)S(1)}, bf16[2,512,128]{2,1,0:T(8,128)(2,1)S(1)}, u32[]{:S(2)}, u32[]{:S(2)}) collective-permute-start(bf16[2,512,128]{2,1,0:T(8,128)(2,1)S(1)} %cast_kernel.1.w0_ref.refs_0_.refs_4_), channel_id=1, source_target_pairs={{0,2},{1,3},{2,0},{3,1},{4,6},{5,7},{6,4},{7,5},{8,10},{9,11},{10,... | collective-permute-start | bytes 786440 | tf_op jit(solution)/shard_map/ppermute | solution.py:533
  4.7 2.6 %collective-permute-start.1 = (bf16[2,512,128]{2,1,0:T(8,128)(2,1)S(1)}, bf16[2,512,128]{2,1,0:T(8,128)(2,1)S(1)}, u32[]{:S(2)}, u32[]{:S(2)}) collective-permute-start(bf16[2,512,128]{2,1,0:T(8,128)(2,1)S(1)} %cast_kernel.1.w0_ref.refs_0_.refs_4_), channel_id=1, source_target_pairs={{0,8},{1,9},{2,10},{3,11},{4,12},{5,13},{6,14},{7,15},{8,0},{9,1},... | collective-permute-start | bytes 786440 | tf_op jit(solution)/shard_map/ppermute | solution.py:529
  7.3 1.6 %collective-permute-start.2 = (bf16[2,512,128]{2,1,0:T(8,128)(2,1)S(1)}, bf16[2,512,128]{2,1,0:T(8,128)(2,1)S(1)}, u32[]{:S(2)}, u32[]{:S(2)}) collective-permute-start(bf16[2,512,128]{2,1,0:T(8,128)(2,1)S(1)} %cast_kernel.1.w0_ref.refs_0_.refs_4_), channel_id=1, source_target_pairs={{0,4},{1,5},{2,6},{3,7},{4,0},{5,1},{6,2},{7,3},{8,12},{9,13},{10,... | collective-permute-start | bytes 786440 | tf_op jit(solution)/shard_map/ppermute | solution.py:533
  9.6 1.5 %collective-permute-done.w1_ref.refs_1_.refs_5_ = bf16[2,512,128]{2,1,0:T(8,128)(2,1)S(1)} collective-permute-done((bf16[2,512,128]{2,1,0:T(8,128)(2,1)S(1)}, bf16[2,512,128]{2,1,0:T(8,128)(2,1)S(1)}, u32[]{:S(2)}, u32[]{:S(2)}) %collective-permute-start) | collective-permute-done | bytes 262176 | tf_op jit(solution)/shard_map/ppermute | solution.py:533
  11.0 0.7 copy-done.8
  11.7 5.2 %pre_kernel.1 = (bf16[2,49,16,512]{3,2,1,0:T(8,128)(2,1)S(1)}, f32[4,16,128]{2,1,0:T(8,128)S(1)}, bf16[784,256]{1,0:T(8,128)(2,1)S(1)}, bf16[784,256]{1,0:T(8,12...) custom-call(s32[1]{0:T(128)S(6)} %copy.29.counts_ref, f32[49,16,512]{2,1,0:T(8,128)} %bitcast.18, ...), custom_call_target="tpu_custom_call" | custom-call | bytes 6446084 | tf_op jit(solution)/shard_map/pre_kernel/pallas_call | solution.py:508
  16.9 2.2 %collective-permute-done.1.refs_3_.refs_7_ = bf16[2,512,128]{2,1,0:T(8,128)(2,1)S(1)} collective-permute-done((bf16[2,512,128]{2,1,0:T(8,128)(2,1)S(1)}, bf16[2,512,128]{2,1,0:T(8,128)(2,1)S(1)}, u32[]{:S(2)}, u32[]{:S(2)}) %collective-permute-start.1) | collective-permute-done | bytes 262176 | tf_op jit(solution)/shard_map/ppermute | solution.py:529
  19.1 0.2 collective-permute-done.2.refs_2_.refs_6_
  19.3 0.0 collective-permute-start.3
  19.3 0.5 collective-permute-start.4
  19.8 2.3 %collective-permute-start.7 = (bf16[2,512,128]{2,1,0:T(8,128)(2,1)S(1)}, bf16[2,512,128]{2,1,0:T(8,128)(2,1)S(1)}, u32[]{:S(2)}, u32[]{:S(2)}) collective-permute-start(bf16[2,512,128]{2,1,0:T(8,128)(2,1)S(1)} %collective-permute-done.1.refs_3_.refs_7_), channel_id=1, source_target_pairs={{0,16},{16,0},{1,17},{17,1},{2,18},{18,2},{3,19},{19,3},{4,20},{20... | collective-permute-start | bytes 786440 | tf_op jit(solution)/shard_map/ppermute | solution.py:541
  22.1 0.7 collective-permute-done.3.oth_ref
  22.8 5.0 %block_kernel.3 = (bf16[2,784,512]{2,1,0:T(8,128)(2,1)S(1)}, bf16[2,784,512]{2,1,0:T(8,128)(2,1)S(1)}, f32[16,128]{1,0:T(8,128)S(1)}, f32[2,512,128]{2,1,0:T(8,1...) custom-call(bf16[2,784,512]{2,1,0:T(8,128)(2,1)S(1)} %bitcast.14, ...), custom_call_target="tpu_custom_call" | custom-call | bytes 10912768 | tf_op jit(solution)/shard_map/block_kernel/pallas_call | solution.py:508
  27.7 0.3 collective-permute-done.4.refs_0_.refs_8_
  28.0 0.6 collective-permute-start.6
  28.7 2.1 %collective-permute-start.5 = (bf16[2,512,128]{2,1,0:T(8,128)(2,1)S(1)}, bf16[2,512,128]{2,1,0:T(8,128)(2,1)S(1)}, u32[]{:S(2)}, u32[]{:S(2)}) collective-permute-start(bf16[2,512,128]{2,1,0:T(8,128)(2,1)S(1)} %collective-permute-done.4.refs_0_.refs_8_), channel_id=1, source_target_pairs={{0,16},{16,0},{1,17},{17,1},{2,18},{18,2},{3,19},{19,3},{4,20},{20... | collective-permute-start | bytes 786440 | tf_op jit(solution)/shard_map/ppermute | solution.py:541
  30.8 3.2 %block_kernel.4 = (bf16[2,784,256]{2,1,0:T(8,128)(2,1)S(1)}, bf16[2,784,256]{2,1,0:T(8,128)(2,1)S(1)}, f32[16,128]{1,0:T(8,128)S(1)}, bf16[2,512,128]{2,1,0:T(8,128)(2,1)S(1)}, bf16[2,512,128]{2,1,0:T(8,128)(2,1)S(1)}) custom-call(bf16[2,784,512]{2,1,0:T(8,128)(2,1)S(1)} %bitcast.15, bf16[2,784,512]{2,1,0:T(8,128)(2,1)S(1)} %collective-permute-done.3.oth_ref, ...), custom_call_target="tpu_custom_call" | custom-call | bytes 5881856 | tf_op jit(solution)/shard_map/block_kernel/pallas_call | solution.py:508
  34.1 1.6 %collective-permute-start.8 = (bf16[2,512,128]{2,1,0:T(8,128)(2,1)S(1)}, bf16[2,512,128]{2,1,0:T(8,128)(2,1)S(1)}, u32[]{:S(2)}, u32[]{:S(2)}) collective-permute-start(bf16[2,512,128]{2,1,0:T(8,128)(2,1)S(1)} %get-tuple-element.95), channel_id=1, source_target_pairs={{0,2},{1,3},{2,0},{3,1},{4,6},{5,7},{6,4},{7,5},{8,10},{9,11},{10,... | collective-permute-start | bytes 786440 | tf_op jit(solution)/shard_map/ppermute | solution.py:533
  35.6 0.0 collective-permute-start.9
  35.7 1.7 %collective-permute-start.10 = (bf16[2,512,128]{2,1,0:T(8,128)(2,1)S(1)}, bf16[2,512,128]{2,1,0:T(8,128)(2,1)S(1)}, u32[]{:S(2)}, u32[]{:S(2)}) collective-permute-start(bf16[2,512,128]{2,1,0:T(8,128)(2,1)S(1)} %get-tuple-element.97), channel_id=1, source_target_pairs={{0,4},{1,5},{2,6},{3,7},{4,0},{5,1},{6,2},{7,3},{8,12},{9,13},{10,... | collective-permute-start | bytes 786440 | tf_op jit(solution)/shard_map/ppermute | solution.py:533
  37.3 2.6 %back_kernel.3 = (f32[2,784,512]{2,1,0:T(8,128)S(1)}, f32[2,784,512]{2,1,0:T(8,128)S(1)}) custom-call(bf16[2,784,512]{2,1,0:T(8,128)(2,1)S(1)} %get-tuple-element.85.refs_0_, bf16[2,784,256]{2,1,0:T(8,128)(2,1)S(1)} %get-tuple-element.86.refs_1_, bf16[2,784,512]{2,1,0:T(8,128)(2,1)S(1)} %get-tuple-element.87.refs_2_, ...), custom_call_target="tpu_custom_call" | custom-call | bytes 12812288 | tf_op jit(solution)/shard_map/back_kernel/pallas_call | solution.py:508
  40.0 0.0 collective-permute-done.6.refs_1_.refs_3_
  40.0 0.0 collective-permute-done.5.refs_0_.refs_2_
  40.0 3.4 %block_kernel.5 = (bf16[2,784,256]{2,1,0:T(8,128)(2,1)S(1)}, bf16[2,784,256]{2,1,0:T(8,128)(2,1)S(1)}, f32[16,128]{1,0:T(8,128)S(1)}, bf16[2,512,128]{2,1,0:T(8,128)(2,1)S(1)}, bf16[2,512,128]{2,1,0:T(8,128)(2,1)S(1)}) custom-call(bf16[2,784,512]{2,1,0:T(8,128)(2,1)S(1)} %bitcast.16, bf16[2,784,512]{2,1,0:T(8,128)(2,1)S(1)} %collective-permute-done.3.oth_ref, ...), custom_call_target="tpu_custom_call" | custom-call | bytes 5881856 | tf_op jit(solution)/shard_map/block_kernel/pallas_call | solution.py:508
  43.5 0.6 back_kernel.5
  44.1 0.0 collective-permute-done.8
  44.1 0.0 collective-permute-done.9
  44.1 0.1 collective-permute-start.11
  44.2 2.0 %collective-permute-start.12 = (bf16[2,512,128]{2,1,0:T(8,128)(2,1)S(1)}, bf16[2,512,128]{2,1,0:T(8,128)(2,1)S(1)}, u32[]{:S(2)}, u32[]{:S(2)}) collective-permute-start(bf16[2,512,128]{2,1,0:T(8,128)(2,1)S(1)} %get-tuple-element.105), channel_id=1, source_target_pairs={{0,18},{1,19},{2,16},{3,17},{4,22},{5,23},{6,20},{7,21},{8,26},{9,... | collective-permute-start | bytes 786440 | tf_op jit(solution)/shard_map/ppermute | solution.py:529
  46.3 0.7 collective-permute-start.13
  47.0 0.6 back_kernel.4
  47.5 0.1 collective-permute-done.11
  47.7 0.0 copy-done
  47.7 0.2 copy-done.1
  47.9 5.8 %post_kernel.1 = (f32[49,16,512]{2,1,0:T(8,128)}, f32[49,16,512]{2,1,0:T(8,128)}, f32[44,128]{1,0:T(8,128)S(1)}) custom-call(s32[1]{0:T(128)S(6)} %copy.29.counts_ref, f32[49,16,512]{2,1,0:T(8,128)S(1)} %bitcast.19, bf16[49,16,512]{2,1,0:T(8,128)(2,1)S(1)} %bitcast.21, f32[7,512]{1,0:T(8,128)S(1)} %copy-done.10, ...), custom_call_target="tpu_custom_call" | custom-call | bytes 10530820 | tf_op jit(solution)/shard_map/post_kernel/pallas_call | solution.py:508
  53.7 0.2 collective-permute-start.14
  53.8 0.8 collective-permute-done.13
  54.6 0.1 add_convert_fusion.1
  54.8 0.0 copy-start.2
  54.8 0.0 copy-start.3
  54.8 0.0 copy-start.4
  54.8 0.0 copy-start.5
  54.8 0.0 copy-start.6
  54.8 0.0 copy-start.7
  54.9 0.0 copy-start.11
  54.9 0.0 copy-start.12
  54.9 0.0 copy-start.13
  54.9 0.0 copy-start.14
  54.9 1.1 %collective-permute-start.16 = (bf16[2,512,128]{2,1,0:T(8,128)(2,1)S(1)}, bf16[2,512,128]{2,1,0:T(8,128)(2,1)S(1)}, u32[]{:S(2)}, u32[]{:S(2)}) collective-permute-start(bf16[2,512,128]{2,1,0:T(8,128)(2,1)S(1)} %add_convert_fusion.1), channel_id=1, source_target_pairs={{0,8},{1,9},{2,10},{3,11},{4,12},{5,13},{6,14},{7,15},{8,0},{9,1},... | collective-permute-start | bytes 786440 | tf_op jit(solution)/shard_map/ppermute | solution.py:529
  56.0 0.1 add_convert_fusion.2
  56.1 1.0 %collective-permute-start.15 = (bf16[2,512,128]{2,1,0:T(8,128)(2,1)S(1)}, bf16[2,512,128]{2,1,0:T(8,128)(2,1)S(1)}, u32[]{:S(2)}, u32[]{:S(2)}) collective-permute-start(bf16[2,512,128]{2,1,0:T(8,128)(2,1)S(1)} %add_convert_fusion.2), channel_id=1, source_target_pairs={{0,2},{1,3},{2,0},{3,1},{4,6},{5,7},{6,4},{7,5},{8,10},{9,11},{10,... | collective-permute-start | bytes 786440 | tf_op jit(solution)/shard_map/ppermute | solution.py:533
  57.2 1.0 %collective-permute-start.17 = (f32[44,128]{1,0:T(8,128)S(1)}, f32[44,128]{1,0:T(8,128)S(1)}, u32[]{:S(2)}, u32[]{:S(2)}) collective-permute-start(f32[44,128]{1,0:T(8,128)S(1)} %add.37), channel_id=1, source_target_pairs={{0,2},{1,3},{2,0},{3,1},{4,6},{5,7},{6,4},{7,5},{8,10},{9,11},{10,... | collective-permute-start | bytes 67592 | tf_op jit(solution)/shard_map/ppermute | solution.py:533
  58.2 6.6 %collective-permute-done.17 = f32[44,128]{1,0:T(8,128)S(1)} collective-permute-done((f32[44,128]{1,0:T(8,128)S(1)}, f32[44,128]{1,0:T(8,128)S(1)}, u32[]{:S(2)}, u32[]{:S(2)}) %collective-permute-start.17) | collective-permute-done | bytes 22560 | tf_op jit(solution)/shard_map/ppermute | solution.py:533
  64.8 0.8 %collective-permute-start.18 = (f32[44,128]{1,0:T(8,128)S(1)}, f32[44,128]{1,0:T(8,128)S(1)}, u32[]{:S(2)}, u32[]{:S(2)}) collective-permute-start(f32[44,128]{1,0:T(8,128)S(1)} %add.44), channel_id=1, source_target_pairs={{0,16},{16,0},{1,17},{17,1},{2,18},{18,2},{3,19},{19,3},{4,20},{20... | collective-permute-start | bytes 67592 | tf_op jit(solution)/shard_map/ppermute | solution.py:541
  65.6 3.0 %collective-permute-done.18 = f32[44,128]{1,0:T(8,128)S(1)} collective-permute-done((f32[44,128]{1,0:T(8,128)S(1)}, f32[44,128]{1,0:T(8,128)S(1)}, u32[]{:S(2)}, u32[]{:S(2)}) %collective-permute-start.18) | collective-permute-done | bytes 22560 | tf_op jit(solution)/shard_map/ppermute | solution.py:541
  68.6 0.6 collective-permute-done.16
  69.2 0.1 add_convert_fusion.own_ref
  69.4 0.3 collective-permute-start.19
  69.7 1.1 %collective-permute-start.20 = (f32[44,128]{1,0:T(8,128)S(1)}, f32[44,128]{1,0:T(8,128)S(1)}, u32[]{:S(2)}, u32[]{:S(2)}) collective-permute-start(f32[44,128]{1,0:T(8,128)S(1)} %add.45), channel_id=1, source_target_pairs={{0,4},{1,5},{2,6},{3,7},{4,0},{5,1},{6,2},{7,3},{8,12},{9,13},{10,... | collective-permute-start | bytes 67592 | tf_op jit(solution)/shard_map/ppermute | solution.py:533
  70.7 2.8 %collective-permute-done.20 = f32[44,128]{1,0:T(8,128)S(1)} collective-permute-done((f32[44,128]{1,0:T(8,128)S(1)}, f32[44,128]{1,0:T(8,128)S(1)}, u32[]{:S(2)}, u32[]{:S(2)}) %collective-permute-start.20) | collective-permute-done | bytes 22560 | tf_op jit(solution)/shard_map/ppermute | solution.py:533
  73.5 1.7 %collective-permute-start.21 = (f32[44,128]{1,0:T(8,128)S(1)}, f32[44,128]{1,0:T(8,128)S(1)}, u32[]{:S(2)}, u32[]{:S(2)}) collective-permute-start(f32[44,128]{1,0:T(8,128)S(1)} %add.46), channel_id=1, source_target_pairs={{0,8},{1,9},{2,10},{3,11},{4,12},{5,13},{6,14},{7,15},{8,0},{9,1},... | collective-permute-start | bytes 67592 | tf_op jit(solution)/shard_map/ppermute | solution.py:533
  75.2 3.0 %collective-permute-done.21 = f32[44,128]{1,0:T(8,128)S(1)} collective-permute-done((f32[44,128]{1,0:T(8,128)S(1)}, f32[44,128]{1,0:T(8,128)S(1)}, u32[]{:S(2)}, u32[]{:S(2)}) %collective-permute-start.21) | collective-permute-done | bytes 22560 | tf_op jit(solution)/shard_map/ppermute | solution.py:533
  78.3 1.5 %update_kernel.1 = (f32[512,128]{1,0:T(8,128)}, f32[512,128]{1,0:T(8,128)}, f32[512,128]{1,0:T(8,128)}, f32[16,128]{1,0:T(8,128)}, f32[16,128]{1,0:T(8,128)}, /*...) custom-call(bf16[2,512,128]{2,1,0:T(8,128)(2,1)S(1)} %add_convert_fu, ...), custom_call_target="tpu_custom_call" | custom-call | bytes 3827712 | tf_op jit(solution)/shard_map/update_kernel/pallas_call | solution.py:508
  (28 shorter events, 0.1 us)
Async XLA Ops:
  1.7 9.3 %collective-permute-start = (bf16[2,512,128]{2,1,0:T(8,128)(2,1)S(1)}, bf16[2,512,128]{2,1,0:T(8,128)(2,1)S(1)}, u32[]{:S(2)}, u32[]{:S(2)}) collective-permute-start(bf16[2,512,128]{2,1,0:T(8,128)(2,1)S(1)} %cast_kernel.1.w0_ref.refs_0_.refs_4_), channel_id=1, source_target_pairs={{0,2},{1,3},{2,0},{3,1},{4,6},{5,7},{6,4},{7,5},{8,10},{9,11},{10,... | collective-permute-start | bytes 786440 | tf_op jit(solution)/shard_map/ppermute | solution.py:533
  4.7 14.4 %collective-permute-start.1 = (bf16[2,512,128]{2,1,0:T(8,128)(2,1)S(1)}, bf16[2,512,128]{2,1,0:T(8,128)(2,1)S(1)}, u32[]{:S(2)}, u32[]{:S(2)}) collective-permute-start(bf16[2,512,128]{2,1,0:T(8,128)(2,1)S(1)} %cast_kernel.1.w0_ref.refs_0_.refs_4_), channel_id=1, source_target_pairs={{0,8},{1,9},{2,10},{3,11},{4,12},{5,13},{6,14},{7,15},{8,0},{9,1},... | collective-permute-start | bytes 786440 | tf_op jit(solution)/shard_map/ppermute | solution.py:529
  7.3 12.0 %collective-permute-start.2 = (bf16[2,512,128]{2,1,0:T(8,128)(2,1)S(1)}, bf16[2,512,128]{2,1,0:T(8,128)(2,1)S(1)}, u32[]{:S(2)}, u32[]{:S(2)}) collective-permute-start(bf16[2,512,128]{2,1,0:T(8,128)(2,1)S(1)} %cast_kernel.1.w0_ref.refs_0_.refs_4_), channel_id=1, source_target_pairs={{0,4},{1,5},{2,6},{3,7},{4,0},{5,1},{6,2},{7,3},{8,12},{9,13},{10,... | collective-permute-start | bytes 786440 | tf_op jit(solution)/shard_map/ppermute | solution.py:533
  11.0 0.7 copy-start.8
  19.3 3.5 %collective-permute-start.3 = (bf16[2,784,512]{2,1,0:T(8,128)(2,1)S(1)}, bf16[2,784,512]{2,1,0:T(8,128)(2,1)S(1)}, u32[]{:S(2)}, u32[]{:S(2)}) collective-permute-start(bf16[2,784,512]{2,1,0:T(8,128)(2,1)S(1)} %bitcast.13), channel_id=1, source_target_pairs={{0,1},{1,0},{2,3},{3,2},{4,5},{5,4},{6,7},{7,6},{8,9},{9,8},{10,11... | collective-permute-start | bytes 4816904 | tf_op jit(solution)/shard_map/ppermute | solution.py:533
  19.3 8.7 %collective-permute-start.4 = (bf16[2,512,128]{2,1,0:T(8,128)(2,1)S(1)}, bf16[2,512,128]{2,1,0:T(8,128)(2,1)S(1)}, u32[]{:S(2)}, u32[]{:S(2)}) collective-permute-start(bf16[2,512,128]{2,1,0:T(8,128)(2,1)S(1)} %collective-permute-done.1.refs_3_.refs_7_), channel_id=1, source_target_pairs={{0,2},{1,3},{2,0},{3,1},{4,6},{5,7},{6,4},{7,5},{8,10},{9,11},{10,... | collective-permute-start | bytes 786440 | tf_op jit(solution)/shard_map/ppermute | solution.py:533
  19.8 11.0 %collective-permute-start.7 = (bf16[2,512,128]{2,1,0:T(8,128)(2,1)S(1)}, bf16[2,512,128]{2,1,0:T(8,128)(2,1)S(1)}, u32[]{:S(2)}, u32[]{:S(2)}) collective-permute-start(bf16[2,512,128]{2,1,0:T(8,128)(2,1)S(1)} %collective-permute-done.1.refs_3_.refs_7_), channel_id=1, source_target_pairs={{0,16},{16,0},{1,17},{17,1},{2,18},{18,2},{3,19},{19,3},{4,20},{20... | collective-permute-start | bytes 786440 | tf_op jit(solution)/shard_map/ppermute | solution.py:541
  28.0 12.0 %collective-permute-start.6 = (bf16[2,512,128]{2,1,0:T(8,128)(2,1)S(1)}, bf16[2,512,128]{2,1,0:T(8,128)(2,1)S(1)}, u32[]{:S(2)}, u32[]{:S(2)}) collective-permute-start(bf16[2,512,128]{2,1,0:T(8,128)(2,1)S(1)} %collective-permute-done.2.refs_2_.refs_6_), channel_id=1, source_target_pairs={{0,2},{1,3},{2,0},{3,1},{4,6},{5,7},{6,4},{7,5},{8,10},{9,11},{10,... | collective-permute-start | bytes 786440 | tf_op jit(solution)/shard_map/ppermute | solution.py:533
  28.7 11.3 %collective-permute-start.5 = (bf16[2,512,128]{2,1,0:T(8,128)(2,1)S(1)}, bf16[2,512,128]{2,1,0:T(8,128)(2,1)S(1)}, u32[]{:S(2)}, u32[]{:S(2)}) collective-permute-start(bf16[2,512,128]{2,1,0:T(8,128)(2,1)S(1)} %collective-permute-done.4.refs_0_.refs_8_), channel_id=1, source_target_pairs={{0,16},{16,0},{1,17},{17,1},{2,18},{18,2},{3,19},{19,3},{4,20},{20... | collective-permute-start | bytes 786440 | tf_op jit(solution)/shard_map/ppermute | solution.py:541
  34.1 10.0 %collective-permute-start.8 = (bf16[2,512,128]{2,1,0:T(8,128)(2,1)S(1)}, bf16[2,512,128]{2,1,0:T(8,128)(2,1)S(1)}, u32[]{:S(2)}, u32[]{:S(2)}) collective-permute-start(bf16[2,512,128]{2,1,0:T(8,128)(2,1)S(1)} %get-tuple-element.95), channel_id=1, source_target_pairs={{0,2},{1,3},{2,0},{3,1},{4,6},{5,7},{6,4},{7,5},{8,10},{9,11},{10,... | collective-permute-start | bytes 786440 | tf_op jit(solution)/shard_map/ppermute | solution.py:533
  35.6 8.5 %collective-permute-start.9 = (bf16[2,512,128]{2,1,0:T(8,128)(2,1)S(1)}, bf16[2,512,128]{2,1,0:T(8,128)(2,1)S(1)}, u32[]{:S(2)}, u32[]{:S(2)}) collective-permute-start(bf16[2,512,128]{2,1,0:T(8,128)(2,1)S(1)} %get-tuple-element.96), channel_id=1, source_target_pairs={{0,16},{16,0},{1,17},{17,1},{2,18},{18,2},{3,19},{19,3},{4,20},{20... | collective-permute-start | bytes 786440 | tf_op jit(solution)/shard_map/ppermute | solution.py:541
  35.7 8.5 %collective-permute-start.10 = (bf16[2,512,128]{2,1,0:T(8,128)(2,1)S(1)}, bf16[2,512,128]{2,1,0:T(8,128)(2,1)S(1)}, u32[]{:S(2)}, u32[]{:S(2)}) collective-permute-start(bf16[2,512,128]{2,1,0:T(8,128)(2,1)S(1)} %get-tuple-element.97), channel_id=1, source_target_pairs={{0,4},{1,5},{2,6},{3,7},{4,0},{5,1},{6,2},{7,3},{8,12},{9,13},{10,... | collective-permute-start | bytes 786440 | tf_op jit(solution)/shard_map/ppermute | solution.py:533
  37.3 2.7 %copy-start.9 = (f32[2048]{0:T(1024)S(1)}, f32[2048]{0:T(1024)}, u32[]{:S(2)}) copy-start(f32[2048]{0:T(1024)} %param.19) | copy-start | bytes 24580
  44.1 3.5 %collective-permute-start.11 = (bf16[2,784,512]{2,1,0:T(8,128)(2,1)S(1)}, bf16[2,784,512]{2,1,0:T(8,128)(2,1)S(1)}, u32[]{:S(2)}, u32[]{:S(2)}) collective-permute-start(bf16[2,784,512]{2,1,0:T(8,128)(2,1)S(1)} %back_kernel.5), channel_id=1, source_target_pairs={{0,1},{1,0},{2,3},{3,2},{4,5},{5,4},{6,7},{7,6},{8,9},{9,8},{10,11... | collective-permute-start | bytes 4816904 | tf_op jit(solution)/shard_map/ppermute | solution.py:533
  44.2 9.6 %collective-permute-start.12 = (bf16[2,512,128]{2,1,0:T(8,128)(2,1)S(1)}, bf16[2,512,128]{2,1,0:T(8,128)(2,1)S(1)}, u32[]{:S(2)}, u32[]{:S(2)}) collective-permute-start(bf16[2,512,128]{2,1,0:T(8,128)(2,1)S(1)} %get-tuple-element.105), channel_id=1, source_target_pairs={{0,18},{1,19},{2,16},{3,17},{4,22},{5,23},{6,20},{7,21},{8,26},{9,... | collective-permute-start | bytes 786440 | tf_op jit(solution)/shard_map/ppermute | solution.py:529
  46.2 1.4 %copy-start = (f32[16,49,512]{2,0,1:T(8,128)S(1)}, f32[16,49,512]{2,0,1:T(8,128)}, u32[]{:S(2)}) copy-start(f32[16,49,512]{2,0,1:T(8,128)} %param.15) | copy-start | bytes 4816900
  46.2 1.6 %copy-start.1 = (bf16[16,49,512]{2,0,1:T(8,128)(2,1)S(1)}, bf16[16,49,512]{2,0,1:T(8,128)(2,1)}, u32[]{:S(2)}) copy-start(bf16[16,49,512]{2,0,1:T(8,128)(2,1)} %param.16) | copy-start | bytes 2408452
  46.3 1.6 %copy-start.10 = (f32[7,512]{1,0:T(8,128)S(1)}, f32[7,512]{1,0:T(8,128)}, u32[]{:S(2)}) copy-start(f32[7,512]{1,0:T(8,128)} %refs_9_.1) | copy-start | bytes 43012
  46.3 8.4 %collective-permute-start.13 = (bf16[2,512,128]{2,1,0:T(8,128)(2,1)S(1)}, bf16[2,512,128]{2,1,0:T(8,128)(2,1)S(1)}, u32[]{:S(2)}, u32[]{:S(2)}) collective-permute-start(bf16[2,512,128]{2,1,0:T(8,128)(2,1)S(1)} %get-tuple-element.106), channel_id=1, source_target_pairs={{0,4},{1,5},{2,6},{3,7},{4,0},{5,1},{6,2},{7,3},{8,12},{9,13},{10,... | collective-permute-start | bytes 786440 | tf_op jit(solution)/shard_map/ppermute | solution.py:533
  53.7 2.4 %collective-permute-start.14 = (f32[44,128]{1,0:T(8,128)S(1)}, f32[44,128]{1,0:T(8,128)S(1)}, u32[]{:S(2)}, u32[]{:S(2)}) collective-permute-start(f32[44,128]{1,0:T(8,128)S(1)} %get-tuple-element.107), channel_id=1, source_target_pairs={{0,1},{1,0},{2,3},{3,2},{4,5},{5,4},{6,7},{7,6},{8,9},{9,8},{10,11... | collective-permute-start | bytes 67592 | tf_op jit(solution)/shard_map/ppermute | solution.py:533
  54.8 23.4 %copy-start.2 = (f32[512,128]{1,0:T(8,128)S(1)}, f32[512,128]{1,0:T(8,128)}, u32[]{:S(2)}) copy-start(f32[512,128]{1,0:T(8,128)} %refs_0_.1) | copy-start | bytes 786436
  54.8 23.4 %copy-start.3 = (f32[128,512]{1,0:T(8,128)S(1)}, f32[128,512]{1,0:T(8,128)}, u32[]{:S(2)}) copy-start(f32[128,512]{1,0:T(8,128)} %refs_6_.1) | copy-start | bytes 786436
  54.8 23.4 %copy-start.4 = (f32[512,128]{1,0:T(8,128)S(1)}, f32[512,128]{1,0:T(8,128)}, u32[]{:S(2)}) copy-start(f32[512,128]{1,0:T(8,128)} %refs_1_.1) | copy-start | bytes 786436
  54.8 23.4 %copy-start.5 = (f32[512,128]{1,0:T(8,128)S(1)}, f32[512,128]{1,0:T(8,128)}, u32[]{:S(2)}) copy-start(f32[512,128]{1,0:T(8,128)} %refs_2_.1) | copy-start | bytes 786436
  54.8 23.4 %copy-start.6 = (f32[128,512]{1,0:T(8,128)S(1)}, f32[128,512]{1,0:T(8,128)}, u32[]{:S(2)}) copy-start(f32[128,512]{1,0:T(8,128)} %refs_7_.1) | copy-start | bytes 786436
  54.8 23.4 %copy-start.7 = (f32[128,512]{1,0:T(8,128)S(1)}, f32[128,512]{1,0:T(8,128)}, u32[]{:S(2)}) copy-start(f32[128,512]{1,0:T(8,128)} %refs_8_.1) | copy-start | bytes 786436
  54.9 23.4 %copy-start.11 = (f32[7,512]{1,0:T(8,128)S(1)}, f32[7,512]{1,0:T(8,128)}, u32[]{:S(2)}) copy-start(f32[7,512]{1,0:T(8,128)} %refs_10_.1) | copy-start | bytes 43012
  54.9 23.4 %copy-start.12 = (f32[7,512]{1,0:T(8,128)S(1)}, f32[7,512]{1,0:T(8,128)}, u32[]{:S(2)}) copy-start(f32[7,512]{1,0:T(8,128)} %refs_11_.1) | copy-start | bytes 43012
  54.9 23.4 %copy-start.13 = (f32[2048]{0:T(1024)S(1)}, f32[2048]{0:T(1024)}, u32[]{:S(2)}) copy-start(f32[2048]{0:T(1024)} %param.24) | copy-start | bytes 24580
  54.9 23.4 %copy-start.14 = (f32[2048]{0:T(1024)S(1)}, f32[2048]{0:T(1024)}, u32[]{:S(2)}) copy-start(f32[2048]{0:T(1024)} %param.25) | copy-start | bytes 24580
  54.9 14.3 %collective-permute-start.16 = (bf16[2,512,128]{2,1,0:T(8,128)(2,1)S(1)}, bf16[2,512,128]{2,1,0:T(8,128)(2,1)S(1)}, u32[]{:S(2)}, u32[]{:S(2)}) collective-permute-start(bf16[2,512,128]{2,1,0:T(8,128)(2,1)S(1)} %add_convert_fusion.1), channel_id=1, source_target_pairs={{0,8},{1,9},{2,10},{3,11},{4,12},{5,13},{6,14},{7,15},{8,0},{9,1},... | collective-permute-start | bytes 786440 | tf_op jit(solution)/shard_map/ppermute | solution.py:529
  56.1 13.1 %collective-permute-start.15 = (bf16[2,512,128]{2,1,0:T(8,128)(2,1)S(1)}, bf16[2,512,128]{2,1,0:T(8,128)(2,1)S(1)}, u32[]{:S(2)}, u32[]{:S(2)}) collective-permute-start(bf16[2,512,128]{2,1,0:T(8,128)(2,1)S(1)} %add_convert_fusion.2), channel_id=1, source_target_pairs={{0,2},{1,3},{2,0},{3,1},{4,6},{5,7},{6,4},{7,5},{8,10},{9,11},{10,... | collective-permute-start | bytes 786440 | tf_op jit(solution)/shard_map/ppermute | solution.py:533
  57.2 7.6 %collective-permute-start.17 = (f32[44,128]{1,0:T(8,128)S(1)}, f32[44,128]{1,0:T(8,128)S(1)}, u32[]{:S(2)}, u32[]{:S(2)}) collective-permute-start(f32[44,128]{1,0:T(8,128)S(1)} %add.37), channel_id=1, source_target_pairs={{0,2},{1,3},{2,0},{3,1},{4,6},{5,7},{6,4},{7,5},{8,10},{9,11},{10,... | collective-permute-start | bytes 67592 | tf_op jit(solution)/shard_map/ppermute | solution.py:533
  64.8 3.8 %collective-permute-start.18 = (f32[44,128]{1,0:T(8,128)S(1)}, f32[44,128]{1,0:T(8,128)S(1)}, u32[]{:S(2)}, u32[]{:S(2)}) collective-permute-start(f32[44,128]{1,0:T(8,128)S(1)} %add.44), channel_id=1, source_target_pairs={{0,16},{16,0},{1,17},{17,1},{2,18},{18,2},{3,19},{19,3},{4,20},{20... | collective-permute-start | bytes 67592 | tf_op jit(solution)/shard_map/ppermute | solution.py:541
  69.4 8.8 %collective-permute-start.19 = (bf16[2,512,128]{2,1,0:T(8,128)(2,1)S(1)}, bf16[2,512,128]{2,1,0:T(8,128)(2,1)S(1)}, u32[]{:S(2)}, u32[]{:S(2)}) collective-permute-start(bf16[2,512,128]{2,1,0:T(8,128)(2,1)S(1)} %add_convert_fusion.own_ref), channel_id=1, source_target_pairs={{0,16},{16,0},{1,17},{17,1},{2,18},{18,2},{3,19},{19,3},{4,20},{20... | collective-permute-start | bytes 786440 | tf_op jit(solution)/shard_map/ppermute | solution.py:541
  69.7 3.8 %collective-permute-start.20 = (f32[44,128]{1,0:T(8,128)S(1)}, f32[44,128]{1,0:T(8,128)S(1)}, u32[]{:S(2)}, u32[]{:S(2)}) collective-permute-start(f32[44,128]{1,0:T(8,128)S(1)} %add.45), channel_id=1, source_target_pairs={{0,4},{1,5},{2,6},{3,7},{4,0},{5,1},{6,2},{7,3},{8,12},{9,13},{10,... | collective-permute-start | bytes 67592 | tf_op jit(solution)/shard_map/ppermute | solution.py:533
  73.5 4.7 %collective-permute-start.21 = (f32[44,128]{1,0:T(8,128)S(1)}, f32[44,128]{1,0:T(8,128)S(1)}, u32[]{:S(2)}, u32[]{:S(2)}) collective-permute-start(f32[44,128]{1,0:T(8,128)S(1)} %add.46), channel_id=1, source_target_pairs={{0,8},{1,9},{2,10},{3,11},{4,12},{5,13},{6,14},{7,15},{8,0},{9,1},... | collective-permute-start | bytes 67592 | tf_op jit(solution)/shard_map/ppermute | solution.py:533
